TPU v7x, 128 devices: a whole 4x4x4 slice. The times are simulated.
128 devices in a mesh: row: 8 (over z, core), col: 16 (over y, x).
Axes of the slice: x: 4, y: 4, z: 4, core: 2. Of those that a mesh axis runs over, the one named last changes fastest.
Arguments:
- block_cells: float32 [1408, 5, 16, 256], P(('row', 'col')), may hold values from -0.6 to 1.4, as said below
- slot_blocks: int32 [128, 11], replicated, may hold values from -1 to 767, as said below
Outputs:
- new_cells: float32 [896, 5, 16, 256], P(('row', 'col'))
Inputs may be any that keep to these rules, and one draw needn't show every extreme that they name: `slot_blocks`: row r * 16 + c lists the blocks held by device (r, c): block ids first, in slot order, then -1. Block b belongs to column group b // 48, and every block of column group c is held by exactly one device of that column group. Each device holds 1 to 11 blocks, the devices of a column group hold 48 blocks together, and in every column group one device holds 11 blocks and one holds 1. `block_cells`: fields 0 and 4 (density, pressure) lie in 0.7 to 1.4 and fields 1 to 3 (velocity) in -0.6 to 0.6. Slots marked -1 in slot_blocks hold values that no output depends on.
All inputs are finite; a program needn't handle non-finite values.
Results may differ from a plain program's by a relative error of at most 0.0001.
Values sent between devices are 32-bit elements; how exact they have to be, the bound alone decides.
No kernel may reach another device: no remote copies, remote signals or barrier semaphores. Data moves between devices by JAX's collectives and lax.ppermute only.
A program may use at most 64 MiB of HBM per device.

v0:
```python
import jax
import jax.numpy as jnp
from jax import lax
from jax.sharding import PartitionSpec as P

BLK_MEAN = 6
OUT = 7


heat_ratio = 1.4
time_step = 0.12
thermal_leading_multiplier = 0.2
thermal_power_law_index = 0.7


def swapped(array, axis, apart):
    return lax.ppermute(array, axis, [(i, i ^ 1 << apart) for i in range(lax.axis_size(axis))])


def from_behind(block, axis, distance):
    devices = range(lax.axis_size(axis))
    route = [((i - distance) % len(devices), i) for i in devices]
    return lax.ppermute(block, axis, route)


def laid_out(pieces, dim):
    dims = list(pieces.shape[1:])
    dims[dim] *= pieces.shape[0]
    return jnp.moveaxis(pieces, 0, dim).reshape(dims)


def one_gather(arrays, axis, dims):
    line = jnp.concatenate([a.reshape(-1) for a in arrays])
    lines, at, outs = (lax.all_gather(line, axis), 0, [])
    for a, dim in zip(arrays, dims):
        pieces = lines[:, at : at + a.size].reshape(-1, *a.shape)
        outs.append(laid_out(pieces, dim))
        at += a.size
    return tuple(outs)


def rebalance_table(anchors, counts):
    row_count, columns, slot_width = anchors.shape
    slot_ids = jnp.arange(slot_width, dtype=jnp.int32)
    row_ids = jnp.arange(row_count, dtype=jnp.int32)
    for section_bit in range(row_count.bit_length() - 1):
        partner = row_ids ^ 1 << section_bit
        other_anchors = anchors[partner]
        other_counts = counts[partner]
        sending = jnp.maximum(counts - other_counts, 0) // 2
        taking = jnp.maximum(other_counts - counts, 0) // 2
        keeping = (counts - sending)[:, :, None]
        anchor_slot = other_counts[:, :, None] - taking[:, :, None] + slot_ids - keeping
        pulled = jnp.take_along_axis(
            other_anchors, jnp.clip(anchor_slot, 0, slot_width - 1), axis=2
        )
        anchors = jnp.where(
            slot_ids < keeping,
            anchors,
            jnp.where(slot_ids < keeping + taking[:, :, None], pulled, -1),
        )
        counts = counts - sending + taking
    return (anchors, counts)


def to_conserved(primitive):
    matter_per_volume = primitive[0]
    velocity = primitive[1:4]
    fluid_static_stress = primitive[4]
    energy = fluid_static_stress / (heat_ratio - 1.0) + 0.5 * matter_per_volume * jnp.sum(
        velocity * velocity, axis=0
    )
    return jnp.concatenate(
        [matter_per_volume[None], matter_per_volume[None] * velocity, energy[None]], axis=0
    )


def to_primitive(conserved):
    matter_per_volume = conserved[0]
    velocity = conserved[1:4] / matter_per_volume
    fluid_static_stress = (heat_ratio - 1.0) * (
        conserved[4] - 0.5 * matter_per_volume * jnp.sum(velocity * velocity, axis=0)
    )
    return jnp.concatenate([matter_per_volume[None], velocity, fluid_static_stress[None]], axis=0)


def cell_terms(conserved, normal):
    matter_per_volume = conserved[0]
    momentum = conserved[1:4]
    velocity = momentum / matter_per_volume
    fluid_static_stress = (heat_ratio - 1.0) * (
        conserved[4] - 0.5 * matter_per_volume * jnp.sum(velocity * velocity, axis=0)
    )
    perpendicular_flow_rate = velocity[normal]
    moment_flux = momentum * perpendicular_flow_rate
    moment_flux = moment_flux.at[normal].add(fluid_static_stress)
    face_transport_amounts = jnp.concatenate(
        [
            momentum[normal][None],
            moment_flux,
            ((conserved[4] + fluid_static_stress) * perpendicular_flow_rate)[None],
        ],
        axis=0,
    )
    sound_signal_rate = jnp.sqrt(heat_ratio * fluid_static_stress / matter_per_volume)
    fluid_thermal_state = fluid_static_stress / matter_per_volume
    thermal_diffusivity_factor = thermal_leading_multiplier * jnp.power(
        fluid_thermal_state, thermal_power_law_index
    )
    return (
        face_transport_amounts,
        jnp.abs(perpendicular_flow_rate) + sound_signal_rate,
        fluid_thermal_state,
        thermal_diffusivity_factor,
        fluid_static_stress,
    )


def face_flux(lower_cons, lower_data, upper_cons, upper_data):
    wave_speed = jnp.maximum(lower_data[1], upper_data[1])
    face_transport_amounts = 0.5 * (lower_data[0] + upper_data[0]) - 0.5 * wave_speed[None] * (
        upper_cons - lower_cons
    )
    heat_flow = 0.5 * (lower_data[3] + upper_data[3]) * (upper_data[2] - lower_data[2])
    return face_transport_amounts.at[4].add(-heat_flow)


def wall_flux(fluid_static_stress, normal):
    nothing = jnp.zeros_like(fluid_static_stress)
    members = [nothing, nothing, nothing, nothing, nothing]
    members[normal + 1] = fluid_static_stress
    return jnp.stack(members, axis=0)


def cut_rows(tree, first_index, last_index):
    return jax.tree.map(lambda member: member[..., first_index:last_index, :], tree)


def cut_flat(tree, first_index, last_index):
    return jax.tree.map(lambda member: member[..., first_index:last_index], tree)


def block_tendency(conserved, low_x, high_x, low_y, high_y):
    block_edge = conserved.shape[1]
    flat_size = conserved.shape[2]
    padded_x = jnp.concatenate([low_x, conserved, high_x], axis=1)
    cell_data = cell_terms(padded_x, 0)
    face_transport_amounts = face_flux(
        padded_x[:, :-1],
        cut_rows(cell_data, 0, block_edge + 1),
        padded_x[:, 1:],
        cut_rows(cell_data, 1, block_edge + 2),
    )
    change_x = face_transport_amounts[:, 1:] - face_transport_amounts[:, :-1]
    padded_y = jnp.concatenate([low_y, conserved, high_y], axis=2)
    cell_data = cell_terms(padded_y, 1)
    reach_end = flat_size + block_edge
    face_transport_amounts = face_flux(
        padded_y[..., :reach_end],
        cut_flat(cell_data, 0, reach_end),
        padded_y[..., block_edge:],
        cut_flat(cell_data, block_edge, reach_end + block_edge),
    )
    change_y = face_transport_amounts[..., block_edge:] - face_transport_amounts[..., :flat_size]
    cell_data = cell_terms(conserved, 2)
    interior = face_flux(
        conserved[..., :-1],
        cut_flat(cell_data, 0, flat_size - 1),
        conserved[..., 1:],
        cut_flat(cell_data, 1, flat_size),
    )
    nothing = jnp.zeros_like(interior[..., :1])
    wall_values = wall_flux(cell_data[4], 2)
    height = jnp.arange(flat_size, dtype=jnp.int32) % block_edge
    upper_face = jnp.where(
        height == block_edge - 1, wall_values, jnp.concatenate([interior, nothing], axis=-1)
    )
    lower_face = jnp.where(height == 0, wall_values, jnp.concatenate([nothing, interior], axis=-1))
    change_z = upper_face - lower_face
    return -(change_x + change_y + change_z)


def body(block_cells, slot_blocks):
    row_count = lax.axis_size("row")
    columns = lax.axis_size("col")
    my_row = lax.axis_index("row")
    my_col = lax.axis_index("col")
    slot_width = slot_blocks.shape[1]
    per_group = BLK_MEAN * row_count
    send_slots = BLK_MEAN - 1
    block_edge = block_cells.shape[2]
    flat_size = block_cells.shape[3]
    every_slot = slot_blocks.reshape(-1)
    occupied = slot_blocks >= 0
    counts = jnp.sum(occupied.astype(jnp.int32), axis=1).reshape(row_count, columns)
    device_ids = jnp.arange(row_count * columns, dtype=jnp.int32)[:, None]
    anchors = jnp.where(
        occupied, device_ids * slot_width + jnp.arange(slot_width, dtype=jnp.int32)[None, :], -1
    )
    anchors = anchors.reshape(row_count, columns, slot_width)
    final_anchors, final_counts = rebalance_table(anchors, counts)
    final_anchors = final_anchors[:, :, :OUT]
    my_anchors = final_anchors[my_row, my_col]
    row_ids = jnp.arange(row_count, dtype=jnp.int32)
    holding = block_cells
    counts_now = counts
    slot_ids = jnp.arange(slot_width, dtype=jnp.int32)
    for section_bit in range(row_count.bit_length() - 1):
        partner = row_ids ^ 1 << section_bit
        other_counts = counts_now[partner]
        sending = jnp.maximum(counts_now - other_counts, 0) // 2
        taking = jnp.maximum(other_counts - counts_now, 0) // 2
        keeping = counts_now[my_row, my_col] - sending[my_row, my_col]
        send_from = jnp.clip(keeping + jnp.arange(send_slots, dtype=jnp.int32), 0, slot_width - 1)
        outgoing = jnp.take(holding, send_from, axis=0)
        incoming = swapped(outgoing, "row", section_bit)
        candidates = jnp.concatenate([holding, incoming], axis=0)
        chosen = jnp.where(
            slot_ids < keeping,
            slot_ids,
            slot_width + jnp.clip(slot_ids - keeping, 0, send_slots - 1),
        )
        holding = jnp.take(candidates, chosen, axis=0)
        counts_now = counts_now - sending + taking
    holding = holding[:OUT]
    active = my_anchors >= 0
    benign = jnp.array([1.0, 0.0, 0.0, 0.0, 1.0], jnp.float32)[None, :, None, None]
    holding = jnp.where(active[:, None, None, None], holding, benign)
    initial = jax.vmap(to_conserved)(holding)
    my_blocks = every_slot[jnp.maximum(my_anchors, 0)]
    along_y = jnp.clip(my_blocks - my_col * per_group, 0, per_group - 1)
    below_col = (my_col - 1) % columns
    above_col = (my_col + 1) % columns

    def located(column, wanted):
        anchors_here = final_anchors[:, column].reshape(-1)
        blocks_here = jnp.where(anchors_here >= 0, every_slot[jnp.maximum(anchors_here, 0)], -1)
        return jnp.argmax(blocks_here[None, :] == wanted[:, None], axis=1)

    from_x_low = located(below_col, below_col * per_group + along_y)
    from_y_low = located(below_col, below_col * per_group + (along_y - 1) % per_group)
    from_x_high = located(above_col, above_col * per_group + along_y)
    from_y_high = located(above_col, above_col * per_group + (along_y + 1) % per_group)

    def section_rate(current):
        highs = jnp.stack(
            [
                current[:, :, block_edge - 1, :],
                current[:, :, :, flat_size - block_edge :].reshape(OUT, 5, flat_size),
            ],
            axis=1,
        )
        lows = jnp.stack(
            [current[:, :, 0, :], current[:, :, :, :block_edge].reshape(OUT, 5, flat_size)], axis=1
        )
        passed_highs = from_behind(highs, "col", 1)
        passed_lows = from_behind(lows, "col", -1)
        from_below, from_above = one_gather((passed_highs, passed_lows), "row", (0, 0))
        low_x = from_below[from_x_low, 0][:, :, None, :]
        low_y = from_below[from_y_low, 1].reshape(OUT, 5, block_edge, block_edge)
        high_x = from_above[from_x_high, 0][:, :, None, :]
        high_y = from_above[from_y_high, 1].reshape(OUT, 5, block_edge, block_edge)
        return jax.vmap(block_tendency)(current, low_x, high_x, low_y, high_y)

    first_section = initial + time_step * section_rate(initial)
    second_section = 0.75 * initial + 0.25 * (
        first_section + time_step * section_rate(first_section)
    )
    third_section = 1.0 / 3.0 * initial + 2.0 / 3.0 * (
        second_section + time_step * section_rate(second_section)
    )
    result = jax.vmap(to_primitive)(third_section)
    return jnp.where(active[:, None, None, None], result, jnp.zeros_like(result)).astype(
        jnp.float32
    )


def solution(mesh):
    in_specs = (P(("row", "col"), None, None, None), P())
    out_specs = P(("row", "col"), None, None, None)
    return jax.shard_map(body, mesh=mesh, in_specs=in_specs, out_specs=out_specs, check_vma=False)
```

profile of v0, /device:TPU:1, one launch (start us, length us, event | category | flops | bytes accessed | tf_op | source)
XLA Modules:
  0.0 243.3 jit_solution(14504656601221737455)
XLA Ops:
  6.6 0.7 add_select_fusion
  7.9 0.6 dynamic_slice.30
  8.5 0.6 dynamic_slice.31
  10.5 1.7 gather_fusion.24
  12.3 1.5 collective-permute-start
  13.9 0.6 dynamic_slice.32
  15.0 0.6 dynamic_slice.33
  17.0 0.7 dynamic_slice.34
  18.2 0.6 dynamic_slice.35
  21.9 11.7 %gather_fusion.21 = s32[1408]{0:T(1024)S(1)} fusion(s32[8,16,11]{2,1,0:T(8,128)S(1)} %gather_fusion.3, s32[1408]{0:T(1024)S(1)} %reshape.1318), kind=kCustom, calls=%fused_computation.clone | custom fusion | bytes 28160 | tf_op jit(solution)/shard_map/jit(take_along_axis)/gather | solution.py:54
  34.5 11.7 %gather_fusion.22 = s32[1408]{0:T(1024)S(1)} fusion(s32[8,16,11]{2,1,0:T(8,128)S(1)} %gather_fusion.4, s32[1408]{0:T(1024)S(1)} %reshape.1323), kind=kCustom, calls=%fused_computation.3.clone | custom fusion | bytes 28160 | tf_op jit(solution)/shard_map/jit(take_along_axis)/gather | solution.py:54
  47.1 11.7 %gather_fusion.23 = s32[1408]{0:T(1024)S(1)} fusion(s32[8,16,11]{2,1,0:T(8,128)S(1)} %gather_fusion.5, s32[1408]{0:T(1024)S(1)} %reshape.1328), kind=kCustom, calls=%fused_computation.4.clone | custom fusion | bytes 28160 | tf_op jit(solution)/shard_map/jit(take_along_axis)/gather | solution.py:54
  60.0 0.8 gather_fusion.9
  60.8 0.6 gather_fusion.7
  61.4 0.8 gather_fusion.6
  62.4 0.6 gather_fusion.25
  63.8 1.8 collective-permute-start.1
  65.6 9.7 %collective-permute-done.1 = f32[5,5,16,256]{3,2,1,0:T(8,128)S(1)} collective-permute-done((f32[5,5,16,256]{3,2,1,0:T(8,128)S(1)}, f32[5,5,16,256]{3,2,1,0:T(8,128)S(1)}, u32[]{:S(2)}, u32[]{:S(2)}) %collective-permute-start.1) | collective-permute-done | bytes 409632 | tf_op jit(solution)/shard_map/ppermute | solution.py:17
  75.5 0.6 gather_fusion.27
  76.9 3.3 %collective-permute-start.2 = (f32[5,5,16,256]{3,2,1,0:T(8,128)S(1)}, f32[5,5,16,256]{3,2,1,0:T(8,128)S(1)}, u32[]{:S(2)}, u32[]{:S(2)}) collective-permute-start(f32[5,5,16,256]{3,2,1,0:T(8,128)S(1)} %broadcast_select_fusion.2), channel_id=1, source_target_pairs={{0,64},{16,80},{32,96},{48,112},{64,0},{80,16},{96,32},{112,48},{1... | collective-permute-start | bytes 1228808 | tf_op jit(solution)/shard_map/ppermute | solution.py:17
  80.2 0.7 iota_reduce_fusion.2
  80.9 8.3 %collective-permute-done.2 = f32[5,5,16,256]{3,2,1,0:T(8,128)S(1)} collective-permute-done((f32[5,5,16,256]{3,2,1,0:T(8,128)S(1)}, f32[5,5,16,256]{3,2,1,0:T(8,128)S(1)}, u32[]{:S(2)}, u32[]{:S(2)}) %collective-permute-start.2) | collective-permute-done | bytes 409632 | tf_op jit(solution)/shard_map/ppermute | solution.py:17
  89.3 0.6 gather_fusion.29
  90.5 0.7 fusion.227
  91.5 0.8 copy.198
  92.6 5.0 %collective-permute-start.4 = (f32[7,2,5,256]{3,1,2,0:T(2,128)S(1)}, f32[7,2,5,256]{3,1,2,0:T(2,128)S(1)}, u32[]{:S(2)}, u32[]{:S(2)}) collective-permute-start(f32[7,2,5,256]{3,1,2,0:T(2,128)S(1)} %pad_maximum_fusion.33), channel_id=1, source_target_pairs={{1,0},{2,1},{3,2},{4,3},{5,4},{6,5},{7,6},{8,7},{9,8},{10,9},{11,1... | collective-permute-start | bytes 215048 | tf_op jit(solution)/shard_map/ppermute | solution.py:23
  97.7 0.7 iota_reduce_fusion.3
  99.0 5.2 %collective-permute-done.3 = f32[7,2,5,256]{3,1,2,0:T(2,128)S(1)} collective-permute-done((f32[7,2,5,256]{3,1,2,0:T(2,128)S(1)}, f32[7,2,5,256]{3,1,2,0:T(2,128)S(1)}, u32[]{:S(2)}, u32[]{:S(2)}) %collective-permute-start.3) | collective-permute-done | bytes 71712 | tf_op jit(solution)/shard_map/ppermute | solution.py:23
  104.3 0.7 pad_maximum_fusion.29
  105.2 0.6 broadcast_compare_fusion.1
  105.8 0.6 pad.119.clone
  106.5 0.7 iota_reduce_fusion
  107.2 0.7 iota_reduce_fusion.1
  108.7 19.4 %all-gather.7.cloned.1.call-done = f32[286720]{0:T(1024)} async-done(((f32[35840]{0:T(1024)}), f32[286720]{0:T(1024)}) %all-gather.7.cloned.1.call-update) | async-done | bytes 1146896 | tf_op jit(solution)/shard_map/all_gather | solution.py:34
  128.2 1.4 reshape.1262
  129.6 0.9 fusion.219
  130.5 2.3 reshape_reshape.18
  132.8 1.8 gather_fusion.11
  134.8 1.2 reshape_reshape.19
  136.0 1.8 gather_fusion.12
  138.4 1.8 gather_fusion.8
  140.2 1.8 gather_fusion.10
  146.6 4.7 %collective-permute-start.6 = (f32[7,2,5,256]{3,1,2,0:T(2,128)S(1)}, f32[7,2,5,256]{3,1,2,0:T(2,128)S(1)}, u32[]{:S(2)}, u32[]{:S(2)}) collective-permute-start(f32[7,2,5,256]{3,1,2,0:T(2,128)S(1)} %pad_maximum_fusion.35), channel_id=1, source_target_pairs={{1,0},{2,1},{3,2},{4,3},{5,4},{6,5},{7,6},{8,7},{9,8},{10,9},{11,1... | collective-permute-start | bytes 215048 | tf_op jit(solution)/shard_map/ppermute | solution.py:23
  151.4 1.2 collective-permute-done.6
  152.6 5.2 %collective-permute-done.5 = f32[7,2,5,256]{3,1,2,0:T(2,128)S(1)} collective-permute-done((f32[7,2,5,256]{3,1,2,0:T(2,128)S(1)}, f32[7,2,5,256]{3,1,2,0:T(2,128)S(1)}, u32[]{:S(2)}, u32[]{:S(2)}) %collective-permute-start.5) | collective-permute-done | bytes 71712 | tf_op jit(solution)/shard_map/ppermute | solution.py:23
  157.9 0.7 pad_maximum_fusion.30
  159.0 0.6 copy-done.3
  160.4 18.6 %all-gather.9.cloned.1.call-done = f32[286720]{0:T(1024)} async-done(((f32[35840]{0:T(1024)}), f32[286720]{0:T(1024)}) %all-gather.9.cloned.1.call-update) | async-done | bytes 1146896 | tf_op jit(solution)/shard_map/all_gather | solution.py:34
  179.0 1.4 reshape.1263
  180.5 0.9 fusion.218
  181.4 1.4 reshape_reshape.20
  183.3 0.6 gather_fusion.13
  184.2 0.6 gather_fusion.16
  191.1 4.7 %collective-permute-start.8 = (f32[7,2,5,256]{3,1,2,0:T(2,128)S(1)}, f32[7,2,5,256]{3,1,2,0:T(2,128)S(1)}, u32[]{:S(2)}, u32[]{:S(2)}) collective-permute-start(f32[7,2,5,256]{3,1,2,0:T(2,128)S(1)} %pad_maximum_fusion.37), channel_id=1, source_target_pairs={{1,0},{2,1},{3,2},{4,3},{5,4},{6,5},{7,6},{8,7},{9,8},{10,9},{11,1... | collective-permute-start | bytes 215048 | tf_op jit(solution)/shard_map/ppermute | solution.py:23
  196.2 0.9 collective-permute-done.8
  197.2 5.5 %collective-permute-done.7 = f32[7,2,5,256]{3,1,2,0:T(2,128)S(1)} collective-permute-done((f32[7,2,5,256]{3,1,2,0:T(2,128)S(1)}, f32[7,2,5,256]{3,1,2,0:T(2,128)S(1)}, u32[]{:S(2)}, u32[]{:S(2)}) %collective-permute-start.7) | collective-permute-done | bytes 71712 | tf_op jit(solution)/shard_map/ppermute | solution.py:23
  202.7 0.7 pad_maximum_fusion.31
  203.6 0.6 copy-done.1
  205.0 18.9 %all-gather.11.cloned.1.call-done = f32[286720]{0:T(1024)} async-done(((f32[35840]{0:T(1024)}), f32[286720]{0:T(1024)}) %all-gather.11.cloned.1.call-update) | async-done | bytes 1146896 | tf_op jit(solution)/shard_map/all_gather | solution.py:34
  223.8 1.4 reshape.1264
  225.3 0.9 fusion.217
  226.2 1.4 reshape_reshape.22
  234.6 0.6 fusion.47
  236.0 0.8 copy.176
  (329 shorter events, 33.9 us)
Async XLA Ops:
  6.5 121.6 %all-gather.7.cloned.1.call-start = ((), (), s32[]{:S(2)}) async-start(), calls=%async_computation | async-start | bytes 1290240 | tf_op jit(solution)/shard_map/all_gather | solution.py:34
  12.3 49.9 %collective-permute-start = (f32[5,5,16,256]{3,2,1,0:T(8,128)S(1)}, f32[5,5,16,256]{3,2,1,0:T(8,128)S(1)}, u32[]{:S(2)}, u32[]{:S(2)}) collective-permute-start(f32[5,5,16,256]{3,2,1,0:T(8,128)S(1)} %broadcast_select_fusion.4), channel_id=1, source_target_pairs={{0,16},{16,0},{32,48},{48,32},{64,80},{80,64},{96,112},{112,96},{1... | collective-permute-start | bytes 1228808 | tf_op jit(solution)/shard_map/ppermute | solution.py:17
  47.1 12.2 %copy-start.17 = (s32[128,11]{0,1:T(8,128)S(1)}, s32[128,11]{0,1:T(8,128)}, u32[]{:S(2)}) copy-start(s32[128,11]{0,1:T(8,128)} %param.46) | copy-start | bytes 16900
  58.8 3.5 %copy-start = (f32[11,5,16,256]{3,2,1,0:T(8,128)S(1)}, f32[11,5,16,256]{3,2,1,0:T(8,128)}, u32[]{:S(2)}) copy-start(f32[11,5,16,256]{3,2,1,0:T(8,128)} %param.45) | copy-start | bytes 2703364
  62.2 27.7 %copy-start.18 = (pred[7]{0:T(512)(128)(4,1)}, pred[7]{0:T(512)(128)(4,1)S(1)}, u32[]{:S(2)}) copy-start(pred[7]{0:T(512)(128)(4,1)S(1)} %compare_bitcast_fusion) | copy-start | bytes 25
  63.8 11.6 %collective-permute-start.1 = (f32[5,5,16,256]{3,2,1,0:T(8,128)S(1)}, f32[5,5,16,256]{3,2,1,0:T(8,128)S(1)}, u32[]{:S(2)}, u32[]{:S(2)}) collective-permute-start(f32[5,5,16,256]{3,2,1,0:T(8,128)S(1)} %broadcast_select_fusion.3), channel_id=1, source_target_pairs={{0,32},{16,48},{32,0},{48,16},{64,96},{80,112},{96,64},{112,80},{1... | collective-permute-start | bytes 1228808 | tf_op jit(solution)/shard_map/ppermute | solution.py:17
  76.9 12.3 %collective-permute-start.2 = (f32[5,5,16,256]{3,2,1,0:T(8,128)S(1)}, f32[5,5,16,256]{3,2,1,0:T(8,128)S(1)}, u32[]{:S(2)}, u32[]{:S(2)}) collective-permute-start(f32[5,5,16,256]{3,2,1,0:T(8,128)S(1)} %broadcast_select_fusion.2), channel_id=1, source_target_pairs={{0,64},{16,80},{32,96},{48,112},{64,0},{80,16},{96,32},{112,48},{1... | collective-permute-start | bytes 1228808 | tf_op jit(solution)/shard_map/ppermute | solution.py:17
  89.3 0.7 copy-start.29
  92.6 6.4 %collective-permute-start.4 = (f32[7,2,5,256]{3,1,2,0:T(2,128)S(1)}, f32[7,2,5,256]{3,1,2,0:T(2,128)S(1)}, u32[]{:S(2)}, u32[]{:S(2)}) collective-permute-start(f32[7,2,5,256]{3,1,2,0:T(2,128)S(1)} %pad_maximum_fusion.33), channel_id=1, source_target_pairs={{1,0},{2,1},{3,2},{4,3},{5,4},{6,5},{7,6},{8,7},{9,8},{10,9},{11,1... | collective-permute-start | bytes 215048 | tf_op jit(solution)/shard_map/ppermute | solution.py:23
  97.7 6.6 %collective-permute-start.3 = (f32[7,2,5,256]{3,1,2,0:T(2,128)S(1)}, f32[7,2,5,256]{3,1,2,0:T(2,128)S(1)}, u32[]{:S(2)}, u32[]{:S(2)}) collective-permute-start(f32[7,2,5,256]{3,1,2,0:T(2,128)S(1)} %pad_maximum_fusion.32), channel_id=1, source_target_pairs={{15,0},{0,1},{1,2},{2,3},{3,4},{4,5},{5,6},{6,7},{7,8},{8,9},{9,10... | collective-permute-start | bytes 215048 | tf_op jit(solution)/shard_map/ppermute | solution.py:23
  105.0 74.1 %all-gather.9.cloned.1.call-start = ((), (), s32[]{:S(2)}) async-start(), calls=%async_computation.1 | async-start | bytes 1290240 | tf_op jit(solution)/shard_map/all_gather | solution.py:34
  106.5 32.0 %copy-start.8 = (s32[7]{0:T(128)}, s32[7]{0:T(128)S(1)}, u32[]{:S(2)}) copy-start(s32[7]{0:T(128)S(1)} %get-tuple-element.352) | copy-start | bytes 88
  106.5 33.8 %copy-start.5 = (s32[7]{0:T(128)}, s32[7]{0:T(128)S(1)}, u32[]{:S(2)}) copy-start(s32[7]{0:T(128)S(1)} %get-tuple-element.353) | copy-start | bytes 88
  107.9 24.9 %copy-start.14 = (s32[7]{0:T(128)}, s32[7]{0:T(128)S(1)}, u32[]{:S(2)}) copy-start(s32[7]{0:T(128)S(1)} %get-tuple-element.354) | copy-start | bytes 88
  107.9 28.1 %copy-start.11 = (s32[7]{0:T(128)}, s32[7]{0:T(128)S(1)}, u32[]{:S(2)}) copy-start(s32[7]{0:T(128)S(1)} %get-tuple-element.355) | copy-start | bytes 88
  144.6 0.6 copy-start.20
  144.6 0.7 copy-start.23
  144.6 0.7 copy-start.26
  146.6 6.0 %collective-permute-start.6 = (f32[7,2,5,256]{3,1,2,0:T(2,128)S(1)}, f32[7,2,5,256]{3,1,2,0:T(2,128)S(1)}, u32[]{:S(2)}, u32[]{:S(2)}) collective-permute-start(f32[7,2,5,256]{3,1,2,0:T(2,128)S(1)} %pad_maximum_fusion.35), channel_id=1, source_target_pairs={{1,0},{2,1},{3,2},{4,3},{5,4},{6,5},{7,6},{8,7},{9,8},{10,9},{11,1... | collective-permute-start | bytes 215048 | tf_op jit(solution)/shard_map/ppermute | solution.py:23
  151.3 6.6 %collective-permute-start.5 = (f32[7,2,5,256]{3,1,2,0:T(2,128)S(1)}, f32[7,2,5,256]{3,1,2,0:T(2,128)S(1)}, u32[]{:S(2)}, u32[]{:S(2)}) collective-permute-start(f32[7,2,5,256]{3,1,2,0:T(2,128)S(1)} %pad_maximum_fusion.34), channel_id=1, source_target_pairs={{15,0},{0,1},{1,2},{2,3},{3,4},{4,5},{5,6},{6,7},{7,8},{8,9},{9,10... | collective-permute-start | bytes 215048 | tf_op jit(solution)/shard_map/ppermute | solution.py:23
  158.6 65.2 %all-gather.11.cloned.1.call-start = ((), (), s32[]{:S(2)}) async-start(), calls=%async_computation.2 | async-start | bytes 1290240 | tf_op jit(solution)/shard_map/all_gather | solution.py:34
  159.0 0.6 copy-start.3
  181.3 1.4 copy-start.15
  181.3 2.0 copy-start.9
  181.4 2.9 %copy-start.12 = (s32[7]{0:T(128)S(1)}, s32[7]{0:T(128)}, u32[]{:S(2)}) copy-start(s32[7]{0:T(128)} %copy-done.11) | copy-start | bytes 88
  181.4 3.5 %copy-start.6 = (s32[7]{0:T(128)S(1)}, s32[7]{0:T(128)}, u32[]{:S(2)}) copy-start(s32[7]{0:T(128)} %copy-done.5) | copy-start | bytes 88
  188.9 0.9 copy-start.4
  188.9 0.9 copy-start.21
  188.9 0.9 copy-start.24
  188.9 0.9 copy-start.27
  191.1 6.0 %collective-permute-start.8 = (f32[7,2,5,256]{3,1,2,0:T(2,128)S(1)}, f32[7,2,5,256]{3,1,2,0:T(2,128)S(1)}, u32[]{:S(2)}, u32[]{:S(2)}) collective-permute-start(f32[7,2,5,256]{3,1,2,0:T(2,128)S(1)} %pad_maximum_fusion.37), channel_id=1, source_target_pairs={{1,0},{2,1},{3,2},{4,3},{5,4},{6,5},{7,6},{8,7},{9,8},{10,9},{11,1... | collective-permute-start | bytes 215048 | tf_op jit(solution)/shard_map/ppermute | solution.py:23
  195.8 6.8 %collective-permute-start.7 = (f32[7,2,5,256]{3,1,2,0:T(2,128)S(1)}, f32[7,2,5,256]{3,1,2,0:T(2,128)S(1)}, u32[]{:S(2)}, u32[]{:S(2)}) collective-permute-start(f32[7,2,5,256]{3,1,2,0:T(2,128)S(1)} %pad_maximum_fusion.36), channel_id=1, source_target_pairs={{15,0},{0,1},{1,2},{2,3},{3,4},{4,5},{5,6},{6,7},{7,8},{8,9},{9,10... | collective-permute-start | bytes 215048 | tf_op jit(solution)/shard_map/ppermute | solution.py:23
  203.5 0.6 copy-start.1
  226.2 1.4 copy-start.16
  226.2 2.0 copy-start.10
  226.2 2.9 %copy-start.13 = (s32[7]{0:T(128)S(1)}, s32[7]{0:T(128)}, u32[]{:S(2)}) copy-start(s32[7]{0:T(128)} %copy-done.11) | copy-start | bytes 88
  226.2 3.5 %copy-start.7 = (s32[7]{0:T(128)S(1)}, s32[7]{0:T(128)}, u32[]{:S(2)}) copy-start(s32[7]{0:T(128)} %copy-done.5) | copy-start | bytes 88
  233.7 0.9 copy-start.2
  233.7 0.9 copy-start.22
  233.7 0.9 copy-start.25
  233.7 0.9 copy-start.28
  235.2 0.7 copy-start.19
Sparse Core Ops, SparseCore 0:
  105.1 23.0 all-gather.6
  158.7 20.2 all-gather.8
  203.5 20.2 all-gather.10
where the time goes:
time: 244 us; the launch traced here: 243 us
  waiting for transfers between devices  93.5 us (38%)
  local copies, waits for them, and re-layouts  85.9 us (35%)
  other arithmetic  23.3 us (10%)
  starting transfers between devices  21.9 us (9%)
  between operations  18.8 us (8%)
    all_gather x3, waiting for transfers between devices, one_gather(): lines, at, outs = (lax.all_gather(line, axis), 0, [])  56.9 us
    gather x9, local copies, waits for them, and re-layouts, rebalance_table(): jnp.take_along_axis(other_anchors, jnp.clip(anchor_slot, 0, slot_width -...  36.2 us
    ppermute x6, waiting for transfers between devices, from_behind(): return lax.ppermute(block, axis, route)  18.5 us
    ppermute x3, waiting for transfers between devices, swapped(): lax.ppermute(array, axis, [(i, i ^ 1 << apart) for i in range(lax.axis_si...  18 us
    ppermute x6, starting transfers between devices, from_behind(): return lax.ppermute(block, axis, route)  14.8 us
    another operation x6, local copies, waits for them, and re-layouts, laid_out(): return jnp.moveaxis(pieces, 0, dim).reshape(dims)  6.87 us
    ppermute x3, starting transfers between devices, swapped(): lax.ppermute(array, axis, [(i, i ^ 1 << apart) for i in range(lax.axis_si...  6.61 us
  transfers between devices with their start and end apart: 12, of which 11 were waited for; matrix products, arithmetic and copies ran while one was open for 22% of the time, Pallas kernels for 0%

commit v1 on v0

v1 whole, which is shorter than its diff:
```python
import jax
import jax.numpy as jnp
from jax import lax
from jax.experimental import pallas as pl
from jax.experimental.pallas import tpu as pltpu
from jax.sharding import PartitionSpec as P

CAP = 11
OUT = 7
NBY = 48
N_ROW = 8
N_COL = 16
HALF = NBY // 2
F = 5
X = 8
L = 128
PAD = 32

GAMMA = 1.4
STEP = 0.12

VMEM = pl.BlockSpec(memory_space=pltpu.VMEM)
SMEM = pl.BlockSpec(memory_space=pltpu.SMEM)
ANY = pl.BlockSpec(memory_space=pl.ANY)
PARAMS = pltpu.CompilerParams(vmem_limit_bytes=48 * 1024 * 1024)


def shape(*dims):
    return jax.ShapeDtypeStruct(dims, jnp.float32)


def tile_x(z):
    return ((z + 1) // 2) % 2


def tile_y(z):
    return z // 2


def pack_in(pos, cells, *rest):
    outs, sems = rest[:4], rest[4]
    z = pos[0]
    copies = []
    for k in (2, 1, 3, 0):
        zk = z ^ k
        copies.append(
            pltpu.make_async_copy(
                cells.at[
                    :, :, pl.ds(pl.multiple_of(tile_x(zk) * X, X), X), pl.ds(pl.multiple_of(tile_y(zk) * L, L), L)
                ],
                outs[k],
                sems.at[k],
            )
        )
    for c in copies:
        c.start()
    for c in copies:
        c.wait()


def unpack_out(pos, *refs):
    parts, out, sems = refs[:4], refs[4], refs[5]
    z = pos[0]
    copies = []
    for k in range(4):
        zk = z ^ k
        copies.append(
            pltpu.make_async_copy(
                parts[k],
                out.at[
                    :, :, pl.ds(pl.multiple_of(tile_x(zk) * X, X), X), pl.ds(pl.multiple_of(tile_y(zk) * L, L), L)
                ],
                sems.at[k],
            )
        )
    for c in copies:
        c.start()
    for c in copies:
        c.wait()


def table(pos, slots, final, held, count):
    g = pos[2]
    for d in range(N_ROW):
        n = jnp.int32(0)
        for s in range(CAP):
            b = slots[d * N_COL + g, s]
            held[d * 16 + s] = b - g * NBY
            n = n + jnp.where(b >= 0, 1, 0)
        count[d] = n
    for bit in range(3):
        for low in range(N_ROW):
            if low >> bit & 1:
                continue
            high = low | 1 << bit
            a, b = count[low], count[high]
            up = a > b
            src = jnp.where(up, low, high)
            dst = jnp.where(up, high, low)
            n_src = jnp.maximum(a, b)
            n_dst = jnp.minimum(a, b)
            moved = (n_src - n_dst) // 2

            def move(i, _, src=src, dst=dst, n_src=n_src, n_dst=n_dst, moved=moved):
                held[dst * 16 + n_dst + i] = held[src * 16 + n_src - moved + i]
                return 0

            lax.fori_loop(0, moved, move, 0)
            count[src] = n_src - moved
            count[dst] = n_dst + moved
    for d in range(N_ROW):
        n = count[d]
        for s in range(8):
            final[d * 8 + s] = jnp.where(s < n, held[d * 16 + s], -1)


def rolled(v, shift):
    shift %= L
    return v if shift == 0 else pltpu.roll(v, shift, 1)


def terms(cons):
    rho, mx, my, mz, energy = cons
    inv = 1.0 / rho
    u, v, w = mx * inv, my * inv, mz * inv
    p = (GAMMA - 1.0) * (energy - 0.5 * rho * (u * u + v * v + w * w))
    theta = p * inv
    sound = jnp.sqrt(GAMMA * theta)
    kappa = 0.2 * jnp.exp(0.7 * jnp.log(theta))
    return (u, v, w), p, theta, sound, kappa


def side(cons, t, n):
    vel, p, theta, sound, kappa = t
    return (*cons, p, theta, kappa, vel[n], jnp.abs(vel[n]) + sound)


def double_flux(low, high, n):
    speed = jnp.maximum(low[9], high[9])
    out = []
    for f in range(F):
        if f == 0:
            total = low[n + 1] + high[n + 1]
        elif f == 4:
            total = (low[4] + low[5]) * low[8] + (high[4] + high[5]) * high[8]
        else:
            total = low[f] * low[8] + high[f] * high[8]
            if f == n + 1:
                total = total + (low[5] + high[5])
        total = total - speed * (high[f] - low[f])
        if f == 4:
            total = total - (low[7] + high[7]) * (high[6] - low[6])
        out.append(total)
    return out


def primitive(cons):
    rho, mx, my, mz, energy = cons
    inv = 1.0 / rho
    u, v, w = mx * inv, my * inv, mz * inv
    return [rho, u, v, w, (GAMMA - 1.0) * (energy - 0.5 * rho * (u * u + v * v + w * w))]


def conserved(prim):
    rho, u, v, w, p = prim
    return [rho, rho * u, rho * v, rho * w, p * (1.0 / (GAMMA - 1.0)) + 0.5 * rho * (u * u + v * v + w * w)]


def rows_of(jv):
    return pl.ds(pl.multiple_of(jv * 8, 8), 8)


def faces(pos, cur, jv, x_in, x_out, y_low, y_high):
    zx = tile_x(pos[0])
    rows = rows_of(jv)
    lane = lax.broadcasted_iota(jnp.int32, (8, L), 1) // 16
    for f in range(F):
        x_in[f, rows, :] = cur[f, 7 - 7 * zx, rows, :]
        x_out[f, rows, :] = cur[f, 7 * zx, rows, :]
        low = high = None
        for x in range(X):
            v = cur[f, x, rows, :]
            a, b = rolled(v, 16 * x), rolled(v, 16 * x + 16)
            low = a if low is None else jnp.where(lane == x, a, low)
            high = b if high is None else jnp.where(lane == x, b, high)
        y_low[f, rows, :] = low
        y_high[f, rows, :] = high


def y_faces(pos, y_low, y_high, y_in, y_out):
    zy = tile_y(pos[0])
    core = pos[1]
    first = jnp.full((HALF, L), zy, jnp.int32) == 0
    turn = jnp.full((HALF, L), jnp.where(core == zy, 1, 0), jnp.int32) == 1
    for f in range(F):
        low, high = y_low[f], y_high[f]
        y_in[f] = jnp.where(first, high, low)
        back = jnp.concatenate([low[1:], low[:1]], axis=0)
        ahead = jnp.concatenate([high[-1:], high[:-1]], axis=0)
        y_out[f] = jnp.where(first, jnp.where(turn, back, low), jnp.where(turn, ahead, high))


def reorder(pos, slots, *refs):
    parts = refs[:8]
    cur, x_in, x_out, y_low, y_high, y_in, y_out = refs[8:15]
    held = refs[15]
    z, core, g = pos[0], pos[1], pos[2]
    for k in range(4):
        for h in range(2):
            d = (z ^ k) * 2 + (core ^ h)
            for s in range(CAP):
                j = slots[d * N_COL + g, s] - g * NBY
                here = jnp.logical_and(j >= 0, j % 2 == core)
                row = jnp.where(here, j // 2, HALF)
                for f in range(F):
                    held[pl.ds(f * X * PAD + row, X, PAD), :] = parts[k * 2 + h][s, f]

    def convert(jv, _):
        for x in range(X):
            prim = [held[pl.ds(pl.multiple_of((f * X + x) * PAD + jv * 8, 8), 8), :] for f in range(F)]
            for f, v in enumerate(conserved(prim)):
                cur[f, x, rows_of(jv), :] = v
        faces(pos, cur, jv, x_in, x_out, y_low, y_high)
        return 0

    lax.fori_loop(0, HALF // 8, convert, 0)
    y_faces(pos, y_low, y_high, y_in, y_out)


def section(number, pos, *refs):
    if number == 0:
        cur = initial = refs[0]
        refs = refs[1:]
    else:
        initial, cur = refs[:2]
        refs = refs[2:]
    x_in, x_out, y_in, y_out, y_low, y_high = refs[:6]
    new = refs[6]
    zx, zy = tile_x(pos[0]), tile_y(pos[0])
    weight = (0.0, 0.75, 1.0 / 3.0)[number]

    def step(jv, _):
        rows = rows_of(jv)
        lane = lax.broadcasted_iota(jnp.int32, (8, L), 1)
        height = lane % 16
        low_y, high_y = lane < 16, lane >= L - 16
        floor, roof = height == 0, height == 15
        first_x = jnp.full((8, L), zx, jnp.int32) == 0
        first_y = jnp.full((8, L), zy, jnp.int32) == 0

        def halo(inner, outer, first):
            a = [inner[f, rows, :] for f in range(F)]
            b = [outer[f, rows, :] for f in range(F)]
            low = [jnp.where(first, o, i) for i, o in zip(a, b)]
            high = [jnp.where(first, i, o) for i, o in zip(a, b)]
            return low, high

        y_before, y_after = halo(y_in, y_out, first_y)
        mine_low = [y_low[f, rows, :] for f in range(F)]
        mine_high = [y_high[f, rows, :] for f in range(F)]
        flux_low = double_flux(side(y_before, terms(y_before), 1), side(mine_low, terms(mine_low), 1), 1)
        flux_high = double_flux(side(mine_high, terms(mine_high), 1), side(y_after, terms(y_after), 1), 1)

        x_before, x_after = halo(x_in, x_out, first_x)
        behind = side(x_before, terms(x_before), 0)
        cons = [cur[f, 0, rows, :] for f in range(F)]
        t = terms(cons)
        here = side(cons, t, 0)
        flux_x = double_flux(behind, here, 0)
        for x in range(X):
            if x < X - 1:
                cons_next = [cur[f, x + 1, rows, :] for f in range(F)]
            else:
                cons_next = x_after
            t_next = terms(cons_next)
            ahead = side(cons_next, t_next, 0)
            flux_next = double_flux(here, ahead, 0)
            change = [b - a for a, b in zip(flux_x, flux_next)]

            low = side(cons, t, 1)
            flux = double_flux(low, [rolled(q, -16) for q in low], 1)
            for f in range(F):
                upper = jnp.where(high_y, rolled(flux_high[f], L - 16 - 16 * x), flux[f])
                lower = jnp.where(low_y, rolled(flux_low[f], -16 * x), rolled(flux[f], 16))
                change[f] = change[f] + (upper - lower)

            low = side(cons, t, 2)
            flux = double_flux(low, [rolled(q, -1) for q in low], 2)
            for f in range(F):
                wall = 2.0 * t[1] if f == 3 else 0.0
                upper = jnp.where(roof, wall, flux[f])
                lower = jnp.where(floor, wall, rolled(flux[f], 1))
                change[f] = change[f] + (upper - lower)

            out = [c - (0.5 * STEP) * d for c, d in zip(cons, change)]
            if number:
                out = [
                    weight * initial[f, x, rows, :] + (1.0 - weight) * o for f, o in enumerate(out)
                ]
            if number == 2:
                out = primitive(out)
            for f in range(F):
                new[f, x, rows, :] = out[f]
            cons, t, here, flux_x = cons_next, t_next, ahead, flux_next
        if number < 2:
            faces(pos, new, jv, *refs[7:11])
        return 0

    lax.fori_loop(0, HALF // 8, step, 0)
    if number < 2:
        y_faces(pos, *refs[9:13])


def pack_out(pos, final, mine, other, *outs):
    z, core = pos[0], pos[1]
    for k in range(4):
        d = (z ^ k) * 2 + core
        for s in range(OUT):
            j = final[d * 8 + s]
            row = jnp.maximum(j, 0) // 2
            kind = jnp.full((X, L), jnp.where(j < 0, 2, j % 2 ^ core), jnp.int32)
            for f in range(F):
                at = pl.ds(f * X * HALF + row, X, HALF)
                a, b = mine[at, :], other[at, :]
                outs[k][s, f] = jnp.where(kind == 0, a, jnp.where(kind == 1, b, 0.0))


def body(block_cells, slot_blocks):
    row, col = lax.axis_index("row"), lax.axis_index("col")
    pos = jnp.stack([row // 2, row % 2, col]).astype(jnp.int32)

    def to(array, route):
        pairs = []
        for r in range(N_ROW):
            for c in range(N_COL):
                z, core, c2 = route(r // 2, r % 2, c)
                pairs.append((r * N_COL + c, (z * 2 + core) * N_COL + c2 % N_COL))
        return lax.ppermute(array, ("row", "col"), pairs)

    def over_z(array, k):
        return array if k == 0 else to(array, lambda z, core, c: (z ^ k, core, c))

    def over_core(array):
        return to(array, lambda z, core, c: (z, 1 - core, c))

    tiles = [shape(CAP, F, X, L)] * 4
    parts = pl.pallas_call(
        pack_in,
        out_shape=tiles,
        in_specs=[SMEM, ANY],
        out_specs=[VMEM] * 4,
        scratch_shapes=[pltpu.SemaphoreType.DMA((4,))],
        compiler_params=PARAMS,
        name="pack_in",
    )(pos, block_cells)
    final = pl.pallas_call(
        table,
        out_shape=jax.ShapeDtypeStruct((N_ROW * 8,), jnp.int32),
        in_specs=[SMEM, SMEM],
        out_specs=SMEM,
        scratch_shapes=[pltpu.SMEM((N_ROW * 16,), jnp.int32), pltpu.SMEM((N_ROW,), jnp.int32)],
        compiler_params=PARAMS,
        name="table",
    )(pos, slot_blocks)
    gathered = []
    for k in range(4):
        here = over_z(parts[k], k)
        gathered += [here, over_core(here)]

    whole = shape(F, X, HALF, L)
    layer = shape(F, HALF, L)
    initial, x_in, x_out, y_low, y_high, y_in, y_out = pl.pallas_call(
        reorder,
        out_shape=[whole] + [layer] * 6,
        in_specs=[SMEM, SMEM] + [VMEM] * 8,
        out_specs=[VMEM] * 7,
        scratch_shapes=[pltpu.VMEM((F * X * PAD, L), jnp.float32)],
        compiler_params=PARAMS,
        name="reorder",
    )(pos, slot_blocks, *gathered)

    def x_partner(z):
        return z ^ 1

    def y_partner(z):
        return z ^ 3

    def exchanged(x_in, x_out, y_in, y_out):
        return (
            to(x_in, lambda z, core, c: (x_partner(z), core, c)),
            to(x_out, lambda z, core, c: (x_partner(z), core, c + 2 * tile_x(z) - 1)),
            to(y_in, lambda z, core, c: (y_partner(z), core, c)),
            to(y_out, lambda z, core, c: (y_partner(z), 1 - core, c + 2 * tile_y(z) - 1)),
        )

    current = initial
    for number in range(3):
        halos = exchanged(x_in, x_out, y_in, y_out)
        states = (current,) if number == 0 else (initial, current)
        outs = [whole] + ([layer] * 6 if number < 2 else [])
        made = pl.pallas_call(
            lambda *refs, number=number: section(number, *refs),
            out_shape=outs,
            in_specs=[SMEM] + [VMEM] * (len(states) + 6),
            out_specs=[VMEM] * len(outs),
            compiler_params=PARAMS,
            name="section" + str(number),
        )(pos, *states, *halos, y_low, y_high)
        current = made[0]
        if number < 2:
            x_in, x_out, y_low, y_high, y_in, y_out = made[1:]

    flat = current.reshape(F * X * HALF, L)
    leaving = pl.pallas_call(
        pack_out,
        out_shape=[shape(OUT, F, X, L)] * 4,
        in_specs=[SMEM, SMEM, VMEM, VMEM],
        out_specs=[VMEM] * 4,
        compiler_params=PARAMS,
        name="pack_out",
    )(pos, final, flat, over_core(flat))
    arrived = [over_z(leaving[k], k) for k in range(4)]
    return pl.pallas_call(
        unpack_out,
        out_shape=shape(OUT, F, 2 * X, 2 * L),
        in_specs=[SMEM] + [ANY] * 4,
        out_specs=ANY,
        scratch_shapes=[pltpu.SemaphoreType.DMA((4,))],
        compiler_params=PARAMS,
        name="unpack_out",
    )(pos, *arrived)


def solution(mesh):
    in_specs = (P(("row", "col"), None, None, None), P())
    out_specs = P(("row", "col"), None, None, None)
    return jax.shard_map(body, mesh=mesh, in_specs=in_specs, out_specs=out_specs, check_vma=False)
```

time: 244 us -> 94.8 us (0.39)
  local copies, waits for them, and re-layouts: 85.9 us -> 1.29 us
  waiting for transfers between devices: 93.5 us -> 34.2 us
  other arithmetic: 23.3 us -> 0.08 us
  Pallas kernels: 0 us -> 21.8 us
  between operations: 18.8 us -> 0.14 us
  starting transfers between devices: 21.9 us -> 37.2 us
    gather x42 -> x0, local copies, waits for them, and re-layouts: 58.3 us -> none  [the longest x9 36.2 us: rebalance_table(): jnp.take_along_axis(other_anchors, jnp.clip(anchor_slot, 0, slot_width -...]
    all_gather x3 -> x0, waiting for transfers between devices: 56.9 us -> none  [one_gather(): lines, at, outs = (lax.all_gather(line, axis), 0, [])]
    pallas_call x0 -> x8, Pallas kernels: none -> 21.8 us  [the longest x3 11.5 us: body(): pl.pallas_call(lambda *refs, number=number: section(number, *refs), out_s...]
    ppermute x9 -> x23, starting transfers between devices: 21.4 us -> 37.2 us  [to(): return lax.ppermute(array, ('row', 'col'), pairs)]
    another operation x21 -> x0, local copies, waits for them, and re-layouts: 8.71 us -> none  [the longest x6 6.87 us: laid_out(): return jnp.moveaxis(pieces, 0, dim).reshape(dims)]
    slice x19 -> x0, local copies, waits for them, and re-layouts: 4.75 us -> none  [the longest x3 2.65 us: one_gather(): pieces = lines[:, at:at + a.size].reshape(-1, *a.shape)]
    concatenate x24 -> x0, other arithmetic: 4.58 us -> none  [the longest x3 2.02 us: one_gather(): line = jnp.concatenate([a.reshape(-1) for a in arrays])]
    all_gather x3 -> x0, local copies, waits for them, and re-layouts: 4.3 us -> none  [one_gather(): lines, at, outs = (lax.all_gather(line, axis), 0, [])]
  transfers between devices with their start and end apart: 12 -> 23, of which waited for: 11 -> 13; matrix products, arithmetic and copies ran while one was open for 22% -> 0% of each run, Pallas kernels for 0% -> 3%
where the time goes in v1:
time: 94.8 us; the launch traced here: 94.7 us
  starting transfers between devices  37.2 us (39%)
  waiting for transfers between devices  34.2 us (36%)
  Pallas kernels  21.8 us (23%)
  local copies, waits for them, and re-layouts  1.29 us (1%)
    ppermute x23, starting transfers between devices, to(): return lax.ppermute(array, ('row', 'col'), pairs)  37.2 us
    ppermute x23, waiting for transfers between devices, to(): return lax.ppermute(array, ('row', 'col'), pairs)  34.2 us
    pallas_call x3, Pallas kernels, body(): pl.pallas_call(lambda *refs, number=number: section(number, *refs), out_s...  11.5 us
    pallas_call x1, Pallas kernels, body(): pl.pallas_call(reorder, out_shape=[whole] + [layer] * 6, in_specs=[SMEM,...  4.47 us
    pallas_call x1, Pallas kernels, body(): pl.pallas_call(table, out_shape=jax.ShapeDtypeStruct((N_ROW * 8,), jnp.in...  2.8 us
  transfers between devices with their start and end apart: 23, of which 13 were waited for; matrix products, arithmetic and copies ran while one was open for 0% of the time, Pallas kernels for 3%

profile of v1, /device:TPU:1, one launch (start us, length us, event | category | flops | bytes accessed | tf_op | source)
XLA Modules:
  0.0 94.7 jit_solution(4037310070818944710)
XLA Ops:
  0.0 0.1 pad_add_fusion.pos.refs_0_
  0.1 0.0 copy-start
  0.1 1.2 %copy-done = f32[11,5,16,256]{3,2,1,0:T(8,128)S(1)} copy-done((f32[11,5,16,256]{3,2,1,0:T(8,128)S(1)}, f32[11,5,16,256]{3,2,1,0:T(8,128)}, u32[]{:S(2)}) %copy-start) | copy-done | bytes 901144
  1.3 0.0 copy-start.1
  1.3 0.8 pack_in.1
  2.0 2.5 %collective-permute-start.1 = (f32[11,5,8,128]{3,2,1,0:T(8,128)S(1)}, f32[11,5,8,128]{3,2,1,0:T(8,128)S(1)}, u32[]{:S(2)}, u32[]{:S(2)}) collective-permute-start(f32[11,5,8,128]{3,2,1,0:T(8,128)S(1)} %get-tuple-element.35), channel_id=1, source_target_pairs={{0,32},{1,33},{2,34},{3,35},{4,36},{5,37},{6,38},{7,39},{8,40},{9,... | collective-permute-start | bytes 675848 | tf_op jit(solution)/shard_map/ppermute | solution.py:338
  4.6 3.3 %collective-permute-start.3 = (f32[11,5,8,128]{3,2,1,0:T(8,128)S(1)}, f32[11,5,8,128]{3,2,1,0:T(8,128)S(1)}, u32[]{:S(2)}, u32[]{:S(2)}) collective-permute-start(f32[11,5,8,128]{3,2,1,0:T(8,128)S(1)} %get-tuple-element.36), channel_id=1, source_target_pairs={{0,64},{1,65},{2,66},{3,67},{4,68},{5,69},{6,70},{7,71},{8,72},{9,... | collective-permute-start | bytes 675848 | tf_op jit(solution)/shard_map/ppermute | solution.py:338
  7.9 0.0 collective-permute-start.5
  7.9 1.2 %collective-permute-start = (f32[11,5,8,128]{3,2,1,0:T(8,128)S(1)}, f32[11,5,8,128]{3,2,1,0:T(8,128)S(1)}, u32[]{:S(2)}, u32[]{:S(2)}) collective-permute-start(f32[11,5,8,128]{3,2,1,0:T(8,128)S(1)} %get-tuple-element.34.refs_0_), channel_id=1, source_target_pairs={{0,16},{1,17},{2,18},{3,19},{4,20},{5,21},{6,22},{7,23},{8,24},{9,... | collective-permute-start | bytes 675848 | tf_op jit(solution)/shard_map/ppermute | solution.py:338
  9.1 0.7 collective-permute-done.1.refs_2_
  9.8 2.1 %collective-permute-start.2 = (f32[11,5,8,128]{3,2,1,0:T(8,128)S(1)}, f32[11,5,8,128]{3,2,1,0:T(8,128)S(1)}, u32[]{:S(2)}, u32[]{:S(2)}) collective-permute-start(f32[11,5,8,128]{3,2,1,0:T(8,128)S(1)} %collective-permute-done.1.refs_2_), channel_id=1, source_target_pairs={{0,16},{1,17},{2,18},{3,19},{4,20},{5,21},{6,22},{7,23},{8,24},{9,... | collective-permute-start | bytes 675848 | tf_op jit(solution)/shard_map/ppermute | solution.py:338
  11.9 5.8 %collective-permute-done.3.refs_4_ = f32[11,5,8,128]{3,2,1,0:T(8,128)S(1)} collective-permute-done((f32[11,5,8,128]{3,2,1,0:T(8,128)S(1)}, f32[11,5,8,128]{3,2,1,0:T(8,128)S(1)}, u32[]{:S(2)}, u32[]{:S(2)}) %collective-permute-start.3) | collective-permute-done | bytes 225312 | tf_op jit(solution)/shard_map/ppermute | solution.py:338
  17.7 1.6 %collective-permute-start.4 = (f32[11,5,8,128]{3,2,1,0:T(8,128)S(1)}, f32[11,5,8,128]{3,2,1,0:T(8,128)S(1)}, u32[]{:S(2)}, u32[]{:S(2)}) collective-permute-start(f32[11,5,8,128]{3,2,1,0:T(8,128)S(1)} %collective-permute-done.3.refs_4_), channel_id=1, source_target_pairs={{0,16},{1,17},{2,18},{3,19},{4,20},{5,21},{6,22},{7,23},{8,24},{9,... | collective-permute-start | bytes 675848 | tf_op jit(solution)/shard_map/ppermute | solution.py:338
  19.3 0.8 collective-permute-done.5.refs_6_
  20.0 1.8 %collective-permute-start.6 = (f32[11,5,8,128]{3,2,1,0:T(8,128)S(1)}, f32[11,5,8,128]{3,2,1,0:T(8,128)S(1)}, u32[]{:S(2)}, u32[]{:S(2)}) collective-permute-start(f32[11,5,8,128]{3,2,1,0:T(8,128)S(1)} %collective-permute-done.5.refs_6_), channel_id=1, source_target_pairs={{0,16},{1,17},{2,18},{3,19},{4,20},{5,21},{6,22},{7,23},{8,24},{9,... | collective-permute-start | bytes 675848 | tf_op jit(solution)/shard_map/ppermute | solution.py:338
  21.8 0.0 copy-done.1
  21.8 0.1 copy.3.slots
  22.0 0.0 collective-permute-done.refs_1_
  22.0 0.0 collective-permute-done.2.refs_3_
  22.0 0.0 collective-permute-done.4.refs_5_
  22.0 1.0 %collective-permute-done.6.refs_7_ = f32[11,5,8,128]{3,2,1,0:T(8,128)S(1)} collective-permute-done((f32[11,5,8,128]{3,2,1,0:T(8,128)S(1)}, f32[11,5,8,128]{3,2,1,0:T(8,128)S(1)}, u32[]{:S(2)}, u32[]{:S(2)}) %collective-permute-start.6) | collective-permute-done | bytes 225312 | tf_op jit(solution)/shard_map/ppermute | solution.py:338
  23.0 4.5 %reorder.1 = (f32[5,8,24,128]{3,2,1,0:T(8,128)S(1)}, f32[5,24,128]{2,1,0:T(8,128)S(1)}, f32[5,24,128]{2,1,0:T(8,128)S(1)}, f32[5,24,128]{2,1,0:T(8,128)S(1)}, f3...) custom-call(s32[3]{0:T(128)S(1)} %pad_add_fusion.pos.refs_0_, ...), custom_call_target="tpu_custom_call" | custom-call | tf_op jit(solution)/shard_map/reorder/pallas_call | solution.py:372
  27.4 5.0 %collective-permute-start.10 = (f32[5,24,128]{2,1,0:T(8,128)S(1)}, f32[5,24,128]{2,1,0:T(8,128)S(1)}, u32[]{:S(2)}, u32[]{:S(2)}) collective-permute-start(f32[5,24,128]{2,1,0:T(8,128)S(1)} %get-tuple-element.42), channel_id=1, source_target_pairs={{0,127},{1,112},{2,113},{3,114},{4,115},{5,116},{6,117},{7,118},{8... | collective-permute-start | bytes 184328 | tf_op jit(solution)/shard_map/ppermute | solution.py:338
  32.4 0.0 collective-permute-start.7
  32.4 1.7 %collective-permute-start.8 = (f32[5,24,128]{2,1,0:T(8,128)S(1)}, f32[5,24,128]{2,1,0:T(8,128)S(1)}, u32[]{:S(2)}, u32[]{:S(2)}) collective-permute-start(f32[5,24,128]{2,1,0:T(8,128)S(1)} %get-tuple-element.40), channel_id=1, source_target_pairs={{0,47},{1,32},{2,33},{3,34},{4,35},{5,36},{6,37},{7,38},{8,39},{9,... | collective-permute-start | bytes 184328 | tf_op jit(solution)/shard_map/ppermute | solution.py:338
  34.1 2.0 %collective-permute-start.9 = (f32[5,24,128]{2,1,0:T(8,128)S(1)}, f32[5,24,128]{2,1,0:T(8,128)S(1)}, u32[]{:S(2)}, u32[]{:S(2)}) collective-permute-start(f32[5,24,128]{2,1,0:T(8,128)S(1)} %get-tuple-element.41), channel_id=1, source_target_pairs={{0,96},{1,97},{2,98},{3,99},{4,100},{5,101},{6,102},{7,103},{8,104... | collective-permute-start | bytes 184328 | tf_op jit(solution)/shard_map/ppermute | solution.py:338
  36.1 0.8 collective-permute-done.10.refs_5_
  36.9 0.0 collective-permute-done.7.refs_2_
  36.9 3.2 %collective-permute-done.8.refs_3_ = f32[5,24,128]{2,1,0:T(8,128)S(1)} collective-permute-done((f32[5,24,128]{2,1,0:T(8,128)S(1)}, f32[5,24,128]{2,1,0:T(8,128)S(1)}, u32[]{:S(2)}, u32[]{:S(2)}) %collective-permute-start.8) | collective-permute-done | bytes 61472 | tf_op jit(solution)/shard_map/ppermute | solution.py:338
  40.1 0.0 collective-permute-done.9.refs_4_
  40.1 4.1 %section0.1 = (f32[5,8,24,128]{3,2,1,0:T(8,128)S(1)}, f32[5,24,128]{2,1,0:T(8,128)S(1)}, f32[5,24,128]{2,1,0:T(8,128)S(1)}, f32[5,24,128]{2,1,0:T(8,128)S(1)}, f...) custom-call(s32[3]{0:T(128)S(1)} %pad_add_fusion.pos.refs_0_, ...), custom_call_target="tpu_custom_call" | custom-call | tf_op jit(solution)/shard_map/section0/pallas_call | solution.py:401
  44.2 0.1 collective-permute-start.11
  44.3 1.4 %collective-permute-start.12 = (f32[5,24,128]{2,1,0:T(8,128)S(1)}, f32[5,24,128]{2,1,0:T(8,128)S(1)}, u32[]{:S(2)}, u32[]{:S(2)}) collective-permute-start(f32[5,24,128]{2,1,0:T(8,128)S(1)} %get-tuple-element.47), channel_id=1, source_target_pairs={{0,47},{1,32},{2,33},{3,34},{4,35},{5,36},{6,37},{7,38},{8,39},{9,... | collective-permute-start | bytes 184328 | tf_op jit(solution)/shard_map/ppermute | solution.py:338
  45.8 2.1 %collective-permute-start.13 = (f32[5,24,128]{2,1,0:T(8,128)S(1)}, f32[5,24,128]{2,1,0:T(8,128)S(1)}, u32[]{:S(2)}, u32[]{:S(2)}) collective-permute-start(f32[5,24,128]{2,1,0:T(8,128)S(1)} %get-tuple-element.48), channel_id=1, source_target_pairs={{0,96},{1,97},{2,98},{3,99},{4,100},{5,101},{6,102},{7,103},{8,104... | collective-permute-start | bytes 184328 | tf_op jit(solution)/shard_map/ppermute | solution.py:338
  47.9 2.4 %collective-permute-start.14 = (f32[5,24,128]{2,1,0:T(8,128)S(1)}, f32[5,24,128]{2,1,0:T(8,128)S(1)}, u32[]{:S(2)}, u32[]{:S(2)}) collective-permute-start(f32[5,24,128]{2,1,0:T(8,128)S(1)} %get-tuple-element.49), channel_id=1, source_target_pairs={{0,127},{1,112},{2,113},{3,114},{4,115},{5,116},{6,117},{7,118},{8... | collective-permute-start | bytes 184328 | tf_op jit(solution)/shard_map/ppermute | solution.py:338
  50.4 0.0 collective-permute-done.11.refs_3_
  50.4 1.3 %collective-permute-done.12.refs_4_ = f32[5,24,128]{2,1,0:T(8,128)S(1)} collective-permute-done((f32[5,24,128]{2,1,0:T(8,128)S(1)}, f32[5,24,128]{2,1,0:T(8,128)S(1)}, u32[]{:S(2)}, u32[]{:S(2)}) %collective-permute-start.12) | collective-permute-done | bytes 61472 | tf_op jit(solution)/shard_map/ppermute | solution.py:338
  51.7 0.0 collective-permute-done.13.refs_5_
  51.7 5.3 %collective-permute-done.14.refs_6_ = f32[5,24,128]{2,1,0:T(8,128)S(1)} collective-permute-done((f32[5,24,128]{2,1,0:T(8,128)S(1)}, f32[5,24,128]{2,1,0:T(8,128)S(1)}, u32[]{:S(2)}, u32[]{:S(2)}) %collective-permute-start.14) | collective-permute-done | bytes 61472 | tf_op jit(solution)/shard_map/ppermute | solution.py:338
  57.0 4.1 %section1.1 = (f32[5,8,24,128]{3,2,1,0:T(8,128)S(1)}, f32[5,24,128]{2,1,0:T(8,128)S(1)}, f32[5,24,128]{2,1,0:T(8,128)S(1)}, f32[5,24,128]{2,1,0:T(8,128)S(1)}, f...) custom-call(s32[3]{0:T(128)S(1)} %pad_add_fusion.pos.refs_0_, ...), custom_call_target="tpu_custom_call" | custom-call | tf_op jit(solution)/shard_map/section1/pallas_call | solution.py:401
  61.1 0.1 collective-permute-start.15
  61.2 0.1 collective-permute-start.16
  61.3 4.1 %collective-permute-start.17 = (f32[5,24,128]{2,1,0:T(8,128)S(1)}, f32[5,24,128]{2,1,0:T(8,128)S(1)}, u32[]{:S(2)}, u32[]{:S(2)}) collective-permute-start(f32[5,24,128]{2,1,0:T(8,128)S(1)} %get-tuple-element.55), channel_id=1, source_target_pairs={{0,96},{1,97},{2,98},{3,99},{4,100},{5,101},{6,102},{7,103},{8,104... | collective-permute-start | bytes 184328 | tf_op jit(solution)/shard_map/ppermute | solution.py:338
  65.4 0.6 collective-permute-start.18
  65.9 0.0 collective-permute-done.15.refs_3_
  65.9 2.6 %collective-permute-done.16.refs_4_ = f32[5,24,128]{2,1,0:T(8,128)S(1)} collective-permute-done((f32[5,24,128]{2,1,0:T(8,128)S(1)}, f32[5,24,128]{2,1,0:T(8,128)S(1)}, u32[]{:S(2)}, u32[]{:S(2)}) %collective-permute-start.16) | collective-permute-done | bytes 61472 | tf_op jit(solution)/shard_map/ppermute | solution.py:338
  68.6 0.0 collective-permute-done.17.refs_5_
  68.6 6.2 %collective-permute-done.18.refs_6_ = f32[5,24,128]{2,1,0:T(8,128)S(1)} collective-permute-done((f32[5,24,128]{2,1,0:T(8,128)S(1)}, f32[5,24,128]{2,1,0:T(8,128)S(1)}, u32[]{:S(2)}, u32[]{:S(2)}) %collective-permute-start.18) | collective-permute-done | bytes 61472 | tf_op jit(solution)/shard_map/ppermute | solution.py:338
  74.8 3.3 %section2.1 = f32[5,8,24,128]{3,2,1,0:T(8,128)S(1)} custom-call(s32[3]{0:T(128)S(1)} %pad_add_fusion.pos.refs_0_, f32[5,8,24,128]{3,2,1,0:T(8,128)S(1)} %get-tuple-element.38.refs_1_, f32[5,8,24,128]{3,2,1,0:T(8,128)S(1)} %get-tuple-element.52.refs_2_, f32[5,24,128]{2,1,0:T(8,128)S(1)} %collective-permute-done.15.refs_3_, ...), custom_call_target="tpu_custom_call" | custom-call | tf_op jit(solution)/shard_map/section2/pallas_call | solution.py:401
  78.1 1.0 %collective-permute-start.19 = (f32[960,128]{1,0:T(8,128)S(1)}, f32[960,128]{1,0:T(8,128)S(1)}, u32[]{:S(2)}, u32[]{:S(2)}) collective-permute-start(f32[960,128]{1,0:T(8,128)S(1)} %bitcast.4), channel_id=1, source_target_pairs={{0,16},{1,17},{2,18},{3,19},{4,20},{5,21},{6,22},{7,23},{8,24},{9,... | collective-permute-start | bytes 1474568 | tf_op jit(solution)/shard_map/ppermute | solution.py:338
  79.2 2.8 %table.1.final = s32[64]{0:T(128)S(1)} custom-call(s32[3]{0:T(128)S(1)} %pad_add_fusion.pos.refs_0_, s32[128,11]{1,0:T(8,128)S(1)} %copy.3.slots), custom_call_target="tpu_custom_call" | custom-call | tf_op jit(solution)/shard_map/table/pallas_call | solution.py:356
  82.0 0.0 collective-permute-done.19.other
  82.0 0.9 pack_out.1
  82.8 0.1 collective-permute-start.20
  82.9 0.1 collective-permute-start.21
  83.0 3.8 %collective-permute-start.22 = (f32[7,5,8,128]{3,2,1,0:T(8,128)S(1)}, f32[7,5,8,128]{3,2,1,0:T(8,128)S(1)}, u32[]{:S(2)}, u32[]{:S(2)}) collective-permute-start(f32[7,5,8,128]{3,2,1,0:T(8,128)S(1)} %get-tuple-element.62), channel_id=1, source_target_pairs={{0,96},{1,97},{2,98},{3,99},{4,100},{5,101},{6,102},{7,103},{8,104... | collective-permute-start | bytes 430088 | tf_op jit(solution)/shard_map/ppermute | solution.py:338
  86.8 1.5 %collective-permute-done.20.refs_1_ = f32[7,5,8,128]{3,2,1,0:T(8,128)S(1)} collective-permute-done((f32[7,5,8,128]{3,2,1,0:T(8,128)S(1)}, f32[7,5,8,128]{3,2,1,0:T(8,128)S(1)}, u32[]{:S(2)}, u32[]{:S(2)}) %collective-permute-start.20) | collective-permute-done | bytes 143392 | tf_op jit(solution)/shard_map/ppermute | solution.py:338
  88.3 1.6 %collective-permute-done.21.refs_2_ = f32[7,5,8,128]{3,2,1,0:T(8,128)S(1)} collective-permute-done((f32[7,5,8,128]{3,2,1,0:T(8,128)S(1)}, f32[7,5,8,128]{3,2,1,0:T(8,128)S(1)}, u32[]{:S(2)}, u32[]{:S(2)}) %collective-permute-start.21) | collective-permute-done | bytes 143392 | tf_op jit(solution)/shard_map/ppermute | solution.py:338
  89.9 3.4 %collective-permute-done.22.refs_3_ = f32[7,5,8,128]{3,2,1,0:T(8,128)S(1)} collective-permute-done((f32[7,5,8,128]{3,2,1,0:T(8,128)S(1)}, f32[7,5,8,128]{3,2,1,0:T(8,128)S(1)}, u32[]{:S(2)}, u32[]{:S(2)}) %collective-permute-start.22) | collective-permute-done | bytes 143392 | tf_op jit(solution)/shard_map/ppermute | solution.py:338
  93.3 1.4 %unpack_out.1 = f32[7,5,16,256]{3,2,1,0:T(8,128)} custom-call(s32[3]{0:T(128)S(1)} %pad_add_fusion.pos.refs_0_, f32[7,5,8,128]{3,2,1,0:T(8,128)S(1)} %get-tuple-element.59.refs_0_, f32[7,5,8,128]{3,2,1,0:T(8,128)S(1)} %collective-permute-done.20.refs_1_, f32[7,5,8,128]{3,2,1,0:T(8,128)S(1)} %collective-permute-done.21.refs_2_, ...), custom_call_target="tpu_custom_call" | custom-call | tf_op jit(solution)/shard_map/unpack_out/pallas_call | solution.py:423
Async XLA Ops:
  0.1 1.2 %copy-start = (f32[11,5,16,256]{3,2,1,0:T(8,128)S(1)}, f32[11,5,16,256]{3,2,1,0:T(8,128)}, u32[]{:S(2)}) copy-start(f32[11,5,16,256]{3,2,1,0:T(8,128)} %cells.1) | copy-start | bytes 2703364
  1.3 20.6 %copy-start.1 = (s32[128,11]{0,1:T(8,128)S(1)}, s32[128,11]{0,1:T(8,128)}, u32[]{:S(2)}) copy-start(s32[128,11]{0,1:T(8,128)} %param.3) | copy-start | bytes 16900
  2.0 7.8 %collective-permute-start.1 = (f32[11,5,8,128]{3,2,1,0:T(8,128)S(1)}, f32[11,5,8,128]{3,2,1,0:T(8,128)S(1)}, u32[]{:S(2)}, u32[]{:S(2)}) collective-permute-start(f32[11,5,8,128]{3,2,1,0:T(8,128)S(1)} %get-tuple-element.35), channel_id=1, source_target_pairs={{0,32},{1,33},{2,34},{3,35},{4,36},{5,37},{6,38},{7,39},{8,40},{9,... | collective-permute-start | bytes 675848 | tf_op jit(solution)/shard_map/ppermute | solution.py:338
  4.6 13.1 %collective-permute-start.3 = (f32[11,5,8,128]{3,2,1,0:T(8,128)S(1)}, f32[11,5,8,128]{3,2,1,0:T(8,128)S(1)}, u32[]{:S(2)}, u32[]{:S(2)}) collective-permute-start(f32[11,5,8,128]{3,2,1,0:T(8,128)S(1)} %get-tuple-element.36), channel_id=1, source_target_pairs={{0,64},{1,65},{2,66},{3,67},{4,68},{5,69},{6,70},{7,71},{8,72},{9,... | collective-permute-start | bytes 675848 | tf_op jit(solution)/shard_map/ppermute | solution.py:338
  7.9 12.2 %collective-permute-start.5 = (f32[11,5,8,128]{3,2,1,0:T(8,128)S(1)}, f32[11,5,8,128]{3,2,1,0:T(8,128)S(1)}, u32[]{:S(2)}, u32[]{:S(2)}) collective-permute-start(f32[11,5,8,128]{3,2,1,0:T(8,128)S(1)} %get-tuple-element.37), channel_id=1, source_target_pairs={{0,96},{1,97},{2,98},{3,99},{4,100},{5,101},{6,102},{7,103},{8,104... | collective-permute-start | bytes 675848 | tf_op jit(solution)/shard_map/ppermute | solution.py:338
  7.9 14.1 %collective-permute-start = (f32[11,5,8,128]{3,2,1,0:T(8,128)S(1)}, f32[11,5,8,128]{3,2,1,0:T(8,128)S(1)}, u32[]{:S(2)}, u32[]{:S(2)}) collective-permute-start(f32[11,5,8,128]{3,2,1,0:T(8,128)S(1)} %get-tuple-element.34.refs_0_), channel_id=1, source_target_pairs={{0,16},{1,17},{2,18},{3,19},{4,20},{5,21},{6,22},{7,23},{8,24},{9,... | collective-permute-start | bytes 675848 | tf_op jit(solution)/shard_map/ppermute | solution.py:338
  9.8 12.2 %collective-permute-start.2 = (f32[11,5,8,128]{3,2,1,0:T(8,128)S(1)}, f32[11,5,8,128]{3,2,1,0:T(8,128)S(1)}, u32[]{:S(2)}, u32[]{:S(2)}) collective-permute-start(f32[11,5,8,128]{3,2,1,0:T(8,128)S(1)} %collective-permute-done.1.refs_2_), channel_id=1, source_target_pairs={{0,16},{1,17},{2,18},{3,19},{4,20},{5,21},{6,22},{7,23},{8,24},{9,... | collective-permute-start | bytes 675848 | tf_op jit(solution)/shard_map/ppermute | solution.py:338
  17.7 4.3 %collective-permute-start.4 = (f32[11,5,8,128]{3,2,1,0:T(8,128)S(1)}, f32[11,5,8,128]{3,2,1,0:T(8,128)S(1)}, u32[]{:S(2)}, u32[]{:S(2)}) collective-permute-start(f32[11,5,8,128]{3,2,1,0:T(8,128)S(1)} %collective-permute-done.3.refs_4_), channel_id=1, source_target_pairs={{0,16},{1,17},{2,18},{3,19},{4,20},{5,21},{6,22},{7,23},{8,24},{9,... | collective-permute-start | bytes 675848 | tf_op jit(solution)/shard_map/ppermute | solution.py:338
  20.0 2.9 %collective-permute-start.6 = (f32[11,5,8,128]{3,2,1,0:T(8,128)S(1)}, f32[11,5,8,128]{3,2,1,0:T(8,128)S(1)}, u32[]{:S(2)}, u32[]{:S(2)}) collective-permute-start(f32[11,5,8,128]{3,2,1,0:T(8,128)S(1)} %collective-permute-done.5.refs_6_), channel_id=1, source_target_pairs={{0,16},{1,17},{2,18},{3,19},{4,20},{5,21},{6,22},{7,23},{8,24},{9,... | collective-permute-start | bytes 675848 | tf_op jit(solution)/shard_map/ppermute | solution.py:338
  27.4 9.5 %collective-permute-start.10 = (f32[5,24,128]{2,1,0:T(8,128)S(1)}, f32[5,24,128]{2,1,0:T(8,128)S(1)}, u32[]{:S(2)}, u32[]{:S(2)}) collective-permute-start(f32[5,24,128]{2,1,0:T(8,128)S(1)} %get-tuple-element.42), channel_id=1, source_target_pairs={{0,127},{1,112},{2,113},{3,114},{4,115},{5,116},{6,117},{7,118},{8... | collective-permute-start | bytes 184328 | tf_op jit(solution)/shard_map/ppermute | solution.py:338
  32.4 4.5 %collective-permute-start.7 = (f32[5,24,128]{2,1,0:T(8,128)S(1)}, f32[5,24,128]{2,1,0:T(8,128)S(1)}, u32[]{:S(2)}, u32[]{:S(2)}) collective-permute-start(f32[5,24,128]{2,1,0:T(8,128)S(1)} %get-tuple-element.39), channel_id=1, source_target_pairs={{0,32},{1,33},{2,34},{3,35},{4,36},{5,37},{6,38},{7,39},{8,40},{9,... | collective-permute-start | bytes 184328 | tf_op jit(solution)/shard_map/ppermute | solution.py:338
  32.4 7.7 %collective-permute-start.8 = (f32[5,24,128]{2,1,0:T(8,128)S(1)}, f32[5,24,128]{2,1,0:T(8,128)S(1)}, u32[]{:S(2)}, u32[]{:S(2)}) collective-permute-start(f32[5,24,128]{2,1,0:T(8,128)S(1)} %get-tuple-element.40), channel_id=1, source_target_pairs={{0,47},{1,32},{2,33},{3,34},{4,35},{5,36},{6,37},{7,38},{8,39},{9,... | collective-permute-start | bytes 184328 | tf_op jit(solution)/shard_map/ppermute | solution.py:338
  34.1 6.0 %collective-permute-start.9 = (f32[5,24,128]{2,1,0:T(8,128)S(1)}, f32[5,24,128]{2,1,0:T(8,128)S(1)}, u32[]{:S(2)}, u32[]{:S(2)}) collective-permute-start(f32[5,24,128]{2,1,0:T(8,128)S(1)} %get-tuple-element.41), channel_id=1, source_target_pairs={{0,96},{1,97},{2,98},{3,99},{4,100},{5,101},{6,102},{7,103},{8,104... | collective-permute-start | bytes 184328 | tf_op jit(solution)/shard_map/ppermute | solution.py:338
  44.2 6.1 %collective-permute-start.11 = (f32[5,24,128]{2,1,0:T(8,128)S(1)}, f32[5,24,128]{2,1,0:T(8,128)S(1)}, u32[]{:S(2)}, u32[]{:S(2)}) collective-permute-start(f32[5,24,128]{2,1,0:T(8,128)S(1)} %get-tuple-element.46), channel_id=1, source_target_pairs={{0,32},{1,33},{2,34},{3,35},{4,36},{5,37},{6,38},{7,39},{8,40},{9,... | collective-permute-start | bytes 184328 | tf_op jit(solution)/shard_map/ppermute | solution.py:338
  44.3 7.4 %collective-permute-start.12 = (f32[5,24,128]{2,1,0:T(8,128)S(1)}, f32[5,24,128]{2,1,0:T(8,128)S(1)}, u32[]{:S(2)}, u32[]{:S(2)}) collective-permute-start(f32[5,24,128]{2,1,0:T(8,128)S(1)} %get-tuple-element.47), channel_id=1, source_target_pairs={{0,47},{1,32},{2,33},{3,34},{4,35},{5,36},{6,37},{7,38},{8,39},{9,... | collective-permute-start | bytes 184328 | tf_op jit(solution)/shard_map/ppermute | solution.py:338
  45.8 5.9 %collective-permute-start.13 = (f32[5,24,128]{2,1,0:T(8,128)S(1)}, f32[5,24,128]{2,1,0:T(8,128)S(1)}, u32[]{:S(2)}, u32[]{:S(2)}) collective-permute-start(f32[5,24,128]{2,1,0:T(8,128)S(1)} %get-tuple-element.48), channel_id=1, source_target_pairs={{0,96},{1,97},{2,98},{3,99},{4,100},{5,101},{6,102},{7,103},{8,104... | collective-permute-start | bytes 184328 | tf_op jit(solution)/shard_map/ppermute | solution.py:338
  47.9 9.1 %collective-permute-start.14 = (f32[5,24,128]{2,1,0:T(8,128)S(1)}, f32[5,24,128]{2,1,0:T(8,128)S(1)}, u32[]{:S(2)}, u32[]{:S(2)}) collective-permute-start(f32[5,24,128]{2,1,0:T(8,128)S(1)} %get-tuple-element.49), channel_id=1, source_target_pairs={{0,127},{1,112},{2,113},{3,114},{4,115},{5,116},{6,117},{7,118},{8... | collective-permute-start | bytes 184328 | tf_op jit(solution)/shard_map/ppermute | solution.py:338
  61.1 4.8 %collective-permute-start.15 = (f32[5,24,128]{2,1,0:T(8,128)S(1)}, f32[5,24,128]{2,1,0:T(8,128)S(1)}, u32[]{:S(2)}, u32[]{:S(2)}) collective-permute-start(f32[5,24,128]{2,1,0:T(8,128)S(1)} %get-tuple-element.53), channel_id=1, source_target_pairs={{0,32},{1,33},{2,34},{3,35},{4,36},{5,37},{6,38},{7,39},{8,40},{9,... | collective-permute-start | bytes 184328 | tf_op jit(solution)/shard_map/ppermute | solution.py:338
  61.2 7.4 %collective-permute-start.16 = (f32[5,24,128]{2,1,0:T(8,128)S(1)}, f32[5,24,128]{2,1,0:T(8,128)S(1)}, u32[]{:S(2)}, u32[]{:S(2)}) collective-permute-start(f32[5,24,128]{2,1,0:T(8,128)S(1)} %get-tuple-element.54), channel_id=1, source_target_pairs={{0,47},{1,32},{2,33},{3,34},{4,35},{5,36},{6,37},{7,38},{8,39},{9,... | collective-permute-start | bytes 184328 | tf_op jit(solution)/shard_map/ppermute | solution.py:338
  61.3 7.3 %collective-permute-start.17 = (f32[5,24,128]{2,1,0:T(8,128)S(1)}, f32[5,24,128]{2,1,0:T(8,128)S(1)}, u32[]{:S(2)}, u32[]{:S(2)}) collective-permute-start(f32[5,24,128]{2,1,0:T(8,128)S(1)} %get-tuple-element.55), channel_id=1, source_target_pairs={{0,96},{1,97},{2,98},{3,99},{4,100},{5,101},{6,102},{7,103},{8,104... | collective-permute-start | bytes 184328 | tf_op jit(solution)/shard_map/ppermute | solution.py:338
  65.4 9.5 %collective-permute-start.18 = (f32[5,24,128]{2,1,0:T(8,128)S(1)}, f32[5,24,128]{2,1,0:T(8,128)S(1)}, u32[]{:S(2)}, u32[]{:S(2)}) collective-permute-start(f32[5,24,128]{2,1,0:T(8,128)S(1)} %get-tuple-element.56), channel_id=1, source_target_pairs={{0,127},{1,112},{2,113},{3,114},{4,115},{5,116},{6,117},{7,118},{8... | collective-permute-start | bytes 184328 | tf_op jit(solution)/shard_map/ppermute | solution.py:338
  78.1 3.8 %collective-permute-start.19 = (f32[960,128]{1,0:T(8,128)S(1)}, f32[960,128]{1,0:T(8,128)S(1)}, u32[]{:S(2)}, u32[]{:S(2)}) collective-permute-start(f32[960,128]{1,0:T(8,128)S(1)} %bitcast.4), channel_id=1, source_target_pairs={{0,16},{1,17},{2,18},{3,19},{4,20},{5,21},{6,22},{7,23},{8,24},{9,... | collective-permute-start | bytes 1474568 | tf_op jit(solution)/shard_map/ppermute | solution.py:338
  82.8 5.5 %collective-permute-start.20 = (f32[7,5,8,128]{3,2,1,0:T(8,128)S(1)}, f32[7,5,8,128]{3,2,1,0:T(8,128)S(1)}, u32[]{:S(2)}, u32[]{:S(2)}) collective-permute-start(f32[7,5,8,128]{3,2,1,0:T(8,128)S(1)} %get-tuple-element.60), channel_id=1, source_target_pairs={{0,32},{1,33},{2,34},{3,35},{4,36},{5,37},{6,38},{7,39},{8,40},{9,... | collective-permute-start | bytes 430088 | tf_op jit(solution)/shard_map/ppermute | solution.py:338
  82.9 7.0 %collective-permute-start.21 = (f32[7,5,8,128]{3,2,1,0:T(8,128)S(1)}, f32[7,5,8,128]{3,2,1,0:T(8,128)S(1)}, u32[]{:S(2)}, u32[]{:S(2)}) collective-permute-start(f32[7,5,8,128]{3,2,1,0:T(8,128)S(1)} %get-tuple-element.61), channel_id=1, source_target_pairs={{0,64},{1,65},{2,66},{3,67},{4,68},{5,69},{6,70},{7,71},{8,72},{9,... | collective-permute-start | bytes 430088 | tf_op jit(solution)/shard_map/ppermute | solution.py:338
  83.0 10.3 %collective-permute-start.22 = (f32[7,5,8,128]{3,2,1,0:T(8,128)S(1)}, f32[7,5,8,128]{3,2,1,0:T(8,128)S(1)}, u32[]{:S(2)}, u32[]{:S(2)}) collective-permute-start(f32[7,5,8,128]{3,2,1,0:T(8,128)S(1)} %get-tuple-element.62), channel_id=1, source_target_pairs={{0,96},{1,97},{2,98},{3,99},{4,100},{5,101},{6,102},{7,103},{8,104... | collective-permute-start | bytes 430088 | tf_op jit(solution)/shard_map/ppermute | solution.py:338

commit v2 on v1

--- a/solution.py
+++ b/solution.py
@@ -12,9 +12,8 @@
 N_COL = 16
 HALF = NBY // 2
 F = 5
-X = 8
+X = Y = 8
 L = 128
-PAD = 32
 
 GAMMA = 1.4
 STEP = 0.12
@@ -79,13 +78,17 @@
         c.wait()
 
 
-def table(pos, slots, final, held, count):
-    g = pos[2]
+def table(pos, slots, _tile, final, rows, _same, held, count):
+    z, core, g = pos[0], pos[1], pos[2]
     for d in range(N_ROW):
         n = jnp.int32(0)
+        place = ((z ^ d // 2) * 2 + (core ^ d % 2)) * CAP
         for s in range(CAP):
             b = slots[d * N_COL + g, s]
-            held[d * 16 + s] = b - g * NBY
+            j = b - g * NBY
+            held[d * 16 + s] = j
+            here = jnp.logical_and(b >= 0, (j & 1) == core)
+            rows[place + s] = jnp.where(here, j >> 1, HALF)
             n = n + jnp.where(b >= 0, 1, 0)
         count[d] = n
     for bit in range(3):
@@ -166,65 +169,75 @@
     return [rho, rho * u, rho * v, rho * w, p * (1.0 / (GAMMA - 1.0)) + 0.5 * rho * (u * u + v * v + w * w)]
 
 
-def rows_of(jv):
-    return pl.ds(pl.multiple_of(jv * 8, 8), 8)
-
-
-def faces(pos, cur, jv, x_in, x_out, y_low, y_high):
-    zx = tile_x(pos[0])
-    rows = rows_of(jv)
-    lane = lax.broadcasted_iota(jnp.int32, (8, L), 1) // 16
+def at(f, y, group):
+    return pl.ds(pl.multiple_of((f * Y + y) * HALF + group * 8, 8), 8)
+
+
+def layer_at(f, group):
+    return pl.ds(pl.multiple_of(f * HALF + group * 8, 8), 8)
+
+
+def x_layer_at(f, group, x):
+    return pl.ds(f * Y * HALF + group * 8 + x, Y, HALF)
+
+
+def transposed(vectors):
+    place = lax.broadcasted_iota(jnp.int32, (8, L), 1) // 16
+    vectors = list(vectors)
+    for bit in (1, 2, 4):
+        clear = (place & bit) == 0
+        for i in range(8):
+            if i & bit:
+                continue
+            a, b = vectors[i], vectors[i | bit]
+            vectors[i] = jnp.where(clear, a, rolled(b, 16 * bit))
+            vectors[i | bit] = jnp.where(clear, rolled(a, -16 * bit), b)
+    return vectors
+
+
+def faces(pos, cur, x_in, x_out, y_in, y_out):
+    zx, zy, core = tile_x(pos[0]), tile_y(pos[0]), pos[1]
+    place = lax.broadcasted_iota(jnp.int32, (8, L), 1) // 16
+    first = jnp.full((8, L), zy, jnp.int32) == 0
+    turn = jnp.full((8, L), jnp.where(core == zy, 1, 0), jnp.int32) == 1
     for f in range(F):
-        x_in[f, rows, :] = cur[f, 7 - 7 * zx, rows, :]
-        x_out[f, rows, :] = cur[f, 7 * zx, rows, :]
-        low = high = None
-        for x in range(X):
-            v = cur[f, x, rows, :]
-            a, b = rolled(v, 16 * x), rolled(v, 16 * x + 16)
-            low = a if low is None else jnp.where(lane == x, a, low)
-            high = b if high is None else jnp.where(lane == x, b, high)
-        y_low[f, rows, :] = low
-        y_high[f, rows, :] = high
-
-
-def y_faces(pos, y_low, y_high, y_in, y_out):
-    zy = tile_y(pos[0])
-    core = pos[1]
-    first = jnp.full((HALF, L), zy, jnp.int32) == 0
-    turn = jnp.full((HALF, L), jnp.where(core == zy, 1, 0), jnp.int32) == 1
-    for f in range(F):
-        low, high = y_low[f], y_high[f]
-        y_in[f] = jnp.where(first, high, low)
-        back = jnp.concatenate([low[1:], low[:1]], axis=0)
-        ahead = jnp.concatenate([high[-1:], high[:-1]], axis=0)
-        y_out[f] = jnp.where(first, jnp.where(turn, back, low), jnp.where(turn, ahead, high))
-
-
-def reorder(pos, slots, *refs):
+        ahead, back = [], []
+        for group in range(3):
+            x_in[layer_at(f, group), :] = cur[x_layer_at(f, group, 7 - 7 * zx), :]
+            x_out[layer_at(f, group), :] = cur[x_layer_at(f, group, 7 * zx), :]
+            y_in[layer_at(f, group), :] = cur[at(f, 7 - 7 * zy, group), :]
+            v = cur[at(f, 7 * zy, group), :]
+            ahead.append(rolled(v, 16))
+            back.append(rolled(v, -16))
+        for group in range(3):
+            high = jnp.where(place == 0, ahead[group - 1], ahead[group])
+            low = jnp.where(place == 7, back[(group + 1) % 3], back[group])
+            v = cur[at(f, 7 * zy, group), :]
+            y_out[layer_at(f, group), :] = jnp.where(turn, jnp.where(first, low, high), v)
+
+
+def reorder(pos, rows, *refs):
     parts = refs[:8]
-    cur, x_in, x_out, y_low, y_high, y_in, y_out = refs[8:15]
-    held = refs[15]
-    z, core, g = pos[0], pos[1], pos[2]
-    for k in range(4):
-        for h in range(2):
-            d = (z ^ k) * 2 + (core ^ h)
-            for s in range(CAP):
-                j = slots[d * N_COL + g, s] - g * NBY
-                here = jnp.logical_and(j >= 0, j % 2 == core)
-                row = jnp.where(here, j // 2, HALF)
-                for f in range(F):
-                    held[pl.ds(f * X * PAD + row, X, PAD), :] = parts[k * 2 + h][s, f]
-
-    def convert(jv, _):
-        for x in range(X):
-            prim = [held[pl.ds(pl.multiple_of((f * X + x) * PAD + jv * 8, 8), 8), :] for f in range(F)]
+    cur, x_in, x_out, y_in, y_out = refs[8:13]
+    held = refs[13]
+    for i in range(8):
+        for s in range(CAP):
+            held[rows[i * CAP + s]] = parts[i][s]
+
+    def convert(group, _):
+        for f in range(F):
+            vectors = [held[group * 8 + i, f] for i in range(8)]
+            for y, v in enumerate(transposed(vectors)):
+                cur[at(f, y, group), :] = v
+        for y in range(Y):
+            prim = [cur[at(f, y, group), :] for f in range(F)]
             for f, v in enumerate(conserved(prim)):
-                cur[f, x, rows_of(jv), :] = v
-        faces(pos, cur, jv, x_in, x_out, y_low, y_high)
+                if f:
+                    cur[at(f, y, group), :] = v
         return 0
 
-    lax.fori_loop(0, HALF // 8, convert, 0)
-    y_faces(pos, y_low, y_high, y_in, y_out)
+    lax.fori_loop(0, 3, convert, 0)
+    faces(pos, cur, x_in, x_out, y_in, y_out)
 
 
 def section(number, pos, *refs):
@@ -234,54 +247,57 @@
     else:
         initial, cur = refs[:2]
         refs = refs[2:]
-    x_in, x_out, y_in, y_out, y_low, y_high = refs[:6]
-    new = refs[6]
+    x_in, x_out, y_in, y_out = refs[:4]
+    new = refs[4]
+    edge = refs[-1]
     zx, zy = tile_x(pos[0]), tile_y(pos[0])
     weight = (0.0, 0.75, 1.0 / 3.0)[number]
 
-    def step(jv, _):
-        rows = rows_of(jv)
-        lane = lax.broadcasted_iota(jnp.int32, (8, L), 1)
-        height = lane % 16
-        low_y, high_y = lane < 16, lane >= L - 16
+    def step(group, _):
+        height = lax.broadcasted_iota(jnp.int32, (8, L), 1) % 16
+        sub = lax.broadcasted_iota(jnp.int32, (8, L), 0)
         floor, roof = height == 0, height == 15
+        left, right = sub == 0, sub == 7
         first_x = jnp.full((8, L), zx, jnp.int32) == 0
         first_y = jnp.full((8, L), zy, jnp.int32) == 0
 
         def halo(inner, outer, first):
-            a = [inner[f, rows, :] for f in range(F)]
-            b = [outer[f, rows, :] for f in range(F)]
+            a = [inner[layer_at(f, group), :] for f in range(F)]
+            b = [outer[layer_at(f, group), :] for f in range(F)]
             low = [jnp.where(first, o, i) for i, o in zip(a, b)]
             high = [jnp.where(first, i, o) for i, o in zip(a, b)]
             return low, high
 
+        def all_of(cons, n):
+            return side(cons, terms(cons), n)
+
+        x_before, x_after = halo(x_in, x_out, first_x)
+        mine_low = [cur[x_layer_at(f, group, 0), :] for f in range(F)]
+        mine_high = [cur[x_layer_at(f, group, 7), :] for f in range(F)]
+        for f, v in enumerate(double_flux(all_of(x_before, 0), all_of(mine_low, 0), 0)):
+            edge[f * 8 : f * 8 + 8, :] = v
+        for f, v in enumerate(double_flux(all_of(mine_high, 0), all_of(x_after, 0), 0)):
+            edge[(F + f) * 8 : (F + f) * 8 + 8, :] = v
+
         y_before, y_after = halo(y_in, y_out, first_y)
-        mine_low = [y_low[f, rows, :] for f in range(F)]
-        mine_high = [y_high[f, rows, :] for f in range(F)]
-        flux_low = double_flux(side(y_before, terms(y_before), 1), side(mine_low, terms(mine_low), 1), 1)
-        flux_high = double_flux(side(mine_high, terms(mine_high), 1), side(y_after, terms(y_after), 1), 1)
-
-        x_before, x_after = halo(x_in, x_out, first_x)
-        behind = side(x_before, terms(x_before), 0)
-        cons = [cur[f, 0, rows, :] for f in range(F)]
+        cons = [cur[at(f, 0, group), :] for f in range(F)]
         t = terms(cons)
-        here = side(cons, t, 0)
-        flux_x = double_flux(behind, here, 0)
-        for x in range(X):
-            if x < X - 1:
-                cons_next = [cur[f, x + 1, rows, :] for f in range(F)]
-            else:
-                cons_next = x_after
+        here = side(cons, t, 1)
+        flux_y = double_flux(all_of(y_before, 1), here, 1)
+        for y in range(Y):
+            cons_next = [cur[at(f, y + 1, group), :] for f in range(F)] if y < Y - 1 else y_after
             t_next = terms(cons_next)
-            ahead = side(cons_next, t_next, 0)
-            flux_next = double_flux(here, ahead, 0)
-            change = [b - a for a, b in zip(flux_x, flux_next)]
-
-            low = side(cons, t, 1)
-            flux = double_flux(low, [rolled(q, -16) for q in low], 1)
+            ahead = side(cons_next, t_next, 1)
+            flux_next = double_flux(here, ahead, 1)
+            change = [b - a for a, b in zip(flux_y, flux_next)]
+
+            low = side(cons, t, 0)
+            flux = double_flux(low, [pltpu.roll(q, 7, 0) for q in low], 0)
             for f in range(F):
-                upper = jnp.where(high_y, rolled(flux_high[f], L - 16 - 16 * x), flux[f])
-                lower = jnp.where(low_y, rolled(flux_low[f], -16 * x), rolled(flux[f], 16))
+                lowest = jnp.broadcast_to(edge[f * 8 + y : f * 8 + y + 1, :], (8, L))
+                highest = jnp.broadcast_to(edge[(F + f) * 8 + y : (F + f) * 8 + y + 1, :], (8, L))
+                upper = jnp.where(right, highest, flux[f])
+                lower = jnp.where(left, lowest, pltpu.roll(flux[f], 1, 0))
                 change[f] = change[f] + (upper - lower)
 
             low = side(cons, t, 2)
@@ -294,21 +310,23 @@
 
             out = [c - (0.5 * STEP) * d for c, d in zip(cons, change)]
             if number:
-                out = [
-                    weight * initial[f, x, rows, :] + (1.0 - weight) * o for f, o in enumerate(out)
-                ]
+                out = [weight * initial[at(f, y, group), :] + (1.0 - weight) * o for f, o in enumerate(out)]
             if number == 2:
                 out = primitive(out)
+            into = refs[-2] if number == 2 else new
             for f in range(F):
-                new[f, x, rows, :] = out[f]
-            cons, t, here, flux_x = cons_next, t_next, ahead, flux_next
-        if number < 2:
-            faces(pos, new, jv, *refs[7:11])
+                into[at(f, y, group), :] = out[f]
+            cons, t, here, flux_y = cons_next, t_next, ahead, flux_next
+        if number == 2:
+            for f in range(F):
+                vectors = [refs[-2][at(f, y, group), :] for y in range(Y)]
+                for i, v in enumerate(transposed(vectors)):
+                    new[group * 8 + i, f] = v
         return 0
 
-    lax.fori_loop(0, HALF // 8, step, 0)
+    lax.fori_loop(0, 3, step, 0)
     if number < 2:
-        y_faces(pos, *refs[9:13])
+        faces(pos, new, *refs[5:9])
 
 
 def pack_out(pos, final, mine, other, *outs):
@@ -317,12 +335,10 @@
         d = (z ^ k) * 2 + core
         for s in range(OUT):
             j = final[d * 8 + s]
-            row = jnp.maximum(j, 0) // 2
-            kind = jnp.full((X, L), jnp.where(j < 0, 2, j % 2 ^ core), jnp.int32)
+            row = jnp.maximum(j, 0) >> 1
+            kind = jnp.full((X, L), jnp.where(j < 0, 2, (j & 1) ^ core), jnp.int32)
             for f in range(F):
-                at = pl.ds(f * X * HALF + row, X, HALF)
-                a, b = mine[at, :], other[at, :]
-                outs[k][s, f] = jnp.where(kind == 0, a, jnp.where(kind == 1, b, 0.0))
+                outs[k][s, f] = jnp.where(kind == 0, mine[row, f], jnp.where(kind == 1, other[row, f], 0.0))
 
 
 def body(block_cells, slot_blocks):
@@ -353,31 +369,37 @@
         compiler_params=PARAMS,
         name="pack_in",
     )(pos, block_cells)
-    final = pl.pallas_call(
+    final, rows, own = pl.pallas_call(
         table,
-        out_shape=jax.ShapeDtypeStruct((N_ROW * 8,), jnp.int32),
-        in_specs=[SMEM, SMEM],
-        out_specs=SMEM,
+        out_shape=[
+            jax.ShapeDtypeStruct((N_ROW * 8,), jnp.int32),
+            jax.ShapeDtypeStruct((N_ROW * CAP,), jnp.int32),
+            tiles[0],
+        ],
+        in_specs=[SMEM, SMEM, ANY],
+        out_specs=[SMEM, SMEM, ANY],
+        input_output_aliases={2: 2},
         scratch_shapes=[pltpu.SMEM((N_ROW * 16,), jnp.int32), pltpu.SMEM((N_ROW,), jnp.int32)],
         compiler_params=PARAMS,
+        cost_estimate=pl.CostEstimate(flops=0, bytes_accessed=20_000_000, transcendentals=0),
         name="table",
-    )(pos, slot_blocks)
+    )(pos, slot_blocks, parts[0])
     gathered = []
     for k in range(4):
-        here = over_z(parts[k], k)
+        here = over_z(parts[k], k) if k else own
         gathered += [here, over_core(here)]
 
-    whole = shape(F, X, HALF, L)
-    layer = shape(F, HALF, L)
-    initial, x_in, x_out, y_low, y_high, y_in, y_out = pl.pallas_call(
+    whole = shape(F * Y * HALF, L)
+    layer = shape(F * HALF, L)
+    initial, x_in, x_out, y_in, y_out = pl.pallas_call(
         reorder,
-        out_shape=[whole] + [layer] * 6,
+        out_shape=[whole] + [layer] * 4,
         in_specs=[SMEM, SMEM] + [VMEM] * 8,
-        out_specs=[VMEM] * 7,
-        scratch_shapes=[pltpu.VMEM((F * X * PAD, L), jnp.float32)],
+        out_specs=[VMEM] * 5,
+        scratch_shapes=[pltpu.VMEM((HALF + 1, F, X, L), jnp.float32)],
         compiler_params=PARAMS,
         name="reorder",
-    )(pos, slot_blocks, *gathered)
+    )(pos, rows, *gathered)
 
     def x_partner(z):
         return z ^ 1
@@ -397,20 +419,23 @@
     for number in range(3):
         halos = exchanged(x_in, x_out, y_in, y_out)
         states = (current,) if number == 0 else (initial, current)
-        outs = [whole] + ([layer] * 6 if number < 2 else [])
+        outs = [whole] + [layer] * 4 if number < 2 else [shape(HALF, F, X, L)]
+        scratch = [pltpu.VMEM((2 * F * 8, L), jnp.float32)]
+        if number == 2:
+            scratch = [pltpu.VMEM((F * Y * HALF, L), jnp.float32)] + scratch
         made = pl.pallas_call(
             lambda *refs, number=number: section(number, *refs),
             out_shape=outs,
-            in_specs=[SMEM] + [VMEM] * (len(states) + 6),
+            in_specs=[SMEM] + [VMEM] * (len(states) + 4),
             out_specs=[VMEM] * len(outs),
+            scratch_shapes=scratch,
             compiler_params=PARAMS,
             name="section" + str(number),
-        )(pos, *states, *halos, y_low, y_high)
+        )(pos, *states, *halos)
         current = made[0]
         if number < 2:
-            x_in, x_out, y_low, y_high, y_in, y_out = made[1:]
-
-    flat = current.reshape(F * X * HALF, L)
+            x_in, x_out, y_in, y_out = made[1:]
+
     leaving = pl.pallas_call(
         pack_out,
         out_shape=[shape(OUT, F, X, L)] * 4,
@@ -418,7 +443,7 @@
         out_specs=[VMEM] * 4,
         compiler_params=PARAMS,
         name="pack_out",
-    )(pos, final, flat, over_core(flat))
+    )(pos, final, current, over_core(current))
     arrived = [over_z(leaving[k], k) for k in range(4)]
     return pl.pallas_call(
         unpack_out,

time: 94.8 us -> 87.2 us (0.920)
  Pallas kernels: 21.8 us -> 13.1 us
  waiting for transfers between devices: 34.2 us -> 37.7 us
  starting transfers between devices: 37.2 us -> 34.8 us
    pallas_call x3, Pallas kernels: 11.5 us -> 5.73 us  [body(): pl.pallas_call(lambda *refs, number=number: section(number, *refs), out_s...]
    ppermute x23, waiting for transfers between devices: 34.2 us -> 37.7 us  [to(): return lax.ppermute(array, ('row', 'col'), pairs)]
    pallas_call x2, Pallas kernels: 7.27 us -> 4.57 us  [the longest x1 2.98 us: body(): pl.pallas_call(table, out_shape=[jax.ShapeDtypeStruct((N_ROW * 8,), jnp.i...]
    ppermute x23, starting transfers between devices: 37.2 us -> 34.8 us  [to(): return lax.ppermute(array, ('row', 'col'), pairs)]
where the time goes in v2:
time: 87.2 us; the launch traced here: 87.1 us
  waiting for transfers between devices  37.7 us (43%)
  starting transfers between devices  34.8 us (40%)
  Pallas kernels  13.1 us (15%)
  local copies, waits for them, and re-layouts  1.29 us (1%)
    ppermute x23, waiting for transfers between devices, to(): return lax.ppermute(array, ('row', 'col'), pairs)  37.7 us
    ppermute x23, starting transfers between devices, to(): return lax.ppermute(array, ('row', 'col'), pairs)  34.8 us
    pallas_call x3, Pallas kernels, body(): pl.pallas_call(lambda *refs, number=number: section(number, *refs), out_s...  5.73 us
    pallas_call x1, Pallas kernels, body(): pl.pallas_call(table, out_shape=[jax.ShapeDtypeStruct((N_ROW * 8,), jnp.i...  2.98 us
  transfers between devices with their start and end apart: 23, of which 13 were waited for; matrix products, arithmetic and copies ran while one was open for 0% of the time, Pallas kernels for 3%

profile of v2, /device:TPU:1, one launch (start us, length us, event | category | flops | bytes accessed | tf_op | source)
XLA Modules:
  0.0 87.1 jit_solution(15082442298513071626)
XLA Ops:
  0.0 0.1 pad_add_fusion.pos.refs_0_
  0.1 0.0 copy-start
  0.1 1.2 %copy-done = f32[11,5,16,256]{3,2,1,0:T(8,128)S(1)} copy-done((f32[11,5,16,256]{3,2,1,0:T(8,128)S(1)}, f32[11,5,16,256]{3,2,1,0:T(8,128)}, u32[]{:S(2)}) %copy-start) | copy-done | bytes 901144
  1.3 0.0 copy-start.1
  1.3 0.8 pack_in.1
  2.0 2.5 %collective-permute-start.1 = (f32[11,5,8,128]{3,2,1,0:T(8,128)S(1)}, f32[11,5,8,128]{3,2,1,0:T(8,128)S(1)}, u32[]{:S(2)}, u32[]{:S(2)}) collective-permute-start(f32[11,5,8,128]{3,2,1,0:T(8,128)S(1)} %get-tuple-element.35), channel_id=1, source_target_pairs={{0,32},{1,33},{2,34},{3,35},{4,36},{5,37},{6,38},{7,39},{8,40},{9,... | collective-permute-start | bytes 675848 | tf_op jit(solution)/shard_map/ppermute | solution.py:354
  4.6 3.3 %collective-permute-start.3 = (f32[11,5,8,128]{3,2,1,0:T(8,128)S(1)}, f32[11,5,8,128]{3,2,1,0:T(8,128)S(1)}, u32[]{:S(2)}, u32[]{:S(2)}) collective-permute-start(f32[11,5,8,128]{3,2,1,0:T(8,128)S(1)} %get-tuple-element.36), channel_id=1, source_target_pairs={{0,64},{1,65},{2,66},{3,67},{4,68},{5,69},{6,70},{7,71},{8,72},{9,... | collective-permute-start | bytes 675848 | tf_op jit(solution)/shard_map/ppermute | solution.py:354
  7.9 0.0 collective-permute-start.5
  7.9 0.0 copy-done.1
  7.9 0.1 copy.4.slots
  8.0 3.0 %table.1 = (s32[64]{0:T(128)S(1)}, s32[88]{0:T(128)S(1)}, f32[11,5,8,128]{3,2,1,0:T(8,128)S(1)}) custom-call(s32[3]{0:T(128)S(1)} %pad_add_fusion.pos.refs_0_, s32[128,11]{1,0:T(8,128)S(1)} %copy.4.slots, f32[11,5,8,128]{3,2,1,0:T(8,128)S(1)} %get-tuple-element.31._tile), custom_call_target="tpu_custom_call", output_to_operand_aliasing={{2}: (2, {})} | custom-call | bytes 20000000 | tf_op jit(solution)/shard_map/table/pallas_call | solution.py:372
  11.0 1.3 %collective-permute-start = (f32[11,5,8,128]{3,2,1,0:T(8,128)S(1)}, f32[11,5,8,128]{3,2,1,0:T(8,128)S(1)}, u32[]{:S(2)}, u32[]{:S(2)}) collective-permute-start(f32[11,5,8,128]{3,2,1,0:T(8,128)S(1)} %get-tuple-element.34.refs_0_), channel_id=1, source_target_pairs={{0,16},{1,17},{2,18},{3,19},{4,20},{5,21},{6,22},{7,23},{8,24},{9,... | collective-permute-start | bytes 675848 | tf_op jit(solution)/shard_map/ppermute | solution.py:354
  12.3 0.0 collective-permute-done.1.refs_2_
  12.3 0.1 collective-permute-start.2
  12.4 5.3 %collective-permute-done.3.refs_4_ = f32[11,5,8,128]{3,2,1,0:T(8,128)S(1)} collective-permute-done((f32[11,5,8,128]{3,2,1,0:T(8,128)S(1)}, f32[11,5,8,128]{3,2,1,0:T(8,128)S(1)}, u32[]{:S(2)}, u32[]{:S(2)}) %collective-permute-start.3) | collective-permute-done | bytes 225312 | tf_op jit(solution)/shard_map/ppermute | solution.py:354
  17.7 1.6 %collective-permute-start.4 = (f32[11,5,8,128]{3,2,1,0:T(8,128)S(1)}, f32[11,5,8,128]{3,2,1,0:T(8,128)S(1)}, u32[]{:S(2)}, u32[]{:S(2)}) collective-permute-start(f32[11,5,8,128]{3,2,1,0:T(8,128)S(1)} %collective-permute-done.3.refs_4_), channel_id=1, source_target_pairs={{0,16},{1,17},{2,18},{3,19},{4,20},{5,21},{6,22},{7,23},{8,24},{9,... | collective-permute-start | bytes 675848 | tf_op jit(solution)/shard_map/ppermute | solution.py:354
  19.3 0.8 collective-permute-done.5.refs_6_
  20.0 1.8 %collective-permute-start.6 = (f32[11,5,8,128]{3,2,1,0:T(8,128)S(1)}, f32[11,5,8,128]{3,2,1,0:T(8,128)S(1)}, u32[]{:S(2)}, u32[]{:S(2)}) collective-permute-start(f32[11,5,8,128]{3,2,1,0:T(8,128)S(1)} %collective-permute-done.5.refs_6_), channel_id=1, source_target_pairs={{0,16},{1,17},{2,18},{3,19},{4,20},{5,21},{6,22},{7,23},{8,24},{9,... | collective-permute-start | bytes 675848 | tf_op jit(solution)/shard_map/ppermute | solution.py:354
  21.8 0.0 collective-permute-done.refs_1_
  21.8 0.0 collective-permute-done.2.refs_3_
  21.9 0.0 collective-permute-done.4.refs_5_
  21.9 1.1 %collective-permute-done.6.refs_7_ = f32[11,5,8,128]{3,2,1,0:T(8,128)S(1)} collective-permute-done((f32[11,5,8,128]{3,2,1,0:T(8,128)S(1)}, f32[11,5,8,128]{3,2,1,0:T(8,128)S(1)}, u32[]{:S(2)}, u32[]{:S(2)}) %collective-permute-start.6) | collective-permute-done | bytes 225312 | tf_op jit(solution)/shard_map/ppermute | solution.py:354
  23.0 1.6 %reorder.1 = (f32[960,128]{1,0:T(8,128)S(1)}, f32[120,128]{1,0:T(8,128)S(1)}, f32[120,128]{1,0:T(8,128)S(1)}, f32[120,128]{1,0:T(8,128)S(1)}, f32[120,128]{1,0:T(8,128)S(1)}) custom-call(s32[3]{0:T(128)S(1)} %pad_add_fusion.pos.refs_0_, s32[88]{0:T(128)S(1)} %get-tuple-element.33.rows, f32[11,5,8,128]{3,2,1,0:T(8,128)S(1)} %get-tuple-element.34.refs_0_, ...), custom_call_target="tpu_custom_call" | custom-call | tf_op jit(solution)/shard_map/reorder/pallas_call | solution.py:394
  24.5 0.1 collective-permute-start.7
  24.6 6.1 %collective-permute-start.8 = (f32[120,128]{1,0:T(8,128)S(1)}, f32[120,128]{1,0:T(8,128)S(1)}, u32[]{:S(2)}, u32[]{:S(2)}) collective-permute-start(f32[120,128]{1,0:T(8,128)S(1)} %get-tuple-element.40), channel_id=1, source_target_pairs={{0,47},{1,32},{2,33},{3,34},{4,35},{5,36},{6,37},{7,38},{8,39},{9,... | collective-permute-start | bytes 184328 | tf_op jit(solution)/shard_map/ppermute | solution.py:354
  30.7 0.0 collective-permute-start.9
  30.7 4.0 %collective-permute-start.10 = (f32[120,128]{1,0:T(8,128)S(1)}, f32[120,128]{1,0:T(8,128)S(1)}, u32[]{:S(2)}, u32[]{:S(2)}) collective-permute-start(f32[120,128]{1,0:T(8,128)S(1)} %get-tuple-element.42), channel_id=1, source_target_pairs={{0,127},{1,112},{2,113},{3,114},{4,115},{5,116},{6,117},{7,118},{8... | collective-permute-start | bytes 184328 | tf_op jit(solution)/shard_map/ppermute | solution.py:354
  34.8 0.0 collective-permute-done.7.refs_2_
  34.8 0.0 collective-permute-done.8.refs_3_
  34.8 0.2 collective-permute-done.9.refs_4_
  35.0 5.3 %collective-permute-done.10.refs_5_ = f32[120,128]{1,0:T(8,128)S(1)} collective-permute-done((f32[120,128]{1,0:T(8,128)S(1)}, f32[120,128]{1,0:T(8,128)S(1)}, u32[]{:S(2)}, u32[]{:S(2)}) %collective-permute-start.10) | collective-permute-done | bytes 61472 | tf_op jit(solution)/shard_map/ppermute | solution.py:354
  40.3 1.7 %section0.1 = (f32[960,128]{1,0:T(8,128)S(1)}, f32[120,128]{1,0:T(8,128)S(1)}, f32[120,128]{1,0:T(8,128)S(1)}, f32[120,128]{1,0:T(8,128)S(1)}, f32[120,128]{1,0:T(8,128)S(1)}) custom-call(s32[3]{0:T(128)S(1)} %pad_add_fusion.pos.refs_0_, f32[960,128]{1,0:T(8,128)S(1)} %get-tuple-element.38.refs_1_, f32[120,128]{1,0:T(8,128)S(1)} %collective-permute-done.7.refs_2_, ...), custom_call_target="tpu_custom_call" | custom-call | tf_op jit(solution)/shard_map/section0/pallas_call | solution.py:426
  42.0 0.1 collective-permute-start.11
  42.1 0.1 collective-permute-start.12
  42.1 4.3 %collective-permute-start.13 = (f32[120,128]{1,0:T(8,128)S(1)}, f32[120,128]{1,0:T(8,128)S(1)}, u32[]{:S(2)}, u32[]{:S(2)}) collective-permute-start(f32[120,128]{1,0:T(8,128)S(1)} %get-tuple-element.46), channel_id=1, source_target_pairs={{0,96},{1,97},{2,98},{3,99},{4,100},{5,101},{6,102},{7,103},{8,104... | collective-permute-start | bytes 184328 | tf_op jit(solution)/shard_map/ppermute | solution.py:354
  46.4 0.0 collective-permute-start.14
  46.5 0.0 collective-permute-done.11.refs_3_
  46.5 3.0 %collective-permute-done.12.refs_4_ = f32[120,128]{1,0:T(8,128)S(1)} collective-permute-done((f32[120,128]{1,0:T(8,128)S(1)}, f32[120,128]{1,0:T(8,128)S(1)}, u32[]{:S(2)}, u32[]{:S(2)}) %collective-permute-start.12) | collective-permute-done | bytes 61472 | tf_op jit(solution)/shard_map/ppermute | solution.py:354
  49.4 0.0 collective-permute-done.13.refs_5_
  49.4 6.1 %collective-permute-done.14.refs_6_ = f32[120,128]{1,0:T(8,128)S(1)} collective-permute-done((f32[120,128]{1,0:T(8,128)S(1)}, f32[120,128]{1,0:T(8,128)S(1)}, u32[]{:S(2)}, u32[]{:S(2)}) %collective-permute-start.14) | collective-permute-done | bytes 61472 | tf_op jit(solution)/shard_map/ppermute | solution.py:354
  55.5 1.7 %section1.1 = (f32[960,128]{1,0:T(8,128)S(1)}, f32[120,128]{1,0:T(8,128)S(1)}, f32[120,128]{1,0:T(8,128)S(1)}, f32[120,128]{1,0:T(8,128)S(1)}, f32[120,128]{1,0:T(8,128)S(1)}) custom-call(s32[3]{0:T(128)S(1)} %pad_add_fusion.pos.refs_0_, f32[960,128]{1,0:T(8,128)S(1)} %get-tuple-element.38.refs_1_, f32[960,128]{1,0:T(8,128)S(1)} %get-tuple-element.43.refs_2_, ...), custom_call_target="tpu_custom_call" | custom-call | tf_op jit(solution)/shard_map/section1/pallas_call | solution.py:426
  57.3 0.1 collective-permute-start.15
  57.4 0.1 collective-permute-start.16
  57.4 2.7 %collective-permute-start.17 = (f32[120,128]{1,0:T(8,128)S(1)}, f32[120,128]{1,0:T(8,128)S(1)}, u32[]{:S(2)}, u32[]{:S(2)}) collective-permute-start(f32[120,128]{1,0:T(8,128)S(1)} %get-tuple-element.51), channel_id=1, source_target_pairs={{0,96},{1,97},{2,98},{3,99},{4,100},{5,101},{6,102},{7,103},{8,104... | collective-permute-start | bytes 184328 | tf_op jit(solution)/shard_map/ppermute | solution.py:354
  60.1 1.1 %collective-permute-start.18 = (f32[120,128]{1,0:T(8,128)S(1)}, f32[120,128]{1,0:T(8,128)S(1)}, u32[]{:S(2)}, u32[]{:S(2)}) collective-permute-start(f32[120,128]{1,0:T(8,128)S(1)} %get-tuple-element.52), channel_id=1, source_target_pairs={{0,127},{1,112},{2,113},{3,114},{4,115},{5,116},{6,117},{7,118},{8... | collective-permute-start | bytes 184328 | tf_op jit(solution)/shard_map/ppermute | solution.py:354
  61.2 0.0 collective-permute-done.15.refs_3_
  61.2 3.6 %collective-permute-done.16.refs_4_ = f32[120,128]{1,0:T(8,128)S(1)} collective-permute-done((f32[120,128]{1,0:T(8,128)S(1)}, f32[120,128]{1,0:T(8,128)S(1)}, u32[]{:S(2)}, u32[]{:S(2)}) %collective-permute-start.16) | collective-permute-done | bytes 61472 | tf_op jit(solution)/shard_map/ppermute | solution.py:354
  64.7 0.0 collective-permute-done.17.refs_5_
  64.7 4.5 %collective-permute-done.18.refs_6_ = f32[120,128]{1,0:T(8,128)S(1)} collective-permute-done((f32[120,128]{1,0:T(8,128)S(1)}, f32[120,128]{1,0:T(8,128)S(1)}, u32[]{:S(2)}, u32[]{:S(2)}) %collective-permute-start.18) | collective-permute-done | bytes 61472 | tf_op jit(solution)/shard_map/ppermute | solution.py:354
  69.2 2.3 %section2.1.mine = f32[24,5,8,128]{3,2,1,0:T(8,128)S(1)} custom-call(s32[3]{0:T(128)S(1)} %pad_add_fusion.pos.refs_0_, f32[960,128]{1,0:T(8,128)S(1)} %get-tuple-element.38.refs_1_, f32[960,128]{1,0:T(8,128)S(1)} %get-tuple-element.48.refs_2_, f32[120,128]{1,0:T(8,128)S(1)} %collective-permute-done.15.refs_3_, ...), custom_call_target="tpu_custom_call" | custom-call | tf_op jit(solution)/shard_map/section2/pallas_call | solution.py:426
  71.5 1.6 %collective-permute-start.19 = (f32[24,5,8,128]{3,2,1,0:T(8,128)S(1)}, f32[24,5,8,128]{3,2,1,0:T(8,128)S(1)}, u32[]{:S(2)}, u32[]{:S(2)}) collective-permute-start(f32[24,5,8,128]{3,2,1,0:T(8,128)S(1)} %section2.1.mine), channel_id=1, source_target_pairs={{0,16},{1,17},{2,18},{3,19},{4,20},{5,21},{6,22},{7,23},{8,24},{9,... | collective-permute-start | bytes 1474568 | tf_op jit(solution)/shard_map/ppermute | solution.py:354
  73.1 1.5 %collective-permute-done.19.other = f32[24,5,8,128]{3,2,1,0:T(8,128)S(1)} collective-permute-done((f32[24,5,8,128]{3,2,1,0:T(8,128)S(1)}, f32[24,5,8,128]{3,2,1,0:T(8,128)S(1)}, u32[]{:S(2)}, u32[]{:S(2)}) %collective-permute-start.19) | collective-permute-done | bytes 491552 | tf_op jit(solution)/shard_map/ppermute | solution.py:354
  74.6 0.7 pack_out.1
  75.3 0.1 collective-permute-start.20
  75.4 0.1 collective-permute-start.21
  75.5 3.8 %collective-permute-start.22 = (f32[7,5,8,128]{3,2,1,0:T(8,128)S(1)}, f32[7,5,8,128]{3,2,1,0:T(8,128)S(1)}, u32[]{:S(2)}, u32[]{:S(2)}) collective-permute-start(f32[7,5,8,128]{3,2,1,0:T(8,128)S(1)} %get-tuple-element.56), channel_id=1, source_target_pairs={{0,96},{1,97},{2,98},{3,99},{4,100},{5,101},{6,102},{7,103},{8,104... | collective-permute-start | bytes 430088 | tf_op jit(solution)/shard_map/ppermute | solution.py:354
  79.2 1.1 %collective-permute-done.20.refs_1_ = f32[7,5,8,128]{3,2,1,0:T(8,128)S(1)} collective-permute-done((f32[7,5,8,128]{3,2,1,0:T(8,128)S(1)}, f32[7,5,8,128]{3,2,1,0:T(8,128)S(1)}, u32[]{:S(2)}, u32[]{:S(2)}) %collective-permute-start.20) | collective-permute-done | bytes 143392 | tf_op jit(solution)/shard_map/ppermute | solution.py:354
  80.3 1.6 %collective-permute-done.21.refs_2_ = f32[7,5,8,128]{3,2,1,0:T(8,128)S(1)} collective-permute-done((f32[7,5,8,128]{3,2,1,0:T(8,128)S(1)}, f32[7,5,8,128]{3,2,1,0:T(8,128)S(1)}, u32[]{:S(2)}, u32[]{:S(2)}) %collective-permute-start.21) | collective-permute-done | bytes 143392 | tf_op jit(solution)/shard_map/ppermute | solution.py:354
  81.9 3.8 %collective-permute-done.22.refs_3_ = f32[7,5,8,128]{3,2,1,0:T(8,128)S(1)} collective-permute-done((f32[7,5,8,128]{3,2,1,0:T(8,128)S(1)}, f32[7,5,8,128]{3,2,1,0:T(8,128)S(1)}, u32[]{:S(2)}, u32[]{:S(2)}) %collective-permute-start.22) | collective-permute-done | bytes 143392 | tf_op jit(solution)/shard_map/ppermute | solution.py:354
  85.7 1.4 %unpack_out.1 = f32[7,5,16,256]{3,2,1,0:T(8,128)} custom-call(s32[3]{0:T(128)S(1)} %pad_add_fusion.pos.refs_0_, f32[7,5,8,128]{3,2,1,0:T(8,128)S(1)} %get-tuple-element.53.refs_0_, f32[7,5,8,128]{3,2,1,0:T(8,128)S(1)} %collective-permute-done.20.refs_1_, f32[7,5,8,128]{3,2,1,0:T(8,128)S(1)} %collective-permute-done.21.refs_2_, ...), custom_call_target="tpu_custom_call" | custom-call | tf_op jit(solution)/shard_map/unpack_out/pallas_call | solution.py:448
Async XLA Ops:
  0.1 1.2 %copy-start = (f32[11,5,16,256]{3,2,1,0:T(8,128)S(1)}, f32[11,5,16,256]{3,2,1,0:T(8,128)}, u32[]{:S(2)}) copy-start(f32[11,5,16,256]{3,2,1,0:T(8,128)} %cells.1) | copy-start | bytes 2703364
  1.3 6.6 %copy-start.1 = (s32[128,11]{0,1:T(8,128)S(1)}, s32[128,11]{0,1:T(8,128)}, u32[]{:S(2)}) copy-start(s32[128,11]{0,1:T(8,128)} %param.3) | copy-start | bytes 16900
  2.0 10.3 %collective-permute-start.1 = (f32[11,5,8,128]{3,2,1,0:T(8,128)S(1)}, f32[11,5,8,128]{3,2,1,0:T(8,128)S(1)}, u32[]{:S(2)}, u32[]{:S(2)}) collective-permute-start(f32[11,5,8,128]{3,2,1,0:T(8,128)S(1)} %get-tuple-element.35), channel_id=1, source_target_pairs={{0,32},{1,33},{2,34},{3,35},{4,36},{5,37},{6,38},{7,39},{8,40},{9,... | collective-permute-start | bytes 675848 | tf_op jit(solution)/shard_map/ppermute | solution.py:354
  4.6 13.1 %collective-permute-start.3 = (f32[11,5,8,128]{3,2,1,0:T(8,128)S(1)}, f32[11,5,8,128]{3,2,1,0:T(8,128)S(1)}, u32[]{:S(2)}, u32[]{:S(2)}) collective-permute-start(f32[11,5,8,128]{3,2,1,0:T(8,128)S(1)} %get-tuple-element.36), channel_id=1, source_target_pairs={{0,64},{1,65},{2,66},{3,67},{4,68},{5,69},{6,70},{7,71},{8,72},{9,... | collective-permute-start | bytes 675848 | tf_op jit(solution)/shard_map/ppermute | solution.py:354
  7.9 12.2 %collective-permute-start.5 = (f32[11,5,8,128]{3,2,1,0:T(8,128)S(1)}, f32[11,5,8,128]{3,2,1,0:T(8,128)S(1)}, u32[]{:S(2)}, u32[]{:S(2)}) collective-permute-start(f32[11,5,8,128]{3,2,1,0:T(8,128)S(1)} %get-tuple-element.37), channel_id=1, source_target_pairs={{0,96},{1,97},{2,98},{3,99},{4,100},{5,101},{6,102},{7,103},{8,104... | collective-permute-start | bytes 675848 | tf_op jit(solution)/shard_map/ppermute | solution.py:354
  11.0 10.9 %collective-permute-start = (f32[11,5,8,128]{3,2,1,0:T(8,128)S(1)}, f32[11,5,8,128]{3,2,1,0:T(8,128)S(1)}, u32[]{:S(2)}, u32[]{:S(2)}) collective-permute-start(f32[11,5,8,128]{3,2,1,0:T(8,128)S(1)} %get-tuple-element.34.refs_0_), channel_id=1, source_target_pairs={{0,16},{1,17},{2,18},{3,19},{4,20},{5,21},{6,22},{7,23},{8,24},{9,... | collective-permute-start | bytes 675848 | tf_op jit(solution)/shard_map/ppermute | solution.py:354
  12.3 9.6 %collective-permute-start.2 = (f32[11,5,8,128]{3,2,1,0:T(8,128)S(1)}, f32[11,5,8,128]{3,2,1,0:T(8,128)S(1)}, u32[]{:S(2)}, u32[]{:S(2)}) collective-permute-start(f32[11,5,8,128]{3,2,1,0:T(8,128)S(1)} %collective-permute-done.1.refs_2_), channel_id=1, source_target_pairs={{0,16},{1,17},{2,18},{3,19},{4,20},{5,21},{6,22},{7,23},{8,24},{9,... | collective-permute-start | bytes 675848 | tf_op jit(solution)/shard_map/ppermute | solution.py:354
  17.7 4.2 %collective-permute-start.4 = (f32[11,5,8,128]{3,2,1,0:T(8,128)S(1)}, f32[11,5,8,128]{3,2,1,0:T(8,128)S(1)}, u32[]{:S(2)}, u32[]{:S(2)}) collective-permute-start(f32[11,5,8,128]{3,2,1,0:T(8,128)S(1)} %collective-permute-done.3.refs_4_), channel_id=1, source_target_pairs={{0,16},{1,17},{2,18},{3,19},{4,20},{5,21},{6,22},{7,23},{8,24},{9,... | collective-permute-start | bytes 675848 | tf_op jit(solution)/shard_map/ppermute | solution.py:354
  20.0 2.9 %collective-permute-start.6 = (f32[11,5,8,128]{3,2,1,0:T(8,128)S(1)}, f32[11,5,8,128]{3,2,1,0:T(8,128)S(1)}, u32[]{:S(2)}, u32[]{:S(2)}) collective-permute-start(f32[11,5,8,128]{3,2,1,0:T(8,128)S(1)} %collective-permute-done.5.refs_6_), channel_id=1, source_target_pairs={{0,16},{1,17},{2,18},{3,19},{4,20},{5,21},{6,22},{7,23},{8,24},{9,... | collective-permute-start | bytes 675848 | tf_op jit(solution)/shard_map/ppermute | solution.py:354
  24.5 10.2 %collective-permute-start.7 = (f32[120,128]{1,0:T(8,128)S(1)}, f32[120,128]{1,0:T(8,128)S(1)}, u32[]{:S(2)}, u32[]{:S(2)}) collective-permute-start(f32[120,128]{1,0:T(8,128)S(1)} %get-tuple-element.39), channel_id=1, source_target_pairs={{0,32},{1,33},{2,34},{3,35},{4,36},{5,37},{6,38},{7,39},{8,40},{9,... | collective-permute-start | bytes 184328 | tf_op jit(solution)/shard_map/ppermute | solution.py:354
  24.6 10.1 %collective-permute-start.8 = (f32[120,128]{1,0:T(8,128)S(1)}, f32[120,128]{1,0:T(8,128)S(1)}, u32[]{:S(2)}, u32[]{:S(2)}) collective-permute-start(f32[120,128]{1,0:T(8,128)S(1)} %get-tuple-element.40), channel_id=1, source_target_pairs={{0,47},{1,32},{2,33},{3,34},{4,35},{5,36},{6,37},{7,38},{8,39},{9,... | collective-permute-start | bytes 184328 | tf_op jit(solution)/shard_map/ppermute | solution.py:354
  30.7 4.3 %collective-permute-start.9 = (f32[120,128]{1,0:T(8,128)S(1)}, f32[120,128]{1,0:T(8,128)S(1)}, u32[]{:S(2)}, u32[]{:S(2)}) collective-permute-start(f32[120,128]{1,0:T(8,128)S(1)} %get-tuple-element.41), channel_id=1, source_target_pairs={{0,96},{1,97},{2,98},{3,99},{4,100},{5,101},{6,102},{7,103},{8,104... | collective-permute-start | bytes 184328 | tf_op jit(solution)/shard_map/ppermute | solution.py:354
  30.7 9.6 %collective-permute-start.10 = (f32[120,128]{1,0:T(8,128)S(1)}, f32[120,128]{1,0:T(8,128)S(1)}, u32[]{:S(2)}, u32[]{:S(2)}) collective-permute-start(f32[120,128]{1,0:T(8,128)S(1)} %get-tuple-element.42), channel_id=1, source_target_pairs={{0,127},{1,112},{2,113},{3,114},{4,115},{5,116},{6,117},{7,118},{8... | collective-permute-start | bytes 184328 | tf_op jit(solution)/shard_map/ppermute | solution.py:354
  42.0 4.5 %collective-permute-start.11 = (f32[120,128]{1,0:T(8,128)S(1)}, f32[120,128]{1,0:T(8,128)S(1)}, u32[]{:S(2)}, u32[]{:S(2)}) collective-permute-start(f32[120,128]{1,0:T(8,128)S(1)} %get-tuple-element.44), channel_id=1, source_target_pairs={{0,32},{1,33},{2,34},{3,35},{4,36},{5,37},{6,38},{7,39},{8,40},{9,... | collective-permute-start | bytes 184328 | tf_op jit(solution)/shard_map/ppermute | solution.py:354
  42.1 7.4 %collective-permute-start.12 = (f32[120,128]{1,0:T(8,128)S(1)}, f32[120,128]{1,0:T(8,128)S(1)}, u32[]{:S(2)}, u32[]{:S(2)}) collective-permute-start(f32[120,128]{1,0:T(8,128)S(1)} %get-tuple-element.45), channel_id=1, source_target_pairs={{0,47},{1,32},{2,33},{3,34},{4,35},{5,36},{6,37},{7,38},{8,39},{9,... | collective-permute-start | bytes 184328 | tf_op jit(solution)/shard_map/ppermute | solution.py:354
  42.1 7.3 %collective-permute-start.13 = (f32[120,128]{1,0:T(8,128)S(1)}, f32[120,128]{1,0:T(8,128)S(1)}, u32[]{:S(2)}, u32[]{:S(2)}) collective-permute-start(f32[120,128]{1,0:T(8,128)S(1)} %get-tuple-element.46), channel_id=1, source_target_pairs={{0,96},{1,97},{2,98},{3,99},{4,100},{5,101},{6,102},{7,103},{8,104... | collective-permute-start | bytes 184328 | tf_op jit(solution)/shard_map/ppermute | solution.py:354
  46.4 9.1 %collective-permute-start.14 = (f32[120,128]{1,0:T(8,128)S(1)}, f32[120,128]{1,0:T(8,128)S(1)}, u32[]{:S(2)}, u32[]{:S(2)}) collective-permute-start(f32[120,128]{1,0:T(8,128)S(1)} %get-tuple-element.47), channel_id=1, source_target_pairs={{0,127},{1,112},{2,113},{3,114},{4,115},{5,116},{6,117},{7,118},{8... | collective-permute-start | bytes 184328 | tf_op jit(solution)/shard_map/ppermute | solution.py:354
  57.3 3.9 %collective-permute-start.15 = (f32[120,128]{1,0:T(8,128)S(1)}, f32[120,128]{1,0:T(8,128)S(1)}, u32[]{:S(2)}, u32[]{:S(2)}) collective-permute-start(f32[120,128]{1,0:T(8,128)S(1)} %get-tuple-element.49), channel_id=1, source_target_pairs={{0,32},{1,33},{2,34},{3,35},{4,36},{5,37},{6,38},{7,39},{8,40},{9,... | collective-permute-start | bytes 184328 | tf_op jit(solution)/shard_map/ppermute | solution.py:354
  57.4 7.4 %collective-permute-start.16 = (f32[120,128]{1,0:T(8,128)S(1)}, f32[120,128]{1,0:T(8,128)S(1)}, u32[]{:S(2)}, u32[]{:S(2)}) collective-permute-start(f32[120,128]{1,0:T(8,128)S(1)} %get-tuple-element.50), channel_id=1, source_target_pairs={{0,47},{1,32},{2,33},{3,34},{4,35},{5,36},{6,37},{7,38},{8,39},{9,... | collective-permute-start | bytes 184328 | tf_op jit(solution)/shard_map/ppermute | solution.py:354
  57.4 7.3 %collective-permute-start.17 = (f32[120,128]{1,0:T(8,128)S(1)}, f32[120,128]{1,0:T(8,128)S(1)}, u32[]{:S(2)}, u32[]{:S(2)}) collective-permute-start(f32[120,128]{1,0:T(8,128)S(1)} %get-tuple-element.51), channel_id=1, source_target_pairs={{0,96},{1,97},{2,98},{3,99},{4,100},{5,101},{6,102},{7,103},{8,104... | collective-permute-start | bytes 184328 | tf_op jit(solution)/shard_map/ppermute | solution.py:354
  60.1 9.1 %collective-permute-start.18 = (f32[120,128]{1,0:T(8,128)S(1)}, f32[120,128]{1,0:T(8,128)S(1)}, u32[]{:S(2)}, u32[]{:S(2)}) collective-permute-start(f32[120,128]{1,0:T(8,128)S(1)} %get-tuple-element.52), channel_id=1, source_target_pairs={{0,127},{1,112},{2,113},{3,114},{4,115},{5,116},{6,117},{7,118},{8... | collective-permute-start | bytes 184328 | tf_op jit(solution)/shard_map/ppermute | solution.py:354
  71.5 3.1 %collective-permute-start.19 = (f32[24,5,8,128]{3,2,1,0:T(8,128)S(1)}, f32[24,5,8,128]{3,2,1,0:T(8,128)S(1)}, u32[]{:S(2)}, u32[]{:S(2)}) collective-permute-start(f32[24,5,8,128]{3,2,1,0:T(8,128)S(1)} %section2.1.mine), channel_id=1, source_target_pairs={{0,16},{1,17},{2,18},{3,19},{4,20},{5,21},{6,22},{7,23},{8,24},{9,... | collective-permute-start | bytes 1474568 | tf_op jit(solution)/shard_map/ppermute | solution.py:354
  75.3 5.1 %collective-permute-start.20 = (f32[7,5,8,128]{3,2,1,0:T(8,128)S(1)}, f32[7,5,8,128]{3,2,1,0:T(8,128)S(1)}, u32[]{:S(2)}, u32[]{:S(2)}) collective-permute-start(f32[7,5,8,128]{3,2,1,0:T(8,128)S(1)} %get-tuple-element.54), channel_id=1, source_target_pairs={{0,32},{1,33},{2,34},{3,35},{4,36},{5,37},{6,38},{7,39},{8,40},{9,... | collective-permute-start | bytes 430088 | tf_op jit(solution)/shard_map/ppermute | solution.py:354
  75.4 6.6 %collective-permute-start.21 = (f32[7,5,8,128]{3,2,1,0:T(8,128)S(1)}, f32[7,5,8,128]{3,2,1,0:T(8,128)S(1)}, u32[]{:S(2)}, u32[]{:S(2)}) collective-permute-start(f32[7,5,8,128]{3,2,1,0:T(8,128)S(1)} %get-tuple-element.55), channel_id=1, source_target_pairs={{0,64},{1,65},{2,66},{3,67},{4,68},{5,69},{6,70},{7,71},{8,72},{9,... | collective-permute-start | bytes 430088 | tf_op jit(solution)/shard_map/ppermute | solution.py:354
  75.5 10.2 %collective-permute-start.22 = (f32[7,5,8,128]{3,2,1,0:T(8,128)S(1)}, f32[7,5,8,128]{3,2,1,0:T(8,128)S(1)}, u32[]{:S(2)}, u32[]{:S(2)}) collective-permute-start(f32[7,5,8,128]{3,2,1,0:T(8,128)S(1)} %get-tuple-element.56), channel_id=1, source_target_pairs={{0,96},{1,97},{2,98},{3,99},{4,100},{5,101},{6,102},{7,103},{8,104... | collective-permute-start | bytes 430088 | tf_op jit(solution)/shard_map/ppermute | solution.py:354

commit v3 on v2

--- a/solution.py
+++ b/solution.py
@@ -14,6 +14,8 @@
 F = 5
 X = Y = 8
 L = 128
+DEEP = 3
+WIDE = Y + 2 * DEEP
 
 GAMMA = 1.4
 STEP = 0.12
@@ -173,8 +175,12 @@
     return pl.ds(pl.multiple_of((f * Y + y) * HALF + group * 8, 8), 8)
 
 
-def layer_at(f, group):
-    return pl.ds(pl.multiple_of(f * HALF + group * 8, 8), 8)
+def wide_at(f, y, group):
+    return pl.ds(pl.multiple_of((f * WIDE + DEEP + y) * HALF + group * 8, 8), 8)
+
+
+def strip_at(f, t, group):
+    return pl.ds(pl.multiple_of((f * DEEP + t) * HALF + group * 8, 8), 8)
 
 
 def x_layer_at(f, group, x):
@@ -200,20 +206,45 @@
     place = lax.broadcasted_iota(jnp.int32, (8, L), 1) // 16
     first = jnp.full((8, L), zy, jnp.int32) == 0
     turn = jnp.full((8, L), jnp.where(core == zy, 1, 0), jnp.int32) == 1
+    far = Y - DEEP
     for f in range(F):
-        ahead, back = [], []
-        for group in range(3):
-            x_in[layer_at(f, group), :] = cur[x_layer_at(f, group, 7 - 7 * zx), :]
-            x_out[layer_at(f, group), :] = cur[x_layer_at(f, group, 7 * zx), :]
-            y_in[layer_at(f, group), :] = cur[at(f, 7 - 7 * zy, group), :]
-            v = cur[at(f, 7 * zy, group), :]
-            ahead.append(rolled(v, 16))
-            back.append(rolled(v, -16))
-        for group in range(3):
-            high = jnp.where(place == 0, ahead[group - 1], ahead[group])
-            low = jnp.where(place == 7, back[(group + 1) % 3], back[group])
-            v = cur[at(f, 7 * zy, group), :]
-            y_out[layer_at(f, group), :] = jnp.where(turn, jnp.where(first, low, high), v)
+        for t in range(DEEP):
+            ahead, back = [], []
+            for group in range(3):
+                to = pl.ds(((f * 3 + group) * DEEP + t) * 8, 8)
+                x_in[to, :] = cur[x_layer_at(f, group, far * (1 - zx) + t), :]
+                x_out[to, :] = cur[x_layer_at(f, group, far * zx + t), :]
+                y_in[strip_at(f, t, group), :] = cur[at(f, far * (1 - zy) + t, group), :]
+                v = cur[at(f, far * zy + t, group), :]
+                ahead.append(rolled(v, 16))
+                back.append(rolled(v, -16))
+            for group in range(3):
+                high = jnp.where(place == 0, ahead[group - 1], ahead[group])
+                low = jnp.where(place == 7, back[(group + 1) % 3], back[group])
+                v = cur[at(f, far * zy + t, group), :]
+                y_out[strip_at(f, t, group), :] = jnp.where(turn, jnp.where(first, low, high), v)
+
+
+def corners(pos, y_in, y_out, to_in, to_out):
+    zx, zy = tile_x(pos[0]), tile_y(pos[0])
+
+    def copy(low, high):
+        for f in range(F):
+            for group in range(3):
+                for r in range(2):
+                    for out, x in ((to_in, 6 * (1 - zx) + r), (to_out, 6 * zx + r)):
+                        row = ((f * 3 + group) * 2 + r) * 4
+                        base = f * DEEP * HALF + group * 8 + x
+                        out[row : row + 2, :] = low[pl.ds(base + HALF, 2, HALF), :]
+                        out[row + 2 : row + 4, :] = high[pl.ds(base, 2, HALF), :]
+
+    @pl.when(zy == 0)
+    def _():
+        copy(y_out, y_in)
+
+    @pl.when(zy == 1)
+    def _():
+        copy(y_in, y_out)
 
 
 def reorder(pos, rows, *refs):
@@ -240,17 +271,29 @@
     faces(pos, cur, x_in, x_out, y_in, y_out)
 
 
-def section(number, pos, *refs):
-    if number == 0:
-        cur = initial = refs[0]
-        refs = refs[1:]
-    else:
-        initial, cur = refs[:2]
-        refs = refs[2:]
-    x_in, x_out, y_in, y_out = refs[:4]
-    new = refs[4]
-    edge = refs[-1]
+def widen(pos, cur, x_in, x_out, y_in, y_out, c_in, c_out, main, side_rows):
     zx, zy = tile_x(pos[0]), tile_y(pos[0])
+    for f in range(F):
+        for group in range(3):
+            for y in range(Y):
+                main[wide_at(f, y, group), :] = cur[at(f, y, group), :]
+            for t in range(DEEP):
+                main[wide_at(f, Y * (1 - zy) - DEEP * zy + t, group), :] = y_in[strip_at(f, t, group), :]
+                main[wide_at(f, Y * zy - DEEP * (1 - zy) + t, group), :] = y_out[strip_at(f, t, group), :]
+                at_t = pl.ds(((f * 3 + group) * DEEP + t) * 8, 8)
+                base = (f * WIDE + DEEP) * HALF + group * 8 + t
+                side_rows[pl.ds(base + 5 * zx, 8, HALF), :] = x_in[at_t, :]
+                side_rows[pl.ds(base + 5 * (1 - zx), 8, HALF), :] = x_out[at_t, :]
+            for r in range(2):
+                row = ((f * 3 + group) * 2 + r) * 4
+                for c, beyond in ((c_in, 6 * zx), (c_out, 6 * (1 - zx))):
+                    for k, y in ((0, -2), (2, Y)):
+                        to = (f * WIDE + DEEP + y) * HALF + group * 8 + r + beyond
+                        side_rows[pl.ds(to, 2, HALF), :] = c[row + k : row + k + 2, :]
+
+
+def advance(number, source, initial, target, made):
+    reach = 2 - number
     weight = (0.0, 0.75, 1.0 / 3.0)[number]
 
     def step(group, _):
@@ -258,75 +301,67 @@
         sub = lax.broadcasted_iota(jnp.int32, (8, L), 0)
         floor, roof = height == 0, height == 15
         left, right = sub == 0, sub == 7
-        first_x = jnp.full((8, L), zx, jnp.int32) == 0
-        first_y = jnp.full((8, L), zy, jnp.int32) == 0
-
-        def halo(inner, outer, first):
-            a = [inner[layer_at(f, group), :] for f in range(F)]
-            b = [outer[layer_at(f, group), :] for f in range(F)]
-            low = [jnp.where(first, o, i) for i, o in zip(a, b)]
-            high = [jnp.where(first, i, o) for i, o in zip(a, b)]
-            return low, high
-
-        def all_of(cons, n):
-            return side(cons, terms(cons), n)
-
-        x_before, x_after = halo(x_in, x_out, first_x)
-        mine_low = [cur[x_layer_at(f, group, 0), :] for f in range(F)]
-        mine_high = [cur[x_layer_at(f, group, 7), :] for f in range(F)]
-        for f, v in enumerate(double_flux(all_of(x_before, 0), all_of(mine_low, 0), 0)):
-            edge[f * 8 : f * 8 + 8, :] = v
-        for f, v in enumerate(double_flux(all_of(mine_high, 0), all_of(x_after, 0), 0)):
-            edge[(F + f) * 8 : (F + f) * 8 + 8, :] = v
-
-        y_before, y_after = halo(y_in, y_out, first_y)
-        cons = [cur[at(f, 0, group), :] for f in range(F)]
-        t = terms(cons)
-        here = side(cons, t, 1)
-        flux_y = double_flux(all_of(y_before, 1), here, 1)
-        for y in range(Y):
-            cons_next = [cur[at(f, y + 1, group), :] for f in range(F)] if y < Y - 1 else y_after
-            t_next = terms(cons_next)
-            ahead = side(cons_next, t_next, 1)
-            flux_next = double_flux(here, ahead, 1)
-            change = [b - a for a, b in zip(flux_y, flux_next)]
-
-            low = side(cons, t, 0)
-            flux = double_flux(low, [pltpu.roll(q, 7, 0) for q in low], 0)
-            for f in range(F):
-                lowest = jnp.broadcast_to(edge[f * 8 + y : f * 8 + y + 1, :], (8, L))
-                highest = jnp.broadcast_to(edge[(F + f) * 8 + y : (F + f) * 8 + y + 1, :], (8, L))
-                upper = jnp.where(right, highest, flux[f])
-                lower = jnp.where(left, lowest, pltpu.roll(flux[f], 1, 0))
-                change[f] = change[f] + (upper - lower)
-
-            low = side(cons, t, 2)
-            flux = double_flux(low, [rolled(q, -1) for q in low], 2)
-            for f in range(F):
-                wall = 2.0 * t[1] if f == 3 else 0.0
-                upper = jnp.where(roof, wall, flux[f])
-                lower = jnp.where(floor, wall, rolled(flux[f], 1))
-                change[f] = change[f] + (upper - lower)
-
-            out = [c - (0.5 * STEP) * d for c, d in zip(cons, change)]
-            if number:
-                out = [weight * initial[at(f, y, group), :] + (1.0 - weight) * o for f, o in enumerate(out)]
-            if number == 2:
-                out = primitive(out)
-            into = refs[-2] if number == 2 else new
-            for f in range(F):
-                into[at(f, y, group), :] = out[f]
-            cons, t, here, flux_y = cons_next, t_next, ahead, flux_next
+        cells, fluxes = {}, {}
+
+        def cell(part, y):
+            if (part, y) not in cells:
+                cons = [source[part][wide_at(f, y, group), :] for f in range(F)]
+                cells[part, y] = cons, terms(cons)
+            return cells[part, y]
+
+        def flux_y(part, y):
+            if (part, y) not in fluxes:
+                fluxes[part, y] = double_flux(side(*cell(part, y), 1), side(*cell(part, y + 1), 1), 1)
+            return fluxes[part, y]
+
+        for y in range(-reach, Y + reach):
+            own = [side(*cell(part, y), 0) for part in range(2)]
+            turned = [[pltpu.roll(q, 7, 0) for q in o] for o in own]
+            flux = []
+            for part in range(2):
+                ahead = [jnp.where(right, q, p) for p, q in zip(turned[part], turned[1 - part])]
+                flux.append(double_flux(own[part], ahead, 0))
+            turned = [[pltpu.roll(q, 1, 0) for q in o] for o in flux]
+            beside = reach > 0 and 1 - reach <= y < Y - 1 + reach
+            for part in range(2 if beside else 1):
+                cons, t = cell(part, y)
+                change = [
+                    v - jnp.where(left, q, p) for v, p, q in zip(flux[part], turned[part], turned[1 - part])
+                ]
+                change = [c + (b - a) for c, a, b in zip(change, flux_y(part, y - 1), flux_y(part, y))]
+                low = side(cons, t, 2)
+                flux_z = double_flux(low, [rolled(q, -1) for q in low], 2)
+                for f in range(F):
+                    wall = 2.0 * t[1] if f == 3 else 0.0
+                    upper = jnp.where(roof, wall, flux_z[f])
+                    lower = jnp.where(floor, wall, rolled(flux_z[f], 1))
+                    change[f] = change[f] + (upper - lower)
+                out = [c - (0.5 * STEP) * d for c, d in zip(cons, change)]
+                if number:
+                    out = [
+                        weight * initial[part][wide_at(f, y, group), :] + (1.0 - weight) * o
+                        for f, o in enumerate(out)
+                    ]
+                if number == 2:
+                    out = primitive(out)
+                for f in range(F):
+                    target[part][wide_at(f, y, group), :] = out[f]
         if number == 2:
             for f in range(F):
-                vectors = [refs[-2][at(f, y, group), :] for y in range(Y)]
+                vectors = [target[0][wide_at(f, y, group), :] for y in range(Y)]
                 for i, v in enumerate(transposed(vectors)):
-                    new[group * 8 + i, f] = v
+                    made[group * 8 + i, f] = v
         return 0
 
     lax.fori_loop(0, 3, step, 0)
-    if number < 2:
-        faces(pos, new, *refs[5:9])
+
+
+def sections(pos, cur, x_in, x_out, y_in, y_out, c_in, c_out, made, *held):
+    initial, first, second = held[0:2], held[2:4], held[4:6]
+    widen(pos, cur, x_in, x_out, y_in, y_out, c_in, c_out, *initial)
+    advance(0, initial, initial, first, made)
+    advance(1, first, initial, second, made)
+    advance(2, second, initial, first, made)
 
 
 def pack_out(pos, final, mine, other, *outs):
@@ -363,7 +398,7 @@
     parts = pl.pallas_call(
         pack_in,
         out_shape=tiles,
-        in_specs=[SMEM, ANY],
+        in_specs=[SMEM, pl.BlockSpec(memory_space=pltpu.HBM)],
         out_specs=[VMEM] * 4,
         scratch_shapes=[pltpu.SemaphoreType.DMA((4,))],
         compiler_params=PARAMS,
@@ -390,7 +425,7 @@
         gathered += [here, over_core(here)]
 
     whole = shape(F * Y * HALF, L)
-    layer = shape(F * HALF, L)
+    layer = shape(F * DEEP * HALF, L)
     initial, x_in, x_out, y_in, y_out = pl.pallas_call(
         reorder,
         out_shape=[whole] + [layer] * 4,
@@ -407,34 +442,38 @@
     def y_partner(z):
         return z ^ 3
 
-    def exchanged(x_in, x_out, y_in, y_out):
+    def over_x(inner, outer):
         return (
-            to(x_in, lambda z, core, c: (x_partner(z), core, c)),
-            to(x_out, lambda z, core, c: (x_partner(z), core, c + 2 * tile_x(z) - 1)),
-            to(y_in, lambda z, core, c: (y_partner(z), core, c)),
-            to(y_out, lambda z, core, c: (y_partner(z), 1 - core, c + 2 * tile_y(z) - 1)),
+            to(inner, lambda z, core, c: (x_partner(z), core, c)),
+            to(outer, lambda z, core, c: (x_partner(z), core, c + 2 * tile_x(z) - 1)),
         )
 
-    current = initial
-    for number in range(3):
-        halos = exchanged(x_in, x_out, y_in, y_out)
-        states = (current,) if number == 0 else (initial, current)
-        outs = [whole] + [layer] * 4 if number < 2 else [shape(HALF, F, X, L)]
-        scratch = [pltpu.VMEM((2 * F * 8, L), jnp.float32)]
-        if number == 2:
-            scratch = [pltpu.VMEM((F * Y * HALF, L), jnp.float32)] + scratch
-        made = pl.pallas_call(
-            lambda *refs, number=number: section(number, *refs),
-            out_shape=outs,
-            in_specs=[SMEM] + [VMEM] * (len(states) + 4),
-            out_specs=[VMEM] * len(outs),
-            scratch_shapes=scratch,
-            compiler_params=PARAMS,
-            name="section" + str(number),
-        )(pos, *states, *halos)
-        current = made[0]
-        if number < 2:
-            x_in, x_out, y_in, y_out = made[1:]
+    def over_y(inner, outer):
+        return (
+            to(inner, lambda z, core, c: (y_partner(z), core, c)),
+            to(outer, lambda z, core, c: (y_partner(z), 1 - core, c + 2 * tile_y(z) - 1)),
+        )
+
+    y_layers = over_y(y_in, y_out)
+    x_layers = over_x(x_in, x_out)
+    corner_cells = pl.pallas_call(
+        corners,
+        out_shape=[shape(F * 3 * 8, L)] * 2,
+        in_specs=[SMEM, VMEM, VMEM],
+        out_specs=[VMEM] * 2,
+        compiler_params=PARAMS,
+        name="corners",
+    )(pos, *y_layers)
+    corner_cells = over_x(*corner_cells)
+    current = pl.pallas_call(
+        sections,
+        out_shape=shape(HALF, F, X, L),
+        in_specs=[SMEM] + [VMEM] * 7,
+        out_specs=VMEM,
+        scratch_shapes=[pltpu.VMEM((F * WIDE * HALF, L), jnp.float32)] * 6,
+        compiler_params=PARAMS,
+        name="sections",
+    )(pos, initial, *x_layers, *y_layers, *corner_cells)
 
     leaving = pl.pallas_call(
         pack_out,

time: 87.2 us -> 73.6 us (0.84)
  waiting for transfers between devices: 37.7 us -> 23.1 us
  Pallas kernels: 13.1 us -> 17.6 us
  starting transfers between devices: 34.8 us -> 31.3 us
    ppermute x23 -> x17, waiting for transfers between devices: 37.7 us -> 23.1 us  [to(): return lax.ppermute(array, ('row', 'col'), pairs)]
    pallas_call x4 -> x3, Pallas kernels: 6.49 us -> 11 us  [the longest x1 9.56 us: body(): pl.pallas_call(sections, out_shape=shape(HALF, F, X, L), in_specs=[SMEM]...]
    ppermute x23 -> x17, starting transfers between devices: 34.8 us -> 31.3 us  [to(): return lax.ppermute(array, ('row', 'col'), pairs)]
  transfers between devices with their start and end apart: 23 -> 17, of which waited for: 13 -> 11; matrix products, arithmetic and copies ran while one was open for 0% -> 0% of each run, Pallas kernels for 3% -> 5%
where the time goes in v3:
time: 73.6 us; the launch traced here: 73.5 us
  starting transfers between devices  31.3 us (43%)
  waiting for transfers between devices  23.1 us (31%)
  Pallas kernels  17.6 us (24%)
  local copies, waits for them, and re-layouts  1.29 us (2%)
    ppermute x17, starting transfers between devices, to(): return lax.ppermute(array, ('row', 'col'), pairs)  31.3 us
    ppermute x17, waiting for transfers between devices, to(): return lax.ppermute(array, ('row', 'col'), pairs)  23.1 us
    pallas_call x1, Pallas kernels, body(): pl.pallas_call(sections, out_shape=shape(HALF, F, X, L), in_specs=[SMEM]...  9.56 us
    pallas_call x1, Pallas kernels, body(): pl.pallas_call(table, out_shape=[jax.ShapeDtypeStruct((N_ROW * 8,), jnp.i...  2.97 us
    pallas_call x1, Pallas kernels, body(): pl.pallas_call(reorder, out_shape=[whole] + [layer] * 4, in_specs=[SMEM,...  1.66 us
  transfers between devices with their start and end apart: 17, of which 11 were waited for; matrix products, arithmetic and copies ran while one was open for 0% of the time, Pallas kernels for 5%

profile of v3, /device:TPU:1, one launch (start us, length us, event | category | flops | bytes accessed | tf_op | source)
XLA Modules:
  0.0 73.5 jit_solution(8434522792275685930)
XLA Ops:
  0.0 0.1 pad_add_fusion.pos
  0.1 0.0 copy-start
  0.1 1.2 %copy-done = f32[11,5,16,256]{3,2,1,0:T(8,128)S(1)} copy-done((f32[11,5,16,256]{3,2,1,0:T(8,128)S(1)}, f32[11,5,16,256]{3,2,1,0:T(8,128)}, u32[]{:S(2)}) %copy-start) | copy-done | bytes 901144
  1.3 0.0 copy-start.1
  1.3 0.8 %pack_in.1 = (f32[11,5,8,128]{3,2,1,0:T(8,128)S(1)}, f32[11,5,8,128]{3,2,1,0:T(8,128)S(1)}, f32[11,5,8,128]{3,2,1,0:T(8,128)S(1)}, f32[11,5,8,128]{3,2,1,0:T(8,128)S(1)}) custom-call(s32[3]{0:T(128)S(1)} %pad_add_fusion.pos, f32[11,5,16,256]{3,2,1,0:T(8,128)S(1)} %copy-done), custom_call_target="tpu_custom_call" | custom-call | tf_op jit(solution)/shard_map/pack_in/pallas_call | solution.py:398
  2.0 2.5 %collective-permute-start.1 = (f32[11,5,8,128]{3,2,1,0:T(8,128)S(1)}, f32[11,5,8,128]{3,2,1,0:T(8,128)S(1)}, u32[]{:S(2)}, u32[]{:S(2)}) collective-permute-start(f32[11,5,8,128]{3,2,1,0:T(8,128)S(1)} %get-tuple-element.27), channel_id=1, source_target_pairs={{0,32},{1,33},{2,34},{3,35},{4,36},{5,37},{6,38},{7,39},{8,40},{9,... | collective-permute-start | bytes 675848 | tf_op jit(solution)/shard_map/ppermute | solution.py:389
  4.6 3.3 %collective-permute-start.3 = (f32[11,5,8,128]{3,2,1,0:T(8,128)S(1)}, f32[11,5,8,128]{3,2,1,0:T(8,128)S(1)}, u32[]{:S(2)}, u32[]{:S(2)}) collective-permute-start(f32[11,5,8,128]{3,2,1,0:T(8,128)S(1)} %get-tuple-element.28), channel_id=1, source_target_pairs={{0,64},{1,65},{2,66},{3,67},{4,68},{5,69},{6,70},{7,71},{8,72},{9,... | collective-permute-start | bytes 675848 | tf_op jit(solution)/shard_map/ppermute | solution.py:389
  7.9 0.0 collective-permute-start.5
  7.9 0.0 copy-done.1
  7.9 0.1 copy.4.slots
  8.0 3.0 %table.1 = (s32[64]{0:T(128)S(1)}, s32[88]{0:T(128)S(1)}, f32[11,5,8,128]{3,2,1,0:T(8,128)S(1)}) custom-call(s32[3]{0:T(128)S(1)} %pad_add_fusion.pos, s32[128,11]{1,0:T(8,128)S(1)} %copy.4.slots, f32[11,5,8,128]{3,2,1,0:T(8,128)S(1)} %get-tuple-element.23._tile), custom_call_target="tpu_custom_call", output_to_operand_aliasing={{2}: (2, {})} | custom-call | bytes 20000000 | tf_op jit(solution)/shard_map/table/pallas_call | solution.py:407
  11.0 1.3 %collective-permute-start = (f32[11,5,8,128]{3,2,1,0:T(8,128)S(1)}, f32[11,5,8,128]{3,2,1,0:T(8,128)S(1)}, u32[]{:S(2)}, u32[]{:S(2)}) collective-permute-start(f32[11,5,8,128]{3,2,1,0:T(8,128)S(1)} %get-tuple-element.26.refs_0_), channel_id=1, source_target_pairs={{0,16},{1,17},{2,18},{3,19},{4,20},{5,21},{6,22},{7,23},{8,24},{9,... | collective-permute-start | bytes 675848 | tf_op jit(solution)/shard_map/ppermute | solution.py:389
  12.3 0.0 collective-permute-done.1.refs_2_
  12.3 0.1 collective-permute-start.2
  12.4 5.3 %collective-permute-done.3.refs_4_ = f32[11,5,8,128]{3,2,1,0:T(8,128)S(1)} collective-permute-done((f32[11,5,8,128]{3,2,1,0:T(8,128)S(1)}, f32[11,5,8,128]{3,2,1,0:T(8,128)S(1)}, u32[]{:S(2)}, u32[]{:S(2)}) %collective-permute-start.3) | collective-permute-done | bytes 225312 | tf_op jit(solution)/shard_map/ppermute | solution.py:389
  17.7 1.6 %collective-permute-start.4 = (f32[11,5,8,128]{3,2,1,0:T(8,128)S(1)}, f32[11,5,8,128]{3,2,1,0:T(8,128)S(1)}, u32[]{:S(2)}, u32[]{:S(2)}) collective-permute-start(f32[11,5,8,128]{3,2,1,0:T(8,128)S(1)} %collective-permute-done.3.refs_4_), channel_id=1, source_target_pairs={{0,16},{1,17},{2,18},{3,19},{4,20},{5,21},{6,22},{7,23},{8,24},{9,... | collective-permute-start | bytes 675848 | tf_op jit(solution)/shard_map/ppermute | solution.py:389
  19.3 0.8 %collective-permute-done.5.refs_6_ = f32[11,5,8,128]{3,2,1,0:T(8,128)S(1)} collective-permute-done((f32[11,5,8,128]{3,2,1,0:T(8,128)S(1)}, f32[11,5,8,128]{3,2,1,0:T(8,128)S(1)}, u32[]{:S(2)}, u32[]{:S(2)}) %collective-permute-start.5) | collective-permute-done | bytes 225312 | tf_op jit(solution)/shard_map/ppermute | solution.py:389
  20.0 1.8 %collective-permute-start.6 = (f32[11,5,8,128]{3,2,1,0:T(8,128)S(1)}, f32[11,5,8,128]{3,2,1,0:T(8,128)S(1)}, u32[]{:S(2)}, u32[]{:S(2)}) collective-permute-start(f32[11,5,8,128]{3,2,1,0:T(8,128)S(1)} %collective-permute-done.5.refs_6_), channel_id=1, source_target_pairs={{0,16},{1,17},{2,18},{3,19},{4,20},{5,21},{6,22},{7,23},{8,24},{9,... | collective-permute-start | bytes 675848 | tf_op jit(solution)/shard_map/ppermute | solution.py:389
  21.8 0.0 collective-permute-done.refs_1_
  21.8 0.0 collective-permute-done.2.refs_3_
  21.9 0.0 collective-permute-done.4.refs_5_
  21.9 1.1 %collective-permute-done.6.refs_7_ = f32[11,5,8,128]{3,2,1,0:T(8,128)S(1)} collective-permute-done((f32[11,5,8,128]{3,2,1,0:T(8,128)S(1)}, f32[11,5,8,128]{3,2,1,0:T(8,128)S(1)}, u32[]{:S(2)}, u32[]{:S(2)}) %collective-permute-start.6) | collective-permute-done | bytes 225312 | tf_op jit(solution)/shard_map/ppermute | solution.py:389
  23.0 1.7 %reorder.1 = (f32[960,128]{1,0:T(8,128)S(1)}, f32[360,128]{1,0:T(8,128)S(1)}, f32[360,128]{1,0:T(8,128)S(1)}, f32[360,128]{1,0:T(8,128)S(1)}, f32[360,128]{1,0:T(8,128)S(1)}) custom-call(s32[3]{0:T(128)S(1)} %pad_add_fusion.pos, s32[88]{0:T(128)S(1)} %get-tuple-element.25.rows, f32[11,5,8,128]{3,2,1,0:T(8,128)S(1)} %get-tuple-element.26.refs_0_, ...), custom_call_target="tpu_custom_call" | custom-call | tf_op jit(solution)/shard_map/reorder/pallas_call | solution.py:429
  24.6 0.1 collective-permute-start.9
  24.7 7.8 %collective-permute-start.10 = (f32[360,128]{1,0:T(8,128)S(1)}, f32[360,128]{1,0:T(8,128)S(1)}, u32[]{:S(2)}, u32[]{:S(2)}) collective-permute-start(f32[360,128]{1,0:T(8,128)S(1)} %get-tuple-element.34), channel_id=1, source_target_pairs={{0,127},{1,112},{2,113},{3,114},{4,115},{5,116},{6,117},{7,118},{8... | collective-permute-start | bytes 552968 | tf_op jit(solution)/shard_map/ppermute | solution.py:389
  32.6 0.0 collective-permute-start.7
  32.6 1.7 %collective-permute-start.8 = (f32[360,128]{1,0:T(8,128)S(1)}, f32[360,128]{1,0:T(8,128)S(1)}, u32[]{:S(2)}, u32[]{:S(2)}) collective-permute-start(f32[360,128]{1,0:T(8,128)S(1)} %get-tuple-element.32), channel_id=1, source_target_pairs={{0,47},{1,32},{2,33},{3,34},{4,35},{5,36},{6,37},{7,38},{8,39},{9,... | collective-permute-start | bytes 552968 | tf_op jit(solution)/shard_map/ppermute | solution.py:389
  34.3 0.0 collective-permute-done.9.y_in
  34.3 2.7 %collective-permute-done.10.y_out = f32[360,128]{1,0:T(8,128)S(1)} collective-permute-done((f32[360,128]{1,0:T(8,128)S(1)}, f32[360,128]{1,0:T(8,128)S(1)}, u32[]{:S(2)}, u32[]{:S(2)}) %collective-permute-start.10) | collective-permute-done | bytes 184352 | tf_op jit(solution)/shard_map/ppermute | solution.py:389
  37.0 0.6 corners.1
  37.7 0.1 collective-permute-start.11
  37.8 4.8 %collective-permute-start.12 = (f32[120,128]{1,0:T(8,128)S(1)}, f32[120,128]{1,0:T(8,128)S(1)}, u32[]{:S(2)}, u32[]{:S(2)}) collective-permute-start(f32[120,128]{1,0:T(8,128)S(1)} %get-tuple-element.36), channel_id=1, source_target_pairs={{0,47},{1,32},{2,33},{3,34},{4,35},{5,36},{6,37},{7,38},{8,39},{9,... | collective-permute-start | bytes 184328 | tf_op jit(solution)/shard_map/ppermute | solution.py:389
  42.5 0.0 collective-permute-done.7.x_in
  42.5 0.6 collective-permute-done.8.x_out
  43.1 1.6 %collective-permute-done.11.c_in = f32[120,128]{1,0:T(8,128)S(1)} collective-permute-done((f32[120,128]{1,0:T(8,128)S(1)}, f32[120,128]{1,0:T(8,128)S(1)}, u32[]{:S(2)}, u32[]{:S(2)}) %collective-permute-start.11) | collective-permute-done | bytes 61472 | tf_op jit(solution)/shard_map/ppermute | solution.py:389
  44.7 0.5 collective-permute-done.12.c_out
  45.1 9.6 %sections.1.mine = f32[24,5,8,128]{3,2,1,0:T(8,128)S(1)} custom-call(s32[3]{0:T(128)S(1)} %pad_add_fusion.pos, f32[960,128]{1,0:T(8,128)S(1)} %get-tuple-element.30.cur, f32[360,128]{1,0:T(8,128)S(1)} %collective-permute-done.7.x_in, f32[360,128]{1,0:T(8,128)S(1)} %collective-permute-done.8.x_out, f32[360,128]{1,0:T(8,128)S(1)} %collective-permute-done.9.y_in, ...), custom_call_target="tpu_custom_call" | custom-call | tf_op jit(solution)/shard_map/sections/pallas_call | solution.py:468
  54.7 1.6 %collective-permute-start.13 = (f32[24,5,8,128]{3,2,1,0:T(8,128)S(1)}, f32[24,5,8,128]{3,2,1,0:T(8,128)S(1)}, u32[]{:S(2)}, u32[]{:S(2)}) collective-permute-start(f32[24,5,8,128]{3,2,1,0:T(8,128)S(1)} %sections.1.mine), channel_id=1, source_target_pairs={{0,16},{1,17},{2,18},{3,19},{4,20},{5,21},{6,22},{7,23},{8,24},{9,... | collective-permute-start | bytes 1474568 | tf_op jit(solution)/shard_map/ppermute | solution.py:389
  56.3 1.5 %collective-permute-done.13.other = f32[24,5,8,128]{3,2,1,0:T(8,128)S(1)} collective-permute-done((f32[24,5,8,128]{3,2,1,0:T(8,128)S(1)}, f32[24,5,8,128]{3,2,1,0:T(8,128)S(1)}, u32[]{:S(2)}, u32[]{:S(2)}) %collective-permute-start.13) | collective-permute-done | bytes 491552 | tf_op jit(solution)/shard_map/ppermute | solution.py:389
  57.8 0.7 pack_out.1
  58.5 0.1 collective-permute-start.14
  58.6 4.4 %collective-permute-start.15 = (f32[7,5,8,128]{3,2,1,0:T(8,128)S(1)}, f32[7,5,8,128]{3,2,1,0:T(8,128)S(1)}, u32[]{:S(2)}, u32[]{:S(2)}) collective-permute-start(f32[7,5,8,128]{3,2,1,0:T(8,128)S(1)} %get-tuple-element.39), channel_id=1, source_target_pairs={{0,64},{1,65},{2,66},{3,67},{4,68},{5,69},{6,70},{7,71},{8,72},{9,... | collective-permute-start | bytes 430088 | tf_op jit(solution)/shard_map/ppermute | solution.py:389
  63.0 0.0 collective-permute-start.16
  63.0 0.5 collective-permute-done.14.refs_1_
  63.5 6.1 %collective-permute-done.15.refs_2_ = f32[7,5,8,128]{3,2,1,0:T(8,128)S(1)} collective-permute-done((f32[7,5,8,128]{3,2,1,0:T(8,128)S(1)}, f32[7,5,8,128]{3,2,1,0:T(8,128)S(1)}, u32[]{:S(2)}, u32[]{:S(2)}) %collective-permute-start.15) | collective-permute-done | bytes 143392 | tf_op jit(solution)/shard_map/ppermute | solution.py:389
  69.6 2.5 %collective-permute-done.16.refs_3_ = f32[7,5,8,128]{3,2,1,0:T(8,128)S(1)} collective-permute-done((f32[7,5,8,128]{3,2,1,0:T(8,128)S(1)}, f32[7,5,8,128]{3,2,1,0:T(8,128)S(1)}, u32[]{:S(2)}, u32[]{:S(2)}) %collective-permute-start.16) | collective-permute-done | bytes 143392 | tf_op jit(solution)/shard_map/ppermute | solution.py:389
  72.1 1.4 %unpack_out.1 = f32[7,5,16,256]{3,2,1,0:T(8,128)} custom-call(s32[3]{0:T(128)S(1)} %pad_add_fusion.pos, f32[7,5,8,128]{3,2,1,0:T(8,128)S(1)} %get-tuple-element.37.refs_0_, f32[7,5,8,128]{3,2,1,0:T(8,128)S(1)} %collective-permute-done.14.refs_1_, f32[7,5,8,128]{3,2,1,0:T(8,128)S(1)} %collective-permute-done.15.refs_2_, ...), custom_call_target="tpu_custom_call" | custom-call | tf_op jit(solution)/shard_map/unpack_out/pallas_call | solution.py:487
Async XLA Ops:
  0.1 1.2 %copy-start = (f32[11,5,16,256]{3,2,1,0:T(8,128)S(1)}, f32[11,5,16,256]{3,2,1,0:T(8,128)}, u32[]{:S(2)}) copy-start(f32[11,5,16,256]{3,2,1,0:T(8,128)} %cells.1) | copy-start | bytes 2703364
  1.3 6.6 %copy-start.1 = (s32[128,11]{0,1:T(8,128)S(1)}, s32[128,11]{0,1:T(8,128)}, u32[]{:S(2)}) copy-start(s32[128,11]{0,1:T(8,128)} %param.3) | copy-start | bytes 16900
  2.0 10.3 %collective-permute-start.1 = (f32[11,5,8,128]{3,2,1,0:T(8,128)S(1)}, f32[11,5,8,128]{3,2,1,0:T(8,128)S(1)}, u32[]{:S(2)}, u32[]{:S(2)}) collective-permute-start(f32[11,5,8,128]{3,2,1,0:T(8,128)S(1)} %get-tuple-element.27), channel_id=1, source_target_pairs={{0,32},{1,33},{2,34},{3,35},{4,36},{5,37},{6,38},{7,39},{8,40},{9,... | collective-permute-start | bytes 675848 | tf_op jit(solution)/shard_map/ppermute | solution.py:389
  4.6 13.1 %collective-permute-start.3 = (f32[11,5,8,128]{3,2,1,0:T(8,128)S(1)}, f32[11,5,8,128]{3,2,1,0:T(8,128)S(1)}, u32[]{:S(2)}, u32[]{:S(2)}) collective-permute-start(f32[11,5,8,128]{3,2,1,0:T(8,128)S(1)} %get-tuple-element.28), channel_id=1, source_target_pairs={{0,64},{1,65},{2,66},{3,67},{4,68},{5,69},{6,70},{7,71},{8,72},{9,... | collective-permute-start | bytes 675848 | tf_op jit(solution)/shard_map/ppermute | solution.py:389
  7.9 12.2 %collective-permute-start.5 = (f32[11,5,8,128]{3,2,1,0:T(8,128)S(1)}, f32[11,5,8,128]{3,2,1,0:T(8,128)S(1)}, u32[]{:S(2)}, u32[]{:S(2)}) collective-permute-start(f32[11,5,8,128]{3,2,1,0:T(8,128)S(1)} %get-tuple-element.29), channel_id=1, source_target_pairs={{0,96},{1,97},{2,98},{3,99},{4,100},{5,101},{6,102},{7,103},{8,104... | collective-permute-start | bytes 675848 | tf_op jit(solution)/shard_map/ppermute | solution.py:389
  11.0 10.9 %collective-permute-start = (f32[11,5,8,128]{3,2,1,0:T(8,128)S(1)}, f32[11,5,8,128]{3,2,1,0:T(8,128)S(1)}, u32[]{:S(2)}, u32[]{:S(2)}) collective-permute-start(f32[11,5,8,128]{3,2,1,0:T(8,128)S(1)} %get-tuple-element.26.refs_0_), channel_id=1, source_target_pairs={{0,16},{1,17},{2,18},{3,19},{4,20},{5,21},{6,22},{7,23},{8,24},{9,... | collective-permute-start | bytes 675848 | tf_op jit(solution)/shard_map/ppermute | solution.py:389
  12.3 9.6 %collective-permute-start.2 = (f32[11,5,8,128]{3,2,1,0:T(8,128)S(1)}, f32[11,5,8,128]{3,2,1,0:T(8,128)S(1)}, u32[]{:S(2)}, u32[]{:S(2)}) collective-permute-start(f32[11,5,8,128]{3,2,1,0:T(8,128)S(1)} %collective-permute-done.1.refs_2_), channel_id=1, source_target_pairs={{0,16},{1,17},{2,18},{3,19},{4,20},{5,21},{6,22},{7,23},{8,24},{9,... | collective-permute-start | bytes 675848 | tf_op jit(solution)/shard_map/ppermute | solution.py:389
  17.7 4.2 %collective-permute-start.4 = (f32[11,5,8,128]{3,2,1,0:T(8,128)S(1)}, f32[11,5,8,128]{3,2,1,0:T(8,128)S(1)}, u32[]{:S(2)}, u32[]{:S(2)}) collective-permute-start(f32[11,5,8,128]{3,2,1,0:T(8,128)S(1)} %collective-permute-done.3.refs_4_), channel_id=1, source_target_pairs={{0,16},{1,17},{2,18},{3,19},{4,20},{5,21},{6,22},{7,23},{8,24},{9,... | collective-permute-start | bytes 675848 | tf_op jit(solution)/shard_map/ppermute | solution.py:389
  20.0 2.9 %collective-permute-start.6 = (f32[11,5,8,128]{3,2,1,0:T(8,128)S(1)}, f32[11,5,8,128]{3,2,1,0:T(8,128)S(1)}, u32[]{:S(2)}, u32[]{:S(2)}) collective-permute-start(f32[11,5,8,128]{3,2,1,0:T(8,128)S(1)} %collective-permute-done.5.refs_6_), channel_id=1, source_target_pairs={{0,16},{1,17},{2,18},{3,19},{4,20},{5,21},{6,22},{7,23},{8,24},{9,... | collective-permute-start | bytes 675848 | tf_op jit(solution)/shard_map/ppermute | solution.py:389
  24.6 9.7 %collective-permute-start.9 = (f32[360,128]{1,0:T(8,128)S(1)}, f32[360,128]{1,0:T(8,128)S(1)}, u32[]{:S(2)}, u32[]{:S(2)}) collective-permute-start(f32[360,128]{1,0:T(8,128)S(1)} %get-tuple-element.33), channel_id=1, source_target_pairs={{0,96},{1,97},{2,98},{3,99},{4,100},{5,101},{6,102},{7,103},{8,104... | collective-permute-start | bytes 552968 | tf_op jit(solution)/shard_map/ppermute | solution.py:389
  24.7 12.3 %collective-permute-start.10 = (f32[360,128]{1,0:T(8,128)S(1)}, f32[360,128]{1,0:T(8,128)S(1)}, u32[]{:S(2)}, u32[]{:S(2)}) collective-permute-start(f32[360,128]{1,0:T(8,128)S(1)} %get-tuple-element.34), channel_id=1, source_target_pairs={{0,127},{1,112},{2,113},{3,114},{4,115},{5,116},{6,117},{7,118},{8... | collective-permute-start | bytes 552968 | tf_op jit(solution)/shard_map/ppermute | solution.py:389
  32.6 10.0 %collective-permute-start.7 = (f32[360,128]{1,0:T(8,128)S(1)}, f32[360,128]{1,0:T(8,128)S(1)}, u32[]{:S(2)}, u32[]{:S(2)}) collective-permute-start(f32[360,128]{1,0:T(8,128)S(1)} %get-tuple-element.31), channel_id=1, source_target_pairs={{0,32},{1,33},{2,34},{3,35},{4,36},{5,37},{6,38},{7,39},{8,40},{9,... | collective-permute-start | bytes 552968 | tf_op jit(solution)/shard_map/ppermute | solution.py:389
  32.6 10.6 %collective-permute-start.8 = (f32[360,128]{1,0:T(8,128)S(1)}, f32[360,128]{1,0:T(8,128)S(1)}, u32[]{:S(2)}, u32[]{:S(2)}) collective-permute-start(f32[360,128]{1,0:T(8,128)S(1)} %get-tuple-element.32), channel_id=1, source_target_pairs={{0,47},{1,32},{2,33},{3,34},{4,35},{5,36},{6,37},{7,38},{8,39},{9,... | collective-permute-start | bytes 552968 | tf_op jit(solution)/shard_map/ppermute | solution.py:389
  37.7 7.0 %collective-permute-start.11 = (f32[120,128]{1,0:T(8,128)S(1)}, f32[120,128]{1,0:T(8,128)S(1)}, u32[]{:S(2)}, u32[]{:S(2)}) collective-permute-start(f32[120,128]{1,0:T(8,128)S(1)} %get-tuple-element.35), channel_id=1, source_target_pairs={{0,32},{1,33},{2,34},{3,35},{4,36},{5,37},{6,38},{7,39},{8,40},{9,... | collective-permute-start | bytes 184328 | tf_op jit(solution)/shard_map/ppermute | solution.py:389
  37.8 7.4 %collective-permute-start.12 = (f32[120,128]{1,0:T(8,128)S(1)}, f32[120,128]{1,0:T(8,128)S(1)}, u32[]{:S(2)}, u32[]{:S(2)}) collective-permute-start(f32[120,128]{1,0:T(8,128)S(1)} %get-tuple-element.36), channel_id=1, source_target_pairs={{0,47},{1,32},{2,33},{3,34},{4,35},{5,36},{6,37},{7,38},{8,39},{9,... | collective-permute-start | bytes 184328 | tf_op jit(solution)/shard_map/ppermute | solution.py:389
  54.7 3.1 %collective-permute-start.13 = (f32[24,5,8,128]{3,2,1,0:T(8,128)S(1)}, f32[24,5,8,128]{3,2,1,0:T(8,128)S(1)}, u32[]{:S(2)}, u32[]{:S(2)}) collective-permute-start(f32[24,5,8,128]{3,2,1,0:T(8,128)S(1)} %sections.1.mine), channel_id=1, source_target_pairs={{0,16},{1,17},{2,18},{3,19},{4,20},{5,21},{6,22},{7,23},{8,24},{9,... | collective-permute-start | bytes 1474568 | tf_op jit(solution)/shard_map/ppermute | solution.py:389
  58.5 5.1 %collective-permute-start.14 = (f32[7,5,8,128]{3,2,1,0:T(8,128)S(1)}, f32[7,5,8,128]{3,2,1,0:T(8,128)S(1)}, u32[]{:S(2)}, u32[]{:S(2)}) collective-permute-start(f32[7,5,8,128]{3,2,1,0:T(8,128)S(1)} %get-tuple-element.38), channel_id=1, source_target_pairs={{0,32},{1,33},{2,34},{3,35},{4,36},{5,37},{6,38},{7,39},{8,40},{9,... | collective-permute-start | bytes 430088 | tf_op jit(solution)/shard_map/ppermute | solution.py:389
  58.6 11.0 %collective-permute-start.15 = (f32[7,5,8,128]{3,2,1,0:T(8,128)S(1)}, f32[7,5,8,128]{3,2,1,0:T(8,128)S(1)}, u32[]{:S(2)}, u32[]{:S(2)}) collective-permute-start(f32[7,5,8,128]{3,2,1,0:T(8,128)S(1)} %get-tuple-element.39), channel_id=1, source_target_pairs={{0,64},{1,65},{2,66},{3,67},{4,68},{5,69},{6,70},{7,71},{8,72},{9,... | collective-permute-start | bytes 430088 | tf_op jit(solution)/shard_map/ppermute | solution.py:389
  63.0 9.1 %collective-permute-start.16 = (f32[7,5,8,128]{3,2,1,0:T(8,128)S(1)}, f32[7,5,8,128]{3,2,1,0:T(8,128)S(1)}, u32[]{:S(2)}, u32[]{:S(2)}) collective-permute-start(f32[7,5,8,128]{3,2,1,0:T(8,128)S(1)} %get-tuple-element.40), channel_id=1, source_target_pairs={{0,96},{1,97},{2,98},{3,99},{4,100},{5,101},{6,102},{7,103},{8,104... | collective-permute-start | bytes 430088 | tf_op jit(solution)/shard_map/ppermute | solution.py:389

commit v4 on v3

--- a/solution.py
+++ b/solution.py
@@ -1,3 +1,5 @@
+import math
+
 import jax
 import jax.numpy as jnp
 from jax import lax
@@ -19,6 +21,7 @@
 
 GAMMA = 1.4
 STEP = 0.12
+LOG2_E = 1.0 / math.log(2.0)
 
 VMEM = pl.BlockSpec(memory_space=pltpu.VMEM)
 SMEM = pl.BlockSpec(memory_space=pltpu.SMEM)
@@ -38,25 +41,14 @@
     return z // 2
 
 
-def pack_in(pos, cells, *rest):
-    outs, sems = rest[:4], rest[4]
+def pack_in(pos, cells, *outs):
     z = pos[0]
-    copies = []
-    for k in (2, 1, 3, 0):
-        zk = z ^ k
-        copies.append(
-            pltpu.make_async_copy(
-                cells.at[
-                    :, :, pl.ds(pl.multiple_of(tile_x(zk) * X, X), X), pl.ds(pl.multiple_of(tile_y(zk) * L, L), L)
-                ],
-                outs[k],
-                sems.at[k],
-            )
-        )
-    for c in copies:
-        c.start()
-    for c in copies:
-        c.wait()
+    for k in range(4):
+        x = pl.ds(pl.multiple_of(tile_x(z ^ k) * X, X), X)
+        y = pl.ds(pl.multiple_of(tile_y(z ^ k) * L, L), L)
+        for s in range(CAP):
+            for f in range(F):
+                outs[k][s, f] = cells[s, f, x, y]
 
 
 def unpack_out(pos, *refs):
@@ -124,44 +116,43 @@
     return v if shift == 0 else pltpu.roll(v, shift, 1)
 
 
+def inverse(rho):
+    guess = pl.reciprocal(rho, approx=True)
+    return guess * (2.0 - rho * guess)
+
+
 def terms(cons):
     rho, mx, my, mz, energy = cons
-    inv = 1.0 / rho
+    inv = inverse(rho)
     u, v, w = mx * inv, my * inv, mz * inv
-    p = (GAMMA - 1.0) * (energy - 0.5 * rho * (u * u + v * v + w * w))
+    p = (GAMMA - 1.0) * energy - (0.5 * (GAMMA - 1.0)) * (mx * u + my * v + mz * w)
     theta = p * inv
-    sound = jnp.sqrt(GAMMA * theta)
-    kappa = 0.2 * jnp.exp(0.7 * jnp.log(theta))
+    power = jnp.log(theta)
+    sound = jnp.exp2(power * (0.5 * LOG2_E) + 0.5 * math.log2(GAMMA))
+    kappa = jnp.exp2(power * (0.7 * LOG2_E) + math.log2(0.2))
     return (u, v, w), p, theta, sound, kappa
 
 
 def side(cons, t, n):
     vel, p, theta, sound, kappa = t
-    return (*cons, p, theta, kappa, vel[n], jnp.abs(vel[n]) + sound)
+    flux = [cons[f] * vel[n] for f in (1, 2, 3)]
+    flux[n] = flux[n] + p
+    return (*cons, *flux, (cons[4] + p) * vel[n], theta, kappa, jnp.abs(vel[n]) + sound)
 
 
 def double_flux(low, high, n):
-    speed = jnp.maximum(low[9], high[9])
+    speed = jnp.maximum(low[11], high[11])
     out = []
     for f in range(F):
-        if f == 0:
-            total = low[n + 1] + high[n + 1]
-        elif f == 4:
-            total = (low[4] + low[5]) * low[8] + (high[4] + high[5]) * high[8]
-        else:
-            total = low[f] * low[8] + high[f] * high[8]
-            if f == n + 1:
-                total = total + (low[5] + high[5])
-        total = total - speed * (high[f] - low[f])
-        if f == 4:
-            total = total - (low[7] + high[7]) * (high[6] - low[6])
-        out.append(total)
+        k = F + f - 1 if f else n + 1
+        out.append((low[k] + high[k]) - speed * (high[f] - low[f]))
+    out[4] = out[4] - (low[10] + high[10]) * (high[9] - low[9])
     return out
 
 
 def primitive(cons):
     rho, mx, my, mz, energy = cons
-    inv = 1.0 / rho
+    inv = inverse(rho)
     u, v, w = mx * inv, my * inv, mz * inv
     return [rho, u, v, w, (GAMMA - 1.0) * (energy - 0.5 * rho * (u * u + v * v + w * w))]
 
@@ -330,11 +321,13 @@
                 ]
                 change = [c + (b - a) for c, a, b in zip(change, flux_y(part, y - 1), flux_y(part, y))]
                 low = side(cons, t, 2)
-                flux_z = double_flux(low, [rolled(q, -1) for q in low], 2)
+                up = [rolled(q, -1) for q in cons]
+                flux_z = double_flux(low, side(up, terms(up), 2), 2)
                 for f in range(F):
-                    wall = 2.0 * t[1] if f == 3 else 0.0
-                    upper = jnp.where(roof, wall, flux_z[f])
-                    lower = jnp.where(floor, wall, rolled(flux_z[f], 1))
+                    upper = jnp.where(roof, 2.0 * t[1] if f == 3 else 0.0, flux_z[f])
+                    lower = rolled(upper, 1)
+                    if f == 3:
+                        lower = jnp.where(floor, 2.0 * t[1], lower)
                     change[f] = change[f] + (upper - lower)
                 out = [c - (0.5 * STEP) * d for c, d in zip(cons, change)]
                 if number:
@@ -398,9 +391,8 @@
     parts = pl.pallas_call(
         pack_in,
         out_shape=tiles,
-        in_specs=[SMEM, pl.BlockSpec(memory_space=pltpu.HBM)],
+        in_specs=[SMEM, VMEM],
         out_specs=[VMEM] * 4,
-        scratch_shapes=[pltpu.SemaphoreType.DMA((4,))],
         compiler_params=PARAMS,
         name="pack_in",
     )(pos, block_cells)

time: 73.6 us -> 71.7 us (0.974)
  Pallas kernels: 17.6 us -> 15.7 us
    pallas_call x1, Pallas kernels: 9.56 us -> 7.7 us  [body(): pl.pallas_call(sections, out_shape=shape(HALF, F, X, L), in_specs=[SMEM]...]
where the time goes in v4:
time: 71.7 us; the launch traced here: 71.6 us
  starting transfers between devices  31.3 us (44%)
  waiting for transfers between devices  23.1 us (32%)
  Pallas kernels  15.7 us (22%)
  local copies, waits for them, and re-layouts  1.29 us (2%)
    ppermute x17, starting transfers between devices, to(): return lax.ppermute(array, ('row', 'col'), pairs)  31.3 us
    ppermute x17, waiting for transfers between devices, to(): return lax.ppermute(array, ('row', 'col'), pairs)  23.1 us
    pallas_call x1, Pallas kernels, body(): pl.pallas_call(sections, out_shape=shape(HALF, F, X, L), in_specs=[SMEM]...  7.7 us
    pallas_call x1, Pallas kernels, body(): pl.pallas_call(table, out_shape=[jax.ShapeDtypeStruct((N_ROW * 8,), jnp.i...  2.96 us
    pallas_call x1, Pallas kernels, body(): pl.pallas_call(reorder, out_shape=[whole] + [layer] * 4, in_specs=[SMEM,...  1.66 us
  transfers between devices with their start and end apart: 17, of which 11 were waited for; matrix products, arithmetic and copies ran while one was open for 0% of the time, Pallas kernels for 5%

profile of v4, /device:TPU:1, one launch (start us, length us, event | category | flops | bytes accessed | tf_op | source)
XLA Modules:
  0.0 71.6 jit_solution(5355644480527433012)
XLA Ops:
  0.0 0.1 pad_add_fusion.pos
  0.1 0.0 copy-start
  0.1 1.2 %copy-done = f32[11,5,16,256]{3,2,1,0:T(8,128)S(1)} copy-done((f32[11,5,16,256]{3,2,1,0:T(8,128)S(1)}, f32[11,5,16,256]{3,2,1,0:T(8,128)}, u32[]{:S(2)}) %copy-start) | copy-done | bytes 901144
  1.3 0.0 copy-start.1
  1.3 0.7 pack_in.1
  1.9 2.5 %collective-permute-start.1 = (f32[11,5,8,128]{3,2,1,0:T(8,128)S(1)}, f32[11,5,8,128]{3,2,1,0:T(8,128)S(1)}, u32[]{:S(2)}, u32[]{:S(2)}) collective-permute-start(f32[11,5,8,128]{3,2,1,0:T(8,128)S(1)} %get-tuple-element.27), channel_id=1, source_target_pairs={{0,32},{1,33},{2,34},{3,35},{4,36},{5,37},{6,38},{7,39},{8,40},{9,... | collective-permute-start | bytes 675848 | tf_op jit(solution)/shard_map/ppermute | solution.py:382
  4.5 3.3 %collective-permute-start.3 = (f32[11,5,8,128]{3,2,1,0:T(8,128)S(1)}, f32[11,5,8,128]{3,2,1,0:T(8,128)S(1)}, u32[]{:S(2)}, u32[]{:S(2)}) collective-permute-start(f32[11,5,8,128]{3,2,1,0:T(8,128)S(1)} %get-tuple-element.28), channel_id=1, source_target_pairs={{0,64},{1,65},{2,66},{3,67},{4,68},{5,69},{6,70},{7,71},{8,72},{9,... | collective-permute-start | bytes 675848 | tf_op jit(solution)/shard_map/ppermute | solution.py:382
  7.8 0.0 collective-permute-start.5
  7.8 0.0 copy-done.1
  7.8 0.1 copy.4.slots
  7.9 3.0 %table.1 = (s32[64]{0:T(128)S(1)}, s32[88]{0:T(128)S(1)}, f32[11,5,8,128]{3,2,1,0:T(8,128)S(1)}) custom-call(s32[3]{0:T(128)S(1)} %pad_add_fusion.pos, s32[128,11]{1,0:T(8,128)S(1)} %copy.4.slots, f32[11,5,8,128]{3,2,1,0:T(8,128)S(1)} %get-tuple-element.23._tile), custom_call_target="tpu_custom_call", output_to_operand_aliasing={{2}: (2, {})} | custom-call | bytes 20000000 | tf_op jit(solution)/shard_map/table/pallas_call | solution.py:399
  10.9 1.3 %collective-permute-start = (f32[11,5,8,128]{3,2,1,0:T(8,128)S(1)}, f32[11,5,8,128]{3,2,1,0:T(8,128)S(1)}, u32[]{:S(2)}, u32[]{:S(2)}) collective-permute-start(f32[11,5,8,128]{3,2,1,0:T(8,128)S(1)} %get-tuple-element.26.refs_0_), channel_id=1, source_target_pairs={{0,16},{1,17},{2,18},{3,19},{4,20},{5,21},{6,22},{7,23},{8,24},{9,... | collective-permute-start | bytes 675848 | tf_op jit(solution)/shard_map/ppermute | solution.py:382
  12.2 0.0 collective-permute-done.1.refs_2_
  12.2 0.1 collective-permute-start.2
  12.3 5.3 %collective-permute-done.3.refs_4_ = f32[11,5,8,128]{3,2,1,0:T(8,128)S(1)} collective-permute-done((f32[11,5,8,128]{3,2,1,0:T(8,128)S(1)}, f32[11,5,8,128]{3,2,1,0:T(8,128)S(1)}, u32[]{:S(2)}, u32[]{:S(2)}) %collective-permute-start.3) | collective-permute-done | bytes 225312 | tf_op jit(solution)/shard_map/ppermute | solution.py:382
  17.6 1.6 %collective-permute-start.4 = (f32[11,5,8,128]{3,2,1,0:T(8,128)S(1)}, f32[11,5,8,128]{3,2,1,0:T(8,128)S(1)}, u32[]{:S(2)}, u32[]{:S(2)}) collective-permute-start(f32[11,5,8,128]{3,2,1,0:T(8,128)S(1)} %collective-permute-done.3.refs_4_), channel_id=1, source_target_pairs={{0,16},{1,17},{2,18},{3,19},{4,20},{5,21},{6,22},{7,23},{8,24},{9,... | collective-permute-start | bytes 675848 | tf_op jit(solution)/shard_map/ppermute | solution.py:382
  19.2 0.8 %collective-permute-done.5.refs_6_ = f32[11,5,8,128]{3,2,1,0:T(8,128)S(1)} collective-permute-done((f32[11,5,8,128]{3,2,1,0:T(8,128)S(1)}, f32[11,5,8,128]{3,2,1,0:T(8,128)S(1)}, u32[]{:S(2)}, u32[]{:S(2)}) %collective-permute-start.5) | collective-permute-done | bytes 225312 | tf_op jit(solution)/shard_map/ppermute | solution.py:382
  19.9 1.8 %collective-permute-start.6 = (f32[11,5,8,128]{3,2,1,0:T(8,128)S(1)}, f32[11,5,8,128]{3,2,1,0:T(8,128)S(1)}, u32[]{:S(2)}, u32[]{:S(2)}) collective-permute-start(f32[11,5,8,128]{3,2,1,0:T(8,128)S(1)} %collective-permute-done.5.refs_6_), channel_id=1, source_target_pairs={{0,16},{1,17},{2,18},{3,19},{4,20},{5,21},{6,22},{7,23},{8,24},{9,... | collective-permute-start | bytes 675848 | tf_op jit(solution)/shard_map/ppermute | solution.py:382
  21.8 0.0 collective-permute-done.refs_1_
  21.8 0.0 collective-permute-done.2.refs_3_
  21.8 0.0 collective-permute-done.4.refs_5_
  21.8 1.1 %collective-permute-done.6.refs_7_ = f32[11,5,8,128]{3,2,1,0:T(8,128)S(1)} collective-permute-done((f32[11,5,8,128]{3,2,1,0:T(8,128)S(1)}, f32[11,5,8,128]{3,2,1,0:T(8,128)S(1)}, u32[]{:S(2)}, u32[]{:S(2)}) %collective-permute-start.6) | collective-permute-done | bytes 225312 | tf_op jit(solution)/shard_map/ppermute | solution.py:382
  22.9 1.7 %reorder.1 = (f32[960,128]{1,0:T(8,128)S(1)}, f32[360,128]{1,0:T(8,128)S(1)}, f32[360,128]{1,0:T(8,128)S(1)}, f32[360,128]{1,0:T(8,128)S(1)}, f32[360,128]{1,0:T(8,128)S(1)}) custom-call(s32[3]{0:T(128)S(1)} %pad_add_fusion.pos, s32[88]{0:T(128)S(1)} %get-tuple-element.25.rows, f32[11,5,8,128]{3,2,1,0:T(8,128)S(1)} %get-tuple-element.26.refs_0_, ...), custom_call_target="tpu_custom_call" | custom-call | tf_op jit(solution)/shard_map/reorder/pallas_call | solution.py:421
  24.5 0.1 collective-permute-start.9
  24.6 7.8 %collective-permute-start.10 = (f32[360,128]{1,0:T(8,128)S(1)}, f32[360,128]{1,0:T(8,128)S(1)}, u32[]{:S(2)}, u32[]{:S(2)}) collective-permute-start(f32[360,128]{1,0:T(8,128)S(1)} %get-tuple-element.34), channel_id=1, source_target_pairs={{0,127},{1,112},{2,113},{3,114},{4,115},{5,116},{6,117},{7,118},{8... | collective-permute-start | bytes 552968 | tf_op jit(solution)/shard_map/ppermute | solution.py:382
  32.5 0.0 collective-permute-start.7
  32.5 1.7 %collective-permute-start.8 = (f32[360,128]{1,0:T(8,128)S(1)}, f32[360,128]{1,0:T(8,128)S(1)}, u32[]{:S(2)}, u32[]{:S(2)}) collective-permute-start(f32[360,128]{1,0:T(8,128)S(1)} %get-tuple-element.32), channel_id=1, source_target_pairs={{0,47},{1,32},{2,33},{3,34},{4,35},{5,36},{6,37},{7,38},{8,39},{9,... | collective-permute-start | bytes 552968 | tf_op jit(solution)/shard_map/ppermute | solution.py:382
  34.2 0.0 collective-permute-done.9.y_in
  34.2 2.7 %collective-permute-done.10.y_out = f32[360,128]{1,0:T(8,128)S(1)} collective-permute-done((f32[360,128]{1,0:T(8,128)S(1)}, f32[360,128]{1,0:T(8,128)S(1)}, u32[]{:S(2)}, u32[]{:S(2)}) %collective-permute-start.10) | collective-permute-done | bytes 184352 | tf_op jit(solution)/shard_map/ppermute | solution.py:382
  36.9 0.6 corners.1
  37.6 0.1 collective-permute-start.11
  37.7 4.8 %collective-permute-start.12 = (f32[120,128]{1,0:T(8,128)S(1)}, f32[120,128]{1,0:T(8,128)S(1)}, u32[]{:S(2)}, u32[]{:S(2)}) collective-permute-start(f32[120,128]{1,0:T(8,128)S(1)} %get-tuple-element.36), channel_id=1, source_target_pairs={{0,47},{1,32},{2,33},{3,34},{4,35},{5,36},{6,37},{7,38},{8,39},{9,... | collective-permute-start | bytes 184328 | tf_op jit(solution)/shard_map/ppermute | solution.py:382
  42.4 0.0 collective-permute-done.7.x_in
  42.5 0.6 collective-permute-done.8.x_out
  43.0 1.6 %collective-permute-done.11.c_in = f32[120,128]{1,0:T(8,128)S(1)} collective-permute-done((f32[120,128]{1,0:T(8,128)S(1)}, f32[120,128]{1,0:T(8,128)S(1)}, u32[]{:S(2)}, u32[]{:S(2)}) %collective-permute-start.11) | collective-permute-done | bytes 61472 | tf_op jit(solution)/shard_map/ppermute | solution.py:382
  44.6 0.5 collective-permute-done.12.c_out
  45.0 7.7 %sections.1.mine = f32[24,5,8,128]{3,2,1,0:T(8,128)S(1)} custom-call(s32[3]{0:T(128)S(1)} %pad_add_fusion.pos, f32[960,128]{1,0:T(8,128)S(1)} %get-tuple-element.30.cur, f32[360,128]{1,0:T(8,128)S(1)} %collective-permute-done.7.x_in, f32[360,128]{1,0:T(8,128)S(1)} %collective-permute-done.8.x_out, f32[360,128]{1,0:T(8,128)S(1)} %collective-permute-done.9.y_in, ...), custom_call_target="tpu_custom_call" | custom-call | tf_op jit(solution)/shard_map/sections/pallas_call | solution.py:460
  52.7 1.6 %collective-permute-start.13 = (f32[24,5,8,128]{3,2,1,0:T(8,128)S(1)}, f32[24,5,8,128]{3,2,1,0:T(8,128)S(1)}, u32[]{:S(2)}, u32[]{:S(2)}) collective-permute-start(f32[24,5,8,128]{3,2,1,0:T(8,128)S(1)} %sections.1.mine), channel_id=1, source_target_pairs={{0,16},{1,17},{2,18},{3,19},{4,20},{5,21},{6,22},{7,23},{8,24},{9,... | collective-permute-start | bytes 1474568 | tf_op jit(solution)/shard_map/ppermute | solution.py:382
  54.4 1.5 %collective-permute-done.13.other = f32[24,5,8,128]{3,2,1,0:T(8,128)S(1)} collective-permute-done((f32[24,5,8,128]{3,2,1,0:T(8,128)S(1)}, f32[24,5,8,128]{3,2,1,0:T(8,128)S(1)}, u32[]{:S(2)}, u32[]{:S(2)}) %collective-permute-start.13) | collective-permute-done | bytes 491552 | tf_op jit(solution)/shard_map/ppermute | solution.py:382
  55.9 0.7 pack_out.1
  56.5 0.1 collective-permute-start.14
  56.6 4.4 %collective-permute-start.15 = (f32[7,5,8,128]{3,2,1,0:T(8,128)S(1)}, f32[7,5,8,128]{3,2,1,0:T(8,128)S(1)}, u32[]{:S(2)}, u32[]{:S(2)}) collective-permute-start(f32[7,5,8,128]{3,2,1,0:T(8,128)S(1)} %get-tuple-element.39), channel_id=1, source_target_pairs={{0,64},{1,65},{2,66},{3,67},{4,68},{5,69},{6,70},{7,71},{8,72},{9,... | collective-permute-start | bytes 430088 | tf_op jit(solution)/shard_map/ppermute | solution.py:382
  61.1 0.0 collective-permute-start.16
  61.1 0.5 collective-permute-done.14.refs_1_
  61.6 6.1 %collective-permute-done.15.refs_2_ = f32[7,5,8,128]{3,2,1,0:T(8,128)S(1)} collective-permute-done((f32[7,5,8,128]{3,2,1,0:T(8,128)S(1)}, f32[7,5,8,128]{3,2,1,0:T(8,128)S(1)}, u32[]{:S(2)}, u32[]{:S(2)}) %collective-permute-start.15) | collective-permute-done | bytes 143392 | tf_op jit(solution)/shard_map/ppermute | solution.py:382
  67.7 2.5 %collective-permute-done.16.refs_3_ = f32[7,5,8,128]{3,2,1,0:T(8,128)S(1)} collective-permute-done((f32[7,5,8,128]{3,2,1,0:T(8,128)S(1)}, f32[7,5,8,128]{3,2,1,0:T(8,128)S(1)}, u32[]{:S(2)}, u32[]{:S(2)}) %collective-permute-start.16) | collective-permute-done | bytes 143392 | tf_op jit(solution)/shard_map/ppermute | solution.py:382
  70.2 1.4 %unpack_out.1 = f32[7,5,16,256]{3,2,1,0:T(8,128)} custom-call(s32[3]{0:T(128)S(1)} %pad_add_fusion.pos, f32[7,5,8,128]{3,2,1,0:T(8,128)S(1)} %get-tuple-element.37.refs_0_, f32[7,5,8,128]{3,2,1,0:T(8,128)S(1)} %collective-permute-done.14.refs_1_, f32[7,5,8,128]{3,2,1,0:T(8,128)S(1)} %collective-permute-done.15.refs_2_, ...), custom_call_target="tpu_custom_call" | custom-call | tf_op jit(solution)/shard_map/unpack_out/pallas_call | solution.py:479
Async XLA Ops:
  0.1 1.2 %copy-start = (f32[11,5,16,256]{3,2,1,0:T(8,128)S(1)}, f32[11,5,16,256]{3,2,1,0:T(8,128)}, u32[]{:S(2)}) copy-start(f32[11,5,16,256]{3,2,1,0:T(8,128)} %cells.1) | copy-start | bytes 2703364
  1.3 6.5 %copy-start.1 = (s32[128,11]{0,1:T(8,128)S(1)}, s32[128,11]{0,1:T(8,128)}, u32[]{:S(2)}) copy-start(s32[128,11]{0,1:T(8,128)} %param.3) | copy-start | bytes 16900
  1.9 10.2 %collective-permute-start.1 = (f32[11,5,8,128]{3,2,1,0:T(8,128)S(1)}, f32[11,5,8,128]{3,2,1,0:T(8,128)S(1)}, u32[]{:S(2)}, u32[]{:S(2)}) collective-permute-start(f32[11,5,8,128]{3,2,1,0:T(8,128)S(1)} %get-tuple-element.27), channel_id=1, source_target_pairs={{0,32},{1,33},{2,34},{3,35},{4,36},{5,37},{6,38},{7,39},{8,40},{9,... | collective-permute-start | bytes 675848 | tf_op jit(solution)/shard_map/ppermute | solution.py:382
  4.5 13.1 %collective-permute-start.3 = (f32[11,5,8,128]{3,2,1,0:T(8,128)S(1)}, f32[11,5,8,128]{3,2,1,0:T(8,128)S(1)}, u32[]{:S(2)}, u32[]{:S(2)}) collective-permute-start(f32[11,5,8,128]{3,2,1,0:T(8,128)S(1)} %get-tuple-element.28), channel_id=1, source_target_pairs={{0,64},{1,65},{2,66},{3,67},{4,68},{5,69},{6,70},{7,71},{8,72},{9,... | collective-permute-start | bytes 675848 | tf_op jit(solution)/shard_map/ppermute | solution.py:382
  7.8 12.2 %collective-permute-start.5 = (f32[11,5,8,128]{3,2,1,0:T(8,128)S(1)}, f32[11,5,8,128]{3,2,1,0:T(8,128)S(1)}, u32[]{:S(2)}, u32[]{:S(2)}) collective-permute-start(f32[11,5,8,128]{3,2,1,0:T(8,128)S(1)} %get-tuple-element.29), channel_id=1, source_target_pairs={{0,96},{1,97},{2,98},{3,99},{4,100},{5,101},{6,102},{7,103},{8,104... | collective-permute-start | bytes 675848 | tf_op jit(solution)/shard_map/ppermute | solution.py:382
  10.9 10.9 %collective-permute-start = (f32[11,5,8,128]{3,2,1,0:T(8,128)S(1)}, f32[11,5,8,128]{3,2,1,0:T(8,128)S(1)}, u32[]{:S(2)}, u32[]{:S(2)}) collective-permute-start(f32[11,5,8,128]{3,2,1,0:T(8,128)S(1)} %get-tuple-element.26.refs_0_), channel_id=1, source_target_pairs={{0,16},{1,17},{2,18},{3,19},{4,20},{5,21},{6,22},{7,23},{8,24},{9,... | collective-permute-start | bytes 675848 | tf_op jit(solution)/shard_map/ppermute | solution.py:382
  12.2 9.6 %collective-permute-start.2 = (f32[11,5,8,128]{3,2,1,0:T(8,128)S(1)}, f32[11,5,8,128]{3,2,1,0:T(8,128)S(1)}, u32[]{:S(2)}, u32[]{:S(2)}) collective-permute-start(f32[11,5,8,128]{3,2,1,0:T(8,128)S(1)} %collective-permute-done.1.refs_2_), channel_id=1, source_target_pairs={{0,16},{1,17},{2,18},{3,19},{4,20},{5,21},{6,22},{7,23},{8,24},{9,... | collective-permute-start | bytes 675848 | tf_op jit(solution)/shard_map/ppermute | solution.py:382
  17.6 4.2 %collective-permute-start.4 = (f32[11,5,8,128]{3,2,1,0:T(8,128)S(1)}, f32[11,5,8,128]{3,2,1,0:T(8,128)S(1)}, u32[]{:S(2)}, u32[]{:S(2)}) collective-permute-start(f32[11,5,8,128]{3,2,1,0:T(8,128)S(1)} %collective-permute-done.3.refs_4_), channel_id=1, source_target_pairs={{0,16},{1,17},{2,18},{3,19},{4,20},{5,21},{6,22},{7,23},{8,24},{9,... | collective-permute-start | bytes 675848 | tf_op jit(solution)/shard_map/ppermute | solution.py:382
  19.9 2.9 %collective-permute-start.6 = (f32[11,5,8,128]{3,2,1,0:T(8,128)S(1)}, f32[11,5,8,128]{3,2,1,0:T(8,128)S(1)}, u32[]{:S(2)}, u32[]{:S(2)}) collective-permute-start(f32[11,5,8,128]{3,2,1,0:T(8,128)S(1)} %collective-permute-done.5.refs_6_), channel_id=1, source_target_pairs={{0,16},{1,17},{2,18},{3,19},{4,20},{5,21},{6,22},{7,23},{8,24},{9,... | collective-permute-start | bytes 675848 | tf_op jit(solution)/shard_map/ppermute | solution.py:382
  24.5 9.7 %collective-permute-start.9 = (f32[360,128]{1,0:T(8,128)S(1)}, f32[360,128]{1,0:T(8,128)S(1)}, u32[]{:S(2)}, u32[]{:S(2)}) collective-permute-start(f32[360,128]{1,0:T(8,128)S(1)} %get-tuple-element.33), channel_id=1, source_target_pairs={{0,96},{1,97},{2,98},{3,99},{4,100},{5,101},{6,102},{7,103},{8,104... | collective-permute-start | bytes 552968 | tf_op jit(solution)/shard_map/ppermute | solution.py:382
  24.6 12.3 %collective-permute-start.10 = (f32[360,128]{1,0:T(8,128)S(1)}, f32[360,128]{1,0:T(8,128)S(1)}, u32[]{:S(2)}, u32[]{:S(2)}) collective-permute-start(f32[360,128]{1,0:T(8,128)S(1)} %get-tuple-element.34), channel_id=1, source_target_pairs={{0,127},{1,112},{2,113},{3,114},{4,115},{5,116},{6,117},{7,118},{8... | collective-permute-start | bytes 552968 | tf_op jit(solution)/shard_map/ppermute | solution.py:382
  32.5 10.0 %collective-permute-start.7 = (f32[360,128]{1,0:T(8,128)S(1)}, f32[360,128]{1,0:T(8,128)S(1)}, u32[]{:S(2)}, u32[]{:S(2)}) collective-permute-start(f32[360,128]{1,0:T(8,128)S(1)} %get-tuple-element.31), channel_id=1, source_target_pairs={{0,32},{1,33},{2,34},{3,35},{4,36},{5,37},{6,38},{7,39},{8,40},{9,... | collective-permute-start | bytes 552968 | tf_op jit(solution)/shard_map/ppermute | solution.py:382
  32.5 10.6 %collective-permute-start.8 = (f32[360,128]{1,0:T(8,128)S(1)}, f32[360,128]{1,0:T(8,128)S(1)}, u32[]{:S(2)}, u32[]{:S(2)}) collective-permute-start(f32[360,128]{1,0:T(8,128)S(1)} %get-tuple-element.32), channel_id=1, source_target_pairs={{0,47},{1,32},{2,33},{3,34},{4,35},{5,36},{6,37},{7,38},{8,39},{9,... | collective-permute-start | bytes 552968 | tf_op jit(solution)/shard_map/ppermute | solution.py:382
  37.6 7.0 %collective-permute-start.11 = (f32[120,128]{1,0:T(8,128)S(1)}, f32[120,128]{1,0:T(8,128)S(1)}, u32[]{:S(2)}, u32[]{:S(2)}) collective-permute-start(f32[120,128]{1,0:T(8,128)S(1)} %get-tuple-element.35), channel_id=1, source_target_pairs={{0,32},{1,33},{2,34},{3,35},{4,36},{5,37},{6,38},{7,39},{8,40},{9,... | collective-permute-start | bytes 184328 | tf_op jit(solution)/shard_map/ppermute | solution.py:382
  37.7 7.4 %collective-permute-start.12 = (f32[120,128]{1,0:T(8,128)S(1)}, f32[120,128]{1,0:T(8,128)S(1)}, u32[]{:S(2)}, u32[]{:S(2)}) collective-permute-start(f32[120,128]{1,0:T(8,128)S(1)} %get-tuple-element.36), channel_id=1, source_target_pairs={{0,47},{1,32},{2,33},{3,34},{4,35},{5,36},{6,37},{7,38},{8,39},{9,... | collective-permute-start | bytes 184328 | tf_op jit(solution)/shard_map/ppermute | solution.py:382
  52.7 3.1 %collective-permute-start.13 = (f32[24,5,8,128]{3,2,1,0:T(8,128)S(1)}, f32[24,5,8,128]{3,2,1,0:T(8,128)S(1)}, u32[]{:S(2)}, u32[]{:S(2)}) collective-permute-start(f32[24,5,8,128]{3,2,1,0:T(8,128)S(1)} %sections.1.mine), channel_id=1, source_target_pairs={{0,16},{1,17},{2,18},{3,19},{4,20},{5,21},{6,22},{7,23},{8,24},{9,... | collective-permute-start | bytes 1474568 | tf_op jit(solution)/shard_map/ppermute | solution.py:382
  56.5 5.1 %collective-permute-start.14 = (f32[7,5,8,128]{3,2,1,0:T(8,128)S(1)}, f32[7,5,8,128]{3,2,1,0:T(8,128)S(1)}, u32[]{:S(2)}, u32[]{:S(2)}) collective-permute-start(f32[7,5,8,128]{3,2,1,0:T(8,128)S(1)} %get-tuple-element.38), channel_id=1, source_target_pairs={{0,32},{1,33},{2,34},{3,35},{4,36},{5,37},{6,38},{7,39},{8,40},{9,... | collective-permute-start | bytes 430088 | tf_op jit(solution)/shard_map/ppermute | solution.py:382
  56.6 11.0 %collective-permute-start.15 = (f32[7,5,8,128]{3,2,1,0:T(8,128)S(1)}, f32[7,5,8,128]{3,2,1,0:T(8,128)S(1)}, u32[]{:S(2)}, u32[]{:S(2)}) collective-permute-start(f32[7,5,8,128]{3,2,1,0:T(8,128)S(1)} %get-tuple-element.39), channel_id=1, source_target_pairs={{0,64},{1,65},{2,66},{3,67},{4,68},{5,69},{6,70},{7,71},{8,72},{9,... | collective-permute-start | bytes 430088 | tf_op jit(solution)/shard_map/ppermute | solution.py:382
  61.1 9.1 %collective-permute-start.16 = (f32[7,5,8,128]{3,2,1,0:T(8,128)S(1)}, f32[7,5,8,128]{3,2,1,0:T(8,128)S(1)}, u32[]{:S(2)}, u32[]{:S(2)}) collective-permute-start(f32[7,5,8,128]{3,2,1,0:T(8,128)S(1)} %get-tuple-element.40), channel_id=1, source_target_pairs={{0,96},{1,97},{2,98},{3,99},{4,100},{5,101},{6,102},{7,103},{8,104... | collective-permute-start | bytes 430088 | tf_op jit(solution)/shard_map/ppermute | solution.py:382

commit v5 on v4

--- a/solution.py
+++ b/solution.py
@@ -262,7 +262,7 @@
     faces(pos, cur, x_in, x_out, y_in, y_out)
 
 
-def widen(pos, cur, x_in, x_out, y_in, y_out, c_in, c_out, main, side_rows):
+def widen(pos, cur, x_in, x_out, y_in, y_out, main, side_rows):
     zx, zy = tile_x(pos[0]), tile_y(pos[0])
     for f in range(F):
         for group in range(3):
@@ -275,6 +275,12 @@
                 base = (f * WIDE + DEEP) * HALF + group * 8 + t
                 side_rows[pl.ds(base + 5 * zx, 8, HALF), :] = x_in[at_t, :]
                 side_rows[pl.ds(base + 5 * (1 - zx), 8, HALF), :] = x_out[at_t, :]
+
+
+def add_corners(pos, c_in, c_out, side_rows):
+    zx = tile_x(pos[0])
+    for f in range(F):
+        for group in range(3):
             for r in range(2):
                 row = ((f * 3 + group) * 2 + r) * 4
                 for c, beyond in ((c_in, 6 * zx), (c_out, 6 * (1 - zx))):
@@ -283,8 +289,7 @@
                         side_rows[pl.ds(to, 2, HALF), :] = c[row + k : row + k + 2, :]
 
 
-def advance(number, source, initial, target, made):
-    reach = 2 - number
+def advance(number, source, initial, target, main_ys, side_ys, made=None):
     weight = (0.0, 0.75, 1.0 / 3.0)[number]
 
     def step(group, _):
@@ -296,7 +301,7 @@
 
         def cell(part, y):
             if (part, y) not in cells:
-                cons = [source[part][wide_at(f, y, group), :] for f in range(F)]
+                cons = [source(part, y)[wide_at(f, y, group), :] for f in range(F)]
                 cells[part, y] = cons, terms(cons)
             return cells[part, y]
 
@@ -305,7 +310,7 @@
                 fluxes[part, y] = double_flux(side(*cell(part, y), 1), side(*cell(part, y + 1), 1), 1)
             return fluxes[part, y]
 
-        for y in range(-reach, Y + reach):
+        for y in sorted({*main_ys, *side_ys}):
             own = [side(*cell(part, y), 0) for part in range(2)]
             turned = [[pltpu.roll(q, 7, 0) for q in o] for o in own]
             flux = []
@@ -313,8 +318,9 @@
                 ahead = [jnp.where(right, q, p) for p, q in zip(turned[part], turned[1 - part])]
                 flux.append(double_flux(own[part], ahead, 0))
             turned = [[pltpu.roll(q, 1, 0) for q in o] for o in flux]
-            beside = reach > 0 and 1 - reach <= y < Y - 1 + reach
-            for part in range(2 if beside else 1):
+            for part, ys in enumerate((main_ys, side_ys)):
+                if y not in ys:
+                    continue
                 cons, t = cell(part, y)
                 change = [
                     v - jnp.where(left, q, p) for v, p, q in zip(flux[part], turned[part], turned[1 - part])
@@ -332,16 +338,16 @@
                 out = [c - (0.5 * STEP) * d for c, d in zip(cons, change)]
                 if number:
                     out = [
-                        weight * initial[part][wide_at(f, y, group), :] + (1.0 - weight) * o
+                        weight * initial(part, y)[wide_at(f, y, group), :] + (1.0 - weight) * o
                         for f, o in enumerate(out)
                     ]
                 if number == 2:
                     out = primitive(out)
                 for f in range(F):
-                    target[part][wide_at(f, y, group), :] = out[f]
+                    target(part, y)[wide_at(f, y, group), :] = out[f]
         if number == 2:
             for f in range(F):
-                vectors = [target[0][wide_at(f, y, group), :] for y in range(Y)]
+                vectors = [target(0, y)[wide_at(f, y, group), :] for y in range(Y)]
                 for i, v in enumerate(transposed(vectors)):
                     made[group * 8 + i, f] = v
         return 0
@@ -349,12 +355,31 @@
     lax.fori_loop(0, 3, step, 0)
 
 
-def sections(pos, cur, x_in, x_out, y_in, y_out, c_in, c_out, made, *held):
-    initial, first, second = held[0:2], held[2:4], held[4:6]
-    widen(pos, cur, x_in, x_out, y_in, y_out, c_in, c_out, *initial)
-    advance(0, initial, initial, first, made)
-    advance(1, first, initial, second, made)
-    advance(2, second, initial, first, made)
+EARLY_MAIN = range(0, Y)
+EARLY_SIDE = range(1, Y - 1)
+
+
+def begin(pos, cur, x_in, x_out, y_in, y_out, main, side_rows, first_main, first_side):
+    widen(pos, cur, x_in, x_out, y_in, y_out, main, side_rows)
+    initial, first = (main, side_rows), (first_main, first_side)
+    advance(0, lambda part, y: initial[part], None, lambda part, y: first[part], EARLY_MAIN, EARLY_SIDE)
+
+
+def finish(pos, main, side_rows, early_main, early_side, c_in, c_out, made, corner_rows, *held):
+    late, second = held[0:2], held[2:4]
+    add_corners(pos, c_in, c_out, corner_rows)
+
+    def initial(part, y):
+        return (side_rows if 0 <= y < Y else corner_rows) if part else main
+
+    def first(part, y):
+        if part:
+            return early_side if y in EARLY_SIDE else late[1]
+        return early_main if y in EARLY_MAIN else late[0]
+
+    advance(0, initial, None, first, (-2, -1, Y, Y + 1), (-1, 0, Y - 1, Y))
+    advance(1, first, initial, lambda part, y: second[part], range(-1, Y + 1), range(0, Y))
+    advance(2, lambda part, y: second[part], initial, lambda part, y: late[part], range(0, Y), (), made)
 
 
 def pack_out(pos, final, mine, other, *outs):
@@ -457,15 +482,25 @@
         name="corners",
     )(pos, *y_layers)
     corner_cells = over_x(*corner_cells)
+    wide = [F * WIDE * HALF, L]
+    early = pl.pallas_call(
+        begin,
+        out_shape=[shape(*wide)] * 4,
+        in_specs=[SMEM] + [VMEM] * 5,
+        out_specs=[VMEM] * 4,
+        compiler_params=PARAMS,
+        cost_estimate=pl.CostEstimate(flops=0, bytes_accessed=10_000_000, transcendentals=0),
+        name="begin",
+    )(pos, initial, *x_layers, *y_layers)
     current = pl.pallas_call(
-        sections,
+        finish,
         out_shape=shape(HALF, F, X, L),
-        in_specs=[SMEM] + [VMEM] * 7,
+        in_specs=[SMEM] + [VMEM] * 6,
         out_specs=VMEM,
-        scratch_shapes=[pltpu.VMEM((F * WIDE * HALF, L), jnp.float32)] * 6,
-        compiler_params=PARAMS,
-        name="sections",
-    )(pos, initial, *x_layers, *y_layers, *corner_cells)
+        scratch_shapes=[pltpu.VMEM(wide, jnp.float32)] * 5,
+        compiler_params=PARAMS,
+        name="finish",
+    )(pos, *early, *corner_cells)
 
     leaving = pl.pallas_call(
         pack_out,

time: 71.7 us -> 70.3 us (0.980)
  waiting for transfers between devices: 23.1 us -> 21.1 us
    ppermute x17, waiting for transfers between devices: 23.1 us -> 21.1 us  [to(): return lax.ppermute(array, ('row', 'col'), pairs)]
    pallas_call x1 -> x2, Pallas kernels: 7.7 us -> 8.46 us  [the longest x1 6.07 us: body(): pl.pallas_call(finish, out_shape=shape(HALF, F, X, L), in_specs=[SMEM] +...]
  transfers between devices with their start and end apart: 17 -> 17, of which waited for: 11 -> 9; matrix products, arithmetic and copies ran while one was open for 0% -> 0% of each run, Pallas kernels for 5% -> 9%
where the time goes in v5:
time: 70.3 us; the launch traced here: 70.2 us
  starting transfers between devices  31.2 us (44%)
  waiting for transfers between devices  21.1 us (30%)
  Pallas kernels  16.4 us (23%)
  local copies, waits for them, and re-layouts  1.29 us (2%)
    ppermute x17, starting transfers between devices, to(): return lax.ppermute(array, ('row', 'col'), pairs)  31.2 us
    ppermute x17, waiting for transfers between devices, to(): return lax.ppermute(array, ('row', 'col'), pairs)  21.1 us
    pallas_call x1, Pallas kernels, body(): pl.pallas_call(finish, out_shape=shape(HALF, F, X, L), in_specs=[SMEM] +...  6.07 us
    pallas_call x1, Pallas kernels, body(): pl.pallas_call(table, out_shape=[jax.ShapeDtypeStruct((N_ROW * 8,), jnp.i...  2.96 us
    pallas_call x1, Pallas kernels, body(): pl.pallas_call(begin, out_shape=[shape(*wide)] * 4, in_specs=[SMEM] + [VM...  2.39 us
    pallas_call x1, Pallas kernels, body(): pl.pallas_call(reorder, out_shape=[whole] + [layer] * 4, in_specs=[SMEM,...  1.66 us
  transfers between devices with their start and end apart: 17, of which 9 were waited for; matrix products, arithmetic and copies ran while one was open for 0% of the time, Pallas kernels for 9%

profile of v5, /device:TPU:1, one launch (start us, length us, event | category | flops | bytes accessed | tf_op | source)
XLA Modules:
  0.0 70.2 jit_solution(7936398135769376917)
XLA Ops:
  0.0 0.1 pad_add_fusion.pos
  0.1 0.0 copy-start
  0.1 1.2 %copy-done = f32[11,5,16,256]{3,2,1,0:T(8,128)S(1)} copy-done((f32[11,5,16,256]{3,2,1,0:T(8,128)S(1)}, f32[11,5,16,256]{3,2,1,0:T(8,128)}, u32[]{:S(2)}) %copy-start) | copy-done | bytes 901144
  1.3 0.0 copy-start.1
  1.3 0.7 pack_in.1
  1.9 2.5 %collective-permute-start.1 = (f32[11,5,8,128]{3,2,1,0:T(8,128)S(1)}, f32[11,5,8,128]{3,2,1,0:T(8,128)S(1)}, u32[]{:S(2)}, u32[]{:S(2)}) collective-permute-start(f32[11,5,8,128]{3,2,1,0:T(8,128)S(1)} %get-tuple-element.31), channel_id=1, source_target_pairs={{0,32},{1,33},{2,34},{3,35},{4,36},{5,37},{6,38},{7,39},{8,40},{9,... | collective-permute-start | bytes 675848 | tf_op jit(solution)/shard_map/ppermute | solution.py:407
  4.5 3.3 %collective-permute-start.3 = (f32[11,5,8,128]{3,2,1,0:T(8,128)S(1)}, f32[11,5,8,128]{3,2,1,0:T(8,128)S(1)}, u32[]{:S(2)}, u32[]{:S(2)}) collective-permute-start(f32[11,5,8,128]{3,2,1,0:T(8,128)S(1)} %get-tuple-element.32), channel_id=1, source_target_pairs={{0,64},{1,65},{2,66},{3,67},{4,68},{5,69},{6,70},{7,71},{8,72},{9,... | collective-permute-start | bytes 675848 | tf_op jit(solution)/shard_map/ppermute | solution.py:407
  7.8 0.0 collective-permute-start.5
  7.8 0.0 copy-done.1
  7.8 0.1 copy.4.slots
  7.9 3.0 %table.1 = (s32[64]{0:T(128)S(1)}, s32[88]{0:T(128)S(1)}, f32[11,5,8,128]{3,2,1,0:T(8,128)S(1)}) custom-call(s32[3]{0:T(128)S(1)} %pad_add_fusion.pos, s32[128,11]{1,0:T(8,128)S(1)} %copy.4.slots, f32[11,5,8,128]{3,2,1,0:T(8,128)S(1)} %get-tuple-element.27._tile), custom_call_target="tpu_custom_call", output_to_operand_aliasing={{2}: (2, {})} | custom-call | bytes 20000000 | tf_op jit(solution)/shard_map/table/pallas_call | solution.py:424
  10.9 1.3 %collective-permute-start = (f32[11,5,8,128]{3,2,1,0:T(8,128)S(1)}, f32[11,5,8,128]{3,2,1,0:T(8,128)S(1)}, u32[]{:S(2)}, u32[]{:S(2)}) collective-permute-start(f32[11,5,8,128]{3,2,1,0:T(8,128)S(1)} %get-tuple-element.30.refs_0_), channel_id=1, source_target_pairs={{0,16},{1,17},{2,18},{3,19},{4,20},{5,21},{6,22},{7,23},{8,24},{9,... | collective-permute-start | bytes 675848 | tf_op jit(solution)/shard_map/ppermute | solution.py:407
  12.2 0.0 collective-permute-done.1.refs_2_
  12.2 0.1 collective-permute-start.2
  12.3 5.3 %collective-permute-done.3.refs_4_ = f32[11,5,8,128]{3,2,1,0:T(8,128)S(1)} collective-permute-done((f32[11,5,8,128]{3,2,1,0:T(8,128)S(1)}, f32[11,5,8,128]{3,2,1,0:T(8,128)S(1)}, u32[]{:S(2)}, u32[]{:S(2)}) %collective-permute-start.3) | collective-permute-done | bytes 225312 | tf_op jit(solution)/shard_map/ppermute | solution.py:407
  17.6 1.6 %collective-permute-start.4 = (f32[11,5,8,128]{3,2,1,0:T(8,128)S(1)}, f32[11,5,8,128]{3,2,1,0:T(8,128)S(1)}, u32[]{:S(2)}, u32[]{:S(2)}) collective-permute-start(f32[11,5,8,128]{3,2,1,0:T(8,128)S(1)} %collective-permute-done.3.refs_4_), channel_id=1, source_target_pairs={{0,16},{1,17},{2,18},{3,19},{4,20},{5,21},{6,22},{7,23},{8,24},{9,... | collective-permute-start | bytes 675848 | tf_op jit(solution)/shard_map/ppermute | solution.py:407
  19.2 0.8 %collective-permute-done.5.refs_6_ = f32[11,5,8,128]{3,2,1,0:T(8,128)S(1)} collective-permute-done((f32[11,5,8,128]{3,2,1,0:T(8,128)S(1)}, f32[11,5,8,128]{3,2,1,0:T(8,128)S(1)}, u32[]{:S(2)}, u32[]{:S(2)}) %collective-permute-start.5) | collective-permute-done | bytes 225312 | tf_op jit(solution)/shard_map/ppermute | solution.py:407
  19.9 1.8 %collective-permute-start.6 = (f32[11,5,8,128]{3,2,1,0:T(8,128)S(1)}, f32[11,5,8,128]{3,2,1,0:T(8,128)S(1)}, u32[]{:S(2)}, u32[]{:S(2)}) collective-permute-start(f32[11,5,8,128]{3,2,1,0:T(8,128)S(1)} %collective-permute-done.5.refs_6_), channel_id=1, source_target_pairs={{0,16},{1,17},{2,18},{3,19},{4,20},{5,21},{6,22},{7,23},{8,24},{9,... | collective-permute-start | bytes 675848 | tf_op jit(solution)/shard_map/ppermute | solution.py:407
  21.8 0.0 collective-permute-done.refs_1_
  21.8 0.0 collective-permute-done.2.refs_3_
  21.8 0.0 collective-permute-done.4.refs_5_
  21.8 1.1 %collective-permute-done.6.refs_7_ = f32[11,5,8,128]{3,2,1,0:T(8,128)S(1)} collective-permute-done((f32[11,5,8,128]{3,2,1,0:T(8,128)S(1)}, f32[11,5,8,128]{3,2,1,0:T(8,128)S(1)}, u32[]{:S(2)}, u32[]{:S(2)}) %collective-permute-start.6) | collective-permute-done | bytes 225312 | tf_op jit(solution)/shard_map/ppermute | solution.py:407
  22.9 1.7 %reorder.1 = (f32[960,128]{1,0:T(8,128)S(1)}, f32[360,128]{1,0:T(8,128)S(1)}, f32[360,128]{1,0:T(8,128)S(1)}, f32[360,128]{1,0:T(8,128)S(1)}, f32[360,128]{1,0:T(8,128)S(1)}) custom-call(s32[3]{0:T(128)S(1)} %pad_add_fusion.pos, s32[88]{0:T(128)S(1)} %get-tuple-element.29.rows, f32[11,5,8,128]{3,2,1,0:T(8,128)S(1)} %get-tuple-element.30.refs_0_, ...), custom_call_target="tpu_custom_call" | custom-call | tf_op jit(solution)/shard_map/reorder/pallas_call | solution.py:446
  24.5 0.1 collective-permute-start.9
  24.6 7.8 %collective-permute-start.10 = (f32[360,128]{1,0:T(8,128)S(1)}, f32[360,128]{1,0:T(8,128)S(1)}, u32[]{:S(2)}, u32[]{:S(2)}) collective-permute-start(f32[360,128]{1,0:T(8,128)S(1)} %get-tuple-element.38), channel_id=1, source_target_pairs={{0,127},{1,112},{2,113},{3,114},{4,115},{5,116},{6,117},{7,118},{8... | collective-permute-start | bytes 552968 | tf_op jit(solution)/shard_map/ppermute | solution.py:407
  32.5 0.0 collective-permute-start.7
  32.5 1.7 %collective-permute-start.8 = (f32[360,128]{1,0:T(8,128)S(1)}, f32[360,128]{1,0:T(8,128)S(1)}, u32[]{:S(2)}, u32[]{:S(2)}) collective-permute-start(f32[360,128]{1,0:T(8,128)S(1)} %get-tuple-element.36), channel_id=1, source_target_pairs={{0,47},{1,32},{2,33},{3,34},{4,35},{5,36},{6,37},{7,38},{8,39},{9,... | collective-permute-start | bytes 552968 | tf_op jit(solution)/shard_map/ppermute | solution.py:407
  34.2 0.0 collective-permute-done.9.y_in
  34.2 2.7 %collective-permute-done.10.y_out = f32[360,128]{1,0:T(8,128)S(1)} collective-permute-done((f32[360,128]{1,0:T(8,128)S(1)}, f32[360,128]{1,0:T(8,128)S(1)}, u32[]{:S(2)}, u32[]{:S(2)}) %collective-permute-start.10) | collective-permute-done | bytes 184352 | tf_op jit(solution)/shard_map/ppermute | solution.py:407
  36.9 0.6 corners.1
  37.6 0.1 collective-permute-start.11
  37.7 4.8 %collective-permute-start.12 = (f32[120,128]{1,0:T(8,128)S(1)}, f32[120,128]{1,0:T(8,128)S(1)}, u32[]{:S(2)}, u32[]{:S(2)}) collective-permute-start(f32[120,128]{1,0:T(8,128)S(1)} %get-tuple-element.44), channel_id=1, source_target_pairs={{0,47},{1,32},{2,33},{3,34},{4,35},{5,36},{6,37},{7,38},{8,39},{9,... | collective-permute-start | bytes 184328 | tf_op jit(solution)/shard_map/ppermute | solution.py:407
  42.4 0.0 collective-permute-done.7.x_in
  42.5 0.6 collective-permute-done.8.x_out
  43.0 2.4 %begin.1 = (f32[1680,128]{1,0:T(8,128)S(1)}, f32[1680,128]{1,0:T(8,128)S(1)}, f32[1680,128]{1,0:T(8,128)S(1)}, f32[1680,128]{1,0:T(8,128)S(1)}) custom-call(s32[3]{0:T(128)S(1)} %pad_add_fusion.pos, f32[960,128]{1,0:T(8,128)S(1)} %get-tuple-element.34.cur, f32[360,128]{1,0:T(8,128)S(1)} %collective-permute-done.7.x_in, ...), custom_call_target="tpu_custom_call" | custom-call | bytes 10000000 | tf_op jit(solution)/shard_map/begin/pallas_call | solution.py:486
  45.4 0.0 collective-permute-done.11.c_in
  45.4 0.0 collective-permute-done.12.c_out
  45.4 6.1 %finish.1.mine = f32[24,5,8,128]{3,2,1,0:T(8,128)S(1)} custom-call(s32[3]{0:T(128)S(1)} %pad_add_fusion.pos, f32[1680,128]{1,0:T(8,128)S(1)} %get-tuple-element.39.main, f32[1680,128]{1,0:T(8,128)S(1)} %get-tuple-element.40.side_rows, f32[1680,128]{1,0:T(8,128)S(1)} %get-tuple-element.41.early_main, f32[1680,128]{1,0:T(8,128)S(1)} %get-tuple-element.42.early_side, ...), custom_call_target="tpu_custom_call" | custom-call | tf_op jit(solution)/shard_map/finish/pallas_call | solution.py:495
  51.5 1.3 %collective-permute-start.13 = (f32[24,5,8,128]{3,2,1,0:T(8,128)S(1)}, f32[24,5,8,128]{3,2,1,0:T(8,128)S(1)}, u32[]{:S(2)}, u32[]{:S(2)}) collective-permute-start(f32[24,5,8,128]{3,2,1,0:T(8,128)S(1)} %finish.1.mine), channel_id=1, source_target_pairs={{0,16},{1,17},{2,18},{3,19},{4,20},{5,21},{6,22},{7,23},{8,24},{9,... | collective-permute-start | bytes 1474568 | tf_op jit(solution)/shard_map/ppermute | solution.py:407
  52.8 1.5 %collective-permute-done.13.other = f32[24,5,8,128]{3,2,1,0:T(8,128)S(1)} collective-permute-done((f32[24,5,8,128]{3,2,1,0:T(8,128)S(1)}, f32[24,5,8,128]{3,2,1,0:T(8,128)S(1)}, u32[]{:S(2)}, u32[]{:S(2)}) %collective-permute-start.13) | collective-permute-done | bytes 491552 | tf_op jit(solution)/shard_map/ppermute | solution.py:407
  54.3 0.7 pack_out.1
  54.9 0.1 collective-permute-start.14
  55.0 4.6 %collective-permute-start.15 = (f32[7,5,8,128]{3,2,1,0:T(8,128)S(1)}, f32[7,5,8,128]{3,2,1,0:T(8,128)S(1)}, u32[]{:S(2)}, u32[]{:S(2)}) collective-permute-start(f32[7,5,8,128]{3,2,1,0:T(8,128)S(1)} %get-tuple-element.47), channel_id=1, source_target_pairs={{0,64},{1,65},{2,66},{3,67},{4,68},{5,69},{6,70},{7,71},{8,72},{9,... | collective-permute-start | bytes 430088 | tf_op jit(solution)/shard_map/ppermute | solution.py:407
  59.6 0.0 collective-permute-start.16
  59.7 0.3 collective-permute-done.14.refs_1_
  60.0 6.3 %collective-permute-done.15.refs_2_ = f32[7,5,8,128]{3,2,1,0:T(8,128)S(1)} collective-permute-done((f32[7,5,8,128]{3,2,1,0:T(8,128)S(1)}, f32[7,5,8,128]{3,2,1,0:T(8,128)S(1)}, u32[]{:S(2)}, u32[]{:S(2)}) %collective-permute-start.15) | collective-permute-done | bytes 143392 | tf_op jit(solution)/shard_map/ppermute | solution.py:407
  66.3 2.5 %collective-permute-done.16.refs_3_ = f32[7,5,8,128]{3,2,1,0:T(8,128)S(1)} collective-permute-done((f32[7,5,8,128]{3,2,1,0:T(8,128)S(1)}, f32[7,5,8,128]{3,2,1,0:T(8,128)S(1)}, u32[]{:S(2)}, u32[]{:S(2)}) %collective-permute-start.16) | collective-permute-done | bytes 143392 | tf_op jit(solution)/shard_map/ppermute | solution.py:407
  68.8 1.4 %unpack_out.1 = f32[7,5,16,256]{3,2,1,0:T(8,128)} custom-call(s32[3]{0:T(128)S(1)} %pad_add_fusion.pos, f32[7,5,8,128]{3,2,1,0:T(8,128)S(1)} %get-tuple-element.45.refs_0_, f32[7,5,8,128]{3,2,1,0:T(8,128)S(1)} %collective-permute-done.14.refs_1_, f32[7,5,8,128]{3,2,1,0:T(8,128)S(1)} %collective-permute-done.15.refs_2_, ...), custom_call_target="tpu_custom_call" | custom-call | tf_op jit(solution)/shard_map/unpack_out/pallas_call | solution.py:514
Async XLA Ops:
  0.1 1.2 %copy-start = (f32[11,5,16,256]{3,2,1,0:T(8,128)S(1)}, f32[11,5,16,256]{3,2,1,0:T(8,128)}, u32[]{:S(2)}) copy-start(f32[11,5,16,256]{3,2,1,0:T(8,128)} %cells.1) | copy-start | bytes 2703364
  1.3 6.5 %copy-start.1 = (s32[128,11]{0,1:T(8,128)S(1)}, s32[128,11]{0,1:T(8,128)}, u32[]{:S(2)}) copy-start(s32[128,11]{0,1:T(8,128)} %param.3) | copy-start | bytes 16900
  1.9 10.3 %collective-permute-start.1 = (f32[11,5,8,128]{3,2,1,0:T(8,128)S(1)}, f32[11,5,8,128]{3,2,1,0:T(8,128)S(1)}, u32[]{:S(2)}, u32[]{:S(2)}) collective-permute-start(f32[11,5,8,128]{3,2,1,0:T(8,128)S(1)} %get-tuple-element.31), channel_id=1, source_target_pairs={{0,32},{1,33},{2,34},{3,35},{4,36},{5,37},{6,38},{7,39},{8,40},{9,... | collective-permute-start | bytes 675848 | tf_op jit(solution)/shard_map/ppermute | solution.py:407
  4.5 13.1 %collective-permute-start.3 = (f32[11,5,8,128]{3,2,1,0:T(8,128)S(1)}, f32[11,5,8,128]{3,2,1,0:T(8,128)S(1)}, u32[]{:S(2)}, u32[]{:S(2)}) collective-permute-start(f32[11,5,8,128]{3,2,1,0:T(8,128)S(1)} %get-tuple-element.32), channel_id=1, source_target_pairs={{0,64},{1,65},{2,66},{3,67},{4,68},{5,69},{6,70},{7,71},{8,72},{9,... | collective-permute-start | bytes 675848 | tf_op jit(solution)/shard_map/ppermute | solution.py:407
  7.8 12.2 %collective-permute-start.5 = (f32[11,5,8,128]{3,2,1,0:T(8,128)S(1)}, f32[11,5,8,128]{3,2,1,0:T(8,128)S(1)}, u32[]{:S(2)}, u32[]{:S(2)}) collective-permute-start(f32[11,5,8,128]{3,2,1,0:T(8,128)S(1)} %get-tuple-element.33), channel_id=1, source_target_pairs={{0,96},{1,97},{2,98},{3,99},{4,100},{5,101},{6,102},{7,103},{8,104... | collective-permute-start | bytes 675848 | tf_op jit(solution)/shard_map/ppermute | solution.py:407
  10.9 10.9 %collective-permute-start = (f32[11,5,8,128]{3,2,1,0:T(8,128)S(1)}, f32[11,5,8,128]{3,2,1,0:T(8,128)S(1)}, u32[]{:S(2)}, u32[]{:S(2)}) collective-permute-start(f32[11,5,8,128]{3,2,1,0:T(8,128)S(1)} %get-tuple-element.30.refs_0_), channel_id=1, source_target_pairs={{0,16},{1,17},{2,18},{3,19},{4,20},{5,21},{6,22},{7,23},{8,24},{9,... | collective-permute-start | bytes 675848 | tf_op jit(solution)/shard_map/ppermute | solution.py:407
  12.2 9.6 %collective-permute-start.2 = (f32[11,5,8,128]{3,2,1,0:T(8,128)S(1)}, f32[11,5,8,128]{3,2,1,0:T(8,128)S(1)}, u32[]{:S(2)}, u32[]{:S(2)}) collective-permute-start(f32[11,5,8,128]{3,2,1,0:T(8,128)S(1)} %collective-permute-done.1.refs_2_), channel_id=1, source_target_pairs={{0,16},{1,17},{2,18},{3,19},{4,20},{5,21},{6,22},{7,23},{8,24},{9,... | collective-permute-start | bytes 675848 | tf_op jit(solution)/shard_map/ppermute | solution.py:407
  17.6 4.2 %collective-permute-start.4 = (f32[11,5,8,128]{3,2,1,0:T(8,128)S(1)}, f32[11,5,8,128]{3,2,1,0:T(8,128)S(1)}, u32[]{:S(2)}, u32[]{:S(2)}) collective-permute-start(f32[11,5,8,128]{3,2,1,0:T(8,128)S(1)} %collective-permute-done.3.refs_4_), channel_id=1, source_target_pairs={{0,16},{1,17},{2,18},{3,19},{4,20},{5,21},{6,22},{7,23},{8,24},{9,... | collective-permute-start | bytes 675848 | tf_op jit(solution)/shard_map/ppermute | solution.py:407
  19.9 2.9 %collective-permute-start.6 = (f32[11,5,8,128]{3,2,1,0:T(8,128)S(1)}, f32[11,5,8,128]{3,2,1,0:T(8,128)S(1)}, u32[]{:S(2)}, u32[]{:S(2)}) collective-permute-start(f32[11,5,8,128]{3,2,1,0:T(8,128)S(1)} %collective-permute-done.5.refs_6_), channel_id=1, source_target_pairs={{0,16},{1,17},{2,18},{3,19},{4,20},{5,21},{6,22},{7,23},{8,24},{9,... | collective-permute-start | bytes 675848 | tf_op jit(solution)/shard_map/ppermute | solution.py:407
  24.5 9.7 %collective-permute-start.9 = (f32[360,128]{1,0:T(8,128)S(1)}, f32[360,128]{1,0:T(8,128)S(1)}, u32[]{:S(2)}, u32[]{:S(2)}) collective-permute-start(f32[360,128]{1,0:T(8,128)S(1)} %get-tuple-element.37), channel_id=1, source_target_pairs={{0,96},{1,97},{2,98},{3,99},{4,100},{5,101},{6,102},{7,103},{8,104... | collective-permute-start | bytes 552968 | tf_op jit(solution)/shard_map/ppermute | solution.py:407
  24.6 12.3 %collective-permute-start.10 = (f32[360,128]{1,0:T(8,128)S(1)}, f32[360,128]{1,0:T(8,128)S(1)}, u32[]{:S(2)}, u32[]{:S(2)}) collective-permute-start(f32[360,128]{1,0:T(8,128)S(1)} %get-tuple-element.38), channel_id=1, source_target_pairs={{0,127},{1,112},{2,113},{3,114},{4,115},{5,116},{6,117},{7,118},{8... | collective-permute-start | bytes 552968 | tf_op jit(solution)/shard_map/ppermute | solution.py:407
  32.5 10.0 %collective-permute-start.7 = (f32[360,128]{1,0:T(8,128)S(1)}, f32[360,128]{1,0:T(8,128)S(1)}, u32[]{:S(2)}, u32[]{:S(2)}) collective-permute-start(f32[360,128]{1,0:T(8,128)S(1)} %get-tuple-element.35), channel_id=1, source_target_pairs={{0,32},{1,33},{2,34},{3,35},{4,36},{5,37},{6,38},{7,39},{8,40},{9,... | collective-permute-start | bytes 552968 | tf_op jit(solution)/shard_map/ppermute | solution.py:407
  32.5 10.6 %collective-permute-start.8 = (f32[360,128]{1,0:T(8,128)S(1)}, f32[360,128]{1,0:T(8,128)S(1)}, u32[]{:S(2)}, u32[]{:S(2)}) collective-permute-start(f32[360,128]{1,0:T(8,128)S(1)} %get-tuple-element.36), channel_id=1, source_target_pairs={{0,47},{1,32},{2,33},{3,34},{4,35},{5,36},{6,37},{7,38},{8,39},{9,... | collective-permute-start | bytes 552968 | tf_op jit(solution)/shard_map/ppermute | solution.py:407
  37.6 7.9 %collective-permute-start.11 = (f32[120,128]{1,0:T(8,128)S(1)}, f32[120,128]{1,0:T(8,128)S(1)}, u32[]{:S(2)}, u32[]{:S(2)}) collective-permute-start(f32[120,128]{1,0:T(8,128)S(1)} %get-tuple-element.43), channel_id=1, source_target_pairs={{0,32},{1,33},{2,34},{3,35},{4,36},{5,37},{6,38},{7,39},{8,40},{9,... | collective-permute-start | bytes 184328 | tf_op jit(solution)/shard_map/ppermute | solution.py:407
  37.7 7.8 %collective-permute-start.12 = (f32[120,128]{1,0:T(8,128)S(1)}, f32[120,128]{1,0:T(8,128)S(1)}, u32[]{:S(2)}, u32[]{:S(2)}) collective-permute-start(f32[120,128]{1,0:T(8,128)S(1)} %get-tuple-element.44), channel_id=1, source_target_pairs={{0,47},{1,32},{2,33},{3,34},{4,35},{5,36},{6,37},{7,38},{8,39},{9,... | collective-permute-start | bytes 184328 | tf_op jit(solution)/shard_map/ppermute | solution.py:407
  51.5 2.7 %collective-permute-start.13 = (f32[24,5,8,128]{3,2,1,0:T(8,128)S(1)}, f32[24,5,8,128]{3,2,1,0:T(8,128)S(1)}, u32[]{:S(2)}, u32[]{:S(2)}) collective-permute-start(f32[24,5,8,128]{3,2,1,0:T(8,128)S(1)} %finish.1.mine), channel_id=1, source_target_pairs={{0,16},{1,17},{2,18},{3,19},{4,20},{5,21},{6,22},{7,23},{8,24},{9,... | collective-permute-start | bytes 1474568 | tf_op jit(solution)/shard_map/ppermute | solution.py:407
  54.9 5.1 %collective-permute-start.14 = (f32[7,5,8,128]{3,2,1,0:T(8,128)S(1)}, f32[7,5,8,128]{3,2,1,0:T(8,128)S(1)}, u32[]{:S(2)}, u32[]{:S(2)}) collective-permute-start(f32[7,5,8,128]{3,2,1,0:T(8,128)S(1)} %get-tuple-element.46), channel_id=1, source_target_pairs={{0,32},{1,33},{2,34},{3,35},{4,36},{5,37},{6,38},{7,39},{8,40},{9,... | collective-permute-start | bytes 430088 | tf_op jit(solution)/shard_map/ppermute | solution.py:407
  55.0 11.2 %collective-permute-start.15 = (f32[7,5,8,128]{3,2,1,0:T(8,128)S(1)}, f32[7,5,8,128]{3,2,1,0:T(8,128)S(1)}, u32[]{:S(2)}, u32[]{:S(2)}) collective-permute-start(f32[7,5,8,128]{3,2,1,0:T(8,128)S(1)} %get-tuple-element.47), channel_id=1, source_target_pairs={{0,64},{1,65},{2,66},{3,67},{4,68},{5,69},{6,70},{7,71},{8,72},{9,... | collective-permute-start | bytes 430088 | tf_op jit(solution)/shard_map/ppermute | solution.py:407
  59.6 9.1 %collective-permute-start.16 = (f32[7,5,8,128]{3,2,1,0:T(8,128)S(1)}, f32[7,5,8,128]{3,2,1,0:T(8,128)S(1)}, u32[]{:S(2)}, u32[]{:S(2)}) collective-permute-start(f32[7,5,8,128]{3,2,1,0:T(8,128)S(1)} %get-tuple-element.48), channel_id=1, source_target_pairs={{0,96},{1,97},{2,98},{3,99},{4,100},{5,101},{6,102},{7,103},{8,104... | collective-permute-start | bytes 430088 | tf_op jit(solution)/shard_map/ppermute | solution.py:407

commit v6 on v5

--- a/solution.py
+++ b/solution.py
@@ -51,38 +51,35 @@
                 outs[k][s, f] = cells[s, f, x, y]
 
 
-def unpack_out(pos, *refs):
-    parts, out, sems = refs[:4], refs[4], refs[5]
+def unpack_out(which, pos, *refs):
+    out, sems = refs[-2:]
     z = pos[0]
     copies = []
-    for k in range(4):
-        zk = z ^ k
-        copies.append(
-            pltpu.make_async_copy(
-                parts[k],
-                out.at[
-                    :, :, pl.ds(pl.multiple_of(tile_x(zk) * X, X), X), pl.ds(pl.multiple_of(tile_y(zk) * L, L), L)
-                ],
-                sems.at[k],
-            )
-        )
+    for i, k in enumerate(which):
+        x = pl.ds(pl.multiple_of(tile_x(z ^ k) * X, X), X)
+        y = pl.ds(pl.multiple_of(tile_y(z ^ k) * L, L), L)
+        copies.append(pltpu.make_async_copy(refs[i], out.at[:, :, x, y], sems.at[i]))
     for c in copies:
         c.start()
     for c in copies:
         c.wait()
 
 
-def table(pos, slots, _tile, final, rows, _same, held, count):
+def table(pos, slots, _tile, final, kept, given, mask, _same, held, count):
     z, core, g = pos[0], pos[1], pos[2]
     for d in range(N_ROW):
         n = jnp.int32(0)
-        place = ((z ^ d // 2) * 2 + (core ^ d % 2)) * CAP
+        place = jnp.where(core == d % 2, (z ^ d // 2) * CAP, 4 * CAP)
         for s in range(CAP):
             b = slots[d * N_COL + g, s]
             j = b - g * NBY
             held[d * 16 + s] = j
-            here = jnp.logical_and(b >= 0, (j & 1) == core)
-            rows[place + s] = jnp.where(here, j >> 1, HALF)
+            match = (j & 1) == core
+            row = jnp.where(b >= 0, j >> 1, HALF)
+            mine = jnp.where(match, row, HALF)
+            kept[place + s] = mine
+            given[place + s] = jnp.where(match, HALF, row)
+            mask[mine] = jnp.where(core == d % 2, 1, 0)
             n = n + jnp.where(b >= 0, 1, 0)
         count[d] = n
     for bit in range(3):
@@ -238,17 +235,20 @@
         copy(y_in, y_out)
 
 
-def reorder(pos, rows, *refs):
-    parts = refs[:8]
-    cur, x_in, x_out, y_in, y_out = refs[8:13]
-    held = refs[13]
-    for i in range(8):
+def sort_out(kept, given, *refs):
+    parts, mine, other = refs[:4], refs[4], refs[5]
+    for i in range(4):
         for s in range(CAP):
-            held[rows[i * CAP + s]] = parts[i][s]
-
+            tile = parts[i][s]
+            mine[kept[i * CAP + s]] = tile
+            other[given[i * CAP + s]] = tile
+
+
+def reorder(pos, mask, mine, other, cur, x_in, x_out, y_in, y_out):
     def convert(group, _):
+        here = [jnp.full((X, L), mask[group * 8 + i], jnp.int32) == 1 for i in range(8)]
         for f in range(F):
-            vectors = [held[group * 8 + i, f] for i in range(8)]
+            vectors = [jnp.where(here[i], mine[group * 8 + i, f], other[group * 8 + i, f]) for i in range(8)]
             for y, v in enumerate(transposed(vectors)):
                 cur[at(f, y, group), :] = v
         for y in range(Y):
@@ -421,37 +421,44 @@
         compiler_params=PARAMS,
         name="pack_in",
     )(pos, block_cells)
-    final, rows, own = pl.pallas_call(
+    index = jax.ShapeDtypeStruct((5 * CAP,), jnp.int32)
+    final, kept, given, mask, own = pl.pallas_call(
         table,
         out_shape=[
             jax.ShapeDtypeStruct((N_ROW * 8,), jnp.int32),
-            jax.ShapeDtypeStruct((N_ROW * CAP,), jnp.int32),
+            index,
+            index,
+            jax.ShapeDtypeStruct((HALF + 1,), jnp.int32),
             tiles[0],
         ],
         in_specs=[SMEM, SMEM, ANY],
-        out_specs=[SMEM, SMEM, ANY],
-        input_output_aliases={2: 2},
+        out_specs=[SMEM] * 4 + [ANY],
+        input_output_aliases={2: 4},
         scratch_shapes=[pltpu.SMEM((N_ROW * 16,), jnp.int32), pltpu.SMEM((N_ROW,), jnp.int32)],
         compiler_params=PARAMS,
         cost_estimate=pl.CostEstimate(flops=0, bytes_accessed=20_000_000, transcendentals=0),
         name="table",
     )(pos, slot_blocks, parts[0])
-    gathered = []
-    for k in range(4):
-        here = over_z(parts[k], k) if k else own
-        gathered += [here, over_core(here)]
+    gathered = [over_z(parts[k], k) if k else own for k in range(4)]
+    mine, other = pl.pallas_call(
+        sort_out,
+        out_shape=[shape(HALF + 1, F, X, L)] * 2,
+        in_specs=[SMEM, SMEM] + [VMEM] * 4,
+        out_specs=[VMEM] * 2,
+        compiler_params=PARAMS,
+        name="sort_out",
+    )(kept, given, *gathered)
 
     whole = shape(F * Y * HALF, L)
     layer = shape(F * DEEP * HALF, L)
     initial, x_in, x_out, y_in, y_out = pl.pallas_call(
         reorder,
         out_shape=[whole] + [layer] * 4,
-        in_specs=[SMEM, SMEM] + [VMEM] * 8,
+        in_specs=[SMEM, SMEM, VMEM, VMEM],
         out_specs=[VMEM] * 5,
-        scratch_shapes=[pltpu.VMEM((HALF + 1, F, X, L), jnp.float32)],
         compiler_params=PARAMS,
         name="reorder",
-    )(pos, rows, *gathered)
+    )(pos, mask, mine, over_core(other))
 
     def x_partner(z):
         return z ^ 1
@@ -511,15 +518,22 @@
         name="pack_out",
     )(pos, final, current, over_core(current))
     arrived = [over_z(leaving[k], k) for k in range(4)]
-    return pl.pallas_call(
-        unpack_out,
-        out_shape=shape(OUT, F, 2 * X, 2 * L),
-        in_specs=[SMEM] + [ANY] * 4,
-        out_specs=ANY,
-        scratch_shapes=[pltpu.SemaphoreType.DMA((4,))],
-        compiler_params=PARAMS,
-        name="unpack_out",
-    )(pos, *arrived)
+    result = []
+    for which in ((0, 1, 3), (2,)):
+        n = len(which)
+        result = [
+            pl.pallas_call(
+                lambda *refs, which=which: unpack_out(which, *refs),
+                out_shape=shape(OUT, F, 2 * X, 2 * L),
+                in_specs=[SMEM] + [ANY] * (n + len(result)),
+                out_specs=ANY,
+                input_output_aliases={n + 1: 0} if result else {},
+                scratch_shapes=[pltpu.SemaphoreType.DMA((n,))],
+                compiler_params=PARAMS,
+                name="unpack_out",
+            )(pos, *[arrived[k] for k in which], *result)
+        ]
+    return result[0]
 
 
 def solution(mesh):

time: 70.3 us -> 69.6 us (0.990); the launches traced: 70.2 us -> 68.5 us
  starting transfers between devices: 31.2 us -> 28.2 us
  Pallas kernels: 16.4 us -> 18.3 us
    ppermute x17 -> x14, starting transfers between devices: 31.2 us -> 28.2 us  [to(): return lax.ppermute(array, ('row', 'col'), pairs)]
    pallas_call x1 -> x3, Pallas kernels: 1.39 us -> 3.22 us  [the longest x2 2.56 us: body(): pl.pallas_call(lambda *refs, which=which: unpack_out(which, *refs), out_s...]
    ppermute x17 -> x14, waiting for transfers between devices: 21.1 us -> 20.5 us  [to(): return lax.ppermute(array, ('row', 'col'), pairs)]
  transfers between devices with their start and end apart: 17 -> 14, of which waited for: 9 -> 9; matrix products, arithmetic and copies ran while one was open for 0% -> 0% of each run, Pallas kernels for 9% -> 11%
where the time goes in v6:
time: 69.6 us; the launch traced here: 68.5 us
  starting transfers between devices  28.2 us (41%)
  waiting for transfers between devices  20.5 us (29%)
  Pallas kernels  18.3 us (26%)
  local copies, waits for them, and re-layouts  1.29 us (2%)
    ppermute x14, starting transfers between devices, to(): return lax.ppermute(array, ('row', 'col'), pairs)  28.2 us
    ppermute x14, waiting for transfers between devices, to(): return lax.ppermute(array, ('row', 'col'), pairs)  20.5 us
    pallas_call x1, Pallas kernels, body(): pl.pallas_call(finish, out_shape=shape(HALF, F, X, L), in_specs=[SMEM] +...  6.07 us
    pallas_call x1, Pallas kernels, body(): pl.pallas_call(table, out_shape=[jax.ShapeDtypeStruct((N_ROW * 8,), jnp.i...  3.07 us
    pallas_call x2, Pallas kernels, body(): pl.pallas_call(lambda *refs, which=which: unpack_out(which, *refs), out_s...  2.56 us
    pallas_call x1, Pallas kernels, body(): pl.pallas_call(begin, out_shape=[shape(*wide)] * 4, in_specs=[SMEM] + [VM...  2.39 us
    pallas_call x1, Pallas kernels, body(): pl.pallas_call(reorder, out_shape=[whole] + [layer] * 4, in_specs=[SMEM,...  1.59 us
  transfers between devices with their start and end apart: 14, of which 9 were waited for; matrix products, arithmetic and copies ran while one was open for 0% of the time, Pallas kernels for 11%

profile of v6, /device:TPU:1, one launch (start us, length us, event | category | flops | bytes accessed | tf_op | source)
XLA Modules:
  0.0 68.5 jit_solution(8157005579659383968)
XLA Ops:
  0.0 0.1 pad_add_fusion.pos.refs_0_
  0.1 0.0 copy-start
  0.1 1.2 %copy-done = f32[11,5,16,256]{3,2,1,0:T(8,128)S(1)} copy-done((f32[11,5,16,256]{3,2,1,0:T(8,128)S(1)}, f32[11,5,16,256]{3,2,1,0:T(8,128)}, u32[]{:S(2)}) %copy-start) | copy-done | bytes 901144
  1.3 0.0 copy-start.1
  1.3 0.7 pack_in.1
  1.9 2.5 %collective-permute-start = (f32[11,5,8,128]{3,2,1,0:T(8,128)S(1)}, f32[11,5,8,128]{3,2,1,0:T(8,128)S(1)}, u32[]{:S(2)}, u32[]{:S(2)}) collective-permute-start(f32[11,5,8,128]{3,2,1,0:T(8,128)S(1)} %get-tuple-element.37), channel_id=1, source_target_pairs={{0,32},{1,33},{2,34},{3,35},{4,36},{5,37},{6,38},{7,39},{8,40},{9,... | collective-permute-start | bytes 675848 | tf_op jit(solution)/shard_map/ppermute | solution.py:407
  4.5 3.3 %collective-permute-start.1 = (f32[11,5,8,128]{3,2,1,0:T(8,128)S(1)}, f32[11,5,8,128]{3,2,1,0:T(8,128)S(1)}, u32[]{:S(2)}, u32[]{:S(2)}) collective-permute-start(f32[11,5,8,128]{3,2,1,0:T(8,128)S(1)} %get-tuple-element.38), channel_id=1, source_target_pairs={{0,64},{1,65},{2,66},{3,67},{4,68},{5,69},{6,70},{7,71},{8,72},{9,... | collective-permute-start | bytes 675848 | tf_op jit(solution)/shard_map/ppermute | solution.py:407
  7.8 0.0 collective-permute-start.2
  7.8 0.0 copy-done.1
  7.8 0.1 copy.5.slots
  7.9 3.1 %table.1 = (s32[64]{0:T(128)S(1)}, s32[55]{0:T(128)S(1)}, s32[55]{0:T(128)S(1)}, s32[25]{0:T(128)S(1)}, f32[11,5,8,128]{3,2,1,0:T(8,128)S(1)}) custom-call(s32[3]{0:T(128)S(1)} %pad_add_fusion.pos.refs_0_, s32[128,11]{1,0:T(8,128)S(1)} %copy.5.slots, f32[11,5,8,128]{3,2,1,0:T(8,128)S(1)} %get-tuple-element.31._tile), custom_call_target="tpu_custom_call", output_to_operand_aliasing={{4}: (2, {})} | custom-call | bytes 20000000 | tf_op jit(solution)/shard_map/table/pallas_call | solution.py:425
  11.0 0.0 collective-permute-done.refs_1_
  11.0 6.6 %collective-permute-done.1.refs_2_ = f32[11,5,8,128]{3,2,1,0:T(8,128)S(1)} collective-permute-done((f32[11,5,8,128]{3,2,1,0:T(8,128)S(1)}, f32[11,5,8,128]{3,2,1,0:T(8,128)S(1)}, u32[]{:S(2)}, u32[]{:S(2)}) %collective-permute-start.1) | collective-permute-done | bytes 225312 | tf_op jit(solution)/shard_map/ppermute | solution.py:407
  17.6 2.4 %collective-permute-done.2.refs_3_ = f32[11,5,8,128]{3,2,1,0:T(8,128)S(1)} collective-permute-done((f32[11,5,8,128]{3,2,1,0:T(8,128)S(1)}, f32[11,5,8,128]{3,2,1,0:T(8,128)S(1)}, u32[]{:S(2)}, u32[]{:S(2)}) %collective-permute-start.2) | collective-permute-done | bytes 225312 | tf_op jit(solution)/shard_map/ppermute | solution.py:407
  19.9 0.7 sort_out.1
  20.6 1.9 %collective-permute-start.3 = (f32[25,5,8,128]{3,2,1,0:T(8,128)S(1)}, f32[25,5,8,128]{3,2,1,0:T(8,128)S(1)}, u32[]{:S(2)}, u32[]{:S(2)}) collective-permute-start(f32[25,5,8,128]{3,2,1,0:T(8,128)S(1)} %get-tuple-element.41), channel_id=1, source_target_pairs={{0,16},{1,17},{2,18},{3,19},{4,20},{5,21},{6,22},{7,23},{8,24},{9,... | collective-permute-start | bytes 1536008 | tf_op jit(solution)/shard_map/ppermute | solution.py:407
  22.5 1.5 %collective-permute-done.3.other = f32[25,5,8,128]{3,2,1,0:T(8,128)S(1)} collective-permute-done((f32[25,5,8,128]{3,2,1,0:T(8,128)S(1)}, f32[25,5,8,128]{3,2,1,0:T(8,128)S(1)}, u32[]{:S(2)}, u32[]{:S(2)}) %collective-permute-start.3) | collective-permute-done | bytes 512032 | tf_op jit(solution)/shard_map/ppermute | solution.py:407
  24.0 1.6 %reorder.1 = (f32[960,128]{1,0:T(8,128)S(1)}, f32[360,128]{1,0:T(8,128)S(1)}, f32[360,128]{1,0:T(8,128)S(1)}, f32[360,128]{1,0:T(8,128)S(1)}, f32[360,128]{1,0:T(8,128)S(1)}) custom-call(s32[3]{0:T(128)S(1)} %pad_add_fusion.pos.refs_0_, s32[25]{0:T(128)S(1)} %get-tuple-element.33.mask, f32[25,5,8,128]{3,2,1,0:T(8,128)S(1)} %get-tuple-element.40.mine, ...), custom_call_target="tpu_custom_call" | custom-call | tf_op jit(solution)/shard_map/reorder/pallas_call | solution.py:454
  25.6 0.1 collective-permute-start.6
  25.7 7.8 %collective-permute-start.7 = (f32[360,128]{1,0:T(8,128)S(1)}, f32[360,128]{1,0:T(8,128)S(1)}, u32[]{:S(2)}, u32[]{:S(2)}) collective-permute-start(f32[360,128]{1,0:T(8,128)S(1)} %get-tuple-element.46), channel_id=1, source_target_pairs={{0,127},{1,112},{2,113},{3,114},{4,115},{5,116},{6,117},{7,118},{8... | collective-permute-start | bytes 552968 | tf_op jit(solution)/shard_map/ppermute | solution.py:407
  33.6 0.0 collective-permute-start.4
  33.6 1.7 %collective-permute-start.5 = (f32[360,128]{1,0:T(8,128)S(1)}, f32[360,128]{1,0:T(8,128)S(1)}, u32[]{:S(2)}, u32[]{:S(2)}) collective-permute-start(f32[360,128]{1,0:T(8,128)S(1)} %get-tuple-element.44), channel_id=1, source_target_pairs={{0,47},{1,32},{2,33},{3,34},{4,35},{5,36},{6,37},{7,38},{8,39},{9,... | collective-permute-start | bytes 552968 | tf_op jit(solution)/shard_map/ppermute | solution.py:407
  35.3 0.0 collective-permute-done.6.y_in
  35.3 2.7 %collective-permute-done.7.y_out = f32[360,128]{1,0:T(8,128)S(1)} collective-permute-done((f32[360,128]{1,0:T(8,128)S(1)}, f32[360,128]{1,0:T(8,128)S(1)}, u32[]{:S(2)}, u32[]{:S(2)}) %collective-permute-start.7) | collective-permute-done | bytes 184352 | tf_op jit(solution)/shard_map/ppermute | solution.py:407
  38.0 0.6 corners.1
  38.7 0.1 collective-permute-start.8
  38.8 4.8 %collective-permute-start.9 = (f32[120,128]{1,0:T(8,128)S(1)}, f32[120,128]{1,0:T(8,128)S(1)}, u32[]{:S(2)}, u32[]{:S(2)}) collective-permute-start(f32[120,128]{1,0:T(8,128)S(1)} %get-tuple-element.52), channel_id=1, source_target_pairs={{0,47},{1,32},{2,33},{3,34},{4,35},{5,36},{6,37},{7,38},{8,39},{9,... | collective-permute-start | bytes 184328 | tf_op jit(solution)/shard_map/ppermute | solution.py:407
  43.5 0.0 collective-permute-done.4.x_in
  43.5 0.6 collective-permute-done.5.x_out
  44.1 2.4 %begin.1 = (f32[1680,128]{1,0:T(8,128)S(1)}, f32[1680,128]{1,0:T(8,128)S(1)}, f32[1680,128]{1,0:T(8,128)S(1)}, f32[1680,128]{1,0:T(8,128)S(1)}) custom-call(s32[3]{0:T(128)S(1)} %pad_add_fusion.pos.refs_0_, f32[960,128]{1,0:T(8,128)S(1)} %get-tuple-element.42.cur, f32[360,128]{1,0:T(8,128)S(1)} %collective-permute-done.4.x_in, ...), custom_call_target="tpu_custom_call" | custom-call | bytes 10000000 | tf_op jit(solution)/shard_map/begin/pallas_call | solution.py:493
  46.5 0.0 collective-permute-done.8.c_in
  46.5 0.0 collective-permute-done.9.c_out
  46.5 6.1 %finish.1.mine = f32[24,5,8,128]{3,2,1,0:T(8,128)S(1)} custom-call(s32[3]{0:T(128)S(1)} %pad_add_fusion.pos.refs_0_, f32[1680,128]{1,0:T(8,128)S(1)} %get-tuple-element.47.main, f32[1680,128]{1,0:T(8,128)S(1)} %get-tuple-element.48.side_rows, f32[1680,128]{1,0:T(8,128)S(1)} %get-tuple-element.49.early_main, f32[1680,128]{1,0:T(8,128)S(1)} %get-tuple-element.50.early_side, ...), custom_call_target="tpu_custom_call" | custom-call | tf_op jit(solution)/shard_map/finish/pallas_call | solution.py:502
  52.6 1.3 %collective-permute-start.10 = (f32[24,5,8,128]{3,2,1,0:T(8,128)S(1)}, f32[24,5,8,128]{3,2,1,0:T(8,128)S(1)}, u32[]{:S(2)}, u32[]{:S(2)}) collective-permute-start(f32[24,5,8,128]{3,2,1,0:T(8,128)S(1)} %finish.1.mine), channel_id=1, source_target_pairs={{0,16},{1,17},{2,18},{3,19},{4,20},{5,21},{6,22},{7,23},{8,24},{9,... | collective-permute-start | bytes 1474568 | tf_op jit(solution)/shard_map/ppermute | solution.py:407
  53.9 1.5 %collective-permute-done.10.other = f32[24,5,8,128]{3,2,1,0:T(8,128)S(1)} collective-permute-done((f32[24,5,8,128]{3,2,1,0:T(8,128)S(1)}, f32[24,5,8,128]{3,2,1,0:T(8,128)S(1)}, u32[]{:S(2)}, u32[]{:S(2)}) %collective-permute-start.10) | collective-permute-done | bytes 491552 | tf_op jit(solution)/shard_map/ppermute | solution.py:407
  55.4 0.7 pack_out.1
  56.0 0.1 collective-permute-start.12
  56.1 3.5 %collective-permute-start.13 = (f32[7,5,8,128]{3,2,1,0:T(8,128)S(1)}, f32[7,5,8,128]{3,2,1,0:T(8,128)S(1)}, u32[]{:S(2)}, u32[]{:S(2)}) collective-permute-start(f32[7,5,8,128]{3,2,1,0:T(8,128)S(1)} %get-tuple-element.56), channel_id=1, source_target_pairs={{0,96},{1,97},{2,98},{3,99},{4,100},{5,101},{6,102},{7,103},{8,104... | collective-permute-start | bytes 430088 | tf_op jit(solution)/shard_map/ppermute | solution.py:407
  59.7 1.1 %collective-permute-start.11 = (f32[7,5,8,128]{3,2,1,0:T(8,128)S(1)}, f32[7,5,8,128]{3,2,1,0:T(8,128)S(1)}, u32[]{:S(2)}, u32[]{:S(2)}) collective-permute-start(f32[7,5,8,128]{3,2,1,0:T(8,128)S(1)} %get-tuple-element.53), channel_id=1, source_target_pairs={{0,64},{1,65},{2,66},{3,67},{4,68},{5,69},{6,70},{7,71},{8,72},{9,... | collective-permute-start | bytes 430088 | tf_op jit(solution)/shard_map/ppermute | solution.py:407
  60.7 0.3 collective-permute-done.12.refs_2_
  61.1 4.5 %collective-permute-done.13.refs_3_ = f32[7,5,8,128]{3,2,1,0:T(8,128)S(1)} collective-permute-done((f32[7,5,8,128]{3,2,1,0:T(8,128)S(1)}, f32[7,5,8,128]{3,2,1,0:T(8,128)S(1)}, u32[]{:S(2)}, u32[]{:S(2)}) %collective-permute-start.13) | collective-permute-done | bytes 143392 | tf_op jit(solution)/shard_map/ppermute | solution.py:407
  65.6 1.3 %unpack_out.2.refs_2_ = f32[7,5,16,256]{3,2,1,0:T(8,128)} custom-call(s32[3]{0:T(128)S(1)} %pad_add_fusion.pos.refs_0_, f32[7,5,8,128]{3,2,1,0:T(8,128)S(1)} %get-tuple-element.54.refs_1_, f32[7,5,8,128]{3,2,1,0:T(8,128)S(1)} %collective-permute-done.12.refs_2_, f32[7,5,8,128]{3,2,1,0:T(8,128)S(1)} %collective-permute-done.13.refs_3_), custom_call_target="tpu_custom_call" | custom-call | tf_op jit(solution)/shard_map/unpack_out/pallas_call | solution.py:525
  67.0 0.3 collective-permute-done.11.refs_1_
  67.3 1.2 %unpack_out.3 = f32[7,5,16,256]{3,2,1,0:T(8,128)} custom-call(s32[3]{0:T(128)S(1)} %pad_add_fusion.pos.refs_0_, f32[7,5,8,128]{3,2,1,0:T(8,128)S(1)} %collective-permute-done.11.refs_1_, f32[7,5,16,256]{3,2,1,0:T(8,128)} %unpack_out.2.refs_2_), custom_call_target="tpu_custom_call", output_to_operand_aliasing={{}: (2, {})} | custom-call | tf_op jit(solution)/shard_map/unpack_out/pallas_call | solution.py:525
Async XLA Ops:
  0.1 1.2 %copy-start = (f32[11,5,16,256]{3,2,1,0:T(8,128)S(1)}, f32[11,5,16,256]{3,2,1,0:T(8,128)}, u32[]{:S(2)}) copy-start(f32[11,5,16,256]{3,2,1,0:T(8,128)} %cells.1) | copy-start | bytes 2703364
  1.3 6.5 %copy-start.1 = (s32[128,11]{0,1:T(8,128)S(1)}, s32[128,11]{0,1:T(8,128)}, u32[]{:S(2)}) copy-start(s32[128,11]{0,1:T(8,128)} %param.3) | copy-start | bytes 16900
  1.9 9.0 %collective-permute-start = (f32[11,5,8,128]{3,2,1,0:T(8,128)S(1)}, f32[11,5,8,128]{3,2,1,0:T(8,128)S(1)}, u32[]{:S(2)}, u32[]{:S(2)}) collective-permute-start(f32[11,5,8,128]{3,2,1,0:T(8,128)S(1)} %get-tuple-element.37), channel_id=1, source_target_pairs={{0,32},{1,33},{2,34},{3,35},{4,36},{5,37},{6,38},{7,39},{8,40},{9,... | collective-permute-start | bytes 675848 | tf_op jit(solution)/shard_map/ppermute | solution.py:407
  4.5 13.1 %collective-permute-start.1 = (f32[11,5,8,128]{3,2,1,0:T(8,128)S(1)}, f32[11,5,8,128]{3,2,1,0:T(8,128)S(1)}, u32[]{:S(2)}, u32[]{:S(2)}) collective-permute-start(f32[11,5,8,128]{3,2,1,0:T(8,128)S(1)} %get-tuple-element.38), channel_id=1, source_target_pairs={{0,64},{1,65},{2,66},{3,67},{4,68},{5,69},{6,70},{7,71},{8,72},{9,... | collective-permute-start | bytes 675848 | tf_op jit(solution)/shard_map/ppermute | solution.py:407
  7.8 12.2 %collective-permute-start.2 = (f32[11,5,8,128]{3,2,1,0:T(8,128)S(1)}, f32[11,5,8,128]{3,2,1,0:T(8,128)S(1)}, u32[]{:S(2)}, u32[]{:S(2)}) collective-permute-start(f32[11,5,8,128]{3,2,1,0:T(8,128)S(1)} %get-tuple-element.39), channel_id=1, source_target_pairs={{0,96},{1,97},{2,98},{3,99},{4,100},{5,101},{6,102},{7,103},{8,104... | collective-permute-start | bytes 675848 | tf_op jit(solution)/shard_map/ppermute | solution.py:407
  20.6 3.4 %collective-permute-start.3 = (f32[25,5,8,128]{3,2,1,0:T(8,128)S(1)}, f32[25,5,8,128]{3,2,1,0:T(8,128)S(1)}, u32[]{:S(2)}, u32[]{:S(2)}) collective-permute-start(f32[25,5,8,128]{3,2,1,0:T(8,128)S(1)} %get-tuple-element.41), channel_id=1, source_target_pairs={{0,16},{1,17},{2,18},{3,19},{4,20},{5,21},{6,22},{7,23},{8,24},{9,... | collective-permute-start | bytes 1536008 | tf_op jit(solution)/shard_map/ppermute | solution.py:407
  25.6 9.7 %collective-permute-start.6 = (f32[360,128]{1,0:T(8,128)S(1)}, f32[360,128]{1,0:T(8,128)S(1)}, u32[]{:S(2)}, u32[]{:S(2)}) collective-permute-start(f32[360,128]{1,0:T(8,128)S(1)} %get-tuple-element.45), channel_id=1, source_target_pairs={{0,96},{1,97},{2,98},{3,99},{4,100},{5,101},{6,102},{7,103},{8,104... | collective-permute-start | bytes 552968 | tf_op jit(solution)/shard_map/ppermute | solution.py:407
  25.7 12.3 %collective-permute-start.7 = (f32[360,128]{1,0:T(8,128)S(1)}, f32[360,128]{1,0:T(8,128)S(1)}, u32[]{:S(2)}, u32[]{:S(2)}) collective-permute-start(f32[360,128]{1,0:T(8,128)S(1)} %get-tuple-element.46), channel_id=1, source_target_pairs={{0,127},{1,112},{2,113},{3,114},{4,115},{5,116},{6,117},{7,118},{8... | collective-permute-start | bytes 552968 | tf_op jit(solution)/shard_map/ppermute | solution.py:407
  33.6 10.0 %collective-permute-start.4 = (f32[360,128]{1,0:T(8,128)S(1)}, f32[360,128]{1,0:T(8,128)S(1)}, u32[]{:S(2)}, u32[]{:S(2)}) collective-permute-start(f32[360,128]{1,0:T(8,128)S(1)} %get-tuple-element.43), channel_id=1, source_target_pairs={{0,32},{1,33},{2,34},{3,35},{4,36},{5,37},{6,38},{7,39},{8,40},{9,... | collective-permute-start | bytes 552968 | tf_op jit(solution)/shard_map/ppermute | solution.py:407
  33.6 10.6 %collective-permute-start.5 = (f32[360,128]{1,0:T(8,128)S(1)}, f32[360,128]{1,0:T(8,128)S(1)}, u32[]{:S(2)}, u32[]{:S(2)}) collective-permute-start(f32[360,128]{1,0:T(8,128)S(1)} %get-tuple-element.44), channel_id=1, source_target_pairs={{0,47},{1,32},{2,33},{3,34},{4,35},{5,36},{6,37},{7,38},{8,39},{9,... | collective-permute-start | bytes 552968 | tf_op jit(solution)/shard_map/ppermute | solution.py:407
  38.7 7.9 %collective-permute-start.8 = (f32[120,128]{1,0:T(8,128)S(1)}, f32[120,128]{1,0:T(8,128)S(1)}, u32[]{:S(2)}, u32[]{:S(2)}) collective-permute-start(f32[120,128]{1,0:T(8,128)S(1)} %get-tuple-element.51), channel_id=1, source_target_pairs={{0,32},{1,33},{2,34},{3,35},{4,36},{5,37},{6,38},{7,39},{8,40},{9,... | collective-permute-start | bytes 184328 | tf_op jit(solution)/shard_map/ppermute | solution.py:407
  38.8 7.8 %collective-permute-start.9 = (f32[120,128]{1,0:T(8,128)S(1)}, f32[120,128]{1,0:T(8,128)S(1)}, u32[]{:S(2)}, u32[]{:S(2)}) collective-permute-start(f32[120,128]{1,0:T(8,128)S(1)} %get-tuple-element.52), channel_id=1, source_target_pairs={{0,47},{1,32},{2,33},{3,34},{4,35},{5,36},{6,37},{7,38},{8,39},{9,... | collective-permute-start | bytes 184328 | tf_op jit(solution)/shard_map/ppermute | solution.py:407
  52.6 2.7 %collective-permute-start.10 = (f32[24,5,8,128]{3,2,1,0:T(8,128)S(1)}, f32[24,5,8,128]{3,2,1,0:T(8,128)S(1)}, u32[]{:S(2)}, u32[]{:S(2)}) collective-permute-start(f32[24,5,8,128]{3,2,1,0:T(8,128)S(1)} %finish.1.mine), channel_id=1, source_target_pairs={{0,16},{1,17},{2,18},{3,19},{4,20},{5,21},{6,22},{7,23},{8,24},{9,... | collective-permute-start | bytes 1474568 | tf_op jit(solution)/shard_map/ppermute | solution.py:407
  56.0 5.1 %collective-permute-start.12 = (f32[7,5,8,128]{3,2,1,0:T(8,128)S(1)}, f32[7,5,8,128]{3,2,1,0:T(8,128)S(1)}, u32[]{:S(2)}, u32[]{:S(2)}) collective-permute-start(f32[7,5,8,128]{3,2,1,0:T(8,128)S(1)} %get-tuple-element.55), channel_id=1, source_target_pairs={{0,32},{1,33},{2,34},{3,35},{4,36},{5,37},{6,38},{7,39},{8,40},{9,... | collective-permute-start | bytes 430088 | tf_op jit(solution)/shard_map/ppermute | solution.py:407
  56.1 9.5 %collective-permute-start.13 = (f32[7,5,8,128]{3,2,1,0:T(8,128)S(1)}, f32[7,5,8,128]{3,2,1,0:T(8,128)S(1)}, u32[]{:S(2)}, u32[]{:S(2)}) collective-permute-start(f32[7,5,8,128]{3,2,1,0:T(8,128)S(1)} %get-tuple-element.56), channel_id=1, source_target_pairs={{0,96},{1,97},{2,98},{3,99},{4,100},{5,101},{6,102},{7,103},{8,104... | collective-permute-start | bytes 430088 | tf_op jit(solution)/shard_map/ppermute | solution.py:407
  59.7 7.7 %collective-permute-start.11 = (f32[7,5,8,128]{3,2,1,0:T(8,128)S(1)}, f32[7,5,8,128]{3,2,1,0:T(8,128)S(1)}, u32[]{:S(2)}, u32[]{:S(2)}) collective-permute-start(f32[7,5,8,128]{3,2,1,0:T(8,128)S(1)} %get-tuple-element.53), channel_id=1, source_target_pairs={{0,64},{1,65},{2,66},{3,67},{4,68},{5,69},{6,70},{7,71},{8,72},{9,... | collective-permute-start | bytes 430088 | tf_op jit(solution)/shard_map/ppermute | solution.py:407

commit v7 on v5

--- a/solution.py
+++ b/solution.py
@@ -51,21 +51,14 @@
                 outs[k][s, f] = cells[s, f, x, y]
 
 
-def unpack_out(pos, *refs):
-    parts, out, sems = refs[:4], refs[4], refs[5]
+def unpack_out(which, pos, *refs):
+    out, sems = refs[-2:]
     z = pos[0]
     copies = []
-    for k in range(4):
-        zk = z ^ k
-        copies.append(
-            pltpu.make_async_copy(
-                parts[k],
-                out.at[
-                    :, :, pl.ds(pl.multiple_of(tile_x(zk) * X, X), X), pl.ds(pl.multiple_of(tile_y(zk) * L, L), L)
-                ],
-                sems.at[k],
-            )
-        )
+    for i, k in enumerate(which):
+        x = pl.ds(pl.multiple_of(tile_x(z ^ k) * X, X), X)
+        y = pl.ds(pl.multiple_of(tile_y(z ^ k) * L, L), L)
+        copies.append(pltpu.make_async_copy(refs[i], out.at[:, :, x, y], sems.at[i]))
     for c in copies:
         c.start()
     for c in copies:
@@ -511,15 +504,22 @@
         name="pack_out",
     )(pos, final, current, over_core(current))
     arrived = [over_z(leaving[k], k) for k in range(4)]
-    return pl.pallas_call(
-        unpack_out,
-        out_shape=shape(OUT, F, 2 * X, 2 * L),
-        in_specs=[SMEM] + [ANY] * 4,
-        out_specs=ANY,
-        scratch_shapes=[pltpu.SemaphoreType.DMA((4,))],
-        compiler_params=PARAMS,
-        name="unpack_out",
-    )(pos, *arrived)
+    result = []
+    for which in ((0, 1, 3), (2,)):
+        n = len(which)
+        result = [
+            pl.pallas_call(
+                lambda *refs, which=which: unpack_out(which, *refs),
+                out_shape=shape(OUT, F, 2 * X, 2 * L),
+                in_specs=[SMEM] + [ANY] * (n + len(result)),
+                out_specs=ANY,
+                input_output_aliases={n + 1: 0} if result else {},
+                scratch_shapes=[pltpu.SemaphoreType.DMA((n,))],
+                compiler_params=PARAMS,
+                name="unpack_out",
+            )(pos, *[arrived[k] for k in which], *result)
+        ]
+    return result[0]
 
 
 def solution(mesh):

time: 70.3 us -> 68.6 us (0.976); the launches traced: 70.2 us -> 67.5 us
  waiting for transfers between devices: 21.1 us -> 17.2 us
  Pallas kernels: 16.4 us -> 17.6 us
    ppermute x17, waiting for transfers between devices: 21.1 us -> 17.2 us  [to(): return lax.ppermute(array, ('row', 'col'), pairs)]
    pallas_call x1 -> x2, Pallas kernels: 1.39 us -> 2.56 us  [body(): pl.pallas_call(lambda *refs, which=which: unpack_out(which, *refs), out_s...]
  transfers between devices with their start and end apart: 17 -> 17, of which waited for: 9 -> 9; matrix products, arithmetic and copies ran while one was open for 0% -> 0% of each run, Pallas kernels for 9% -> 11%
where the time goes in v7:
time: 68.6 us; the launch traced here: 67.5 us
  starting transfers between devices  31.2 us (45%)
  Pallas kernels  17.6 us (26%)
  waiting for transfers between devices  17.2 us (25%)
  local copies, waits for them, and re-layouts  1.29 us (2%)
    ppermute x17, starting transfers between devices, to(): return lax.ppermute(array, ('row', 'col'), pairs)  31.2 us
    ppermute x17, waiting for transfers between devices, to(): return lax.ppermute(array, ('row', 'col'), pairs)  17.2 us
    pallas_call x1, Pallas kernels, body(): pl.pallas_call(finish, out_shape=shape(HALF, F, X, L), in_specs=[SMEM] +...  6.07 us
    pallas_call x1, Pallas kernels, body(): pl.pallas_call(table, out_shape=[jax.ShapeDtypeStruct((N_ROW * 8,), jnp.i...  2.99 us
    pallas_call x2, Pallas kernels, body(): pl.pallas_call(lambda *refs, which=which: unpack_out(which, *refs), out_s...  2.56 us
    pallas_call x1, Pallas kernels, body(): pl.pallas_call(begin, out_shape=[shape(*wide)] * 4, in_specs=[SMEM] + [VM...  2.39 us
    pallas_call x1, Pallas kernels, body(): pl.pallas_call(reorder, out_shape=[whole] + [layer] * 4, in_specs=[SMEM,...  1.66 us
  transfers between devices with their start and end apart: 17, of which 9 were waited for; matrix products, arithmetic and copies ran while one was open for 0% of the time, Pallas kernels for 11%

profile of v7, /device:TPU:1, one launch (start us, length us, event | category | flops | bytes accessed | tf_op | source)
XLA Modules:
  0.0 67.5 jit_solution(7234597365700404900)
XLA Ops:
  0.0 0.1 pad_add_fusion.pos.refs_0_
  0.1 0.0 copy-start
  0.1 1.2 %copy-done = f32[11,5,16,256]{3,2,1,0:T(8,128)S(1)} copy-done((f32[11,5,16,256]{3,2,1,0:T(8,128)S(1)}, f32[11,5,16,256]{3,2,1,0:T(8,128)}, u32[]{:S(2)}) %copy-start) | copy-done | bytes 901144
  1.3 0.0 copy-start.1
  1.3 0.7 %pack_in.1 = (f32[11,5,8,128]{3,2,1,0:T(8,128)S(1)}, f32[11,5,8,128]{3,2,1,0:T(8,128)S(1)}, f32[11,5,8,128]{3,2,1,0:T(8,128)S(1)}, f32[11,5,8,128]{3,2,1,0:T(8,128)S(1)}) custom-call(s32[3]{0:T(128)S(1)} %pad_add_fusion.pos.refs_0_, f32[11,5,16,256]{3,2,1,0:T(8,128)S(1)} %copy-done), custom_call_target="tpu_custom_call" | custom-call | tf_op jit(solution)/shard_map/pack_in/pallas_call | solution.py:409
  1.9 2.5 %collective-permute-start.1 = (f32[11,5,8,128]{3,2,1,0:T(8,128)S(1)}, f32[11,5,8,128]{3,2,1,0:T(8,128)S(1)}, u32[]{:S(2)}, u32[]{:S(2)}) collective-permute-start(f32[11,5,8,128]{3,2,1,0:T(8,128)S(1)} %get-tuple-element.31), channel_id=1, source_target_pairs={{0,32},{1,33},{2,34},{3,35},{4,36},{5,37},{6,38},{7,39},{8,40},{9,... | collective-permute-start | bytes 675848 | tf_op jit(solution)/shard_map/ppermute | solution.py:400
  4.5 3.3 %collective-permute-start.3 = (f32[11,5,8,128]{3,2,1,0:T(8,128)S(1)}, f32[11,5,8,128]{3,2,1,0:T(8,128)S(1)}, u32[]{:S(2)}, u32[]{:S(2)}) collective-permute-start(f32[11,5,8,128]{3,2,1,0:T(8,128)S(1)} %get-tuple-element.32), channel_id=1, source_target_pairs={{0,64},{1,65},{2,66},{3,67},{4,68},{5,69},{6,70},{7,71},{8,72},{9,... | collective-permute-start | bytes 675848 | tf_op jit(solution)/shard_map/ppermute | solution.py:400
  7.8 0.0 collective-permute-start.5
  7.8 0.0 copy-done.1
  7.8 0.1 copy.5.slots
  7.9 3.0 %table.1 = (s32[64]{0:T(128)S(1)}, s32[88]{0:T(128)S(1)}, f32[11,5,8,128]{3,2,1,0:T(8,128)S(1)}) custom-call(s32[3]{0:T(128)S(1)} %pad_add_fusion.pos.refs_0_, s32[128,11]{1,0:T(8,128)S(1)} %copy.5.slots, f32[11,5,8,128]{3,2,1,0:T(8,128)S(1)} %get-tuple-element.27._tile), custom_call_target="tpu_custom_call", output_to_operand_aliasing={{2}: (2, {})} | custom-call | bytes 20000000 | tf_op jit(solution)/shard_map/table/pallas_call | solution.py:417
  10.9 1.3 %collective-permute-start = (f32[11,5,8,128]{3,2,1,0:T(8,128)S(1)}, f32[11,5,8,128]{3,2,1,0:T(8,128)S(1)}, u32[]{:S(2)}, u32[]{:S(2)}) collective-permute-start(f32[11,5,8,128]{3,2,1,0:T(8,128)S(1)} %get-tuple-element.30.refs_0_), channel_id=1, source_target_pairs={{0,16},{1,17},{2,18},{3,19},{4,20},{5,21},{6,22},{7,23},{8,24},{9,... | collective-permute-start | bytes 675848 | tf_op jit(solution)/shard_map/ppermute | solution.py:400
  12.2 0.0 collective-permute-done.1.refs_2_
  12.2 0.1 collective-permute-start.2
  12.3 5.3 %collective-permute-done.3.refs_4_ = f32[11,5,8,128]{3,2,1,0:T(8,128)S(1)} collective-permute-done((f32[11,5,8,128]{3,2,1,0:T(8,128)S(1)}, f32[11,5,8,128]{3,2,1,0:T(8,128)S(1)}, u32[]{:S(2)}, u32[]{:S(2)}) %collective-permute-start.3) | collective-permute-done | bytes 225312 | tf_op jit(solution)/shard_map/ppermute | solution.py:400
  17.6 1.6 %collective-permute-start.4 = (f32[11,5,8,128]{3,2,1,0:T(8,128)S(1)}, f32[11,5,8,128]{3,2,1,0:T(8,128)S(1)}, u32[]{:S(2)}, u32[]{:S(2)}) collective-permute-start(f32[11,5,8,128]{3,2,1,0:T(8,128)S(1)} %collective-permute-done.3.refs_4_), channel_id=1, source_target_pairs={{0,16},{1,17},{2,18},{3,19},{4,20},{5,21},{6,22},{7,23},{8,24},{9,... | collective-permute-start | bytes 675848 | tf_op jit(solution)/shard_map/ppermute | solution.py:400
  19.2 0.8 %collective-permute-done.5.refs_6_ = f32[11,5,8,128]{3,2,1,0:T(8,128)S(1)} collective-permute-done((f32[11,5,8,128]{3,2,1,0:T(8,128)S(1)}, f32[11,5,8,128]{3,2,1,0:T(8,128)S(1)}, u32[]{:S(2)}, u32[]{:S(2)}) %collective-permute-start.5) | collective-permute-done | bytes 225312 | tf_op jit(solution)/shard_map/ppermute | solution.py:400
  19.9 1.8 %collective-permute-start.6 = (f32[11,5,8,128]{3,2,1,0:T(8,128)S(1)}, f32[11,5,8,128]{3,2,1,0:T(8,128)S(1)}, u32[]{:S(2)}, u32[]{:S(2)}) collective-permute-start(f32[11,5,8,128]{3,2,1,0:T(8,128)S(1)} %collective-permute-done.5.refs_6_), channel_id=1, source_target_pairs={{0,16},{1,17},{2,18},{3,19},{4,20},{5,21},{6,22},{7,23},{8,24},{9,... | collective-permute-start | bytes 675848 | tf_op jit(solution)/shard_map/ppermute | solution.py:400
  21.8 0.0 collective-permute-done.refs_1_
  21.8 0.0 collective-permute-done.2.refs_3_
  21.8 0.0 collective-permute-done.4.refs_5_
  21.8 1.1 %collective-permute-done.6.refs_7_ = f32[11,5,8,128]{3,2,1,0:T(8,128)S(1)} collective-permute-done((f32[11,5,8,128]{3,2,1,0:T(8,128)S(1)}, f32[11,5,8,128]{3,2,1,0:T(8,128)S(1)}, u32[]{:S(2)}, u32[]{:S(2)}) %collective-permute-start.6) | collective-permute-done | bytes 225312 | tf_op jit(solution)/shard_map/ppermute | solution.py:400
  22.9 1.7 %reorder.1 = (f32[960,128]{1,0:T(8,128)S(1)}, f32[360,128]{1,0:T(8,128)S(1)}, f32[360,128]{1,0:T(8,128)S(1)}, f32[360,128]{1,0:T(8,128)S(1)}, f32[360,128]{1,0:T(8,128)S(1)}) custom-call(s32[3]{0:T(128)S(1)} %pad_add_fusion.pos.refs_0_, s32[88]{0:T(128)S(1)} %get-tuple-element.29.rows, f32[11,5,8,128]{3,2,1,0:T(8,128)S(1)} %get-tuple-element.30.refs_0_, ...), custom_call_target="tpu_custom_call" | custom-call | tf_op jit(solution)/shard_map/reorder/pallas_call | solution.py:439
  24.5 0.1 collective-permute-start.9
  24.6 7.8 %collective-permute-start.10 = (f32[360,128]{1,0:T(8,128)S(1)}, f32[360,128]{1,0:T(8,128)S(1)}, u32[]{:S(2)}, u32[]{:S(2)}) collective-permute-start(f32[360,128]{1,0:T(8,128)S(1)} %get-tuple-element.38), channel_id=1, source_target_pairs={{0,127},{1,112},{2,113},{3,114},{4,115},{5,116},{6,117},{7,118},{8... | collective-permute-start | bytes 552968 | tf_op jit(solution)/shard_map/ppermute | solution.py:400
  32.5 0.0 collective-permute-start.7
  32.5 1.7 %collective-permute-start.8 = (f32[360,128]{1,0:T(8,128)S(1)}, f32[360,128]{1,0:T(8,128)S(1)}, u32[]{:S(2)}, u32[]{:S(2)}) collective-permute-start(f32[360,128]{1,0:T(8,128)S(1)} %get-tuple-element.36), channel_id=1, source_target_pairs={{0,47},{1,32},{2,33},{3,34},{4,35},{5,36},{6,37},{7,38},{8,39},{9,... | collective-permute-start | bytes 552968 | tf_op jit(solution)/shard_map/ppermute | solution.py:400
  34.2 0.0 collective-permute-done.9.y_in
  34.2 2.7 %collective-permute-done.10.y_out = f32[360,128]{1,0:T(8,128)S(1)} collective-permute-done((f32[360,128]{1,0:T(8,128)S(1)}, f32[360,128]{1,0:T(8,128)S(1)}, u32[]{:S(2)}, u32[]{:S(2)}) %collective-permute-start.10) | collective-permute-done | bytes 184352 | tf_op jit(solution)/shard_map/ppermute | solution.py:400
  36.9 0.6 corners.1
  37.6 0.1 collective-permute-start.11
  37.7 4.8 %collective-permute-start.12 = (f32[120,128]{1,0:T(8,128)S(1)}, f32[120,128]{1,0:T(8,128)S(1)}, u32[]{:S(2)}, u32[]{:S(2)}) collective-permute-start(f32[120,128]{1,0:T(8,128)S(1)} %get-tuple-element.44), channel_id=1, source_target_pairs={{0,47},{1,32},{2,33},{3,34},{4,35},{5,36},{6,37},{7,38},{8,39},{9,... | collective-permute-start | bytes 184328 | tf_op jit(solution)/shard_map/ppermute | solution.py:400
  42.4 0.0 collective-permute-done.7.x_in
  42.5 0.6 collective-permute-done.8.x_out
  43.0 2.4 %begin.1 = (f32[1680,128]{1,0:T(8,128)S(1)}, f32[1680,128]{1,0:T(8,128)S(1)}, f32[1680,128]{1,0:T(8,128)S(1)}, f32[1680,128]{1,0:T(8,128)S(1)}) custom-call(s32[3]{0:T(128)S(1)} %pad_add_fusion.pos.refs_0_, f32[960,128]{1,0:T(8,128)S(1)} %get-tuple-element.34.cur, f32[360,128]{1,0:T(8,128)S(1)} %collective-permute-done.7.x_in, ...), custom_call_target="tpu_custom_call" | custom-call | bytes 10000000 | tf_op jit(solution)/shard_map/begin/pallas_call | solution.py:479
  45.4 0.0 collective-permute-done.11.c_in
  45.4 0.0 collective-permute-done.12.c_out
  45.4 6.1 %finish.1.mine = f32[24,5,8,128]{3,2,1,0:T(8,128)S(1)} custom-call(s32[3]{0:T(128)S(1)} %pad_add_fusion.pos.refs_0_, f32[1680,128]{1,0:T(8,128)S(1)} %get-tuple-element.39.main, f32[1680,128]{1,0:T(8,128)S(1)} %get-tuple-element.40.side_rows, f32[1680,128]{1,0:T(8,128)S(1)} %get-tuple-element.41.early_main, f32[1680,128]{1,0:T(8,128)S(1)} %get-tuple-element.42.early_side, ...), custom_call_target="tpu_custom_call" | custom-call | tf_op jit(solution)/shard_map/finish/pallas_call | solution.py:488
  51.5 1.3 %collective-permute-start.13 = (f32[24,5,8,128]{3,2,1,0:T(8,128)S(1)}, f32[24,5,8,128]{3,2,1,0:T(8,128)S(1)}, u32[]{:S(2)}, u32[]{:S(2)}) collective-permute-start(f32[24,5,8,128]{3,2,1,0:T(8,128)S(1)} %finish.1.mine), channel_id=1, source_target_pairs={{0,16},{1,17},{2,18},{3,19},{4,20},{5,21},{6,22},{7,23},{8,24},{9,... | collective-permute-start | bytes 1474568 | tf_op jit(solution)/shard_map/ppermute | solution.py:400
  52.8 1.5 %collective-permute-done.13.other = f32[24,5,8,128]{3,2,1,0:T(8,128)S(1)} collective-permute-done((f32[24,5,8,128]{3,2,1,0:T(8,128)S(1)}, f32[24,5,8,128]{3,2,1,0:T(8,128)S(1)}, u32[]{:S(2)}, u32[]{:S(2)}) %collective-permute-start.13) | collective-permute-done | bytes 491552 | tf_op jit(solution)/shard_map/ppermute | solution.py:400
  54.3 0.7 pack_out.1
  54.9 0.1 collective-permute-start.15
  55.0 3.5 %collective-permute-start.16 = (f32[7,5,8,128]{3,2,1,0:T(8,128)S(1)}, f32[7,5,8,128]{3,2,1,0:T(8,128)S(1)}, u32[]{:S(2)}, u32[]{:S(2)}) collective-permute-start(f32[7,5,8,128]{3,2,1,0:T(8,128)S(1)} %get-tuple-element.48), channel_id=1, source_target_pairs={{0,96},{1,97},{2,98},{3,99},{4,100},{5,101},{6,102},{7,103},{8,104... | collective-permute-start | bytes 430088 | tf_op jit(solution)/shard_map/ppermute | solution.py:400
  58.6 1.1 %collective-permute-start.14 = (f32[7,5,8,128]{3,2,1,0:T(8,128)S(1)}, f32[7,5,8,128]{3,2,1,0:T(8,128)S(1)}, u32[]{:S(2)}, u32[]{:S(2)}) collective-permute-start(f32[7,5,8,128]{3,2,1,0:T(8,128)S(1)} %get-tuple-element.45), channel_id=1, source_target_pairs={{0,64},{1,65},{2,66},{3,67},{4,68},{5,69},{6,70},{7,71},{8,72},{9,... | collective-permute-start | bytes 430088 | tf_op jit(solution)/shard_map/ppermute | solution.py:400
  59.7 0.3 collective-permute-done.15.refs_2_
  60.0 4.5 %collective-permute-done.16.refs_3_ = f32[7,5,8,128]{3,2,1,0:T(8,128)S(1)} collective-permute-done((f32[7,5,8,128]{3,2,1,0:T(8,128)S(1)}, f32[7,5,8,128]{3,2,1,0:T(8,128)S(1)}, u32[]{:S(2)}, u32[]{:S(2)}) %collective-permute-start.16) | collective-permute-done | bytes 143392 | tf_op jit(solution)/shard_map/ppermute | solution.py:400
  64.5 1.3 %unpack_out.2.refs_2_ = f32[7,5,16,256]{3,2,1,0:T(8,128)} custom-call(s32[3]{0:T(128)S(1)} %pad_add_fusion.pos.refs_0_, f32[7,5,8,128]{3,2,1,0:T(8,128)S(1)} %get-tuple-element.46.refs_1_, f32[7,5,8,128]{3,2,1,0:T(8,128)S(1)} %collective-permute-done.15.refs_2_, f32[7,5,8,128]{3,2,1,0:T(8,128)S(1)} %collective-permute-done.16.refs_3_), custom_call_target="tpu_custom_call" | custom-call | tf_op jit(solution)/shard_map/unpack_out/pallas_call | solution.py:511
  65.9 0.3 collective-permute-done.14.refs_1_
  66.2 1.2 %unpack_out.3 = f32[7,5,16,256]{3,2,1,0:T(8,128)} custom-call(s32[3]{0:T(128)S(1)} %pad_add_fusion.pos.refs_0_, f32[7,5,8,128]{3,2,1,0:T(8,128)S(1)} %collective-permute-done.14.refs_1_, f32[7,5,16,256]{3,2,1,0:T(8,128)} %unpack_out.2.refs_2_), custom_call_target="tpu_custom_call", output_to_operand_aliasing={{}: (2, {})} | custom-call | tf_op jit(solution)/shard_map/unpack_out/pallas_call | solution.py:511
Async XLA Ops:
  0.1 1.2 %copy-start = (f32[11,5,16,256]{3,2,1,0:T(8,128)S(1)}, f32[11,5,16,256]{3,2,1,0:T(8,128)}, u32[]{:S(2)}) copy-start(f32[11,5,16,256]{3,2,1,0:T(8,128)} %cells.1) | copy-start | bytes 2703364
  1.3 6.5 %copy-start.1 = (s32[128,11]{0,1:T(8,128)S(1)}, s32[128,11]{0,1:T(8,128)}, u32[]{:S(2)}) copy-start(s32[128,11]{0,1:T(8,128)} %param.3) | copy-start | bytes 16900
  1.9 10.3 %collective-permute-start.1 = (f32[11,5,8,128]{3,2,1,0:T(8,128)S(1)}, f32[11,5,8,128]{3,2,1,0:T(8,128)S(1)}, u32[]{:S(2)}, u32[]{:S(2)}) collective-permute-start(f32[11,5,8,128]{3,2,1,0:T(8,128)S(1)} %get-tuple-element.31), channel_id=1, source_target_pairs={{0,32},{1,33},{2,34},{3,35},{4,36},{5,37},{6,38},{7,39},{8,40},{9,... | collective-permute-start | bytes 675848 | tf_op jit(solution)/shard_map/ppermute | solution.py:400
  4.5 13.1 %collective-permute-start.3 = (f32[11,5,8,128]{3,2,1,0:T(8,128)S(1)}, f32[11,5,8,128]{3,2,1,0:T(8,128)S(1)}, u32[]{:S(2)}, u32[]{:S(2)}) collective-permute-start(f32[11,5,8,128]{3,2,1,0:T(8,128)S(1)} %get-tuple-element.32), channel_id=1, source_target_pairs={{0,64},{1,65},{2,66},{3,67},{4,68},{5,69},{6,70},{7,71},{8,72},{9,... | collective-permute-start | bytes 675848 | tf_op jit(solution)/shard_map/ppermute | solution.py:400
  7.8 12.2 %collective-permute-start.5 = (f32[11,5,8,128]{3,2,1,0:T(8,128)S(1)}, f32[11,5,8,128]{3,2,1,0:T(8,128)S(1)}, u32[]{:S(2)}, u32[]{:S(2)}) collective-permute-start(f32[11,5,8,128]{3,2,1,0:T(8,128)S(1)} %get-tuple-element.33), channel_id=1, source_target_pairs={{0,96},{1,97},{2,98},{3,99},{4,100},{5,101},{6,102},{7,103},{8,104... | collective-permute-start | bytes 675848 | tf_op jit(solution)/shard_map/ppermute | solution.py:400
  10.9 10.9 %collective-permute-start = (f32[11,5,8,128]{3,2,1,0:T(8,128)S(1)}, f32[11,5,8,128]{3,2,1,0:T(8,128)S(1)}, u32[]{:S(2)}, u32[]{:S(2)}) collective-permute-start(f32[11,5,8,128]{3,2,1,0:T(8,128)S(1)} %get-tuple-element.30.refs_0_), channel_id=1, source_target_pairs={{0,16},{1,17},{2,18},{3,19},{4,20},{5,21},{6,22},{7,23},{8,24},{9,... | collective-permute-start | bytes 675848 | tf_op jit(solution)/shard_map/ppermute | solution.py:400
  12.2 9.5 %collective-permute-start.2 = (f32[11,5,8,128]{3,2,1,0:T(8,128)S(1)}, f32[11,5,8,128]{3,2,1,0:T(8,128)S(1)}, u32[]{:S(2)}, u32[]{:S(2)}) collective-permute-start(f32[11,5,8,128]{3,2,1,0:T(8,128)S(1)} %collective-permute-done.1.refs_2_), channel_id=1, source_target_pairs={{0,16},{1,17},{2,18},{3,19},{4,20},{5,21},{6,22},{7,23},{8,24},{9,... | collective-permute-start | bytes 675848 | tf_op jit(solution)/shard_map/ppermute | solution.py:400
  17.6 4.2 %collective-permute-start.4 = (f32[11,5,8,128]{3,2,1,0:T(8,128)S(1)}, f32[11,5,8,128]{3,2,1,0:T(8,128)S(1)}, u32[]{:S(2)}, u32[]{:S(2)}) collective-permute-start(f32[11,5,8,128]{3,2,1,0:T(8,128)S(1)} %collective-permute-done.3.refs_4_), channel_id=1, source_target_pairs={{0,16},{1,17},{2,18},{3,19},{4,20},{5,21},{6,22},{7,23},{8,24},{9,... | collective-permute-start | bytes 675848 | tf_op jit(solution)/shard_map/ppermute | solution.py:400
  19.9 2.9 %collective-permute-start.6 = (f32[11,5,8,128]{3,2,1,0:T(8,128)S(1)}, f32[11,5,8,128]{3,2,1,0:T(8,128)S(1)}, u32[]{:S(2)}, u32[]{:S(2)}) collective-permute-start(f32[11,5,8,128]{3,2,1,0:T(8,128)S(1)} %collective-permute-done.5.refs_6_), channel_id=1, source_target_pairs={{0,16},{1,17},{2,18},{3,19},{4,20},{5,21},{6,22},{7,23},{8,24},{9,... | collective-permute-start | bytes 675848 | tf_op jit(solution)/shard_map/ppermute | solution.py:400
  24.5 9.7 %collective-permute-start.9 = (f32[360,128]{1,0:T(8,128)S(1)}, f32[360,128]{1,0:T(8,128)S(1)}, u32[]{:S(2)}, u32[]{:S(2)}) collective-permute-start(f32[360,128]{1,0:T(8,128)S(1)} %get-tuple-element.37), channel_id=1, source_target_pairs={{0,96},{1,97},{2,98},{3,99},{4,100},{5,101},{6,102},{7,103},{8,104... | collective-permute-start | bytes 552968 | tf_op jit(solution)/shard_map/ppermute | solution.py:400
  24.6 12.3 %collective-permute-start.10 = (f32[360,128]{1,0:T(8,128)S(1)}, f32[360,128]{1,0:T(8,128)S(1)}, u32[]{:S(2)}, u32[]{:S(2)}) collective-permute-start(f32[360,128]{1,0:T(8,128)S(1)} %get-tuple-element.38), channel_id=1, source_target_pairs={{0,127},{1,112},{2,113},{3,114},{4,115},{5,116},{6,117},{7,118},{8... | collective-permute-start | bytes 552968 | tf_op jit(solution)/shard_map/ppermute | solution.py:400
  32.5 10.0 %collective-permute-start.7 = (f32[360,128]{1,0:T(8,128)S(1)}, f32[360,128]{1,0:T(8,128)S(1)}, u32[]{:S(2)}, u32[]{:S(2)}) collective-permute-start(f32[360,128]{1,0:T(8,128)S(1)} %get-tuple-element.35), channel_id=1, source_target_pairs={{0,32},{1,33},{2,34},{3,35},{4,36},{5,37},{6,38},{7,39},{8,40},{9,... | collective-permute-start | bytes 552968 | tf_op jit(solution)/shard_map/ppermute | solution.py:400
  32.5 10.6 %collective-permute-start.8 = (f32[360,128]{1,0:T(8,128)S(1)}, f32[360,128]{1,0:T(8,128)S(1)}, u32[]{:S(2)}, u32[]{:S(2)}) collective-permute-start(f32[360,128]{1,0:T(8,128)S(1)} %get-tuple-element.36), channel_id=1, source_target_pairs={{0,47},{1,32},{2,33},{3,34},{4,35},{5,36},{6,37},{7,38},{8,39},{9,... | collective-permute-start | bytes 552968 | tf_op jit(solution)/shard_map/ppermute | solution.py:400
  37.6 7.9 %collective-permute-start.11 = (f32[120,128]{1,0:T(8,128)S(1)}, f32[120,128]{1,0:T(8,128)S(1)}, u32[]{:S(2)}, u32[]{:S(2)}) collective-permute-start(f32[120,128]{1,0:T(8,128)S(1)} %get-tuple-element.43), channel_id=1, source_target_pairs={{0,32},{1,33},{2,34},{3,35},{4,36},{5,37},{6,38},{7,39},{8,40},{9,... | collective-permute-start | bytes 184328 | tf_op jit(solution)/shard_map/ppermute | solution.py:400
  37.7 7.8 %collective-permute-start.12 = (f32[120,128]{1,0:T(8,128)S(1)}, f32[120,128]{1,0:T(8,128)S(1)}, u32[]{:S(2)}, u32[]{:S(2)}) collective-permute-start(f32[120,128]{1,0:T(8,128)S(1)} %get-tuple-element.44), channel_id=1, source_target_pairs={{0,47},{1,32},{2,33},{3,34},{4,35},{5,36},{6,37},{7,38},{8,39},{9,... | collective-permute-start | bytes 184328 | tf_op jit(solution)/shard_map/ppermute | solution.py:400
  51.5 2.7 %collective-permute-start.13 = (f32[24,5,8,128]{3,2,1,0:T(8,128)S(1)}, f32[24,5,8,128]{3,2,1,0:T(8,128)S(1)}, u32[]{:S(2)}, u32[]{:S(2)}) collective-permute-start(f32[24,5,8,128]{3,2,1,0:T(8,128)S(1)} %finish.1.mine), channel_id=1, source_target_pairs={{0,16},{1,17},{2,18},{3,19},{4,20},{5,21},{6,22},{7,23},{8,24},{9,... | collective-permute-start | bytes 1474568 | tf_op jit(solution)/shard_map/ppermute | solution.py:400
  54.9 5.1 %collective-permute-start.15 = (f32[7,5,8,128]{3,2,1,0:T(8,128)S(1)}, f32[7,5,8,128]{3,2,1,0:T(8,128)S(1)}, u32[]{:S(2)}, u32[]{:S(2)}) collective-permute-start(f32[7,5,8,128]{3,2,1,0:T(8,128)S(1)} %get-tuple-element.47), channel_id=1, source_target_pairs={{0,32},{1,33},{2,34},{3,35},{4,36},{5,37},{6,38},{7,39},{8,40},{9,... | collective-permute-start | bytes 430088 | tf_op jit(solution)/shard_map/ppermute | solution.py:400
  55.0 9.5 %collective-permute-start.16 = (f32[7,5,8,128]{3,2,1,0:T(8,128)S(1)}, f32[7,5,8,128]{3,2,1,0:T(8,128)S(1)}, u32[]{:S(2)}, u32[]{:S(2)}) collective-permute-start(f32[7,5,8,128]{3,2,1,0:T(8,128)S(1)} %get-tuple-element.48), channel_id=1, source_target_pairs={{0,96},{1,97},{2,98},{3,99},{4,100},{5,101},{6,102},{7,103},{8,104... | collective-permute-start | bytes 430088 | tf_op jit(solution)/shard_map/ppermute | solution.py:400
  58.6 7.7 %collective-permute-start.14 = (f32[7,5,8,128]{3,2,1,0:T(8,128)S(1)}, f32[7,5,8,128]{3,2,1,0:T(8,128)S(1)}, u32[]{:S(2)}, u32[]{:S(2)}) collective-permute-start(f32[7,5,8,128]{3,2,1,0:T(8,128)S(1)} %get-tuple-element.45), channel_id=1, source_target_pairs={{0,64},{1,65},{2,66},{3,67},{4,68},{5,69},{6,70},{7,71},{8,72},{9,... | collective-permute-start | bytes 430088 | tf_op jit(solution)/shard_map/ppermute | solution.py:400

commit v8 on v7

--- a/solution.py
+++ b/solution.py
@@ -209,7 +209,7 @@
                 y_out[strip_at(f, t, group), :] = jnp.where(turn, jnp.where(first, low, high), v)
 
 
-def corners(pos, y_in, y_out, to_in, to_out):
+def corners(pos, y_out, y_in, to_in, to_out):
     zx, zy = tile_x(pos[0]), tile_y(pos[0])
 
     def copy(low, high):
@@ -352,13 +352,13 @@
 EARLY_SIDE = range(1, Y - 1)
 
 
-def begin(pos, cur, x_in, x_out, y_in, y_out, main, side_rows, first_main, first_side):
+def begin(pos, cur, y_out, y_in, x_out, x_in, main, side_rows, first_main, first_side):
     widen(pos, cur, x_in, x_out, y_in, y_out, main, side_rows)
     initial, first = (main, side_rows), (first_main, first_side)
     advance(0, lambda part, y: initial[part], None, lambda part, y: first[part], EARLY_MAIN, EARLY_SIDE)
 
 
-def finish(pos, main, side_rows, early_main, early_side, c_in, c_out, made, corner_rows, *held):
+def finish(pos, main, side_rows, early_main, early_side, c_out, c_in, made, corner_rows, *held):
     late, second = held[0:2], held[2:4]
     add_corners(pos, c_in, c_out, corner_rows)
 
@@ -453,16 +453,12 @@
         return z ^ 3
 
     def over_x(inner, outer):
-        return (
-            to(inner, lambda z, core, c: (x_partner(z), core, c)),
-            to(outer, lambda z, core, c: (x_partner(z), core, c + 2 * tile_x(z) - 1)),
-        )
+        outer = to(outer, lambda z, core, c: (x_partner(z), core, c + 2 * tile_x(z) - 1))
+        return to(inner, lambda z, core, c: (x_partner(z), core, c)), outer
 
     def over_y(inner, outer):
-        return (
-            to(inner, lambda z, core, c: (y_partner(z), core, c)),
-            to(outer, lambda z, core, c: (y_partner(z), 1 - core, c + 2 * tile_y(z) - 1)),
-        )
+        outer = to(outer, lambda z, core, c: (y_partner(z), 1 - core, c + 2 * tile_y(z) - 1))
+        return to(inner, lambda z, core, c: (y_partner(z), core, c)), outer
 
     y_layers = over_y(y_in, y_out)
     x_layers = over_x(x_in, x_out)
@@ -473,7 +469,7 @@
         out_specs=[VMEM] * 2,
         compiler_params=PARAMS,
         name="corners",
-    )(pos, *y_layers)
+    )(pos, *y_layers[::-1])
     corner_cells = over_x(*corner_cells)
     wide = [F * WIDE * HALF, L]
     early = pl.pallas_call(
@@ -484,7 +480,7 @@
         compiler_params=PARAMS,
         cost_estimate=pl.CostEstimate(flops=0, bytes_accessed=10_000_000, transcendentals=0),
         name="begin",
-    )(pos, initial, *x_layers, *y_layers)
+    )(pos, initial, *y_layers[::-1], *x_layers[::-1])
     current = pl.pallas_call(
         finish,
         out_shape=shape(HALF, F, X, L),
@@ -493,7 +489,7 @@
         scratch_shapes=[pltpu.VMEM(wide, jnp.float32)] * 5,
         compiler_params=PARAMS,
         name="finish",
-    )(pos, *early, *corner_cells)
+    )(pos, *early, *corner_cells[::-1])
 
     leaving = pl.pallas_call(
         pack_out,

time: 68.6 us -> 71.1 us (1.036); the launches traced: 67.5 us -> 70.9 us
  waiting for transfers between devices: 17.2 us -> 29.6 us
  starting transfers between devices: 31.2 us -> 22.2 us
    ppermute x17, waiting for transfers between devices: 17.2 us -> 29.6 us  [to(): return lax.ppermute(array, ('row', 'col'), pairs)]
    ppermute x17, starting transfers between devices: 31.2 us -> 22.2 us  [to(): return lax.ppermute(array, ('row', 'col'), pairs)]
  transfers between devices with their start and end apart: 17 -> 17, of which waited for: 9 -> 9; matrix products, arithmetic and copies ran while one was open for 0% -> 0% of each run, Pallas kernels for 11% -> 10%
where the time goes in v8:
time: 71.1 us; the launch traced here: 70.9 us
  waiting for transfers between devices  29.6 us (42%)
  starting transfers between devices  22.2 us (31%)
  Pallas kernels  17.7 us (25%)
  local copies, waits for them, and re-layouts  1.29 us (2%)
    ppermute x17, waiting for transfers between devices, to(): return lax.ppermute(array, ('row', 'col'), pairs)  29.6 us
    ppermute x17, starting transfers between devices, to(): return lax.ppermute(array, ('row', 'col'), pairs)  22.2 us
    pallas_call x1, Pallas kernels, body(): pl.pallas_call(finish, out_shape=shape(HALF, F, X, L), in_specs=[SMEM] +...  6.07 us
    pallas_call x1, Pallas kernels, body(): pl.pallas_call(table, out_shape=[jax.ShapeDtypeStruct((N_ROW * 8,), jnp.i...  3.01 us
    pallas_call x2, Pallas kernels, body(): pl.pallas_call(lambda *refs, which=which: unpack_out(which, *refs), out_s...  2.57 us
    pallas_call x1, Pallas kernels, body(): pl.pallas_call(begin, out_shape=[shape(*wide)] * 4, in_specs=[SMEM] + [VM...  2.39 us
    pallas_call x1, Pallas kernels, body(): pl.pallas_call(reorder, out_shape=[whole] + [layer] * 4, in_specs=[SMEM,...  1.66 us
  transfers between devices with their start and end apart: 17, of which 9 were waited for; matrix products, arithmetic and copies ran while one was open for 0% of the time, Pallas kernels for 10%

profile of v8, /device:TPU:1, one launch (start us, length us, event | category | flops | bytes accessed | tf_op | source)
XLA Modules:
  0.0 70.9 jit_solution(501425712912291321)
XLA Ops:
  0.0 0.1 pad_add_fusion.pos.refs_0_
  0.1 0.0 copy-start
  0.1 1.2 %copy-done = f32[11,5,16,256]{3,2,1,0:T(8,128)S(1)} copy-done((f32[11,5,16,256]{3,2,1,0:T(8,128)S(1)}, f32[11,5,16,256]{3,2,1,0:T(8,128)}, u32[]{:S(2)}) %copy-start) | copy-done | bytes 901144
  1.3 0.0 copy-start.1
  1.3 0.7 pack_in.1
  1.9 2.5 %collective-permute-start.1 = (f32[11,5,8,128]{3,2,1,0:T(8,128)S(1)}, f32[11,5,8,128]{3,2,1,0:T(8,128)S(1)}, u32[]{:S(2)}, u32[]{:S(2)}) collective-permute-start(f32[11,5,8,128]{3,2,1,0:T(8,128)S(1)} %get-tuple-element.31), channel_id=1, source_target_pairs={{0,32},{1,33},{2,34},{3,35},{4,36},{5,37},{6,38},{7,39},{8,40},{9,... | collective-permute-start | bytes 675848 | tf_op jit(solution)/shard_map/ppermute | solution.py:400
  4.5 3.3 %collective-permute-start.3 = (f32[11,5,8,128]{3,2,1,0:T(8,128)S(1)}, f32[11,5,8,128]{3,2,1,0:T(8,128)S(1)}, u32[]{:S(2)}, u32[]{:S(2)}) collective-permute-start(f32[11,5,8,128]{3,2,1,0:T(8,128)S(1)} %get-tuple-element.32), channel_id=1, source_target_pairs={{0,64},{1,65},{2,66},{3,67},{4,68},{5,69},{6,70},{7,71},{8,72},{9,... | collective-permute-start | bytes 675848 | tf_op jit(solution)/shard_map/ppermute | solution.py:400
  7.8 0.0 collective-permute-start.5
  7.8 0.0 copy-done.1
  7.8 0.1 copy.5.slots
  7.9 3.0 %table.1 = (s32[64]{0:T(128)S(1)}, s32[88]{0:T(128)S(1)}, f32[11,5,8,128]{3,2,1,0:T(8,128)S(1)}) custom-call(s32[3]{0:T(128)S(1)} %pad_add_fusion.pos.refs_0_, s32[128,11]{1,0:T(8,128)S(1)} %copy.5.slots, f32[11,5,8,128]{3,2,1,0:T(8,128)S(1)} %get-tuple-element.27._tile), custom_call_target="tpu_custom_call", output_to_operand_aliasing={{2}: (2, {})} | custom-call | bytes 20000000 | tf_op jit(solution)/shard_map/table/pallas_call | solution.py:417
  10.9 1.3 %collective-permute-start = (f32[11,5,8,128]{3,2,1,0:T(8,128)S(1)}, f32[11,5,8,128]{3,2,1,0:T(8,128)S(1)}, u32[]{:S(2)}, u32[]{:S(2)}) collective-permute-start(f32[11,5,8,128]{3,2,1,0:T(8,128)S(1)} %get-tuple-element.30.refs_0_), channel_id=1, source_target_pairs={{0,16},{1,17},{2,18},{3,19},{4,20},{5,21},{6,22},{7,23},{8,24},{9,... | collective-permute-start | bytes 675848 | tf_op jit(solution)/shard_map/ppermute | solution.py:400
  12.2 0.0 collective-permute-done.1.refs_2_
  12.2 0.1 collective-permute-start.2
  12.3 5.2 %collective-permute-done.3.refs_4_ = f32[11,5,8,128]{3,2,1,0:T(8,128)S(1)} collective-permute-done((f32[11,5,8,128]{3,2,1,0:T(8,128)S(1)}, f32[11,5,8,128]{3,2,1,0:T(8,128)S(1)}, u32[]{:S(2)}, u32[]{:S(2)}) %collective-permute-start.3) | collective-permute-done | bytes 225312 | tf_op jit(solution)/shard_map/ppermute | solution.py:400
  17.6 1.6 %collective-permute-start.4 = (f32[11,5,8,128]{3,2,1,0:T(8,128)S(1)}, f32[11,5,8,128]{3,2,1,0:T(8,128)S(1)}, u32[]{:S(2)}, u32[]{:S(2)}) collective-permute-start(f32[11,5,8,128]{3,2,1,0:T(8,128)S(1)} %collective-permute-done.3.refs_4_), channel_id=1, source_target_pairs={{0,16},{1,17},{2,18},{3,19},{4,20},{5,21},{6,22},{7,23},{8,24},{9,... | collective-permute-start | bytes 675848 | tf_op jit(solution)/shard_map/ppermute | solution.py:400
  19.2 0.8 %collective-permute-done.5.refs_6_ = f32[11,5,8,128]{3,2,1,0:T(8,128)S(1)} collective-permute-done((f32[11,5,8,128]{3,2,1,0:T(8,128)S(1)}, f32[11,5,8,128]{3,2,1,0:T(8,128)S(1)}, u32[]{:S(2)}, u32[]{:S(2)}) %collective-permute-start.5) | collective-permute-done | bytes 225312 | tf_op jit(solution)/shard_map/ppermute | solution.py:400
  19.9 1.8 %collective-permute-start.6 = (f32[11,5,8,128]{3,2,1,0:T(8,128)S(1)}, f32[11,5,8,128]{3,2,1,0:T(8,128)S(1)}, u32[]{:S(2)}, u32[]{:S(2)}) collective-permute-start(f32[11,5,8,128]{3,2,1,0:T(8,128)S(1)} %collective-permute-done.5.refs_6_), channel_id=1, source_target_pairs={{0,16},{1,17},{2,18},{3,19},{4,20},{5,21},{6,22},{7,23},{8,24},{9,... | collective-permute-start | bytes 675848 | tf_op jit(solution)/shard_map/ppermute | solution.py:400
  21.8 0.0 collective-permute-done.refs_1_
  21.8 0.0 collective-permute-done.2.refs_3_
  21.8 0.0 collective-permute-done.4.refs_5_
  21.8 1.1 %collective-permute-done.6.refs_7_ = f32[11,5,8,128]{3,2,1,0:T(8,128)S(1)} collective-permute-done((f32[11,5,8,128]{3,2,1,0:T(8,128)S(1)}, f32[11,5,8,128]{3,2,1,0:T(8,128)S(1)}, u32[]{:S(2)}, u32[]{:S(2)}) %collective-permute-start.6) | collective-permute-done | bytes 225312 | tf_op jit(solution)/shard_map/ppermute | solution.py:400
  22.9 1.7 %reorder.1 = (f32[960,128]{1,0:T(8,128)S(1)}, f32[360,128]{1,0:T(8,128)S(1)}, f32[360,128]{1,0:T(8,128)S(1)}, f32[360,128]{1,0:T(8,128)S(1)}, f32[360,128]{1,0:T(8,128)S(1)}) custom-call(s32[3]{0:T(128)S(1)} %pad_add_fusion.pos.refs_0_, s32[88]{0:T(128)S(1)} %get-tuple-element.29.rows, f32[11,5,8,128]{3,2,1,0:T(8,128)S(1)} %get-tuple-element.30.refs_0_, ...), custom_call_target="tpu_custom_call" | custom-call | tf_op jit(solution)/shard_map/reorder/pallas_call | solution.py:439
  24.5 5.0 %collective-permute-start.7 = (f32[360,128]{1,0:T(8,128)S(1)}, f32[360,128]{1,0:T(8,128)S(1)}, u32[]{:S(2)}, u32[]{:S(2)}) collective-permute-start(f32[360,128]{1,0:T(8,128)S(1)} %get-tuple-element.35), channel_id=1, source_target_pairs={{0,127},{1,112},{2,113},{3,114},{4,115},{5,116},{6,117},{7,118},{8... | collective-permute-start | bytes 552968 | tf_op jit(solution)/shard_map/ppermute | solution.py:400
  29.5 0.0 collective-permute-start.8
  29.5 0.0 collective-permute-start.9
  29.5 1.3 %collective-permute-start.10 = (f32[360,128]{1,0:T(8,128)S(1)}, f32[360,128]{1,0:T(8,128)S(1)}, u32[]{:S(2)}, u32[]{:S(2)}) collective-permute-start(f32[360,128]{1,0:T(8,128)S(1)} %get-tuple-element.38), channel_id=1, source_target_pairs={{0,32},{1,33},{2,34},{3,35},{4,36},{5,37},{6,38},{7,39},{8,40},{9,... | collective-permute-start | bytes 552968 | tf_op jit(solution)/shard_map/ppermute | solution.py:400
  30.9 5.9 %collective-permute-done.7.y_out = f32[360,128]{1,0:T(8,128)S(1)} collective-permute-done((f32[360,128]{1,0:T(8,128)S(1)}, f32[360,128]{1,0:T(8,128)S(1)}, u32[]{:S(2)}, u32[]{:S(2)}) %collective-permute-start.7) | collective-permute-done | bytes 184352 | tf_op jit(solution)/shard_map/ppermute | solution.py:400
  36.8 4.1 %collective-permute-done.8.y_in = f32[360,128]{1,0:T(8,128)S(1)} collective-permute-done((f32[360,128]{1,0:T(8,128)S(1)}, f32[360,128]{1,0:T(8,128)S(1)}, u32[]{:S(2)}, u32[]{:S(2)}) %collective-permute-start.8) | collective-permute-done | bytes 184352 | tf_op jit(solution)/shard_map/ppermute | solution.py:400
  40.8 0.6 corners.1
  41.5 0.1 collective-permute-start.11
  41.6 0.1 collective-permute-start.12
  41.7 0.0 collective-permute-done.9.x_out
  41.7 0.0 collective-permute-done.10.x_in
  41.7 2.4 %begin.1 = (f32[1680,128]{1,0:T(8,128)S(1)}, f32[1680,128]{1,0:T(8,128)S(1)}, f32[1680,128]{1,0:T(8,128)S(1)}, f32[1680,128]{1,0:T(8,128)S(1)}) custom-call(s32[3]{0:T(128)S(1)} %pad_add_fusion.pos.refs_0_, f32[960,128]{1,0:T(8,128)S(1)} %get-tuple-element.34.cur, f32[360,128]{1,0:T(8,128)S(1)} %collective-permute-done.7.y_out, ...), custom_call_target="tpu_custom_call" | custom-call | bytes 10000000 | tf_op jit(solution)/shard_map/begin/pallas_call | solution.py:475
  44.1 4.8 %collective-permute-done.11.c_out = f32[120,128]{1,0:T(8,128)S(1)} collective-permute-done((f32[120,128]{1,0:T(8,128)S(1)}, f32[120,128]{1,0:T(8,128)S(1)}, u32[]{:S(2)}, u32[]{:S(2)}) %collective-permute-start.11) | collective-permute-done | bytes 61472 | tf_op jit(solution)/shard_map/ppermute | solution.py:400
  48.8 0.0 collective-permute-done.12.c_in
  48.9 6.1 %finish.1.mine = f32[24,5,8,128]{3,2,1,0:T(8,128)S(1)} custom-call(s32[3]{0:T(128)S(1)} %pad_add_fusion.pos.refs_0_, f32[1680,128]{1,0:T(8,128)S(1)} %get-tuple-element.39.main, f32[1680,128]{1,0:T(8,128)S(1)} %get-tuple-element.40.side_rows, f32[1680,128]{1,0:T(8,128)S(1)} %get-tuple-element.41.early_main, f32[1680,128]{1,0:T(8,128)S(1)} %get-tuple-element.42.early_side, ...), custom_call_target="tpu_custom_call" | custom-call | tf_op jit(solution)/shard_map/finish/pallas_call | solution.py:484
  54.9 1.7 %collective-permute-start.13 = (f32[24,5,8,128]{3,2,1,0:T(8,128)S(1)}, f32[24,5,8,128]{3,2,1,0:T(8,128)S(1)}, u32[]{:S(2)}, u32[]{:S(2)}) collective-permute-start(f32[24,5,8,128]{3,2,1,0:T(8,128)S(1)} %finish.1.mine), channel_id=1, source_target_pairs={{0,16},{1,17},{2,18},{3,19},{4,20},{5,21},{6,22},{7,23},{8,24},{9,... | collective-permute-start | bytes 1474568 | tf_op jit(solution)/shard_map/ppermute | solution.py:400
  56.6 1.5 %collective-permute-done.13.other = f32[24,5,8,128]{3,2,1,0:T(8,128)S(1)} collective-permute-done((f32[24,5,8,128]{3,2,1,0:T(8,128)S(1)}, f32[24,5,8,128]{3,2,1,0:T(8,128)S(1)}, u32[]{:S(2)}, u32[]{:S(2)}) %collective-permute-start.13) | collective-permute-done | bytes 491552 | tf_op jit(solution)/shard_map/ppermute | solution.py:400
  58.1 0.7 pack_out.1
  58.8 0.1 collective-permute-start.15
  58.9 0.1 collective-permute-start.16
  59.0 3.1 %collective-permute-start.14 = (f32[7,5,8,128]{3,2,1,0:T(8,128)S(1)}, f32[7,5,8,128]{3,2,1,0:T(8,128)S(1)}, u32[]{:S(2)}, u32[]{:S(2)}) collective-permute-start(f32[7,5,8,128]{3,2,1,0:T(8,128)S(1)} %get-tuple-element.45), channel_id=1, source_target_pairs={{0,64},{1,65},{2,66},{3,67},{4,68},{5,69},{6,70},{7,71},{8,72},{9,... | collective-permute-start | bytes 430088 | tf_op jit(solution)/shard_map/ppermute | solution.py:400
  62.1 1.7 %collective-permute-done.15.refs_2_ = f32[7,5,8,128]{3,2,1,0:T(8,128)S(1)} collective-permute-done((f32[7,5,8,128]{3,2,1,0:T(8,128)S(1)}, f32[7,5,8,128]{3,2,1,0:T(8,128)S(1)}, u32[]{:S(2)}, u32[]{:S(2)}) %collective-permute-start.15) | collective-permute-done | bytes 143392 | tf_op jit(solution)/shard_map/ppermute | solution.py:400
  63.8 4.5 %collective-permute-done.16.refs_3_ = f32[7,5,8,128]{3,2,1,0:T(8,128)S(1)} collective-permute-done((f32[7,5,8,128]{3,2,1,0:T(8,128)S(1)}, f32[7,5,8,128]{3,2,1,0:T(8,128)S(1)}, u32[]{:S(2)}, u32[]{:S(2)}) %collective-permute-start.16) | collective-permute-done | bytes 143392 | tf_op jit(solution)/shard_map/ppermute | solution.py:400
  68.3 1.3 %unpack_out.2.refs_2_ = f32[7,5,16,256]{3,2,1,0:T(8,128)} custom-call(s32[3]{0:T(128)S(1)} %pad_add_fusion.pos.refs_0_, f32[7,5,8,128]{3,2,1,0:T(8,128)S(1)} %get-tuple-element.46.refs_1_, f32[7,5,8,128]{3,2,1,0:T(8,128)S(1)} %collective-permute-done.15.refs_2_, f32[7,5,8,128]{3,2,1,0:T(8,128)S(1)} %collective-permute-done.16.refs_3_), custom_call_target="tpu_custom_call" | custom-call | tf_op jit(solution)/shard_map/unpack_out/pallas_call | solution.py:507
  69.7 0.0 collective-permute-done.14.refs_1_
  69.7 1.2 %unpack_out.3 = f32[7,5,16,256]{3,2,1,0:T(8,128)} custom-call(s32[3]{0:T(128)S(1)} %pad_add_fusion.pos.refs_0_, f32[7,5,8,128]{3,2,1,0:T(8,128)S(1)} %collective-permute-done.14.refs_1_, f32[7,5,16,256]{3,2,1,0:T(8,128)} %unpack_out.2.refs_2_), custom_call_target="tpu_custom_call", output_to_operand_aliasing={{}: (2, {})} | custom-call | tf_op jit(solution)/shard_map/unpack_out/pallas_call | solution.py:507
Async XLA Ops:
  0.1 1.2 %copy-start = (f32[11,5,16,256]{3,2,1,0:T(8,128)S(1)}, f32[11,5,16,256]{3,2,1,0:T(8,128)}, u32[]{:S(2)}) copy-start(f32[11,5,16,256]{3,2,1,0:T(8,128)} %cells.1) | copy-start | bytes 2703364
  1.3 6.5 %copy-start.1 = (s32[128,11]{0,1:T(8,128)S(1)}, s32[128,11]{0,1:T(8,128)}, u32[]{:S(2)}) copy-start(s32[128,11]{0,1:T(8,128)} %param.3) | copy-start | bytes 16900
  1.9 10.3 %collective-permute-start.1 = (f32[11,5,8,128]{3,2,1,0:T(8,128)S(1)}, f32[11,5,8,128]{3,2,1,0:T(8,128)S(1)}, u32[]{:S(2)}, u32[]{:S(2)}) collective-permute-start(f32[11,5,8,128]{3,2,1,0:T(8,128)S(1)} %get-tuple-element.31), channel_id=1, source_target_pairs={{0,32},{1,33},{2,34},{3,35},{4,36},{5,37},{6,38},{7,39},{8,40},{9,... | collective-permute-start | bytes 675848 | tf_op jit(solution)/shard_map/ppermute | solution.py:400
  4.5 13.1 %collective-permute-start.3 = (f32[11,5,8,128]{3,2,1,0:T(8,128)S(1)}, f32[11,5,8,128]{3,2,1,0:T(8,128)S(1)}, u32[]{:S(2)}, u32[]{:S(2)}) collective-permute-start(f32[11,5,8,128]{3,2,1,0:T(8,128)S(1)} %get-tuple-element.32), channel_id=1, source_target_pairs={{0,64},{1,65},{2,66},{3,67},{4,68},{5,69},{6,70},{7,71},{8,72},{9,... | collective-permute-start | bytes 675848 | tf_op jit(solution)/shard_map/ppermute | solution.py:400
  7.8 12.2 %collective-permute-start.5 = (f32[11,5,8,128]{3,2,1,0:T(8,128)S(1)}, f32[11,5,8,128]{3,2,1,0:T(8,128)S(1)}, u32[]{:S(2)}, u32[]{:S(2)}) collective-permute-start(f32[11,5,8,128]{3,2,1,0:T(8,128)S(1)} %get-tuple-element.33), channel_id=1, source_target_pairs={{0,96},{1,97},{2,98},{3,99},{4,100},{5,101},{6,102},{7,103},{8,104... | collective-permute-start | bytes 675848 | tf_op jit(solution)/shard_map/ppermute | solution.py:400
  10.9 10.8 %collective-permute-start = (f32[11,5,8,128]{3,2,1,0:T(8,128)S(1)}, f32[11,5,8,128]{3,2,1,0:T(8,128)S(1)}, u32[]{:S(2)}, u32[]{:S(2)}) collective-permute-start(f32[11,5,8,128]{3,2,1,0:T(8,128)S(1)} %get-tuple-element.30.refs_0_), channel_id=1, source_target_pairs={{0,16},{1,17},{2,18},{3,19},{4,20},{5,21},{6,22},{7,23},{8,24},{9,... | collective-permute-start | bytes 675848 | tf_op jit(solution)/shard_map/ppermute | solution.py:400
  12.2 9.5 %collective-permute-start.2 = (f32[11,5,8,128]{3,2,1,0:T(8,128)S(1)}, f32[11,5,8,128]{3,2,1,0:T(8,128)S(1)}, u32[]{:S(2)}, u32[]{:S(2)}) collective-permute-start(f32[11,5,8,128]{3,2,1,0:T(8,128)S(1)} %collective-permute-done.1.refs_2_), channel_id=1, source_target_pairs={{0,16},{1,17},{2,18},{3,19},{4,20},{5,21},{6,22},{7,23},{8,24},{9,... | collective-permute-start | bytes 675848 | tf_op jit(solution)/shard_map/ppermute | solution.py:400
  17.6 4.2 %collective-permute-start.4 = (f32[11,5,8,128]{3,2,1,0:T(8,128)S(1)}, f32[11,5,8,128]{3,2,1,0:T(8,128)S(1)}, u32[]{:S(2)}, u32[]{:S(2)}) collective-permute-start(f32[11,5,8,128]{3,2,1,0:T(8,128)S(1)} %collective-permute-done.3.refs_4_), channel_id=1, source_target_pairs={{0,16},{1,17},{2,18},{3,19},{4,20},{5,21},{6,22},{7,23},{8,24},{9,... | collective-permute-start | bytes 675848 | tf_op jit(solution)/shard_map/ppermute | solution.py:400
  19.9 2.9 %collective-permute-start.6 = (f32[11,5,8,128]{3,2,1,0:T(8,128)S(1)}, f32[11,5,8,128]{3,2,1,0:T(8,128)S(1)}, u32[]{:S(2)}, u32[]{:S(2)}) collective-permute-start(f32[11,5,8,128]{3,2,1,0:T(8,128)S(1)} %collective-permute-done.5.refs_6_), channel_id=1, source_target_pairs={{0,16},{1,17},{2,18},{3,19},{4,20},{5,21},{6,22},{7,23},{8,24},{9,... | collective-permute-start | bytes 675848 | tf_op jit(solution)/shard_map/ppermute | solution.py:400
  24.5 12.2 %collective-permute-start.7 = (f32[360,128]{1,0:T(8,128)S(1)}, f32[360,128]{1,0:T(8,128)S(1)}, u32[]{:S(2)}, u32[]{:S(2)}) collective-permute-start(f32[360,128]{1,0:T(8,128)S(1)} %get-tuple-element.35), channel_id=1, source_target_pairs={{0,127},{1,112},{2,113},{3,114},{4,115},{5,116},{6,117},{7,118},{8... | collective-permute-start | bytes 552968 | tf_op jit(solution)/shard_map/ppermute | solution.py:400
  29.5 11.3 %collective-permute-start.8 = (f32[360,128]{1,0:T(8,128)S(1)}, f32[360,128]{1,0:T(8,128)S(1)}, u32[]{:S(2)}, u32[]{:S(2)}) collective-permute-start(f32[360,128]{1,0:T(8,128)S(1)} %get-tuple-element.36), channel_id=1, source_target_pairs={{0,96},{1,97},{2,98},{3,99},{4,100},{5,101},{6,102},{7,103},{8,104... | collective-permute-start | bytes 552968 | tf_op jit(solution)/shard_map/ppermute | solution.py:400
  29.5 12.2 %collective-permute-start.9 = (f32[360,128]{1,0:T(8,128)S(1)}, f32[360,128]{1,0:T(8,128)S(1)}, u32[]{:S(2)}, u32[]{:S(2)}) collective-permute-start(f32[360,128]{1,0:T(8,128)S(1)} %get-tuple-element.37), channel_id=1, source_target_pairs={{0,47},{1,32},{2,33},{3,34},{4,35},{5,36},{6,37},{7,38},{8,39},{9,... | collective-permute-start | bytes 552968 | tf_op jit(solution)/shard_map/ppermute | solution.py:400
  29.5 12.2 %collective-permute-start.10 = (f32[360,128]{1,0:T(8,128)S(1)}, f32[360,128]{1,0:T(8,128)S(1)}, u32[]{:S(2)}, u32[]{:S(2)}) collective-permute-start(f32[360,128]{1,0:T(8,128)S(1)} %get-tuple-element.38), channel_id=1, source_target_pairs={{0,32},{1,33},{2,34},{3,35},{4,36},{5,37},{6,38},{7,39},{8,40},{9,... | collective-permute-start | bytes 552968 | tf_op jit(solution)/shard_map/ppermute | solution.py:400
  41.5 7.4 %collective-permute-start.11 = (f32[120,128]{1,0:T(8,128)S(1)}, f32[120,128]{1,0:T(8,128)S(1)}, u32[]{:S(2)}, u32[]{:S(2)}) collective-permute-start(f32[120,128]{1,0:T(8,128)S(1)} %get-tuple-element.43), channel_id=1, source_target_pairs={{0,47},{1,32},{2,33},{3,34},{4,35},{5,36},{6,37},{7,38},{8,39},{9,... | collective-permute-start | bytes 184328 | tf_op jit(solution)/shard_map/ppermute | solution.py:400
  41.6 7.3 %collective-permute-start.12 = (f32[120,128]{1,0:T(8,128)S(1)}, f32[120,128]{1,0:T(8,128)S(1)}, u32[]{:S(2)}, u32[]{:S(2)}) collective-permute-start(f32[120,128]{1,0:T(8,128)S(1)} %get-tuple-element.44), channel_id=1, source_target_pairs={{0,32},{1,33},{2,34},{3,35},{4,36},{5,37},{6,38},{7,39},{8,40},{9,... | collective-permute-start | bytes 184328 | tf_op jit(solution)/shard_map/ppermute | solution.py:400
  54.9 3.2 %collective-permute-start.13 = (f32[24,5,8,128]{3,2,1,0:T(8,128)S(1)}, f32[24,5,8,128]{3,2,1,0:T(8,128)S(1)}, u32[]{:S(2)}, u32[]{:S(2)}) collective-permute-start(f32[24,5,8,128]{3,2,1,0:T(8,128)S(1)} %finish.1.mine), channel_id=1, source_target_pairs={{0,16},{1,17},{2,18},{3,19},{4,20},{5,21},{6,22},{7,23},{8,24},{9,... | collective-permute-start | bytes 1474568 | tf_op jit(solution)/shard_map/ppermute | solution.py:400
  58.8 5.1 %collective-permute-start.15 = (f32[7,5,8,128]{3,2,1,0:T(8,128)S(1)}, f32[7,5,8,128]{3,2,1,0:T(8,128)S(1)}, u32[]{:S(2)}, u32[]{:S(2)}) collective-permute-start(f32[7,5,8,128]{3,2,1,0:T(8,128)S(1)} %get-tuple-element.47), channel_id=1, source_target_pairs={{0,32},{1,33},{2,34},{3,35},{4,36},{5,37},{6,38},{7,39},{8,40},{9,... | collective-permute-start | bytes 430088 | tf_op jit(solution)/shard_map/ppermute | solution.py:400
  58.9 9.5 %collective-permute-start.16 = (f32[7,5,8,128]{3,2,1,0:T(8,128)S(1)}, f32[7,5,8,128]{3,2,1,0:T(8,128)S(1)}, u32[]{:S(2)}, u32[]{:S(2)}) collective-permute-start(f32[7,5,8,128]{3,2,1,0:T(8,128)S(1)} %get-tuple-element.48), channel_id=1, source_target_pairs={{0,96},{1,97},{2,98},{3,99},{4,100},{5,101},{6,102},{7,103},{8,104... | collective-permute-start | bytes 430088 | tf_op jit(solution)/shard_map/ppermute | solution.py:400
  59.0 10.7 %collective-permute-start.14 = (f32[7,5,8,128]{3,2,1,0:T(8,128)S(1)}, f32[7,5,8,128]{3,2,1,0:T(8,128)S(1)}, u32[]{:S(2)}, u32[]{:S(2)}) collective-permute-start(f32[7,5,8,128]{3,2,1,0:T(8,128)S(1)} %get-tuple-element.45), channel_id=1, source_target_pairs={{0,64},{1,65},{2,66},{3,67},{4,68},{5,69},{6,70},{7,71},{8,72},{9,... | collective-permute-start | bytes 430088 | tf_op jit(solution)/shard_map/ppermute | solution.py:400

commit v9 on v7

--- a/solution.py
+++ b/solution.py
@@ -26,7 +26,7 @@
 VMEM = pl.BlockSpec(memory_space=pltpu.VMEM)
 SMEM = pl.BlockSpec(memory_space=pltpu.SMEM)
 ANY = pl.BlockSpec(memory_space=pl.ANY)
-PARAMS = pltpu.CompilerParams(vmem_limit_bytes=48 * 1024 * 1024)
+PARAMS = pltpu.CompilerParams(vmem_limit_bytes=24 * 1024 * 1024)
 
 
 def shape(*dims):
@@ -348,31 +348,32 @@
     lax.fori_loop(0, 3, step, 0)
 
 
-EARLY_MAIN = range(0, Y)
-EARLY_SIDE = range(1, Y - 1)
-
-
-def begin(pos, cur, x_in, x_out, y_in, y_out, main, side_rows, first_main, first_side):
+EARLY = ((range(0, Y), range(1, Y - 1)), (range(1, Y - 1), range(2, Y - 2)))
+
+
+def begin(pos, cur, x_in, x_out, y_in, y_out, main, side_rows, *made):
     widen(pos, cur, x_in, x_out, y_in, y_out, main, side_rows)
-    initial, first = (main, side_rows), (first_main, first_side)
-    advance(0, lambda part, y: initial[part], None, lambda part, y: first[part], EARLY_MAIN, EARLY_SIDE)
-
-
-def finish(pos, main, side_rows, early_main, early_side, c_in, c_out, made, corner_rows, *held):
-    late, second = held[0:2], held[2:4]
+    initial = (main, side_rows)
+    advance(0, lambda part, y: initial[part], None, lambda part, y: made[part], *EARLY[0])
+    advance(1, lambda part, y: made[part], lambda part, y: initial[part], lambda part, y: made[2 + part], *EARLY[1])
+
+
+def finish(pos, main, side_rows, *refs):
+    early, (c_in, c_out, made, corner_rows), late = refs[:4], refs[4:8], refs[8:12]
     add_corners(pos, c_in, c_out, corner_rows)
 
     def initial(part, y):
         return (side_rows if 0 <= y < Y else corner_rows) if part else main
 
     def first(part, y):
-        if part:
-            return early_side if y in EARLY_SIDE else late[1]
-        return early_main if y in EARLY_MAIN else late[0]
+        return (early if y in EARLY[0][part] else late)[part]
+
+    def second(part, y):
+        return (early if y in EARLY[1][part] else late)[2 + part]
 
     advance(0, initial, None, first, (-2, -1, Y, Y + 1), (-1, 0, Y - 1, Y))
-    advance(1, first, initial, lambda part, y: second[part], range(-1, Y + 1), range(0, Y))
-    advance(2, lambda part, y: second[part], initial, lambda part, y: late[part], range(0, Y), (), made)
+    advance(1, first, initial, second, (-1, 0, Y - 1, Y), (0, 1, Y - 2, Y - 1))
+    advance(2, second, initial, lambda part, y: late[part], range(0, Y), (), made)
 
 
 def pack_out(pos, final, mine, other, *outs):
@@ -478,9 +479,9 @@
     wide = [F * WIDE * HALF, L]
     early = pl.pallas_call(
         begin,
-        out_shape=[shape(*wide)] * 4,
+        out_shape=[shape(*wide)] * 6,
         in_specs=[SMEM] + [VMEM] * 5,
-        out_specs=[VMEM] * 4,
+        out_specs=[VMEM] * 6,
         compiler_params=PARAMS,
         cost_estimate=pl.CostEstimate(flops=0, bytes_accessed=10_000_000, transcendentals=0),
         name="begin",
@@ -488,7 +489,7 @@
     current = pl.pallas_call(
         finish,
         out_shape=shape(HALF, F, X, L),
-        in_specs=[SMEM] + [VMEM] * 6,
+        in_specs=[SMEM] + [VMEM] * 8,
         out_specs=VMEM,
         scratch_shapes=[pltpu.VMEM(wide, jnp.float32)] * 5,
         compiler_params=PARAMS,

time: 68.6 us -> 68 us (level); the launches traced: 67.5 us -> 67.9 us
    pallas_call x1, Pallas kernels: 2.39 us -> 3.74 us  [body(): pl.pallas_call(begin, out_shape=[shape(*wide)] * 6, in_specs=[SMEM] + [VM...]
    pallas_call x1, Pallas kernels: 6.07 us -> 5.16 us  [body(): pl.pallas_call(finish, out_shape=shape(HALF, F, X, L), in_specs=[SMEM] +...]
  transfers between devices with their start and end apart: 17 -> 17, of which waited for: 9 -> 9; matrix products, arithmetic and copies ran while one was open for 0% -> 0% of each run, Pallas kernels for 11% -> 13%
where the time goes in v9:
time: 68 us; the launch traced here: 67.9 us
  starting transfers between devices  31.2 us (46%)
  Pallas kernels  18.1 us (27%)
  waiting for transfers between devices  17.2 us (25%)
  local copies, waits for them, and re-layouts  1.29 us (2%)
    ppermute x17, starting transfers between devices, to(): return lax.ppermute(array, ('row', 'col'), pairs)  31.2 us
    ppermute x17, waiting for transfers between devices, to(): return lax.ppermute(array, ('row', 'col'), pairs)  17.2 us
    pallas_call x1, Pallas kernels, body(): pl.pallas_call(finish, out_shape=shape(HALF, F, X, L), in_specs=[SMEM] +...  5.16 us
    pallas_call x1, Pallas kernels, body(): pl.pallas_call(begin, out_shape=[shape(*wide)] * 6, in_specs=[SMEM] + [VM...  3.74 us
    pallas_call x1, Pallas kernels, body(): pl.pallas_call(table, out_shape=[jax.ShapeDtypeStruct((N_ROW * 8,), jnp.i...  2.97 us
    pallas_call x2, Pallas kernels, body(): pl.pallas_call(lambda *refs, which=which: unpack_out(which, *refs), out_s...  2.56 us
    pallas_call x1, Pallas kernels, body(): pl.pallas_call(reorder, out_shape=[whole] + [layer] * 4, in_specs=[SMEM,...  1.66 us
  transfers between devices with their start and end apart: 17, of which 9 were waited for; matrix products, arithmetic and copies ran while one was open for 0% of the time, Pallas kernels for 13%

profile of v9, /device:TPU:1, one launch (start us, length us, event | category | flops | bytes accessed | tf_op | source)
XLA Modules:
  0.0 67.9 jit_solution(3323944440641607385)
XLA Ops:
  0.0 0.1 pad_add_fusion.pos.refs_0_
  0.1 0.0 copy-start
  0.1 1.2 %copy-done = f32[11,5,16,256]{3,2,1,0:T(8,128)S(1)} copy-done((f32[11,5,16,256]{3,2,1,0:T(8,128)S(1)}, f32[11,5,16,256]{3,2,1,0:T(8,128)}, u32[]{:S(2)}) %copy-start) | copy-done | bytes 901144
  1.3 0.0 copy-start.1
  1.3 0.7 pack_in.1
  1.9 2.5 %collective-permute-start.1 = (f32[11,5,8,128]{3,2,1,0:T(8,128)S(1)}, f32[11,5,8,128]{3,2,1,0:T(8,128)S(1)}, u32[]{:S(2)}, u32[]{:S(2)}) collective-permute-start(f32[11,5,8,128]{3,2,1,0:T(8,128)S(1)} %get-tuple-element.33), channel_id=1, source_target_pairs={{0,32},{1,33},{2,34},{3,35},{4,36},{5,37},{6,38},{7,39},{8,40},{9,... | collective-permute-start | bytes 675848 | tf_op jit(solution)/shard_map/ppermute | solution.py:401
  4.5 3.3 %collective-permute-start.3 = (f32[11,5,8,128]{3,2,1,0:T(8,128)S(1)}, f32[11,5,8,128]{3,2,1,0:T(8,128)S(1)}, u32[]{:S(2)}, u32[]{:S(2)}) collective-permute-start(f32[11,5,8,128]{3,2,1,0:T(8,128)S(1)} %get-tuple-element.34), channel_id=1, source_target_pairs={{0,64},{1,65},{2,66},{3,67},{4,68},{5,69},{6,70},{7,71},{8,72},{9,... | collective-permute-start | bytes 675848 | tf_op jit(solution)/shard_map/ppermute | solution.py:401
  7.8 0.0 collective-permute-start.5
  7.8 0.0 copy-done.1
  7.8 0.1 copy.5.slots
  7.9 3.0 %table.1 = (s32[64]{0:T(128)S(1)}, s32[88]{0:T(128)S(1)}, f32[11,5,8,128]{3,2,1,0:T(8,128)S(1)}) custom-call(s32[3]{0:T(128)S(1)} %pad_add_fusion.pos.refs_0_, s32[128,11]{1,0:T(8,128)S(1)} %copy.5.slots, f32[11,5,8,128]{3,2,1,0:T(8,128)S(1)} %get-tuple-element.29._tile), custom_call_target="tpu_custom_call", output_to_operand_aliasing={{2}: (2, {})} | custom-call | bytes 20000000 | tf_op jit(solution)/shard_map/table/pallas_call | solution.py:418
  10.9 1.3 %collective-permute-start = (f32[11,5,8,128]{3,2,1,0:T(8,128)S(1)}, f32[11,5,8,128]{3,2,1,0:T(8,128)S(1)}, u32[]{:S(2)}, u32[]{:S(2)}) collective-permute-start(f32[11,5,8,128]{3,2,1,0:T(8,128)S(1)} %get-tuple-element.32.refs_0_), channel_id=1, source_target_pairs={{0,16},{1,17},{2,18},{3,19},{4,20},{5,21},{6,22},{7,23},{8,24},{9,... | collective-permute-start | bytes 675848 | tf_op jit(solution)/shard_map/ppermute | solution.py:401
  12.2 0.0 collective-permute-done.1.refs_2_
  12.2 0.1 collective-permute-start.2
  12.3 5.3 %collective-permute-done.3.refs_4_ = f32[11,5,8,128]{3,2,1,0:T(8,128)S(1)} collective-permute-done((f32[11,5,8,128]{3,2,1,0:T(8,128)S(1)}, f32[11,5,8,128]{3,2,1,0:T(8,128)S(1)}, u32[]{:S(2)}, u32[]{:S(2)}) %collective-permute-start.3) | collective-permute-done | bytes 225312 | tf_op jit(solution)/shard_map/ppermute | solution.py:401
  17.6 1.6 %collective-permute-start.4 = (f32[11,5,8,128]{3,2,1,0:T(8,128)S(1)}, f32[11,5,8,128]{3,2,1,0:T(8,128)S(1)}, u32[]{:S(2)}, u32[]{:S(2)}) collective-permute-start(f32[11,5,8,128]{3,2,1,0:T(8,128)S(1)} %collective-permute-done.3.refs_4_), channel_id=1, source_target_pairs={{0,16},{1,17},{2,18},{3,19},{4,20},{5,21},{6,22},{7,23},{8,24},{9,... | collective-permute-start | bytes 675848 | tf_op jit(solution)/shard_map/ppermute | solution.py:401
  19.2 0.8 %collective-permute-done.5.refs_6_ = f32[11,5,8,128]{3,2,1,0:T(8,128)S(1)} collective-permute-done((f32[11,5,8,128]{3,2,1,0:T(8,128)S(1)}, f32[11,5,8,128]{3,2,1,0:T(8,128)S(1)}, u32[]{:S(2)}, u32[]{:S(2)}) %collective-permute-start.5) | collective-permute-done | bytes 225312 | tf_op jit(solution)/shard_map/ppermute | solution.py:401
  19.9 1.8 %collective-permute-start.6 = (f32[11,5,8,128]{3,2,1,0:T(8,128)S(1)}, f32[11,5,8,128]{3,2,1,0:T(8,128)S(1)}, u32[]{:S(2)}, u32[]{:S(2)}) collective-permute-start(f32[11,5,8,128]{3,2,1,0:T(8,128)S(1)} %collective-permute-done.5.refs_6_), channel_id=1, source_target_pairs={{0,16},{1,17},{2,18},{3,19},{4,20},{5,21},{6,22},{7,23},{8,24},{9,... | collective-permute-start | bytes 675848 | tf_op jit(solution)/shard_map/ppermute | solution.py:401
  21.8 0.0 collective-permute-done.refs_1_
  21.8 0.0 collective-permute-done.2.refs_3_
  21.8 0.0 collective-permute-done.4.refs_5_
  21.8 1.1 %collective-permute-done.6.refs_7_ = f32[11,5,8,128]{3,2,1,0:T(8,128)S(1)} collective-permute-done((f32[11,5,8,128]{3,2,1,0:T(8,128)S(1)}, f32[11,5,8,128]{3,2,1,0:T(8,128)S(1)}, u32[]{:S(2)}, u32[]{:S(2)}) %collective-permute-start.6) | collective-permute-done | bytes 225312 | tf_op jit(solution)/shard_map/ppermute | solution.py:401
  22.9 1.7 %reorder.1 = (f32[960,128]{1,0:T(8,128)S(1)}, f32[360,128]{1,0:T(8,128)S(1)}, f32[360,128]{1,0:T(8,128)S(1)}, f32[360,128]{1,0:T(8,128)S(1)}, f32[360,128]{1,0:T(8,128)S(1)}) custom-call(s32[3]{0:T(128)S(1)} %pad_add_fusion.pos.refs_0_, s32[88]{0:T(128)S(1)} %get-tuple-element.31.rows, f32[11,5,8,128]{3,2,1,0:T(8,128)S(1)} %get-tuple-element.32.refs_0_, ...), custom_call_target="tpu_custom_call" | custom-call | tf_op jit(solution)/shard_map/reorder/pallas_call | solution.py:440
  24.5 0.1 collective-permute-start.9
  24.6 7.8 %collective-permute-start.10 = (f32[360,128]{1,0:T(8,128)S(1)}, f32[360,128]{1,0:T(8,128)S(1)}, u32[]{:S(2)}, u32[]{:S(2)}) collective-permute-start(f32[360,128]{1,0:T(8,128)S(1)} %get-tuple-element.40), channel_id=1, source_target_pairs={{0,127},{1,112},{2,113},{3,114},{4,115},{5,116},{6,117},{7,118},{8... | collective-permute-start | bytes 552968 | tf_op jit(solution)/shard_map/ppermute | solution.py:401
  32.5 0.0 collective-permute-start.7
  32.5 1.7 %collective-permute-start.8 = (f32[360,128]{1,0:T(8,128)S(1)}, f32[360,128]{1,0:T(8,128)S(1)}, u32[]{:S(2)}, u32[]{:S(2)}) collective-permute-start(f32[360,128]{1,0:T(8,128)S(1)} %get-tuple-element.38), channel_id=1, source_target_pairs={{0,47},{1,32},{2,33},{3,34},{4,35},{5,36},{6,37},{7,38},{8,39},{9,... | collective-permute-start | bytes 552968 | tf_op jit(solution)/shard_map/ppermute | solution.py:401
  34.2 0.0 collective-permute-done.9.y_in
  34.2 2.7 %collective-permute-done.10.y_out = f32[360,128]{1,0:T(8,128)S(1)} collective-permute-done((f32[360,128]{1,0:T(8,128)S(1)}, f32[360,128]{1,0:T(8,128)S(1)}, u32[]{:S(2)}, u32[]{:S(2)}) %collective-permute-start.10) | collective-permute-done | bytes 184352 | tf_op jit(solution)/shard_map/ppermute | solution.py:401
  36.9 0.6 corners.1
  37.6 0.1 collective-permute-start.11
  37.7 4.8 %collective-permute-start.12 = (f32[120,128]{1,0:T(8,128)S(1)}, f32[120,128]{1,0:T(8,128)S(1)}, u32[]{:S(2)}, u32[]{:S(2)}) collective-permute-start(f32[120,128]{1,0:T(8,128)S(1)} %get-tuple-element.48), channel_id=1, source_target_pairs={{0,47},{1,32},{2,33},{3,34},{4,35},{5,36},{6,37},{7,38},{8,39},{9,... | collective-permute-start | bytes 184328 | tf_op jit(solution)/shard_map/ppermute | solution.py:401
  42.4 0.0 collective-permute-done.7.x_in
  42.5 0.6 collective-permute-done.8.x_out
  43.0 3.7 %begin.1 = (f32[1680,128]{1,0:T(8,128)S(1)}, f32[1680,128]{1,0:T(8,128)S(1)}, f32[1680,128]{1,0:T(8,128)S(1)}, f32[1680,128]{1,0:T(8,128)S(1)}, f32[1680,128]{1,0:T(8,128)S(1)}, /*index=5*/f32[1680,128]{1,0:T(8,128)S(1)}) custom-call(s32[3]{0:T(128)S(1)} %pad_add_fusion.pos.refs_0_, f32[960,128]{1,0:T(8,128)S(1)} %get-tuple-element.36.cur, ...), custom_call_target="tpu_custom_call" | custom-call | bytes 10000000 | tf_op jit(solution)/shard_map/begin/pallas_call | solution.py:480
  46.8 0.0 collective-permute-done.11.refs_4_
  46.8 0.0 collective-permute-done.12.refs_5_
  46.8 5.2 %finish.1.mine = f32[24,5,8,128]{3,2,1,0:T(8,128)S(1)} custom-call(s32[3]{0:T(128)S(1)} %pad_add_fusion.pos.refs_0_, f32[1680,128]{1,0:T(8,128)S(1)} %get-tuple-element.41.main, f32[1680,128]{1,0:T(8,128)S(1)} %get-tuple-element.42.side_rows, f32[1680,128]{1,0:T(8,128)S(1)} %get-tuple-element.43.refs_0_, f32[1680,128]{1,0:T(8,128)S(1)} %get-tuple-element.44.refs_1_, ...), custom_call_target="tpu_custom_call" | custom-call | tf_op jit(solution)/shard_map/finish/pallas_call | solution.py:489
  52.0 1.3 %collective-permute-start.13 = (f32[24,5,8,128]{3,2,1,0:T(8,128)S(1)}, f32[24,5,8,128]{3,2,1,0:T(8,128)S(1)}, u32[]{:S(2)}, u32[]{:S(2)}) collective-permute-start(f32[24,5,8,128]{3,2,1,0:T(8,128)S(1)} %finish.1.mine), channel_id=1, source_target_pairs={{0,16},{1,17},{2,18},{3,19},{4,20},{5,21},{6,22},{7,23},{8,24},{9,... | collective-permute-start | bytes 1474568 | tf_op jit(solution)/shard_map/ppermute | solution.py:401
  53.2 1.5 %collective-permute-done.13.other = f32[24,5,8,128]{3,2,1,0:T(8,128)S(1)} collective-permute-done((f32[24,5,8,128]{3,2,1,0:T(8,128)S(1)}, f32[24,5,8,128]{3,2,1,0:T(8,128)S(1)}, u32[]{:S(2)}, u32[]{:S(2)}) %collective-permute-start.13) | collective-permute-done | bytes 491552 | tf_op jit(solution)/shard_map/ppermute | solution.py:401
  54.7 0.7 pack_out.1
  55.4 0.1 collective-permute-start.15
  55.5 3.5 %collective-permute-start.16 = (f32[7,5,8,128]{3,2,1,0:T(8,128)S(1)}, f32[7,5,8,128]{3,2,1,0:T(8,128)S(1)}, u32[]{:S(2)}, u32[]{:S(2)}) collective-permute-start(f32[7,5,8,128]{3,2,1,0:T(8,128)S(1)} %get-tuple-element.52), channel_id=1, source_target_pairs={{0,96},{1,97},{2,98},{3,99},{4,100},{5,101},{6,102},{7,103},{8,104... | collective-permute-start | bytes 430088 | tf_op jit(solution)/shard_map/ppermute | solution.py:401
  59.0 1.1 %collective-permute-start.14 = (f32[7,5,8,128]{3,2,1,0:T(8,128)S(1)}, f32[7,5,8,128]{3,2,1,0:T(8,128)S(1)}, u32[]{:S(2)}, u32[]{:S(2)}) collective-permute-start(f32[7,5,8,128]{3,2,1,0:T(8,128)S(1)} %get-tuple-element.49), channel_id=1, source_target_pairs={{0,64},{1,65},{2,66},{3,67},{4,68},{5,69},{6,70},{7,71},{8,72},{9,... | collective-permute-start | bytes 430088 | tf_op jit(solution)/shard_map/ppermute | solution.py:401
  60.1 0.3 collective-permute-done.15.refs_2_
  60.4 4.5 %collective-permute-done.16.refs_3_ = f32[7,5,8,128]{3,2,1,0:T(8,128)S(1)} collective-permute-done((f32[7,5,8,128]{3,2,1,0:T(8,128)S(1)}, f32[7,5,8,128]{3,2,1,0:T(8,128)S(1)}, u32[]{:S(2)}, u32[]{:S(2)}) %collective-permute-start.16) | collective-permute-done | bytes 143392 | tf_op jit(solution)/shard_map/ppermute | solution.py:401
  65.0 1.3 %unpack_out.2.refs_2_ = f32[7,5,16,256]{3,2,1,0:T(8,128)} custom-call(s32[3]{0:T(128)S(1)} %pad_add_fusion.pos.refs_0_, f32[7,5,8,128]{3,2,1,0:T(8,128)S(1)} %get-tuple-element.50.refs_1_, f32[7,5,8,128]{3,2,1,0:T(8,128)S(1)} %collective-permute-done.15.refs_2_, f32[7,5,8,128]{3,2,1,0:T(8,128)S(1)} %collective-permute-done.16.refs_3_), custom_call_target="tpu_custom_call" | custom-call | tf_op jit(solution)/shard_map/unpack_out/pallas_call | solution.py:512
  66.3 0.3 collective-permute-done.14.refs_1_
  66.7 1.2 %unpack_out.3 = f32[7,5,16,256]{3,2,1,0:T(8,128)} custom-call(s32[3]{0:T(128)S(1)} %pad_add_fusion.pos.refs_0_, f32[7,5,8,128]{3,2,1,0:T(8,128)S(1)} %collective-permute-done.14.refs_1_, f32[7,5,16,256]{3,2,1,0:T(8,128)} %unpack_out.2.refs_2_), custom_call_target="tpu_custom_call", output_to_operand_aliasing={{}: (2, {})} | custom-call | tf_op jit(solution)/shard_map/unpack_out/pallas_call | solution.py:512
Async XLA Ops:
  0.1 1.2 %copy-start = (f32[11,5,16,256]{3,2,1,0:T(8,128)S(1)}, f32[11,5,16,256]{3,2,1,0:T(8,128)}, u32[]{:S(2)}) copy-start(f32[11,5,16,256]{3,2,1,0:T(8,128)} %cells.1) | copy-start | bytes 2703364
  1.3 6.5 %copy-start.1 = (s32[128,11]{0,1:T(8,128)S(1)}, s32[128,11]{0,1:T(8,128)}, u32[]{:S(2)}) copy-start(s32[128,11]{0,1:T(8,128)} %param.3) | copy-start | bytes 16900
  1.9 10.3 %collective-permute-start.1 = (f32[11,5,8,128]{3,2,1,0:T(8,128)S(1)}, f32[11,5,8,128]{3,2,1,0:T(8,128)S(1)}, u32[]{:S(2)}, u32[]{:S(2)}) collective-permute-start(f32[11,5,8,128]{3,2,1,0:T(8,128)S(1)} %get-tuple-element.33), channel_id=1, source_target_pairs={{0,32},{1,33},{2,34},{3,35},{4,36},{5,37},{6,38},{7,39},{8,40},{9,... | collective-permute-start | bytes 675848 | tf_op jit(solution)/shard_map/ppermute | solution.py:401
  4.5 13.1 %collective-permute-start.3 = (f32[11,5,8,128]{3,2,1,0:T(8,128)S(1)}, f32[11,5,8,128]{3,2,1,0:T(8,128)S(1)}, u32[]{:S(2)}, u32[]{:S(2)}) collective-permute-start(f32[11,5,8,128]{3,2,1,0:T(8,128)S(1)} %get-tuple-element.34), channel_id=1, source_target_pairs={{0,64},{1,65},{2,66},{3,67},{4,68},{5,69},{6,70},{7,71},{8,72},{9,... | collective-permute-start | bytes 675848 | tf_op jit(solution)/shard_map/ppermute | solution.py:401
  7.8 12.2 %collective-permute-start.5 = (f32[11,5,8,128]{3,2,1,0:T(8,128)S(1)}, f32[11,5,8,128]{3,2,1,0:T(8,128)S(1)}, u32[]{:S(2)}, u32[]{:S(2)}) collective-permute-start(f32[11,5,8,128]{3,2,1,0:T(8,128)S(1)} %get-tuple-element.35), channel_id=1, source_target_pairs={{0,96},{1,97},{2,98},{3,99},{4,100},{5,101},{6,102},{7,103},{8,104... | collective-permute-start | bytes 675848 | tf_op jit(solution)/shard_map/ppermute | solution.py:401
  10.9 10.9 %collective-permute-start = (f32[11,5,8,128]{3,2,1,0:T(8,128)S(1)}, f32[11,5,8,128]{3,2,1,0:T(8,128)S(1)}, u32[]{:S(2)}, u32[]{:S(2)}) collective-permute-start(f32[11,5,8,128]{3,2,1,0:T(8,128)S(1)} %get-tuple-element.32.refs_0_), channel_id=1, source_target_pairs={{0,16},{1,17},{2,18},{3,19},{4,20},{5,21},{6,22},{7,23},{8,24},{9,... | collective-permute-start | bytes 675848 | tf_op jit(solution)/shard_map/ppermute | solution.py:401
  12.2 9.6 %collective-permute-start.2 = (f32[11,5,8,128]{3,2,1,0:T(8,128)S(1)}, f32[11,5,8,128]{3,2,1,0:T(8,128)S(1)}, u32[]{:S(2)}, u32[]{:S(2)}) collective-permute-start(f32[11,5,8,128]{3,2,1,0:T(8,128)S(1)} %collective-permute-done.1.refs_2_), channel_id=1, source_target_pairs={{0,16},{1,17},{2,18},{3,19},{4,20},{5,21},{6,22},{7,23},{8,24},{9,... | collective-permute-start | bytes 675848 | tf_op jit(solution)/shard_map/ppermute | solution.py:401
  17.6 4.2 %collective-permute-start.4 = (f32[11,5,8,128]{3,2,1,0:T(8,128)S(1)}, f32[11,5,8,128]{3,2,1,0:T(8,128)S(1)}, u32[]{:S(2)}, u32[]{:S(2)}) collective-permute-start(f32[11,5,8,128]{3,2,1,0:T(8,128)S(1)} %collective-permute-done.3.refs_4_), channel_id=1, source_target_pairs={{0,16},{1,17},{2,18},{3,19},{4,20},{5,21},{6,22},{7,23},{8,24},{9,... | collective-permute-start | bytes 675848 | tf_op jit(solution)/shard_map/ppermute | solution.py:401
  19.9 2.9 %collective-permute-start.6 = (f32[11,5,8,128]{3,2,1,0:T(8,128)S(1)}, f32[11,5,8,128]{3,2,1,0:T(8,128)S(1)}, u32[]{:S(2)}, u32[]{:S(2)}) collective-permute-start(f32[11,5,8,128]{3,2,1,0:T(8,128)S(1)} %collective-permute-done.5.refs_6_), channel_id=1, source_target_pairs={{0,16},{1,17},{2,18},{3,19},{4,20},{5,21},{6,22},{7,23},{8,24},{9,... | collective-permute-start | bytes 675848 | tf_op jit(solution)/shard_map/ppermute | solution.py:401
  24.5 9.7 %collective-permute-start.9 = (f32[360,128]{1,0:T(8,128)S(1)}, f32[360,128]{1,0:T(8,128)S(1)}, u32[]{:S(2)}, u32[]{:S(2)}) collective-permute-start(f32[360,128]{1,0:T(8,128)S(1)} %get-tuple-element.39), channel_id=1, source_target_pairs={{0,96},{1,97},{2,98},{3,99},{4,100},{5,101},{6,102},{7,103},{8,104... | collective-permute-start | bytes 552968 | tf_op jit(solution)/shard_map/ppermute | solution.py:401
  24.6 12.3 %collective-permute-start.10 = (f32[360,128]{1,0:T(8,128)S(1)}, f32[360,128]{1,0:T(8,128)S(1)}, u32[]{:S(2)}, u32[]{:S(2)}) collective-permute-start(f32[360,128]{1,0:T(8,128)S(1)} %get-tuple-element.40), channel_id=1, source_target_pairs={{0,127},{1,112},{2,113},{3,114},{4,115},{5,116},{6,117},{7,118},{8... | collective-permute-start | bytes 552968 | tf_op jit(solution)/shard_map/ppermute | solution.py:401
  32.5 10.0 %collective-permute-start.7 = (f32[360,128]{1,0:T(8,128)S(1)}, f32[360,128]{1,0:T(8,128)S(1)}, u32[]{:S(2)}, u32[]{:S(2)}) collective-permute-start(f32[360,128]{1,0:T(8,128)S(1)} %get-tuple-element.37), channel_id=1, source_target_pairs={{0,32},{1,33},{2,34},{3,35},{4,36},{5,37},{6,38},{7,39},{8,40},{9,... | collective-permute-start | bytes 552968 | tf_op jit(solution)/shard_map/ppermute | solution.py:401
  32.5 10.6 %collective-permute-start.8 = (f32[360,128]{1,0:T(8,128)S(1)}, f32[360,128]{1,0:T(8,128)S(1)}, u32[]{:S(2)}, u32[]{:S(2)}) collective-permute-start(f32[360,128]{1,0:T(8,128)S(1)} %get-tuple-element.38), channel_id=1, source_target_pairs={{0,47},{1,32},{2,33},{3,34},{4,35},{5,36},{6,37},{7,38},{8,39},{9,... | collective-permute-start | bytes 552968 | tf_op jit(solution)/shard_map/ppermute | solution.py:401
  37.6 9.2 %collective-permute-start.11 = (f32[120,128]{1,0:T(8,128)S(1)}, f32[120,128]{1,0:T(8,128)S(1)}, u32[]{:S(2)}, u32[]{:S(2)}) collective-permute-start(f32[120,128]{1,0:T(8,128)S(1)} %get-tuple-element.47), channel_id=1, source_target_pairs={{0,32},{1,33},{2,34},{3,35},{4,36},{5,37},{6,38},{7,39},{8,40},{9,... | collective-permute-start | bytes 184328 | tf_op jit(solution)/shard_map/ppermute | solution.py:401
  37.7 9.1 %collective-permute-start.12 = (f32[120,128]{1,0:T(8,128)S(1)}, f32[120,128]{1,0:T(8,128)S(1)}, u32[]{:S(2)}, u32[]{:S(2)}) collective-permute-start(f32[120,128]{1,0:T(8,128)S(1)} %get-tuple-element.48), channel_id=1, source_target_pairs={{0,47},{1,32},{2,33},{3,34},{4,35},{5,36},{6,37},{7,38},{8,39},{9,... | collective-permute-start | bytes 184328 | tf_op jit(solution)/shard_map/ppermute | solution.py:401
  52.0 2.7 %collective-permute-start.13 = (f32[24,5,8,128]{3,2,1,0:T(8,128)S(1)}, f32[24,5,8,128]{3,2,1,0:T(8,128)S(1)}, u32[]{:S(2)}, u32[]{:S(2)}) collective-permute-start(f32[24,5,8,128]{3,2,1,0:T(8,128)S(1)} %finish.1.mine), channel_id=1, source_target_pairs={{0,16},{1,17},{2,18},{3,19},{4,20},{5,21},{6,22},{7,23},{8,24},{9,... | collective-permute-start | bytes 1474568 | tf_op jit(solution)/shard_map/ppermute | solution.py:401
  55.4 5.1 %collective-permute-start.15 = (f32[7,5,8,128]{3,2,1,0:T(8,128)S(1)}, f32[7,5,8,128]{3,2,1,0:T(8,128)S(1)}, u32[]{:S(2)}, u32[]{:S(2)}) collective-permute-start(f32[7,5,8,128]{3,2,1,0:T(8,128)S(1)} %get-tuple-element.51), channel_id=1, source_target_pairs={{0,32},{1,33},{2,34},{3,35},{4,36},{5,37},{6,38},{7,39},{8,40},{9,... | collective-permute-start | bytes 430088 | tf_op jit(solution)/shard_map/ppermute | solution.py:401
  55.5 9.5 %collective-permute-start.16 = (f32[7,5,8,128]{3,2,1,0:T(8,128)S(1)}, f32[7,5,8,128]{3,2,1,0:T(8,128)S(1)}, u32[]{:S(2)}, u32[]{:S(2)}) collective-permute-start(f32[7,5,8,128]{3,2,1,0:T(8,128)S(1)} %get-tuple-element.52), channel_id=1, source_target_pairs={{0,96},{1,97},{2,98},{3,99},{4,100},{5,101},{6,102},{7,103},{8,104... | collective-permute-start | bytes 430088 | tf_op jit(solution)/shard_map/ppermute | solution.py:401
  59.0 7.7 %collective-permute-start.14 = (f32[7,5,8,128]{3,2,1,0:T(8,128)S(1)}, f32[7,5,8,128]{3,2,1,0:T(8,128)S(1)}, u32[]{:S(2)}, u32[]{:S(2)}) collective-permute-start(f32[7,5,8,128]{3,2,1,0:T(8,128)S(1)} %get-tuple-element.49), channel_id=1, source_target_pairs={{0,64},{1,65},{2,66},{3,67},{4,68},{5,69},{6,70},{7,71},{8,72},{9,... | collective-permute-start | bytes 430088 | tf_op jit(solution)/shard_map/ppermute | solution.py:401

commit v10 on v9

--- a/solution.py
+++ b/solution.py
@@ -506,7 +506,7 @@
     )(pos, final, current, over_core(current))
     arrived = [over_z(leaving[k], k) for k in range(4)]
     result = []
-    for which in ((0, 1, 3), (2,)):
+    for which in ((0,), (2, 1, 3)):
         n = len(which)
         result = [
             pl.pallas_call(

time: 68 us -> 67.6 us (level)
  transfers between devices with their start and end apart: 17 -> 17, of which waited for: 9 -> 8; matrix products, arithmetic and copies ran while one was open for 0% -> 0% of each run, Pallas kernels for 13% -> 13%
where the time goes in v10:
time: 67.6 us; the launch traced here: 67.4 us
  starting transfers between devices  30.6 us (45%)
  Pallas kernels  18 us (27%)
  waiting for transfers between devices  17.4 us (26%)
  local copies, waits for them, and re-layouts  1.29 us (2%)
    ppermute x17, starting transfers between devices, to(): return lax.ppermute(array, ('row', 'col'), pairs)  30.6 us
    ppermute x17, waiting for transfers between devices, to(): return lax.ppermute(array, ('row', 'col'), pairs)  17.4 us
    pallas_call x1, Pallas kernels, body(): pl.pallas_call(finish, out_shape=shape(HALF, F, X, L), in_specs=[SMEM] +...  5.16 us
    pallas_call x1, Pallas kernels, body(): pl.pallas_call(begin, out_shape=[shape(*wide)] * 6, in_specs=[SMEM] + [VM...  3.74 us
    pallas_call x1, Pallas kernels, body(): pl.pallas_call(table, out_shape=[jax.ShapeDtypeStruct((N_ROW * 8,), jnp.i...  2.94 us
    pallas_call x2, Pallas kernels, body(): pl.pallas_call(lambda *refs, which=which: unpack_out(which, *refs), out_s...  2.56 us
    pallas_call x1, Pallas kernels, body(): pl.pallas_call(reorder, out_shape=[whole] + [layer] * 4, in_specs=[SMEM,...  1.66 us
  transfers between devices with their start and end apart: 17, of which 8 were waited for; matrix products, arithmetic and copies ran while one was open for 0% of the time, Pallas kernels for 13%

profile of v10, /device:TPU:1, one launch (start us, length us, event | category | flops | bytes accessed | tf_op | source)
XLA Modules:
  0.0 67.4 jit_solution(9704693642653040532)
XLA Ops:
  0.0 0.1 pad_add_fusion.pos.refs_0_
  0.1 0.0 copy-start
  0.1 1.2 %copy-done = f32[11,5,16,256]{3,2,1,0:T(8,128)S(1)} copy-done((f32[11,5,16,256]{3,2,1,0:T(8,128)S(1)}, f32[11,5,16,256]{3,2,1,0:T(8,128)}, u32[]{:S(2)}) %copy-start) | copy-done | bytes 901144
  1.3 0.0 copy-start.1
  1.3 0.7 %pack_in.1 = (f32[11,5,8,128]{3,2,1,0:T(8,128)S(1)}, f32[11,5,8,128]{3,2,1,0:T(8,128)S(1)}, f32[11,5,8,128]{3,2,1,0:T(8,128)S(1)}, f32[11,5,8,128]{3,2,1,0:T(8,128)S(1)}) custom-call(s32[3]{0:T(128)S(1)} %pad_add_fusion.pos.refs_0_, f32[11,5,16,256]{3,2,1,0:T(8,128)S(1)} %copy-done), custom_call_target="tpu_custom_call" | custom-call | tf_op jit(solution)/shard_map/pack_in/pallas_call | solution.py:410
  1.9 2.5 %collective-permute-start.1 = (f32[11,5,8,128]{3,2,1,0:T(8,128)S(1)}, f32[11,5,8,128]{3,2,1,0:T(8,128)S(1)}, u32[]{:S(2)}, u32[]{:S(2)}) collective-permute-start(f32[11,5,8,128]{3,2,1,0:T(8,128)S(1)} %get-tuple-element.33), channel_id=1, source_target_pairs={{0,32},{1,33},{2,34},{3,35},{4,36},{5,37},{6,38},{7,39},{8,40},{9,... | collective-permute-start | bytes 675848 | tf_op jit(solution)/shard_map/ppermute | solution.py:401
  4.5 3.3 %collective-permute-start.3 = (f32[11,5,8,128]{3,2,1,0:T(8,128)S(1)}, f32[11,5,8,128]{3,2,1,0:T(8,128)S(1)}, u32[]{:S(2)}, u32[]{:S(2)}) collective-permute-start(f32[11,5,8,128]{3,2,1,0:T(8,128)S(1)} %get-tuple-element.34), channel_id=1, source_target_pairs={{0,64},{1,65},{2,66},{3,67},{4,68},{5,69},{6,70},{7,71},{8,72},{9,... | collective-permute-start | bytes 675848 | tf_op jit(solution)/shard_map/ppermute | solution.py:401
  7.8 0.0 collective-permute-start.5
  7.8 0.0 copy-done.1
  7.8 0.1 copy.5.slots
  7.9 2.9 %table.1 = (s32[64]{0:T(128)S(1)}, s32[88]{0:T(128)S(1)}, f32[11,5,8,128]{3,2,1,0:T(8,128)S(1)}) custom-call(s32[3]{0:T(128)S(1)} %pad_add_fusion.pos.refs_0_, s32[128,11]{1,0:T(8,128)S(1)} %copy.5.slots, f32[11,5,8,128]{3,2,1,0:T(8,128)S(1)} %get-tuple-element.29._tile), custom_call_target="tpu_custom_call", output_to_operand_aliasing={{2}: (2, {})} | custom-call | bytes 20000000 | tf_op jit(solution)/shard_map/table/pallas_call | solution.py:418
  10.8 1.3 %collective-permute-start = (f32[11,5,8,128]{3,2,1,0:T(8,128)S(1)}, f32[11,5,8,128]{3,2,1,0:T(8,128)S(1)}, u32[]{:S(2)}, u32[]{:S(2)}) collective-permute-start(f32[11,5,8,128]{3,2,1,0:T(8,128)S(1)} %get-tuple-element.32.refs_0_), channel_id=1, source_target_pairs={{0,16},{1,17},{2,18},{3,19},{4,20},{5,21},{6,22},{7,23},{8,24},{9,... | collective-permute-start | bytes 675848 | tf_op jit(solution)/shard_map/ppermute | solution.py:401
  12.2 0.0 collective-permute-done.1.refs_2_
  12.2 0.1 collective-permute-start.2
  12.3 5.3 %collective-permute-done.3.refs_4_ = f32[11,5,8,128]{3,2,1,0:T(8,128)S(1)} collective-permute-done((f32[11,5,8,128]{3,2,1,0:T(8,128)S(1)}, f32[11,5,8,128]{3,2,1,0:T(8,128)S(1)}, u32[]{:S(2)}, u32[]{:S(2)}) %collective-permute-start.3) | collective-permute-done | bytes 225312 | tf_op jit(solution)/shard_map/ppermute | solution.py:401
  17.6 1.6 %collective-permute-start.4 = (f32[11,5,8,128]{3,2,1,0:T(8,128)S(1)}, f32[11,5,8,128]{3,2,1,0:T(8,128)S(1)}, u32[]{:S(2)}, u32[]{:S(2)}) collective-permute-start(f32[11,5,8,128]{3,2,1,0:T(8,128)S(1)} %collective-permute-done.3.refs_4_), channel_id=1, source_target_pairs={{0,16},{1,17},{2,18},{3,19},{4,20},{5,21},{6,22},{7,23},{8,24},{9,... | collective-permute-start | bytes 675848 | tf_op jit(solution)/shard_map/ppermute | solution.py:401
  19.2 0.8 %collective-permute-done.5.refs_6_ = f32[11,5,8,128]{3,2,1,0:T(8,128)S(1)} collective-permute-done((f32[11,5,8,128]{3,2,1,0:T(8,128)S(1)}, f32[11,5,8,128]{3,2,1,0:T(8,128)S(1)}, u32[]{:S(2)}, u32[]{:S(2)}) %collective-permute-start.5) | collective-permute-done | bytes 225312 | tf_op jit(solution)/shard_map/ppermute | solution.py:401
  19.9 1.8 %collective-permute-start.6 = (f32[11,5,8,128]{3,2,1,0:T(8,128)S(1)}, f32[11,5,8,128]{3,2,1,0:T(8,128)S(1)}, u32[]{:S(2)}, u32[]{:S(2)}) collective-permute-start(f32[11,5,8,128]{3,2,1,0:T(8,128)S(1)} %collective-permute-done.5.refs_6_), channel_id=1, source_target_pairs={{0,16},{1,17},{2,18},{3,19},{4,20},{5,21},{6,22},{7,23},{8,24},{9,... | collective-permute-start | bytes 675848 | tf_op jit(solution)/shard_map/ppermute | solution.py:401
  21.8 0.0 collective-permute-done.refs_1_
  21.8 0.0 collective-permute-done.2.refs_3_
  21.8 0.0 collective-permute-done.4.refs_5_
  21.8 1.1 %collective-permute-done.6.refs_7_ = f32[11,5,8,128]{3,2,1,0:T(8,128)S(1)} collective-permute-done((f32[11,5,8,128]{3,2,1,0:T(8,128)S(1)}, f32[11,5,8,128]{3,2,1,0:T(8,128)S(1)}, u32[]{:S(2)}, u32[]{:S(2)}) %collective-permute-start.6) | collective-permute-done | bytes 225312 | tf_op jit(solution)/shard_map/ppermute | solution.py:401
  22.9 1.7 %reorder.1 = (f32[960,128]{1,0:T(8,128)S(1)}, f32[360,128]{1,0:T(8,128)S(1)}, f32[360,128]{1,0:T(8,128)S(1)}, f32[360,128]{1,0:T(8,128)S(1)}, f32[360,128]{1,0:T(8,128)S(1)}) custom-call(s32[3]{0:T(128)S(1)} %pad_add_fusion.pos.refs_0_, s32[88]{0:T(128)S(1)} %get-tuple-element.31.rows, f32[11,5,8,128]{3,2,1,0:T(8,128)S(1)} %get-tuple-element.32.refs_0_, ...), custom_call_target="tpu_custom_call" | custom-call | tf_op jit(solution)/shard_map/reorder/pallas_call | solution.py:440
  24.5 0.1 collective-permute-start.9
  24.6 7.8 %collective-permute-start.10 = (f32[360,128]{1,0:T(8,128)S(1)}, f32[360,128]{1,0:T(8,128)S(1)}, u32[]{:S(2)}, u32[]{:S(2)}) collective-permute-start(f32[360,128]{1,0:T(8,128)S(1)} %get-tuple-element.40), channel_id=1, source_target_pairs={{0,127},{1,112},{2,113},{3,114},{4,115},{5,116},{6,117},{7,118},{8... | collective-permute-start | bytes 552968 | tf_op jit(solution)/shard_map/ppermute | solution.py:401
  32.5 0.0 collective-permute-start.7
  32.5 1.7 %collective-permute-start.8 = (f32[360,128]{1,0:T(8,128)S(1)}, f32[360,128]{1,0:T(8,128)S(1)}, u32[]{:S(2)}, u32[]{:S(2)}) collective-permute-start(f32[360,128]{1,0:T(8,128)S(1)} %get-tuple-element.38), channel_id=1, source_target_pairs={{0,47},{1,32},{2,33},{3,34},{4,35},{5,36},{6,37},{7,38},{8,39},{9,... | collective-permute-start | bytes 552968 | tf_op jit(solution)/shard_map/ppermute | solution.py:401
  34.2 0.0 collective-permute-done.9.y_in
  34.2 2.7 %collective-permute-done.10.y_out = f32[360,128]{1,0:T(8,128)S(1)} collective-permute-done((f32[360,128]{1,0:T(8,128)S(1)}, f32[360,128]{1,0:T(8,128)S(1)}, u32[]{:S(2)}, u32[]{:S(2)}) %collective-permute-start.10) | collective-permute-done | bytes 184352 | tf_op jit(solution)/shard_map/ppermute | solution.py:401
  36.9 0.6 corners.1
  37.6 0.1 collective-permute-start.11
  37.7 4.8 %collective-permute-start.12 = (f32[120,128]{1,0:T(8,128)S(1)}, f32[120,128]{1,0:T(8,128)S(1)}, u32[]{:S(2)}, u32[]{:S(2)}) collective-permute-start(f32[120,128]{1,0:T(8,128)S(1)} %get-tuple-element.48), channel_id=1, source_target_pairs={{0,47},{1,32},{2,33},{3,34},{4,35},{5,36},{6,37},{7,38},{8,39},{9,... | collective-permute-start | bytes 184328 | tf_op jit(solution)/shard_map/ppermute | solution.py:401
  42.4 0.0 collective-permute-done.7.x_in
  42.5 0.6 collective-permute-done.8.x_out
  43.0 3.7 %begin.1 = (f32[1680,128]{1,0:T(8,128)S(1)}, f32[1680,128]{1,0:T(8,128)S(1)}, f32[1680,128]{1,0:T(8,128)S(1)}, f32[1680,128]{1,0:T(8,128)S(1)}, f32[1680,128]{1,0:T(8,128)S(1)}, /*index=5*/f32[1680,128]{1,0:T(8,128)S(1)}) custom-call(s32[3]{0:T(128)S(1)} %pad_add_fusion.pos.refs_0_, f32[960,128]{1,0:T(8,128)S(1)} %get-tuple-element.36.cur, ...), custom_call_target="tpu_custom_call" | custom-call | bytes 10000000 | tf_op jit(solution)/shard_map/begin/pallas_call | solution.py:480
  46.8 0.0 collective-permute-done.11.refs_4_
  46.8 0.0 collective-permute-done.12.refs_5_
  46.8 5.2 %finish.1.mine = f32[24,5,8,128]{3,2,1,0:T(8,128)S(1)} custom-call(s32[3]{0:T(128)S(1)} %pad_add_fusion.pos.refs_0_, f32[1680,128]{1,0:T(8,128)S(1)} %get-tuple-element.41.main, f32[1680,128]{1,0:T(8,128)S(1)} %get-tuple-element.42.side_rows, f32[1680,128]{1,0:T(8,128)S(1)} %get-tuple-element.43.refs_0_, f32[1680,128]{1,0:T(8,128)S(1)} %get-tuple-element.44.refs_1_, ...), custom_call_target="tpu_custom_call" | custom-call | tf_op jit(solution)/shard_map/finish/pallas_call | solution.py:489
  52.0 1.3 %collective-permute-start.13 = (f32[24,5,8,128]{3,2,1,0:T(8,128)S(1)}, f32[24,5,8,128]{3,2,1,0:T(8,128)S(1)}, u32[]{:S(2)}, u32[]{:S(2)}) collective-permute-start(f32[24,5,8,128]{3,2,1,0:T(8,128)S(1)} %finish.1.mine), channel_id=1, source_target_pairs={{0,16},{1,17},{2,18},{3,19},{4,20},{5,21},{6,22},{7,23},{8,24},{9,... | collective-permute-start | bytes 1474568 | tf_op jit(solution)/shard_map/ppermute | solution.py:401
  53.2 1.5 %collective-permute-done.13.other = f32[24,5,8,128]{3,2,1,0:T(8,128)S(1)} collective-permute-done((f32[24,5,8,128]{3,2,1,0:T(8,128)S(1)}, f32[24,5,8,128]{3,2,1,0:T(8,128)S(1)}, u32[]{:S(2)}, u32[]{:S(2)}) %collective-permute-start.13) | collective-permute-done | bytes 491552 | tf_op jit(solution)/shard_map/ppermute | solution.py:401
  54.7 0.7 pack_out.1
  55.4 0.1 collective-permute-start.14
  55.5 4.0 %collective-permute-start.15 = (f32[7,5,8,128]{3,2,1,0:T(8,128)S(1)}, f32[7,5,8,128]{3,2,1,0:T(8,128)S(1)}, u32[]{:S(2)}, u32[]{:S(2)}) collective-permute-start(f32[7,5,8,128]{3,2,1,0:T(8,128)S(1)} %get-tuple-element.50), channel_id=1, source_target_pairs={{0,32},{1,33},{2,34},{3,35},{4,36},{5,37},{6,38},{7,39},{8,40},{9,... | collective-permute-start | bytes 430088 | tf_op jit(solution)/shard_map/ppermute | solution.py:401
  59.5 0.0 collective-permute-start.16
  59.5 1.2 %unpack_out.2.refs_4_ = f32[7,5,16,256]{3,2,1,0:T(8,128)} custom-call(s32[3]{0:T(128)S(1)} %pad_add_fusion.pos.refs_0_, f32[7,5,8,128]{3,2,1,0:T(8,128)S(1)} %get-tuple-element.52.refs_1_), custom_call_target="tpu_custom_call" | custom-call | tf_op jit(solution)/shard_map/unpack_out/pallas_call | solution.py:512
  60.7 1.2 %collective-permute-done.14.refs_1_ = f32[7,5,8,128]{3,2,1,0:T(8,128)S(1)} collective-permute-done((f32[7,5,8,128]{3,2,1,0:T(8,128)S(1)}, f32[7,5,8,128]{3,2,1,0:T(8,128)S(1)}, u32[]{:S(2)}, u32[]{:S(2)}) %collective-permute-start.14) | collective-permute-done | bytes 143392 | tf_op jit(solution)/shard_map/ppermute | solution.py:401
  61.9 4.2 %collective-permute-done.15.refs_2_ = f32[7,5,8,128]{3,2,1,0:T(8,128)S(1)} collective-permute-done((f32[7,5,8,128]{3,2,1,0:T(8,128)S(1)}, f32[7,5,8,128]{3,2,1,0:T(8,128)S(1)}, u32[]{:S(2)}, u32[]{:S(2)}) %collective-permute-start.15) | collective-permute-done | bytes 143392 | tf_op jit(solution)/shard_map/ppermute | solution.py:401
  66.1 0.0 collective-permute-done.16.refs_3_
  66.1 1.3 %unpack_out.3 = f32[7,5,16,256]{3,2,1,0:T(8,128)} custom-call(s32[3]{0:T(128)S(1)} %pad_add_fusion.pos.refs_0_, f32[7,5,8,128]{3,2,1,0:T(8,128)S(1)} %collective-permute-done.14.refs_1_, f32[7,5,8,128]{3,2,1,0:T(8,128)S(1)} %collective-permute-done.15.refs_2_, f32[7,5,8,128]{3,2,1,0:T(8,128)S(1)} %collective-permute-done.16.refs_3_, ...), custom_call_target="tpu_custom_call", output_to_operand_aliasing={{}: (4, {})} | custom-call | tf_op jit(solution)/shard_map/unpack_out/pallas_call | solution.py:512
Async XLA Ops:
  0.1 1.2 %copy-start = (f32[11,5,16,256]{3,2,1,0:T(8,128)S(1)}, f32[11,5,16,256]{3,2,1,0:T(8,128)}, u32[]{:S(2)}) copy-start(f32[11,5,16,256]{3,2,1,0:T(8,128)} %cells.1) | copy-start | bytes 2703364
  1.3 6.5 %copy-start.1 = (s32[128,11]{0,1:T(8,128)S(1)}, s32[128,11]{0,1:T(8,128)}, u32[]{:S(2)}) copy-start(s32[128,11]{0,1:T(8,128)} %param.3) | copy-start | bytes 16900
  1.9 10.2 %collective-permute-start.1 = (f32[11,5,8,128]{3,2,1,0:T(8,128)S(1)}, f32[11,5,8,128]{3,2,1,0:T(8,128)S(1)}, u32[]{:S(2)}, u32[]{:S(2)}) collective-permute-start(f32[11,5,8,128]{3,2,1,0:T(8,128)S(1)} %get-tuple-element.33), channel_id=1, source_target_pairs={{0,32},{1,33},{2,34},{3,35},{4,36},{5,37},{6,38},{7,39},{8,40},{9,... | collective-permute-start | bytes 675848 | tf_op jit(solution)/shard_map/ppermute | solution.py:401
  4.5 13.1 %collective-permute-start.3 = (f32[11,5,8,128]{3,2,1,0:T(8,128)S(1)}, f32[11,5,8,128]{3,2,1,0:T(8,128)S(1)}, u32[]{:S(2)}, u32[]{:S(2)}) collective-permute-start(f32[11,5,8,128]{3,2,1,0:T(8,128)S(1)} %get-tuple-element.34), channel_id=1, source_target_pairs={{0,64},{1,65},{2,66},{3,67},{4,68},{5,69},{6,70},{7,71},{8,72},{9,... | collective-permute-start | bytes 675848 | tf_op jit(solution)/shard_map/ppermute | solution.py:401
  7.8 12.2 %collective-permute-start.5 = (f32[11,5,8,128]{3,2,1,0:T(8,128)S(1)}, f32[11,5,8,128]{3,2,1,0:T(8,128)S(1)}, u32[]{:S(2)}, u32[]{:S(2)}) collective-permute-start(f32[11,5,8,128]{3,2,1,0:T(8,128)S(1)} %get-tuple-element.35), channel_id=1, source_target_pairs={{0,96},{1,97},{2,98},{3,99},{4,100},{5,101},{6,102},{7,103},{8,104... | collective-permute-start | bytes 675848 | tf_op jit(solution)/shard_map/ppermute | solution.py:401
  10.8 10.9 %collective-permute-start = (f32[11,5,8,128]{3,2,1,0:T(8,128)S(1)}, f32[11,5,8,128]{3,2,1,0:T(8,128)S(1)}, u32[]{:S(2)}, u32[]{:S(2)}) collective-permute-start(f32[11,5,8,128]{3,2,1,0:T(8,128)S(1)} %get-tuple-element.32.refs_0_), channel_id=1, source_target_pairs={{0,16},{1,17},{2,18},{3,19},{4,20},{5,21},{6,22},{7,23},{8,24},{9,... | collective-permute-start | bytes 675848 | tf_op jit(solution)/shard_map/ppermute | solution.py:401
  12.2 9.6 %collective-permute-start.2 = (f32[11,5,8,128]{3,2,1,0:T(8,128)S(1)}, f32[11,5,8,128]{3,2,1,0:T(8,128)S(1)}, u32[]{:S(2)}, u32[]{:S(2)}) collective-permute-start(f32[11,5,8,128]{3,2,1,0:T(8,128)S(1)} %collective-permute-done.1.refs_2_), channel_id=1, source_target_pairs={{0,16},{1,17},{2,18},{3,19},{4,20},{5,21},{6,22},{7,23},{8,24},{9,... | collective-permute-start | bytes 675848 | tf_op jit(solution)/shard_map/ppermute | solution.py:401
  17.6 4.2 %collective-permute-start.4 = (f32[11,5,8,128]{3,2,1,0:T(8,128)S(1)}, f32[11,5,8,128]{3,2,1,0:T(8,128)S(1)}, u32[]{:S(2)}, u32[]{:S(2)}) collective-permute-start(f32[11,5,8,128]{3,2,1,0:T(8,128)S(1)} %collective-permute-done.3.refs_4_), channel_id=1, source_target_pairs={{0,16},{1,17},{2,18},{3,19},{4,20},{5,21},{6,22},{7,23},{8,24},{9,... | collective-permute-start | bytes 675848 | tf_op jit(solution)/shard_map/ppermute | solution.py:401
  19.9 2.9 %collective-permute-start.6 = (f32[11,5,8,128]{3,2,1,0:T(8,128)S(1)}, f32[11,5,8,128]{3,2,1,0:T(8,128)S(1)}, u32[]{:S(2)}, u32[]{:S(2)}) collective-permute-start(f32[11,5,8,128]{3,2,1,0:T(8,128)S(1)} %collective-permute-done.5.refs_6_), channel_id=1, source_target_pairs={{0,16},{1,17},{2,18},{3,19},{4,20},{5,21},{6,22},{7,23},{8,24},{9,... | collective-permute-start | bytes 675848 | tf_op jit(solution)/shard_map/ppermute | solution.py:401
  24.5 9.7 %collective-permute-start.9 = (f32[360,128]{1,0:T(8,128)S(1)}, f32[360,128]{1,0:T(8,128)S(1)}, u32[]{:S(2)}, u32[]{:S(2)}) collective-permute-start(f32[360,128]{1,0:T(8,128)S(1)} %get-tuple-element.39), channel_id=1, source_target_pairs={{0,96},{1,97},{2,98},{3,99},{4,100},{5,101},{6,102},{7,103},{8,104... | collective-permute-start | bytes 552968 | tf_op jit(solution)/shard_map/ppermute | solution.py:401
  24.6 12.3 %collective-permute-start.10 = (f32[360,128]{1,0:T(8,128)S(1)}, f32[360,128]{1,0:T(8,128)S(1)}, u32[]{:S(2)}, u32[]{:S(2)}) collective-permute-start(f32[360,128]{1,0:T(8,128)S(1)} %get-tuple-element.40), channel_id=1, source_target_pairs={{0,127},{1,112},{2,113},{3,114},{4,115},{5,116},{6,117},{7,118},{8... | collective-permute-start | bytes 552968 | tf_op jit(solution)/shard_map/ppermute | solution.py:401
  32.5 10.0 %collective-permute-start.7 = (f32[360,128]{1,0:T(8,128)S(1)}, f32[360,128]{1,0:T(8,128)S(1)}, u32[]{:S(2)}, u32[]{:S(2)}) collective-permute-start(f32[360,128]{1,0:T(8,128)S(1)} %get-tuple-element.37), channel_id=1, source_target_pairs={{0,32},{1,33},{2,34},{3,35},{4,36},{5,37},{6,38},{7,39},{8,40},{9,... | collective-permute-start | bytes 552968 | tf_op jit(solution)/shard_map/ppermute | solution.py:401
  32.5 10.6 %collective-permute-start.8 = (f32[360,128]{1,0:T(8,128)S(1)}, f32[360,128]{1,0:T(8,128)S(1)}, u32[]{:S(2)}, u32[]{:S(2)}) collective-permute-start(f32[360,128]{1,0:T(8,128)S(1)} %get-tuple-element.38), channel_id=1, source_target_pairs={{0,47},{1,32},{2,33},{3,34},{4,35},{5,36},{6,37},{7,38},{8,39},{9,... | collective-permute-start | bytes 552968 | tf_op jit(solution)/shard_map/ppermute | solution.py:401
  37.6 9.2 %collective-permute-start.11 = (f32[120,128]{1,0:T(8,128)S(1)}, f32[120,128]{1,0:T(8,128)S(1)}, u32[]{:S(2)}, u32[]{:S(2)}) collective-permute-start(f32[120,128]{1,0:T(8,128)S(1)} %get-tuple-element.47), channel_id=1, source_target_pairs={{0,32},{1,33},{2,34},{3,35},{4,36},{5,37},{6,38},{7,39},{8,40},{9,... | collective-permute-start | bytes 184328 | tf_op jit(solution)/shard_map/ppermute | solution.py:401
  37.7 9.1 %collective-permute-start.12 = (f32[120,128]{1,0:T(8,128)S(1)}, f32[120,128]{1,0:T(8,128)S(1)}, u32[]{:S(2)}, u32[]{:S(2)}) collective-permute-start(f32[120,128]{1,0:T(8,128)S(1)} %get-tuple-element.48), channel_id=1, source_target_pairs={{0,47},{1,32},{2,33},{3,34},{4,35},{5,36},{6,37},{7,38},{8,39},{9,... | collective-permute-start | bytes 184328 | tf_op jit(solution)/shard_map/ppermute | solution.py:401
  52.0 2.7 %collective-permute-start.13 = (f32[24,5,8,128]{3,2,1,0:T(8,128)S(1)}, f32[24,5,8,128]{3,2,1,0:T(8,128)S(1)}, u32[]{:S(2)}, u32[]{:S(2)}) collective-permute-start(f32[24,5,8,128]{3,2,1,0:T(8,128)S(1)} %finish.1.mine), channel_id=1, source_target_pairs={{0,16},{1,17},{2,18},{3,19},{4,20},{5,21},{6,22},{7,23},{8,24},{9,... | collective-permute-start | bytes 1474568 | tf_op jit(solution)/shard_map/ppermute | solution.py:401
  55.4 6.6 %collective-permute-start.14 = (f32[7,5,8,128]{3,2,1,0:T(8,128)S(1)}, f32[7,5,8,128]{3,2,1,0:T(8,128)S(1)}, u32[]{:S(2)}, u32[]{:S(2)}) collective-permute-start(f32[7,5,8,128]{3,2,1,0:T(8,128)S(1)} %get-tuple-element.49), channel_id=1, source_target_pairs={{0,64},{1,65},{2,66},{3,67},{4,68},{5,69},{6,70},{7,71},{8,72},{9,... | collective-permute-start | bytes 430088 | tf_op jit(solution)/shard_map/ppermute | solution.py:401
  55.5 10.6 %collective-permute-start.15 = (f32[7,5,8,128]{3,2,1,0:T(8,128)S(1)}, f32[7,5,8,128]{3,2,1,0:T(8,128)S(1)}, u32[]{:S(2)}, u32[]{:S(2)}) collective-permute-start(f32[7,5,8,128]{3,2,1,0:T(8,128)S(1)} %get-tuple-element.50), channel_id=1, source_target_pairs={{0,32},{1,33},{2,34},{3,35},{4,36},{5,37},{6,38},{7,39},{8,40},{9,... | collective-permute-start | bytes 430088 | tf_op jit(solution)/shard_map/ppermute | solution.py:401
  59.5 6.6 %collective-permute-start.16 = (f32[7,5,8,128]{3,2,1,0:T(8,128)S(1)}, f32[7,5,8,128]{3,2,1,0:T(8,128)S(1)}, u32[]{:S(2)}, u32[]{:S(2)}) collective-permute-start(f32[7,5,8,128]{3,2,1,0:T(8,128)S(1)} %get-tuple-element.51), channel_id=1, source_target_pairs={{0,96},{1,97},{2,98},{3,99},{4,100},{5,101},{6,102},{7,103},{8,104... | collective-permute-start | bytes 430088 | tf_op jit(solution)/shard_map/ppermute | solution.py:401

commit v11 on v10

--- a/solution.py
+++ b/solution.py
@@ -18,6 +18,7 @@
 L = 128
 DEEP = 3
 WIDE = Y + 2 * DEEP
+ORDER = (0, 2, 1, 3)
 
 GAMMA = 1.4
 STEP = 0.12
@@ -237,7 +238,7 @@
     held = refs[13]
     for i in range(8):
         for s in range(CAP):
-            held[rows[i * CAP + s]] = parts[i][s]
+            held[rows[(ORDER[i // 2] * 2 + i % 2) * CAP + s]] = parts[i][s]
 
     def convert(group, _):
         for f in range(F):
@@ -431,7 +432,7 @@
         name="table",
     )(pos, slot_blocks, parts[0])
     gathered = []
-    for k in range(4):
+    for k in ORDER:
         here = over_z(parts[k], k) if k else own
         gathered += [here, over_core(here)]
 

time: 67.6 us -> 64.6 us (0.956)
  starting transfers between devices: 30.6 us -> 27.6 us
    ppermute x17, starting transfers between devices: 30.6 us -> 27.6 us  [to(): return lax.ppermute(array, ('row', 'col'), pairs)]
  transfers between devices with their start and end apart: 17 -> 17, of which waited for: 8 -> 10; matrix products, arithmetic and copies ran while one was open for 0% -> 0% of each run, Pallas kernels for 13% -> 13%
where the time goes in v11:
time: 64.6 us; the launch traced here: 64.5 us
  starting transfers between devices  27.6 us (43%)
  Pallas kernels  18.1 us (28%)
  waiting for transfers between devices  17.3 us (27%)
  local copies, waits for them, and re-layouts  1.29 us (2%)
    ppermute x17, starting transfers between devices, to(): return lax.ppermute(array, ('row', 'col'), pairs)  27.6 us
    ppermute x17, waiting for transfers between devices, to(): return lax.ppermute(array, ('row', 'col'), pairs)  17.3 us
    pallas_call x1, Pallas kernels, body(): pl.pallas_call(finish, out_shape=shape(HALF, F, X, L), in_specs=[SMEM] +...  5.16 us
    pallas_call x1, Pallas kernels, body(): pl.pallas_call(begin, out_shape=[shape(*wide)] * 6, in_specs=[SMEM] + [VM...  3.74 us
    pallas_call x1, Pallas kernels, body(): pl.pallas_call(table, out_shape=[jax.ShapeDtypeStruct((N_ROW * 8,), jnp.i...  2.97 us
    pallas_call x2, Pallas kernels, body(): pl.pallas_call(lambda *refs, which=which: unpack_out(which, *refs), out_s...  2.56 us
    pallas_call x1, Pallas kernels, body(): pl.pallas_call(reorder, out_shape=[whole] + [layer] * 4, in_specs=[SMEM,...  1.66 us
  transfers between devices with their start and end apart: 17, of which 10 were waited for; matrix products, arithmetic and copies ran while one was open for 0% of the time, Pallas kernels for 13%

profile of v11, /device:TPU:1, one launch (start us, length us, event | category | flops | bytes accessed | tf_op | source)
XLA Modules:
  0.0 64.5 jit_solution(7168995776658644229)
XLA Ops:
  0.0 0.1 pad_add_fusion.pos.refs_0_
  0.1 0.0 copy-start
  0.1 1.2 %copy-done = f32[11,5,16,256]{3,2,1,0:T(8,128)S(1)} copy-done((f32[11,5,16,256]{3,2,1,0:T(8,128)S(1)}, f32[11,5,16,256]{3,2,1,0:T(8,128)}, u32[]{:S(2)}) %copy-start) | copy-done | bytes 901144
  1.3 0.0 copy-start.1
  1.3 0.7 %pack_in.1 = (f32[11,5,8,128]{3,2,1,0:T(8,128)S(1)}, f32[11,5,8,128]{3,2,1,0:T(8,128)S(1)}, f32[11,5,8,128]{3,2,1,0:T(8,128)S(1)}, f32[11,5,8,128]{3,2,1,0:T(8,128)S(1)}) custom-call(s32[3]{0:T(128)S(1)} %pad_add_fusion.pos.refs_0_, f32[11,5,16,256]{3,2,1,0:T(8,128)S(1)} %copy-done), custom_call_target="tpu_custom_call" | custom-call | tf_op jit(solution)/shard_map/pack_in/pallas_call | solution.py:411
  1.9 4.5 %collective-permute-start.1 = (f32[11,5,8,128]{3,2,1,0:T(8,128)S(1)}, f32[11,5,8,128]{3,2,1,0:T(8,128)S(1)}, u32[]{:S(2)}, u32[]{:S(2)}) collective-permute-start(f32[11,5,8,128]{3,2,1,0:T(8,128)S(1)} %get-tuple-element.33), channel_id=1, source_target_pairs={{0,64},{1,65},{2,66},{3,67},{4,68},{5,69},{6,70},{7,71},{8,72},{9,... | collective-permute-start | bytes 675848 | tf_op jit(solution)/shard_map/ppermute | solution.py:402
  6.4 0.7 %collective-permute-start.3 = (f32[11,5,8,128]{3,2,1,0:T(8,128)S(1)}, f32[11,5,8,128]{3,2,1,0:T(8,128)S(1)}, u32[]{:S(2)}, u32[]{:S(2)}) collective-permute-start(f32[11,5,8,128]{3,2,1,0:T(8,128)S(1)} %get-tuple-element.34), channel_id=1, source_target_pairs={{0,32},{1,33},{2,34},{3,35},{4,36},{5,37},{6,38},{7,39},{8,40},{9,... | collective-permute-start | bytes 675848 | tf_op jit(solution)/shard_map/ppermute | solution.py:402
  7.2 0.0 collective-permute-start.5
  7.2 0.0 copy-done.1
  7.2 0.1 copy.5.slots
  7.3 3.0 %table.1 = (s32[64]{0:T(128)S(1)}, s32[88]{0:T(128)S(1)}, f32[11,5,8,128]{3,2,1,0:T(8,128)S(1)}) custom-call(s32[3]{0:T(128)S(1)} %pad_add_fusion.pos.refs_0_, s32[128,11]{1,0:T(8,128)S(1)} %copy.5.slots, f32[11,5,8,128]{3,2,1,0:T(8,128)S(1)} %get-tuple-element.29._tile), custom_call_target="tpu_custom_call", output_to_operand_aliasing={{2}: (2, {})} | custom-call | bytes 20000000 | tf_op jit(solution)/shard_map/table/pallas_call | solution.py:419
  10.3 1.3 %collective-permute-start = (f32[11,5,8,128]{3,2,1,0:T(8,128)S(1)}, f32[11,5,8,128]{3,2,1,0:T(8,128)S(1)}, u32[]{:S(2)}, u32[]{:S(2)}) collective-permute-start(f32[11,5,8,128]{3,2,1,0:T(8,128)S(1)} %get-tuple-element.32.refs_0_), channel_id=1, source_target_pairs={{0,16},{1,17},{2,18},{3,19},{4,20},{5,21},{6,22},{7,23},{8,24},{9,... | collective-permute-start | bytes 675848 | tf_op jit(solution)/shard_map/ppermute | solution.py:402
  11.6 0.1 collective-permute-done.1.refs_2_
  11.7 2.1 %collective-permute-start.2 = (f32[11,5,8,128]{3,2,1,0:T(8,128)S(1)}, f32[11,5,8,128]{3,2,1,0:T(8,128)S(1)}, u32[]{:S(2)}, u32[]{:S(2)}) collective-permute-start(f32[11,5,8,128]{3,2,1,0:T(8,128)S(1)} %collective-permute-done.1.refs_2_), channel_id=1, source_target_pairs={{0,16},{1,17},{2,18},{3,19},{4,20},{5,21},{6,22},{7,23},{8,24},{9,... | collective-permute-start | bytes 675848 | tf_op jit(solution)/shard_map/ppermute | solution.py:402
  13.7 3.2 %collective-permute-done.3.refs_4_ = f32[11,5,8,128]{3,2,1,0:T(8,128)S(1)} collective-permute-done((f32[11,5,8,128]{3,2,1,0:T(8,128)S(1)}, f32[11,5,8,128]{3,2,1,0:T(8,128)S(1)}, u32[]{:S(2)}, u32[]{:S(2)}) %collective-permute-start.3) | collective-permute-done | bytes 225312 | tf_op jit(solution)/shard_map/ppermute | solution.py:402
  17.0 1.5 %collective-permute-start.4 = (f32[11,5,8,128]{3,2,1,0:T(8,128)S(1)}, f32[11,5,8,128]{3,2,1,0:T(8,128)S(1)}, u32[]{:S(2)}, u32[]{:S(2)}) collective-permute-start(f32[11,5,8,128]{3,2,1,0:T(8,128)S(1)} %collective-permute-done.3.refs_4_), channel_id=1, source_target_pairs={{0,16},{1,17},{2,18},{3,19},{4,20},{5,21},{6,22},{7,23},{8,24},{9,... | collective-permute-start | bytes 675848 | tf_op jit(solution)/shard_map/ppermute | solution.py:402
  18.5 0.0 collective-permute-done.5.refs_6_
  18.5 0.0 collective-permute-start.6
  18.5 0.0 collective-permute-done.refs_1_
  18.5 0.0 collective-permute-done.2.refs_3_
  18.5 1.1 %collective-permute-done.4.refs_5_ = f32[11,5,8,128]{3,2,1,0:T(8,128)S(1)} collective-permute-done((f32[11,5,8,128]{3,2,1,0:T(8,128)S(1)}, f32[11,5,8,128]{3,2,1,0:T(8,128)S(1)}, u32[]{:S(2)}, u32[]{:S(2)}) %collective-permute-start.4) | collective-permute-done | bytes 225312 | tf_op jit(solution)/shard_map/ppermute | solution.py:402
  19.6 0.4 collective-permute-done.6.refs_7_
  20.0 1.7 %reorder.1 = (f32[960,128]{1,0:T(8,128)S(1)}, f32[360,128]{1,0:T(8,128)S(1)}, f32[360,128]{1,0:T(8,128)S(1)}, f32[360,128]{1,0:T(8,128)S(1)}, f32[360,128]{1,0:T(8,128)S(1)}) custom-call(s32[3]{0:T(128)S(1)} %pad_add_fusion.pos.refs_0_, s32[88]{0:T(128)S(1)} %get-tuple-element.31.rows, f32[11,5,8,128]{3,2,1,0:T(8,128)S(1)} %get-tuple-element.32.refs_0_, ...), custom_call_target="tpu_custom_call" | custom-call | tf_op jit(solution)/shard_map/reorder/pallas_call | solution.py:441
  21.7 2.1 %collective-permute-start.9 = (f32[360,128]{1,0:T(8,128)S(1)}, f32[360,128]{1,0:T(8,128)S(1)}, u32[]{:S(2)}, u32[]{:S(2)}) collective-permute-start(f32[360,128]{1,0:T(8,128)S(1)} %get-tuple-element.39), channel_id=1, source_target_pairs={{0,96},{1,97},{2,98},{3,99},{4,100},{5,101},{6,102},{7,103},{8,104... | collective-permute-start | bytes 552968 | tf_op jit(solution)/shard_map/ppermute | solution.py:402
  23.7 5.8 %collective-permute-start.10 = (f32[360,128]{1,0:T(8,128)S(1)}, f32[360,128]{1,0:T(8,128)S(1)}, u32[]{:S(2)}, u32[]{:S(2)}) collective-permute-start(f32[360,128]{1,0:T(8,128)S(1)} %get-tuple-element.40), channel_id=1, source_target_pairs={{0,127},{1,112},{2,113},{3,114},{4,115},{5,116},{6,117},{7,118},{8... | collective-permute-start | bytes 552968 | tf_op jit(solution)/shard_map/ppermute | solution.py:402
  29.6 0.0 collective-permute-start.7
  29.6 1.7 %collective-permute-start.8 = (f32[360,128]{1,0:T(8,128)S(1)}, f32[360,128]{1,0:T(8,128)S(1)}, u32[]{:S(2)}, u32[]{:S(2)}) collective-permute-start(f32[360,128]{1,0:T(8,128)S(1)} %get-tuple-element.38), channel_id=1, source_target_pairs={{0,47},{1,32},{2,33},{3,34},{4,35},{5,36},{6,37},{7,38},{8,39},{9,... | collective-permute-start | bytes 552968 | tf_op jit(solution)/shard_map/ppermute | solution.py:402
  31.3 0.0 collective-permute-done.9.y_in
  31.3 5.0 %collective-permute-done.10.y_out = f32[360,128]{1,0:T(8,128)S(1)} collective-permute-done((f32[360,128]{1,0:T(8,128)S(1)}, f32[360,128]{1,0:T(8,128)S(1)}, u32[]{:S(2)}, u32[]{:S(2)}) %collective-permute-start.10) | collective-permute-done | bytes 184352 | tf_op jit(solution)/shard_map/ppermute | solution.py:402
  36.3 0.6 corners.1
  36.9 0.1 collective-permute-start.11
  37.0 2.8 %collective-permute-start.12 = (f32[120,128]{1,0:T(8,128)S(1)}, f32[120,128]{1,0:T(8,128)S(1)}, u32[]{:S(2)}, u32[]{:S(2)}) collective-permute-start(f32[120,128]{1,0:T(8,128)S(1)} %get-tuple-element.48), channel_id=1, source_target_pairs={{0,47},{1,32},{2,33},{3,34},{4,35},{5,36},{6,37},{7,38},{8,39},{9,... | collective-permute-start | bytes 184328 | tf_op jit(solution)/shard_map/ppermute | solution.py:402
  39.9 0.0 collective-permute-done.7.x_in
  39.9 0.3 collective-permute-done.8.x_out
  40.1 3.7 %begin.1 = (f32[1680,128]{1,0:T(8,128)S(1)}, f32[1680,128]{1,0:T(8,128)S(1)}, f32[1680,128]{1,0:T(8,128)S(1)}, f32[1680,128]{1,0:T(8,128)S(1)}, f32[1680,128]{1,0:T(8,128)S(1)}, /*index=5*/f32[1680,128]{1,0:T(8,128)S(1)}) custom-call(s32[3]{0:T(128)S(1)} %pad_add_fusion.pos.refs_0_, f32[960,128]{1,0:T(8,128)S(1)} %get-tuple-element.36.cur, ...), custom_call_target="tpu_custom_call" | custom-call | bytes 10000000 | tf_op jit(solution)/shard_map/begin/pallas_call | solution.py:481
  43.9 0.0 collective-permute-done.11.refs_4_
  43.9 0.5 collective-permute-done.12.refs_5_
  44.4 5.2 %finish.1.mine = f32[24,5,8,128]{3,2,1,0:T(8,128)S(1)} custom-call(s32[3]{0:T(128)S(1)} %pad_add_fusion.pos.refs_0_, f32[1680,128]{1,0:T(8,128)S(1)} %get-tuple-element.41.main, f32[1680,128]{1,0:T(8,128)S(1)} %get-tuple-element.42.side_rows, f32[1680,128]{1,0:T(8,128)S(1)} %get-tuple-element.43.refs_0_, f32[1680,128]{1,0:T(8,128)S(1)} %get-tuple-element.44.refs_1_, ...), custom_call_target="tpu_custom_call" | custom-call | tf_op jit(solution)/shard_map/finish/pallas_call | solution.py:490
  49.6 1.6 %collective-permute-start.13 = (f32[24,5,8,128]{3,2,1,0:T(8,128)S(1)}, f32[24,5,8,128]{3,2,1,0:T(8,128)S(1)}, u32[]{:S(2)}, u32[]{:S(2)}) collective-permute-start(f32[24,5,8,128]{3,2,1,0:T(8,128)S(1)} %finish.1.mine), channel_id=1, source_target_pairs={{0,16},{1,17},{2,18},{3,19},{4,20},{5,21},{6,22},{7,23},{8,24},{9,... | collective-permute-start | bytes 1474568 | tf_op jit(solution)/shard_map/ppermute | solution.py:402
  51.2 1.5 %collective-permute-done.13.other = f32[24,5,8,128]{3,2,1,0:T(8,128)S(1)} collective-permute-done((f32[24,5,8,128]{3,2,1,0:T(8,128)S(1)}, f32[24,5,8,128]{3,2,1,0:T(8,128)S(1)}, u32[]{:S(2)}, u32[]{:S(2)}) %collective-permute-start.13) | collective-permute-done | bytes 491552 | tf_op jit(solution)/shard_map/ppermute | solution.py:402
  52.7 0.7 %pack_out.1 = (f32[7,5,8,128]{3,2,1,0:T(8,128)S(1)}, f32[7,5,8,128]{3,2,1,0:T(8,128)S(1)}, f32[7,5,8,128]{3,2,1,0:T(8,128)S(1)}, f32[7,5,8,128]{3,2,1,0:T(8,128)S(1)}) custom-call(s32[3]{0:T(128)S(1)} %pad_add_fusion.pos.refs_0_, s32[64]{0:T(128)S(1)} %get-tuple-element.30.final, f32[24,5,8,128]{3,2,1,0:T(8,128)S(1)} %finish.1.mine, ...), custom_call_target="tpu_custom_call" | custom-call | tf_op jit(solution)/shard_map/pack_out/pallas_call | solution.py:500
  53.3 0.1 collective-permute-start.14
  53.4 3.1 %collective-permute-start.15 = (f32[7,5,8,128]{3,2,1,0:T(8,128)S(1)}, f32[7,5,8,128]{3,2,1,0:T(8,128)S(1)}, u32[]{:S(2)}, u32[]{:S(2)}) collective-permute-start(f32[7,5,8,128]{3,2,1,0:T(8,128)S(1)} %get-tuple-element.50), channel_id=1, source_target_pairs={{0,32},{1,33},{2,34},{3,35},{4,36},{5,37},{6,38},{7,39},{8,40},{9,... | collective-permute-start | bytes 430088 | tf_op jit(solution)/shard_map/ppermute | solution.py:402
  56.5 0.2 collective-permute-start.16
  56.7 1.2 %unpack_out.2.refs_4_ = f32[7,5,16,256]{3,2,1,0:T(8,128)} custom-call(s32[3]{0:T(128)S(1)} %pad_add_fusion.pos.refs_0_, f32[7,5,8,128]{3,2,1,0:T(8,128)S(1)} %get-tuple-element.52.refs_1_), custom_call_target="tpu_custom_call" | custom-call | tf_op jit(solution)/shard_map/unpack_out/pallas_call | solution.py:513
  57.9 2.0 %collective-permute-done.14.refs_1_ = f32[7,5,8,128]{3,2,1,0:T(8,128)S(1)} collective-permute-done((f32[7,5,8,128]{3,2,1,0:T(8,128)S(1)}, f32[7,5,8,128]{3,2,1,0:T(8,128)S(1)}, u32[]{:S(2)}, u32[]{:S(2)}) %collective-permute-start.14) | collective-permute-done | bytes 143392 | tf_op jit(solution)/shard_map/ppermute | solution.py:402
  59.9 3.2 %collective-permute-done.15.refs_2_ = f32[7,5,8,128]{3,2,1,0:T(8,128)S(1)} collective-permute-done((f32[7,5,8,128]{3,2,1,0:T(8,128)S(1)}, f32[7,5,8,128]{3,2,1,0:T(8,128)S(1)}, u32[]{:S(2)}, u32[]{:S(2)}) %collective-permute-start.15) | collective-permute-done | bytes 143392 | tf_op jit(solution)/shard_map/ppermute | solution.py:402
  63.1 0.0 collective-permute-done.16.refs_3_
  63.1 1.3 %unpack_out.3 = f32[7,5,16,256]{3,2,1,0:T(8,128)} custom-call(s32[3]{0:T(128)S(1)} %pad_add_fusion.pos.refs_0_, f32[7,5,8,128]{3,2,1,0:T(8,128)S(1)} %collective-permute-done.14.refs_1_, f32[7,5,8,128]{3,2,1,0:T(8,128)S(1)} %collective-permute-done.15.refs_2_, f32[7,5,8,128]{3,2,1,0:T(8,128)S(1)} %collective-permute-done.16.refs_3_, ...), custom_call_target="tpu_custom_call", output_to_operand_aliasing={{}: (4, {})} | custom-call | tf_op jit(solution)/shard_map/unpack_out/pallas_call | solution.py:513
Async XLA Ops:
  0.1 1.2 %copy-start = (f32[11,5,16,256]{3,2,1,0:T(8,128)S(1)}, f32[11,5,16,256]{3,2,1,0:T(8,128)}, u32[]{:S(2)}) copy-start(f32[11,5,16,256]{3,2,1,0:T(8,128)} %cells.1) | copy-start | bytes 2703364
  1.3 5.9 %copy-start.1 = (s32[128,11]{0,1:T(8,128)S(1)}, s32[128,11]{0,1:T(8,128)}, u32[]{:S(2)}) copy-start(s32[128,11]{0,1:T(8,128)} %param.3) | copy-start | bytes 16900
  1.9 9.7 %collective-permute-start.1 = (f32[11,5,8,128]{3,2,1,0:T(8,128)S(1)}, f32[11,5,8,128]{3,2,1,0:T(8,128)S(1)}, u32[]{:S(2)}, u32[]{:S(2)}) collective-permute-start(f32[11,5,8,128]{3,2,1,0:T(8,128)S(1)} %get-tuple-element.33), channel_id=1, source_target_pairs={{0,64},{1,65},{2,66},{3,67},{4,68},{5,69},{6,70},{7,71},{8,72},{9,... | collective-permute-start | bytes 675848 | tf_op jit(solution)/shard_map/ppermute | solution.py:402
  6.4 10.5 %collective-permute-start.3 = (f32[11,5,8,128]{3,2,1,0:T(8,128)S(1)}, f32[11,5,8,128]{3,2,1,0:T(8,128)S(1)}, u32[]{:S(2)}, u32[]{:S(2)}) collective-permute-start(f32[11,5,8,128]{3,2,1,0:T(8,128)S(1)} %get-tuple-element.34), channel_id=1, source_target_pairs={{0,32},{1,33},{2,34},{3,35},{4,36},{5,37},{6,38},{7,39},{8,40},{9,... | collective-permute-start | bytes 675848 | tf_op jit(solution)/shard_map/ppermute | solution.py:402
  7.2 11.3 %collective-permute-start.5 = (f32[11,5,8,128]{3,2,1,0:T(8,128)S(1)}, f32[11,5,8,128]{3,2,1,0:T(8,128)S(1)}, u32[]{:S(2)}, u32[]{:S(2)}) collective-permute-start(f32[11,5,8,128]{3,2,1,0:T(8,128)S(1)} %get-tuple-element.35), channel_id=1, source_target_pairs={{0,96},{1,97},{2,98},{3,99},{4,100},{5,101},{6,102},{7,103},{8,104... | collective-permute-start | bytes 675848 | tf_op jit(solution)/shard_map/ppermute | solution.py:402
  10.3 8.2 %collective-permute-start = (f32[11,5,8,128]{3,2,1,0:T(8,128)S(1)}, f32[11,5,8,128]{3,2,1,0:T(8,128)S(1)}, u32[]{:S(2)}, u32[]{:S(2)}) collective-permute-start(f32[11,5,8,128]{3,2,1,0:T(8,128)S(1)} %get-tuple-element.32.refs_0_), channel_id=1, source_target_pairs={{0,16},{1,17},{2,18},{3,19},{4,20},{5,21},{6,22},{7,23},{8,24},{9,... | collective-permute-start | bytes 675848 | tf_op jit(solution)/shard_map/ppermute | solution.py:402
  11.7 6.8 %collective-permute-start.2 = (f32[11,5,8,128]{3,2,1,0:T(8,128)S(1)}, f32[11,5,8,128]{3,2,1,0:T(8,128)S(1)}, u32[]{:S(2)}, u32[]{:S(2)}) collective-permute-start(f32[11,5,8,128]{3,2,1,0:T(8,128)S(1)} %collective-permute-done.1.refs_2_), channel_id=1, source_target_pairs={{0,16},{1,17},{2,18},{3,19},{4,20},{5,21},{6,22},{7,23},{8,24},{9,... | collective-permute-start | bytes 675848 | tf_op jit(solution)/shard_map/ppermute | solution.py:402
  17.0 2.7 %collective-permute-start.4 = (f32[11,5,8,128]{3,2,1,0:T(8,128)S(1)}, f32[11,5,8,128]{3,2,1,0:T(8,128)S(1)}, u32[]{:S(2)}, u32[]{:S(2)}) collective-permute-start(f32[11,5,8,128]{3,2,1,0:T(8,128)S(1)} %collective-permute-done.3.refs_4_), channel_id=1, source_target_pairs={{0,16},{1,17},{2,18},{3,19},{4,20},{5,21},{6,22},{7,23},{8,24},{9,... | collective-permute-start | bytes 675848 | tf_op jit(solution)/shard_map/ppermute | solution.py:402
  18.5 1.5 %collective-permute-start.6 = (f32[11,5,8,128]{3,2,1,0:T(8,128)S(1)}, f32[11,5,8,128]{3,2,1,0:T(8,128)S(1)}, u32[]{:S(2)}, u32[]{:S(2)}) collective-permute-start(f32[11,5,8,128]{3,2,1,0:T(8,128)S(1)} %collective-permute-done.5.refs_6_), channel_id=1, source_target_pairs={{0,16},{1,17},{2,18},{3,19},{4,20},{5,21},{6,22},{7,23},{8,24},{9,... | collective-permute-start | bytes 675848 | tf_op jit(solution)/shard_map/ppermute | solution.py:402
  21.7 9.6 %collective-permute-start.9 = (f32[360,128]{1,0:T(8,128)S(1)}, f32[360,128]{1,0:T(8,128)S(1)}, u32[]{:S(2)}, u32[]{:S(2)}) collective-permute-start(f32[360,128]{1,0:T(8,128)S(1)} %get-tuple-element.39), channel_id=1, source_target_pairs={{0,96},{1,97},{2,98},{3,99},{4,100},{5,101},{6,102},{7,103},{8,104... | collective-permute-start | bytes 552968 | tf_op jit(solution)/shard_map/ppermute | solution.py:402
  23.7 12.6 %collective-permute-start.10 = (f32[360,128]{1,0:T(8,128)S(1)}, f32[360,128]{1,0:T(8,128)S(1)}, u32[]{:S(2)}, u32[]{:S(2)}) collective-permute-start(f32[360,128]{1,0:T(8,128)S(1)} %get-tuple-element.40), channel_id=1, source_target_pairs={{0,127},{1,112},{2,113},{3,114},{4,115},{5,116},{6,117},{7,118},{8... | collective-permute-start | bytes 552968 | tf_op jit(solution)/shard_map/ppermute | solution.py:402
  29.6 10.3 %collective-permute-start.7 = (f32[360,128]{1,0:T(8,128)S(1)}, f32[360,128]{1,0:T(8,128)S(1)}, u32[]{:S(2)}, u32[]{:S(2)}) collective-permute-start(f32[360,128]{1,0:T(8,128)S(1)} %get-tuple-element.37), channel_id=1, source_target_pairs={{0,32},{1,33},{2,34},{3,35},{4,36},{5,37},{6,38},{7,39},{8,40},{9,... | collective-permute-start | bytes 552968 | tf_op jit(solution)/shard_map/ppermute | solution.py:402
  29.6 10.6 %collective-permute-start.8 = (f32[360,128]{1,0:T(8,128)S(1)}, f32[360,128]{1,0:T(8,128)S(1)}, u32[]{:S(2)}, u32[]{:S(2)}) collective-permute-start(f32[360,128]{1,0:T(8,128)S(1)} %get-tuple-element.38), channel_id=1, source_target_pairs={{0,47},{1,32},{2,33},{3,34},{4,35},{5,36},{6,37},{7,38},{8,39},{9,... | collective-permute-start | bytes 552968 | tf_op jit(solution)/shard_map/ppermute | solution.py:402
  36.9 7.0 %collective-permute-start.11 = (f32[120,128]{1,0:T(8,128)S(1)}, f32[120,128]{1,0:T(8,128)S(1)}, u32[]{:S(2)}, u32[]{:S(2)}) collective-permute-start(f32[120,128]{1,0:T(8,128)S(1)} %get-tuple-element.47), channel_id=1, source_target_pairs={{0,32},{1,33},{2,34},{3,35},{4,36},{5,37},{6,38},{7,39},{8,40},{9,... | collective-permute-start | bytes 184328 | tf_op jit(solution)/shard_map/ppermute | solution.py:402
  37.0 7.4 %collective-permute-start.12 = (f32[120,128]{1,0:T(8,128)S(1)}, f32[120,128]{1,0:T(8,128)S(1)}, u32[]{:S(2)}, u32[]{:S(2)}) collective-permute-start(f32[120,128]{1,0:T(8,128)S(1)} %get-tuple-element.48), channel_id=1, source_target_pairs={{0,47},{1,32},{2,33},{3,34},{4,35},{5,36},{6,37},{7,38},{8,39},{9,... | collective-permute-start | bytes 184328 | tf_op jit(solution)/shard_map/ppermute | solution.py:402
  49.6 3.1 %collective-permute-start.13 = (f32[24,5,8,128]{3,2,1,0:T(8,128)S(1)}, f32[24,5,8,128]{3,2,1,0:T(8,128)S(1)}, u32[]{:S(2)}, u32[]{:S(2)}) collective-permute-start(f32[24,5,8,128]{3,2,1,0:T(8,128)S(1)} %finish.1.mine), channel_id=1, source_target_pairs={{0,16},{1,17},{2,18},{3,19},{4,20},{5,21},{6,22},{7,23},{8,24},{9,... | collective-permute-start | bytes 1474568 | tf_op jit(solution)/shard_map/ppermute | solution.py:402
  53.3 6.6 %collective-permute-start.14 = (f32[7,5,8,128]{3,2,1,0:T(8,128)S(1)}, f32[7,5,8,128]{3,2,1,0:T(8,128)S(1)}, u32[]{:S(2)}, u32[]{:S(2)}) collective-permute-start(f32[7,5,8,128]{3,2,1,0:T(8,128)S(1)} %get-tuple-element.49), channel_id=1, source_target_pairs={{0,64},{1,65},{2,66},{3,67},{4,68},{5,69},{6,70},{7,71},{8,72},{9,... | collective-permute-start | bytes 430088 | tf_op jit(solution)/shard_map/ppermute | solution.py:402
  53.4 9.7 %collective-permute-start.15 = (f32[7,5,8,128]{3,2,1,0:T(8,128)S(1)}, f32[7,5,8,128]{3,2,1,0:T(8,128)S(1)}, u32[]{:S(2)}, u32[]{:S(2)}) collective-permute-start(f32[7,5,8,128]{3,2,1,0:T(8,128)S(1)} %get-tuple-element.50), channel_id=1, source_target_pairs={{0,32},{1,33},{2,34},{3,35},{4,36},{5,37},{6,38},{7,39},{8,40},{9,... | collective-permute-start | bytes 430088 | tf_op jit(solution)/shard_map/ppermute | solution.py:402
  56.5 6.6 %collective-permute-start.16 = (f32[7,5,8,128]{3,2,1,0:T(8,128)S(1)}, f32[7,5,8,128]{3,2,1,0:T(8,128)S(1)}, u32[]{:S(2)}, u32[]{:S(2)}) collective-permute-start(f32[7,5,8,128]{3,2,1,0:T(8,128)S(1)} %get-tuple-element.51), channel_id=1, source_target_pairs={{0,96},{1,97},{2,98},{3,99},{4,100},{5,101},{6,102},{7,103},{8,104... | collective-permute-start | bytes 430088 | tf_op jit(solution)/shard_map/ppermute | solution.py:402

commit v12 on v11

--- a/solution.py
+++ b/solution.py
@@ -360,7 +360,7 @@
 
 
 def finish(pos, main, side_rows, *refs):
-    early, (c_in, c_out, made, corner_rows), late = refs[:4], refs[4:8], refs[8:12]
+    early, (c_out, c_in, made, corner_rows), late = refs[:4], refs[4:8], refs[8:12]
     add_corners(pos, c_in, c_out, corner_rows)
 
     def initial(part, y):
@@ -495,7 +495,7 @@
         scratch_shapes=[pltpu.VMEM(wide, jnp.float32)] * 5,
         compiler_params=PARAMS,
         name="finish",
-    )(pos, *early, *corner_cells)
+    )(pos, *early, *corner_cells[::-1])
 
     leaving = pl.pallas_call(
         pack_out,

time: 64.6 us -> 65.1 us (level)
  waiting for transfers between devices: 17.3 us -> 19.9 us
  starting transfers between devices: 27.6 us -> 25.5 us
    ppermute x17, waiting for transfers between devices: 17.3 us -> 19.9 us  [to(): return lax.ppermute(array, ('row', 'col'), pairs)]
    ppermute x17, starting transfers between devices: 27.6 us -> 25.5 us  [to(): return lax.ppermute(array, ('row', 'col'), pairs)]
  transfers between devices with their start and end apart: 17 -> 17, of which waited for: 10 -> 11; matrix products, arithmetic and copies ran while one was open for 0% -> 0% of each run, Pallas kernels for 13% -> 13%
where the time goes in v12:
time: 65.1 us; the launch traced here: 64.9 us
  starting transfers between devices  25.5 us (39%)
  waiting for transfers between devices  19.9 us (31%)
  Pallas kernels  18.1 us (28%)
  local copies, waits for them, and re-layouts  1.29 us (2%)
    ppermute x17, starting transfers between devices, to(): return lax.ppermute(array, ('row', 'col'), pairs)  25.5 us
    ppermute x17, waiting for transfers between devices, to(): return lax.ppermute(array, ('row', 'col'), pairs)  19.9 us
    pallas_call x1, Pallas kernels, body(): pl.pallas_call(finish, out_shape=shape(HALF, F, X, L), in_specs=[SMEM] +...  5.16 us
    pallas_call x1, Pallas kernels, body(): pl.pallas_call(begin, out_shape=[shape(*wide)] * 6, in_specs=[SMEM] + [VM...  3.74 us
    pallas_call x1, Pallas kernels, body(): pl.pallas_call(table, out_shape=[jax.ShapeDtypeStruct((N_ROW * 8,), jnp.i...  3.03 us
    pallas_call x2, Pallas kernels, body(): pl.pallas_call(lambda *refs, which=which: unpack_out(which, *refs), out_s...  2.56 us
    pallas_call x1, Pallas kernels, body(): pl.pallas_call(reorder, out_shape=[whole] + [layer] * 4, in_specs=[SMEM,...  1.66 us
  transfers between devices with their start and end apart: 17, of which 11 were waited for; matrix products, arithmetic and copies ran while one was open for 0% of the time, Pallas kernels for 13%

profile of v12, /device:TPU:1, one launch (start us, length us, event | category | flops | bytes accessed | tf_op | source)
XLA Modules:
  0.0 64.9 jit_solution(12228182013200893272)
XLA Ops:
  0.0 0.1 pad_add_fusion.pos.refs_0_
  0.1 0.0 copy-start
  0.1 1.2 %copy-done = f32[11,5,16,256]{3,2,1,0:T(8,128)S(1)} copy-done((f32[11,5,16,256]{3,2,1,0:T(8,128)S(1)}, f32[11,5,16,256]{3,2,1,0:T(8,128)}, u32[]{:S(2)}) %copy-start) | copy-done | bytes 901144
  1.3 0.0 copy-start.1
  1.3 0.7 %pack_in.1 = (f32[11,5,8,128]{3,2,1,0:T(8,128)S(1)}, f32[11,5,8,128]{3,2,1,0:T(8,128)S(1)}, f32[11,5,8,128]{3,2,1,0:T(8,128)S(1)}, f32[11,5,8,128]{3,2,1,0:T(8,128)S(1)}) custom-call(s32[3]{0:T(128)S(1)} %pad_add_fusion.pos.refs_0_, f32[11,5,16,256]{3,2,1,0:T(8,128)S(1)} %copy-done), custom_call_target="tpu_custom_call" | custom-call | tf_op jit(solution)/shard_map/pack_in/pallas_call | solution.py:411
  1.9 4.5 %collective-permute-start.1 = (f32[11,5,8,128]{3,2,1,0:T(8,128)S(1)}, f32[11,5,8,128]{3,2,1,0:T(8,128)S(1)}, u32[]{:S(2)}, u32[]{:S(2)}) collective-permute-start(f32[11,5,8,128]{3,2,1,0:T(8,128)S(1)} %get-tuple-element.33), channel_id=1, source_target_pairs={{0,64},{1,65},{2,66},{3,67},{4,68},{5,69},{6,70},{7,71},{8,72},{9,... | collective-permute-start | bytes 675848 | tf_op jit(solution)/shard_map/ppermute | solution.py:402
  6.4 0.7 %collective-permute-start.3 = (f32[11,5,8,128]{3,2,1,0:T(8,128)S(1)}, f32[11,5,8,128]{3,2,1,0:T(8,128)S(1)}, u32[]{:S(2)}, u32[]{:S(2)}) collective-permute-start(f32[11,5,8,128]{3,2,1,0:T(8,128)S(1)} %get-tuple-element.34), channel_id=1, source_target_pairs={{0,32},{1,33},{2,34},{3,35},{4,36},{5,37},{6,38},{7,39},{8,40},{9,... | collective-permute-start | bytes 675848 | tf_op jit(solution)/shard_map/ppermute | solution.py:402
  7.2 0.0 collective-permute-start.5
  7.2 0.0 copy-done.1
  7.2 0.1 copy.5.slots
  7.3 3.0 %table.1 = (s32[64]{0:T(128)S(1)}, s32[88]{0:T(128)S(1)}, f32[11,5,8,128]{3,2,1,0:T(8,128)S(1)}) custom-call(s32[3]{0:T(128)S(1)} %pad_add_fusion.pos.refs_0_, s32[128,11]{1,0:T(8,128)S(1)} %copy.5.slots, f32[11,5,8,128]{3,2,1,0:T(8,128)S(1)} %get-tuple-element.29._tile), custom_call_target="tpu_custom_call", output_to_operand_aliasing={{2}: (2, {})} | custom-call | bytes 20000000 | tf_op jit(solution)/shard_map/table/pallas_call | solution.py:419
  10.3 1.3 %collective-permute-start = (f32[11,5,8,128]{3,2,1,0:T(8,128)S(1)}, f32[11,5,8,128]{3,2,1,0:T(8,128)S(1)}, u32[]{:S(2)}, u32[]{:S(2)}) collective-permute-start(f32[11,5,8,128]{3,2,1,0:T(8,128)S(1)} %get-tuple-element.32.refs_0_), channel_id=1, source_target_pairs={{0,16},{1,17},{2,18},{3,19},{4,20},{5,21},{6,22},{7,23},{8,24},{9,... | collective-permute-start | bytes 675848 | tf_op jit(solution)/shard_map/ppermute | solution.py:402
  11.7 0.0 collective-permute-done.1.refs_2_
  11.7 2.1 %collective-permute-start.2 = (f32[11,5,8,128]{3,2,1,0:T(8,128)S(1)}, f32[11,5,8,128]{3,2,1,0:T(8,128)S(1)}, u32[]{:S(2)}, u32[]{:S(2)}) collective-permute-start(f32[11,5,8,128]{3,2,1,0:T(8,128)S(1)} %collective-permute-done.1.refs_2_), channel_id=1, source_target_pairs={{0,16},{1,17},{2,18},{3,19},{4,20},{5,21},{6,22},{7,23},{8,24},{9,... | collective-permute-start | bytes 675848 | tf_op jit(solution)/shard_map/ppermute | solution.py:402
  13.7 3.2 %collective-permute-done.3.refs_4_ = f32[11,5,8,128]{3,2,1,0:T(8,128)S(1)} collective-permute-done((f32[11,5,8,128]{3,2,1,0:T(8,128)S(1)}, f32[11,5,8,128]{3,2,1,0:T(8,128)S(1)}, u32[]{:S(2)}, u32[]{:S(2)}) %collective-permute-start.3) | collective-permute-done | bytes 225312 | tf_op jit(solution)/shard_map/ppermute | solution.py:402
  17.0 1.5 %collective-permute-start.4 = (f32[11,5,8,128]{3,2,1,0:T(8,128)S(1)}, f32[11,5,8,128]{3,2,1,0:T(8,128)S(1)}, u32[]{:S(2)}, u32[]{:S(2)}) collective-permute-start(f32[11,5,8,128]{3,2,1,0:T(8,128)S(1)} %collective-permute-done.3.refs_4_), channel_id=1, source_target_pairs={{0,16},{1,17},{2,18},{3,19},{4,20},{5,21},{6,22},{7,23},{8,24},{9,... | collective-permute-start | bytes 675848 | tf_op jit(solution)/shard_map/ppermute | solution.py:402
  18.5 0.0 collective-permute-done.5.refs_6_
  18.5 0.0 collective-permute-start.6
  18.5 0.0 collective-permute-done.refs_1_
  18.5 0.0 collective-permute-done.2.refs_3_
  18.5 1.1 %collective-permute-done.4.refs_5_ = f32[11,5,8,128]{3,2,1,0:T(8,128)S(1)} collective-permute-done((f32[11,5,8,128]{3,2,1,0:T(8,128)S(1)}, f32[11,5,8,128]{3,2,1,0:T(8,128)S(1)}, u32[]{:S(2)}, u32[]{:S(2)}) %collective-permute-start.4) | collective-permute-done | bytes 225312 | tf_op jit(solution)/shard_map/ppermute | solution.py:402
  19.6 0.4 collective-permute-done.6.refs_7_
  20.0 1.7 %reorder.1 = (f32[960,128]{1,0:T(8,128)S(1)}, f32[360,128]{1,0:T(8,128)S(1)}, f32[360,128]{1,0:T(8,128)S(1)}, f32[360,128]{1,0:T(8,128)S(1)}, f32[360,128]{1,0:T(8,128)S(1)}) custom-call(s32[3]{0:T(128)S(1)} %pad_add_fusion.pos.refs_0_, s32[88]{0:T(128)S(1)} %get-tuple-element.31.rows, f32[11,5,8,128]{3,2,1,0:T(8,128)S(1)} %get-tuple-element.32.refs_0_, ...), custom_call_target="tpu_custom_call" | custom-call | tf_op jit(solution)/shard_map/reorder/pallas_call | solution.py:441
  21.7 2.1 %collective-permute-start.9 = (f32[360,128]{1,0:T(8,128)S(1)}, f32[360,128]{1,0:T(8,128)S(1)}, u32[]{:S(2)}, u32[]{:S(2)}) collective-permute-start(f32[360,128]{1,0:T(8,128)S(1)} %get-tuple-element.39), channel_id=1, source_target_pairs={{0,96},{1,97},{2,98},{3,99},{4,100},{5,101},{6,102},{7,103},{8,104... | collective-permute-start | bytes 552968 | tf_op jit(solution)/shard_map/ppermute | solution.py:402
  23.7 5.8 %collective-permute-start.10 = (f32[360,128]{1,0:T(8,128)S(1)}, f32[360,128]{1,0:T(8,128)S(1)}, u32[]{:S(2)}, u32[]{:S(2)}) collective-permute-start(f32[360,128]{1,0:T(8,128)S(1)} %get-tuple-element.40), channel_id=1, source_target_pairs={{0,127},{1,112},{2,113},{3,114},{4,115},{5,116},{6,117},{7,118},{8... | collective-permute-start | bytes 552968 | tf_op jit(solution)/shard_map/ppermute | solution.py:402
  29.6 0.0 collective-permute-start.7
  29.6 1.7 %collective-permute-start.8 = (f32[360,128]{1,0:T(8,128)S(1)}, f32[360,128]{1,0:T(8,128)S(1)}, u32[]{:S(2)}, u32[]{:S(2)}) collective-permute-start(f32[360,128]{1,0:T(8,128)S(1)} %get-tuple-element.38), channel_id=1, source_target_pairs={{0,47},{1,32},{2,33},{3,34},{4,35},{5,36},{6,37},{7,38},{8,39},{9,... | collective-permute-start | bytes 552968 | tf_op jit(solution)/shard_map/ppermute | solution.py:402
  31.3 0.0 collective-permute-done.9.y_in
  31.3 5.0 %collective-permute-done.10.y_out = f32[360,128]{1,0:T(8,128)S(1)} collective-permute-done((f32[360,128]{1,0:T(8,128)S(1)}, f32[360,128]{1,0:T(8,128)S(1)}, u32[]{:S(2)}, u32[]{:S(2)}) %collective-permute-start.10) | collective-permute-done | bytes 184352 | tf_op jit(solution)/shard_map/ppermute | solution.py:402
  36.3 0.6 corners.1
  36.9 0.8 %collective-permute-start.11 = (f32[120,128]{1,0:T(8,128)S(1)}, f32[120,128]{1,0:T(8,128)S(1)}, u32[]{:S(2)}, u32[]{:S(2)}) collective-permute-start(f32[120,128]{1,0:T(8,128)S(1)} %get-tuple-element.47), channel_id=1, source_target_pairs={{0,47},{1,32},{2,33},{3,34},{4,35},{5,36},{6,37},{7,38},{8,39},{9,... | collective-permute-start | bytes 184328 | tf_op jit(solution)/shard_map/ppermute | solution.py:402
  37.7 0.0 collective-permute-start.12
  37.7 1.5 %collective-permute-done.7.x_in = f32[360,128]{1,0:T(8,128)S(1)} collective-permute-done((f32[360,128]{1,0:T(8,128)S(1)}, f32[360,128]{1,0:T(8,128)S(1)}, u32[]{:S(2)}, u32[]{:S(2)}) %collective-permute-start.7) | collective-permute-done | bytes 184352 | tf_op jit(solution)/shard_map/ppermute | solution.py:402
  39.2 1.0 %collective-permute-done.8.x_out = f32[360,128]{1,0:T(8,128)S(1)} collective-permute-done((f32[360,128]{1,0:T(8,128)S(1)}, f32[360,128]{1,0:T(8,128)S(1)}, u32[]{:S(2)}, u32[]{:S(2)}) %collective-permute-start.8) | collective-permute-done | bytes 184352 | tf_op jit(solution)/shard_map/ppermute | solution.py:402
  40.1 3.7 %begin.1 = (f32[1680,128]{1,0:T(8,128)S(1)}, f32[1680,128]{1,0:T(8,128)S(1)}, f32[1680,128]{1,0:T(8,128)S(1)}, f32[1680,128]{1,0:T(8,128)S(1)}, f32[1680,128]{1,0:T(8,128)S(1)}, /*index=5*/f32[1680,128]{1,0:T(8,128)S(1)}) custom-call(s32[3]{0:T(128)S(1)} %pad_add_fusion.pos.refs_0_, f32[960,128]{1,0:T(8,128)S(1)} %get-tuple-element.36.cur, ...), custom_call_target="tpu_custom_call" | custom-call | bytes 10000000 | tf_op jit(solution)/shard_map/begin/pallas_call | solution.py:481
  43.9 0.4 collective-permute-done.11.refs_4_
  44.3 0.0 collective-permute-done.12.refs_5_
  44.3 5.2 %finish.1.mine = f32[24,5,8,128]{3,2,1,0:T(8,128)S(1)} custom-call(s32[3]{0:T(128)S(1)} %pad_add_fusion.pos.refs_0_, f32[1680,128]{1,0:T(8,128)S(1)} %get-tuple-element.41.main, f32[1680,128]{1,0:T(8,128)S(1)} %get-tuple-element.42.side_rows, f32[1680,128]{1,0:T(8,128)S(1)} %get-tuple-element.43.refs_0_, f32[1680,128]{1,0:T(8,128)S(1)} %get-tuple-element.44.refs_1_, ...), custom_call_target="tpu_custom_call" | custom-call | tf_op jit(solution)/shard_map/finish/pallas_call | solution.py:490
  49.5 1.6 %collective-permute-start.13 = (f32[24,5,8,128]{3,2,1,0:T(8,128)S(1)}, f32[24,5,8,128]{3,2,1,0:T(8,128)S(1)}, u32[]{:S(2)}, u32[]{:S(2)}) collective-permute-start(f32[24,5,8,128]{3,2,1,0:T(8,128)S(1)} %finish.1.mine), channel_id=1, source_target_pairs={{0,16},{1,17},{2,18},{3,19},{4,20},{5,21},{6,22},{7,23},{8,24},{9,... | collective-permute-start | bytes 1474568 | tf_op jit(solution)/shard_map/ppermute | solution.py:402
  51.1 1.5 %collective-permute-done.13.other = f32[24,5,8,128]{3,2,1,0:T(8,128)S(1)} collective-permute-done((f32[24,5,8,128]{3,2,1,0:T(8,128)S(1)}, f32[24,5,8,128]{3,2,1,0:T(8,128)S(1)}, u32[]{:S(2)}, u32[]{:S(2)}) %collective-permute-start.13) | collective-permute-done | bytes 491552 | tf_op jit(solution)/shard_map/ppermute | solution.py:402
  52.6 0.7 %pack_out.1 = (f32[7,5,8,128]{3,2,1,0:T(8,128)S(1)}, f32[7,5,8,128]{3,2,1,0:T(8,128)S(1)}, f32[7,5,8,128]{3,2,1,0:T(8,128)S(1)}, f32[7,5,8,128]{3,2,1,0:T(8,128)S(1)}) custom-call(s32[3]{0:T(128)S(1)} %pad_add_fusion.pos.refs_0_, s32[64]{0:T(128)S(1)} %get-tuple-element.30.final, f32[24,5,8,128]{3,2,1,0:T(8,128)S(1)} %finish.1.mine, ...), custom_call_target="tpu_custom_call" | custom-call | tf_op jit(solution)/shard_map/pack_out/pallas_call | solution.py:500
  53.3 1.3 %collective-permute-start.14 = (f32[7,5,8,128]{3,2,1,0:T(8,128)S(1)}, f32[7,5,8,128]{3,2,1,0:T(8,128)S(1)}, u32[]{:S(2)}, u32[]{:S(2)}) collective-permute-start(f32[7,5,8,128]{3,2,1,0:T(8,128)S(1)} %get-tuple-element.49), channel_id=1, source_target_pairs={{0,64},{1,65},{2,66},{3,67},{4,68},{5,69},{6,70},{7,71},{8,72},{9,... | collective-permute-start | bytes 430088 | tf_op jit(solution)/shard_map/ppermute | solution.py:402
  54.6 0.0 collective-permute-start.15
  54.6 2.0 %collective-permute-start.16 = (f32[7,5,8,128]{3,2,1,0:T(8,128)S(1)}, f32[7,5,8,128]{3,2,1,0:T(8,128)S(1)}, u32[]{:S(2)}, u32[]{:S(2)}) collective-permute-start(f32[7,5,8,128]{3,2,1,0:T(8,128)S(1)} %get-tuple-element.51), channel_id=1, source_target_pairs={{0,96},{1,97},{2,98},{3,99},{4,100},{5,101},{6,102},{7,103},{8,104... | collective-permute-start | bytes 430088 | tf_op jit(solution)/shard_map/ppermute | solution.py:402
  56.6 1.2 %unpack_out.2.refs_4_ = f32[7,5,16,256]{3,2,1,0:T(8,128)} custom-call(s32[3]{0:T(128)S(1)} %pad_add_fusion.pos.refs_0_, f32[7,5,8,128]{3,2,1,0:T(8,128)S(1)} %get-tuple-element.52.refs_1_), custom_call_target="tpu_custom_call" | custom-call | tf_op jit(solution)/shard_map/unpack_out/pallas_call | solution.py:513
  57.8 2.0 %collective-permute-done.14.refs_1_ = f32[7,5,8,128]{3,2,1,0:T(8,128)S(1)} collective-permute-done((f32[7,5,8,128]{3,2,1,0:T(8,128)S(1)}, f32[7,5,8,128]{3,2,1,0:T(8,128)S(1)}, u32[]{:S(2)}, u32[]{:S(2)}) %collective-permute-start.14) | collective-permute-done | bytes 143392 | tf_op jit(solution)/shard_map/ppermute | solution.py:402
  59.8 1.2 %collective-permute-done.15.refs_2_ = f32[7,5,8,128]{3,2,1,0:T(8,128)S(1)} collective-permute-done((f32[7,5,8,128]{3,2,1,0:T(8,128)S(1)}, f32[7,5,8,128]{3,2,1,0:T(8,128)S(1)}, u32[]{:S(2)}, u32[]{:S(2)}) %collective-permute-start.15) | collective-permute-done | bytes 143392 | tf_op jit(solution)/shard_map/ppermute | solution.py:402
  61.0 2.6 %collective-permute-done.16.refs_3_ = f32[7,5,8,128]{3,2,1,0:T(8,128)S(1)} collective-permute-done((f32[7,5,8,128]{3,2,1,0:T(8,128)S(1)}, f32[7,5,8,128]{3,2,1,0:T(8,128)S(1)}, u32[]{:S(2)}, u32[]{:S(2)}) %collective-permute-start.16) | collective-permute-done | bytes 143392 | tf_op jit(solution)/shard_map/ppermute | solution.py:402
  63.6 1.3 %unpack_out.3 = f32[7,5,16,256]{3,2,1,0:T(8,128)} custom-call(s32[3]{0:T(128)S(1)} %pad_add_fusion.pos.refs_0_, f32[7,5,8,128]{3,2,1,0:T(8,128)S(1)} %collective-permute-done.14.refs_1_, f32[7,5,8,128]{3,2,1,0:T(8,128)S(1)} %collective-permute-done.15.refs_2_, f32[7,5,8,128]{3,2,1,0:T(8,128)S(1)} %collective-permute-done.16.refs_3_, ...), custom_call_target="tpu_custom_call", output_to_operand_aliasing={{}: (4, {})} | custom-call | tf_op jit(solution)/shard_map/unpack_out/pallas_call | solution.py:513
Async XLA Ops:
  0.1 1.2 %copy-start = (f32[11,5,16,256]{3,2,1,0:T(8,128)S(1)}, f32[11,5,16,256]{3,2,1,0:T(8,128)}, u32[]{:S(2)}) copy-start(f32[11,5,16,256]{3,2,1,0:T(8,128)} %cells.1) | copy-start | bytes 2703364
  1.3 5.9 %copy-start.1 = (s32[128,11]{0,1:T(8,128)S(1)}, s32[128,11]{0,1:T(8,128)}, u32[]{:S(2)}) copy-start(s32[128,11]{0,1:T(8,128)} %param.3) | copy-start | bytes 16900
  1.9 9.7 %collective-permute-start.1 = (f32[11,5,8,128]{3,2,1,0:T(8,128)S(1)}, f32[11,5,8,128]{3,2,1,0:T(8,128)S(1)}, u32[]{:S(2)}, u32[]{:S(2)}) collective-permute-start(f32[11,5,8,128]{3,2,1,0:T(8,128)S(1)} %get-tuple-element.33), channel_id=1, source_target_pairs={{0,64},{1,65},{2,66},{3,67},{4,68},{5,69},{6,70},{7,71},{8,72},{9,... | collective-permute-start | bytes 675848 | tf_op jit(solution)/shard_map/ppermute | solution.py:402
  6.4 10.5 %collective-permute-start.3 = (f32[11,5,8,128]{3,2,1,0:T(8,128)S(1)}, f32[11,5,8,128]{3,2,1,0:T(8,128)S(1)}, u32[]{:S(2)}, u32[]{:S(2)}) collective-permute-start(f32[11,5,8,128]{3,2,1,0:T(8,128)S(1)} %get-tuple-element.34), channel_id=1, source_target_pairs={{0,32},{1,33},{2,34},{3,35},{4,36},{5,37},{6,38},{7,39},{8,40},{9,... | collective-permute-start | bytes 675848 | tf_op jit(solution)/shard_map/ppermute | solution.py:402
  7.2 11.3 %collective-permute-start.5 = (f32[11,5,8,128]{3,2,1,0:T(8,128)S(1)}, f32[11,5,8,128]{3,2,1,0:T(8,128)S(1)}, u32[]{:S(2)}, u32[]{:S(2)}) collective-permute-start(f32[11,5,8,128]{3,2,1,0:T(8,128)S(1)} %get-tuple-element.35), channel_id=1, source_target_pairs={{0,96},{1,97},{2,98},{3,99},{4,100},{5,101},{6,102},{7,103},{8,104... | collective-permute-start | bytes 675848 | tf_op jit(solution)/shard_map/ppermute | solution.py:402
  10.3 8.2 %collective-permute-start = (f32[11,5,8,128]{3,2,1,0:T(8,128)S(1)}, f32[11,5,8,128]{3,2,1,0:T(8,128)S(1)}, u32[]{:S(2)}, u32[]{:S(2)}) collective-permute-start(f32[11,5,8,128]{3,2,1,0:T(8,128)S(1)} %get-tuple-element.32.refs_0_), channel_id=1, source_target_pairs={{0,16},{1,17},{2,18},{3,19},{4,20},{5,21},{6,22},{7,23},{8,24},{9,... | collective-permute-start | bytes 675848 | tf_op jit(solution)/shard_map/ppermute | solution.py:402
  11.7 6.8 %collective-permute-start.2 = (f32[11,5,8,128]{3,2,1,0:T(8,128)S(1)}, f32[11,5,8,128]{3,2,1,0:T(8,128)S(1)}, u32[]{:S(2)}, u32[]{:S(2)}) collective-permute-start(f32[11,5,8,128]{3,2,1,0:T(8,128)S(1)} %collective-permute-done.1.refs_2_), channel_id=1, source_target_pairs={{0,16},{1,17},{2,18},{3,19},{4,20},{5,21},{6,22},{7,23},{8,24},{9,... | collective-permute-start | bytes 675848 | tf_op jit(solution)/shard_map/ppermute | solution.py:402
  17.0 2.7 %collective-permute-start.4 = (f32[11,5,8,128]{3,2,1,0:T(8,128)S(1)}, f32[11,5,8,128]{3,2,1,0:T(8,128)S(1)}, u32[]{:S(2)}, u32[]{:S(2)}) collective-permute-start(f32[11,5,8,128]{3,2,1,0:T(8,128)S(1)} %collective-permute-done.3.refs_4_), channel_id=1, source_target_pairs={{0,16},{1,17},{2,18},{3,19},{4,20},{5,21},{6,22},{7,23},{8,24},{9,... | collective-permute-start | bytes 675848 | tf_op jit(solution)/shard_map/ppermute | solution.py:402
  18.5 1.5 %collective-permute-start.6 = (f32[11,5,8,128]{3,2,1,0:T(8,128)S(1)}, f32[11,5,8,128]{3,2,1,0:T(8,128)S(1)}, u32[]{:S(2)}, u32[]{:S(2)}) collective-permute-start(f32[11,5,8,128]{3,2,1,0:T(8,128)S(1)} %collective-permute-done.5.refs_6_), channel_id=1, source_target_pairs={{0,16},{1,17},{2,18},{3,19},{4,20},{5,21},{6,22},{7,23},{8,24},{9,... | collective-permute-start | bytes 675848 | tf_op jit(solution)/shard_map/ppermute | solution.py:402
  21.7 9.6 %collective-permute-start.9 = (f32[360,128]{1,0:T(8,128)S(1)}, f32[360,128]{1,0:T(8,128)S(1)}, u32[]{:S(2)}, u32[]{:S(2)}) collective-permute-start(f32[360,128]{1,0:T(8,128)S(1)} %get-tuple-element.39), channel_id=1, source_target_pairs={{0,96},{1,97},{2,98},{3,99},{4,100},{5,101},{6,102},{7,103},{8,104... | collective-permute-start | bytes 552968 | tf_op jit(solution)/shard_map/ppermute | solution.py:402
  23.7 12.6 %collective-permute-start.10 = (f32[360,128]{1,0:T(8,128)S(1)}, f32[360,128]{1,0:T(8,128)S(1)}, u32[]{:S(2)}, u32[]{:S(2)}) collective-permute-start(f32[360,128]{1,0:T(8,128)S(1)} %get-tuple-element.40), channel_id=1, source_target_pairs={{0,127},{1,112},{2,113},{3,114},{4,115},{5,116},{6,117},{7,118},{8... | collective-permute-start | bytes 552968 | tf_op jit(solution)/shard_map/ppermute | solution.py:402
  29.6 9.6 %collective-permute-start.7 = (f32[360,128]{1,0:T(8,128)S(1)}, f32[360,128]{1,0:T(8,128)S(1)}, u32[]{:S(2)}, u32[]{:S(2)}) collective-permute-start(f32[360,128]{1,0:T(8,128)S(1)} %get-tuple-element.37), channel_id=1, source_target_pairs={{0,32},{1,33},{2,34},{3,35},{4,36},{5,37},{6,38},{7,39},{8,40},{9,... | collective-permute-start | bytes 552968 | tf_op jit(solution)/shard_map/ppermute | solution.py:402
  29.6 10.6 %collective-permute-start.8 = (f32[360,128]{1,0:T(8,128)S(1)}, f32[360,128]{1,0:T(8,128)S(1)}, u32[]{:S(2)}, u32[]{:S(2)}) collective-permute-start(f32[360,128]{1,0:T(8,128)S(1)} %get-tuple-element.38), channel_id=1, source_target_pairs={{0,47},{1,32},{2,33},{3,34},{4,35},{5,36},{6,37},{7,38},{8,39},{9,... | collective-permute-start | bytes 552968 | tf_op jit(solution)/shard_map/ppermute | solution.py:402
  36.9 7.4 %collective-permute-start.11 = (f32[120,128]{1,0:T(8,128)S(1)}, f32[120,128]{1,0:T(8,128)S(1)}, u32[]{:S(2)}, u32[]{:S(2)}) collective-permute-start(f32[120,128]{1,0:T(8,128)S(1)} %get-tuple-element.47), channel_id=1, source_target_pairs={{0,47},{1,32},{2,33},{3,34},{4,35},{5,36},{6,37},{7,38},{8,39},{9,... | collective-permute-start | bytes 184328 | tf_op jit(solution)/shard_map/ppermute | solution.py:402
  37.7 6.6 %collective-permute-start.12 = (f32[120,128]{1,0:T(8,128)S(1)}, f32[120,128]{1,0:T(8,128)S(1)}, u32[]{:S(2)}, u32[]{:S(2)}) collective-permute-start(f32[120,128]{1,0:T(8,128)S(1)} %get-tuple-element.48), channel_id=1, source_target_pairs={{0,32},{1,33},{2,34},{3,35},{4,36},{5,37},{6,38},{7,39},{8,40},{9,... | collective-permute-start | bytes 184328 | tf_op jit(solution)/shard_map/ppermute | solution.py:402
  49.5 3.1 %collective-permute-start.13 = (f32[24,5,8,128]{3,2,1,0:T(8,128)S(1)}, f32[24,5,8,128]{3,2,1,0:T(8,128)S(1)}, u32[]{:S(2)}, u32[]{:S(2)}) collective-permute-start(f32[24,5,8,128]{3,2,1,0:T(8,128)S(1)} %finish.1.mine), channel_id=1, source_target_pairs={{0,16},{1,17},{2,18},{3,19},{4,20},{5,21},{6,22},{7,23},{8,24},{9,... | collective-permute-start | bytes 1474568 | tf_op jit(solution)/shard_map/ppermute | solution.py:402
  53.3 6.6 %collective-permute-start.14 = (f32[7,5,8,128]{3,2,1,0:T(8,128)S(1)}, f32[7,5,8,128]{3,2,1,0:T(8,128)S(1)}, u32[]{:S(2)}, u32[]{:S(2)}) collective-permute-start(f32[7,5,8,128]{3,2,1,0:T(8,128)S(1)} %get-tuple-element.49), channel_id=1, source_target_pairs={{0,64},{1,65},{2,66},{3,67},{4,68},{5,69},{6,70},{7,71},{8,72},{9,... | collective-permute-start | bytes 430088 | tf_op jit(solution)/shard_map/ppermute | solution.py:402
  54.6 6.4 %collective-permute-start.15 = (f32[7,5,8,128]{3,2,1,0:T(8,128)S(1)}, f32[7,5,8,128]{3,2,1,0:T(8,128)S(1)}, u32[]{:S(2)}, u32[]{:S(2)}) collective-permute-start(f32[7,5,8,128]{3,2,1,0:T(8,128)S(1)} %get-tuple-element.50), channel_id=1, source_target_pairs={{0,32},{1,33},{2,34},{3,35},{4,36},{5,37},{6,38},{7,39},{8,40},{9,... | collective-permute-start | bytes 430088 | tf_op jit(solution)/shard_map/ppermute | solution.py:402
  54.6 9.0 %collective-permute-start.16 = (f32[7,5,8,128]{3,2,1,0:T(8,128)S(1)}, f32[7,5,8,128]{3,2,1,0:T(8,128)S(1)}, u32[]{:S(2)}, u32[]{:S(2)}) collective-permute-start(f32[7,5,8,128]{3,2,1,0:T(8,128)S(1)} %get-tuple-element.51), channel_id=1, source_target_pairs={{0,96},{1,97},{2,98},{3,99},{4,100},{5,101},{6,102},{7,103},{8,104... | collective-permute-start | bytes 430088 | tf_op jit(solution)/shard_map/ppermute | solution.py:402
